TPU v7x, 32 devices: a whole 2x2x4 slice. The times are simulated.
32 devices in a mesh: dp: 2 (over core), row: 8 (over z, y), col: 2 (over x).
Axes of the slice: x: 2, y: 2, z: 4, core: 2. Of those that a mesh axis runs over, the one named last changes fastest.
Arguments:
- features: bfloat16 [2, 64, 128, 512], P('dp', None, 'row', 'col'), may hold values from -6 to 6
- grad_out: bfloat16 [2, 64, 128, 512], P('dp', None, 'row', 'col'), may hold values from -6 to 6
- kernel_one: bfloat16 [3, 3, 64, 64], replicated, may hold values from -0.25 to 0.25
- kernel_two: bfloat16 [3, 3, 64, 64], replicated, may hold values from -0.25 to 0.25
Outputs:
- grad_features: bfloat16 [2, 64, 128, 512], P('dp', None, 'row', 'col')
- grad_kernel_one: float32 [3, 3, 64, 64], replicated
- grad_kernel_two: float32 [3, 3, 64, 64], replicated
All inputs are finite; a program needn't handle non-finite values.
Results may differ from a plain program's by a relative error of at most 0.0061.
Values may be sent and summed in bfloat16 or wider, within the bound.
No kernel may reach another device: no remote copies, remote signals or barrier semaphores. Data moves between devices by JAX's collectives and lax.ppermute only.
A program may use at most 64 MiB of HBM per device.

v0:
```python
import jax
import jax.numpy as jnp
from jax import lax
from jax.sharding import PartitionSpec as P


def extended(cells, sides, width):
    for axis, dim in sides:
        count = lax.axis_size(axis)
        ends = count - 1
        head = lax.slice_in_dim(cells, 0, width, axis=dim)
        tail = lax.slice_in_dim(cells, cells.shape[dim] - width, cells.shape[dim], axis=dim)
        cells = jnp.concatenate(
            [
                lax.ppermute(tail, axis, [(i, (i + 1) % count) for i in range(ends)]),
                cells,
                lax.ppermute(head, axis, [((i + 1) % count, i) for i in range(ends)]),
            ],
            axis=dim,
        )
    return cells


def convolve(padded, kernel, rows, cols):
    total = jnp.zeros((padded.shape[0], kernel.shape[2], rows, cols), jnp.float32)
    for ky in range(3):
        for kx in range(3):
            total = total + jnp.einsum(
                "oi,sihw->sohw",
                kernel[ky, kx],
                padded[:, :, ky : ky + rows, kx : kx + cols],
                preferred_element_type=jnp.float32,
            )
    return total


def transposed(padded, kernel, rows, cols):
    total = jnp.zeros((padded.shape[0], kernel.shape[3], rows, cols), jnp.float32)
    for ky in range(3):
        for kx in range(3):
            total = total + jnp.einsum(
                "oi,sohw->sihw",
                kernel[ky, kx],
                padded[:, :, 2 - ky : 2 - ky + rows, 2 - kx : 2 - kx + cols],
                preferred_element_type=jnp.float32,
            )
    return total


def kernel_grad(padded, delta, rows, cols):
    taps = []
    for ky in range(3):
        line = []
        for kx in range(3):
            line.append(
                jnp.einsum(
                    "sohw,sihw->oi",
                    delta,
                    padded[:, :, ky : ky + rows, kx : kx + cols],
                    preferred_element_type=jnp.float32,
                )
            )
        taps.append(jnp.stack(line))
    return jnp.stack(taps)


def dsilu(value):
    sig = jax.nn.sigmoid(value)
    return sig * (1.0 + value * (1.0 - sig))


def inside_mask(rows, cols, margin):
    row_pos = lax.axis_index("row") * rows - margin + jnp.arange(rows + 2 * margin, dtype=jnp.int32)
    col_pos = lax.axis_index("col") * cols - margin + jnp.arange(cols + 2 * margin, dtype=jnp.int32)
    row_ok = (row_pos >= 0) & (row_pos < rows * lax.axis_size("row"))
    col_ok = (col_pos >= 0) & (col_pos < cols * lax.axis_size("col"))
    return (row_ok[:, None] & col_ok[None, :]).astype(jnp.float32)


def shards(features, grad_out, kernel_one, kernel_two):
    slides, chans, rows, cols = features.shape
    joined = jnp.concatenate((features, grad_out), axis=1)
    wide = extended(joined, (("row", 2), ("col", 3)), 4)
    feat_four = wide[:, :chans]
    grad_two_rim = wide[:, chans:, 2:-2, 2:-2]
    pre_three = convolve(feat_four, kernel_one, rows + 6, cols + 6)
    hidden_three = (jax.nn.silu(pre_three) * inside_mask(rows, cols, 3)).astype(jnp.bfloat16)
    pre_two_rim = convolve(hidden_three, kernel_two, rows + 4, cols + 4)
    delta_two_rim = (grad_two_rim.astype(jnp.float32) * dsilu(pre_two_rim)).astype(jnp.bfloat16)
    back_rim = transposed(delta_two_rim, kernel_two, rows + 2, cols + 2)
    pre_one_rim = pre_three[:, :, 2:-2, 2:-2]
    delta_one_pad = (back_rim * dsilu(pre_one_rim) * inside_mask(rows, cols, 1)).astype(
        jnp.bfloat16
    )
    grad_features = transposed(delta_one_pad, kernel_one, rows, cols).astype(jnp.bfloat16)
    hid_pad = hidden_three[:, :, 2:-2, 2:-2]
    delta_two = delta_two_rim[:, :, 2:-2, 2:-2]
    feat_pad = feat_four[:, :, 3:-3, 3:-3]
    delta_one = delta_one_pad[:, :, 1:-1, 1:-1]
    term_two = kernel_grad(hid_pad, delta_two, rows, cols)
    term_one = kernel_grad(feat_pad, delta_one, rows, cols)
    summed_one, summed_two = lax.psum((term_one, term_two), ("dp", "row", "col"))
    count = slides * lax.axis_size("dp") * rows * lax.axis_size("row") * cols * lax.axis_size("col")
    scale = 1.0 / jnp.sqrt(jnp.float32(count))
    return (grad_features, summed_one * scale, summed_two * scale)


def solution(mesh):
    return jax.shard_map(
        shards,
        mesh=mesh,
        in_specs=(P("dp", None, "row", "col"), P("dp", None, "row", "col"), P(), P()),
        out_specs=(P("dp", None, "row", "col"), P(), P()),
        check_vma=False,
    )
```

profile of v0, /device:TPU:0, one launch (start us, length us, event | category | flops | bytes accessed | tf_op | source)
XLA Modules:
  0.0 211.5 jit_solution(18266908912762243592)
XLA Ops:
  7.2 1.2 copy_dynamic-update-slice_fusion.1
  8.4 1.2 copy_dynamic-update-slice_fusion
  9.7 4.9 %collective-permute-start = (bf16[1,128,4,256]{3,1,2,0:T(8,128)(2,1)S(1)}, bf16[1,128,4,256]{3,1,2,0:T(8,128)(2,1)S(1)}, u32[]{:S(2)}, u32[]{:S(2)}) collective-permute-start(bf16[1,128,4,256]{3,1,2,0:T(8,128)(2,1)S(1)} %get-tuple-element.13), channel_id=1, source_target_pairs={{0,2},{2,4},{4,6},{6,8},{8,10},{10,12},{12,14},{1,3},{3,5},{5,7},{... | collective-permute-start | bytes 786440 | tf_op jit(solution)/shard_map/ppermute | solution.py:15
  14.6 1.3 collective-permute-start.1
  16.0 9.7 %collective-permute-done = bf16[1,128,4,256]{3,1,2,0:T(8,128)(2,1)S(1)} collective-permute-done((bf16[1,128,4,256]{3,1,2,0:T(8,128)(2,1)S(1)}, bf16[1,128,4,256]{3,1,2,0:T(8,128)(2,1)S(1)}, u32[]{:S(2)}, u32[]{:S(2)}) %collective-permute-start) | collective-permute-done | bytes 262176 | tf_op jit(solution)/shard_map/ppermute | solution.py:15
  26.6 3.4 %collective-permute-start.2 = (bf16[1,128,24,4]{1,2,3,0:T(8,128)(2,1)S(1)}, bf16[1,128,24,4]{1,2,3,0:T(8,128)(2,1)S(1)}, u32[]{:S(2)}, u32[]{:S(2)}) collective-permute-start(bf16[1,128,24,4]{1,2,3,0:T(8,128)(2,1)S(1)} %copy.31), channel_id=1, source_target_pairs={{0,1},{2,3},{4,5},{6,7},{8,9},{10,11},{12,13},{14,15},{16,17},{18,... | collective-permute-start | bytes 73736 | tf_op jit(solution)/shard_map/ppermute | solution.py:15
  30.3 1.3 collective-permute-start.3
  32.1 3.9 %collective-permute-done.3 = bf16[1,128,24,4]{1,2,3,0:T(8,128)(2,1)S(1)} collective-permute-done((bf16[1,128,24,4]{1,2,3,0:T(8,128)(2,1)S(1)}, bf16[1,128,24,4]{1,2,3,0:T(8,128)(2,1)S(1)}, u32[]{:S(2)}, u32[]{:S(2)}) %collective-permute-start.3) | collective-permute-done | bytes 24608 | tf_op jit(solution)/shard_map/ppermute | solution.py:17
  36.5 2.3 %pad_maximum_fusion = bf16[1,128,24,264]{3,1,2,0:T(8,128)(2,1)S(1)} fusion(bf16[1,128,24,4]{3,1,2,0:T(8,128)(2,1)S(1)} %copy.34, bf16[1,128,4,256]{3,1,2,0:T(8,128)(2,1)S(1)} %collective-permute-done.1, bf16[1,128,16,256]{3,1,2,0:T(8,128)(2,1)S(1)} %copy_dynamic-update-slice_fusion, bf16[1,128,4,256]{3,1,2,0:T(8,128)(2,1)S(1)} %collective-permute-done, ...), kind=kLoop, calls=%fused_computation | loop fusion | flops 8110080 | bytes 3244032 | tf_op jit(solution)/shard_map/concatenate | solution.py:13
  38.8 0.5 fusion.11
  39.8 0.5 fusion.13
  40.3 0.5 fusion.14
  41.3 0.5 fusion.16
  41.8 0.5 fusion.17
  42.8 1.8 multiply_convert_fusion
  44.6 0.5 fusion.20
  45.5 0.5 fusion.22
  46.0 0.5 fusion.23
  47.0 0.5 fusion.25
  47.5 0.5 fusion.26
  48.4 2.0 fusion.6
  50.4 0.5 convolution_bitcast_fusion.5
  50.9 0.5 convolution_bitcast_fusion.4
  51.4 0.5 convolution_bitcast_fusion.3
  51.9 0.7 convolution_bitcast_fusion.8
  52.7 0.5 convolution_bitcast_fusion.7
  53.2 0.5 convolution_bitcast_fusion.6
  53.7 0.5 convolution_bitcast_fusion.2
  54.2 0.5 convolution_bitcast_fusion.1
  54.7 0.5 convolution_bitcast_fusion
  56.7 0.5 fusion.31
  57.2 0.5 fusion.32
  58.2 0.5 fusion.34
  58.7 0.5 fusion.35
  59.2 2.1 fusion.8
  64.5 1.4 convolution_add_fusion.1
  65.9 0.7 pad_maximum_fusion.15
  66.7 0.6 convolution_bitcast_fusion.11
  67.2 0.6 convolution_bitcast_fusion.9
  68.2 0.8 convolution_bitcast_fusion.14
  69.0 0.6 convolution_bitcast_fusion.12
  69.6 0.6 convolution_bitcast_fusion.17
  70.2 0.6 convolution_bitcast_fusion.15
  71.2 0.7 pad_maximum_fusion.14
  72.4 1.1 copy.56
  73.4 127.8 %all-reduce.3.cloned.1.call-done = (f32[3,3,64,64]{3,2,1,0:T(8,128)}, f32[3,3,64,64]{3,2,1,0:T(8,128)}) async-done(((f32[3,3,64,64]{3,2,1,0:T(8,128)}, f32[3,3,64,64]{3,2,1,0:T(8,128)}), (f32[3,3,64,64]{3,2,1,0:T(8,128)}, f32[3,3,64,64]{3,2,1,0:T(8,128)})) %all-reduce.3.cloned.1.call-update) | async-done | bytes 294928 | tf_op jit(solution)/shard_map/psum | solution.py:102
  201.2 1.7 broadcast_multiply_fusion
  202.9 1.7 broadcast_multiply_fusion.1
  (54 shorter events, 11.0 us)
Async XLA Ops:
  7.2 194.1 %all-reduce.3.cloned.1.call-start = ((), (), s32[]{:S(2)}) async-start(), calls=%async_computation | async-start | bytes 1179648 | tf_op jit(solution)/shard_map/psum | solution.py:102
  9.7 16.0 %collective-permute-start = (bf16[1,128,4,256]{3,1,2,0:T(8,128)(2,1)S(1)}, bf16[1,128,4,256]{3,1,2,0:T(8,128)(2,1)S(1)}, u32[]{:S(2)}, u32[]{:S(2)}) collective-permute-start(bf16[1,128,4,256]{3,1,2,0:T(8,128)(2,1)S(1)} %get-tuple-element.13), channel_id=1, source_target_pairs={{0,2},{2,4},{4,6},{6,8},{8,10},{10,12},{12,14},{1,3},{3,5},{5,7},{... | collective-permute-start | bytes 786440 | tf_op jit(solution)/shard_map/ppermute | solution.py:15
  14.6 11.2 %collective-permute-start.1 = (bf16[1,128,4,256]{3,1,2,0:T(8,128)(2,1)S(1)}, bf16[1,128,4,256]{3,1,2,0:T(8,128)(2,1)S(1)}, u32[]{:S(2)}, u32[]{:S(2)}) collective-permute-start(bf16[1,128,4,256]{3,1,2,0:T(8,128)(2,1)S(1)} %get-tuple-element.14), channel_id=1, source_target_pairs={{2,0},{4,2},{6,4},{8,6},{10,8},{12,10},{14,12},{3,1},{5,3},{7,5},{... | collective-permute-start | bytes 786440 | tf_op jit(solution)/shard_map/ppermute | solution.py:17
  26.6 5.1 %collective-permute-start.2 = (bf16[1,128,24,4]{1,2,3,0:T(8,128)(2,1)S(1)}, bf16[1,128,24,4]{1,2,3,0:T(8,128)(2,1)S(1)}, u32[]{:S(2)}, u32[]{:S(2)}) collective-permute-start(bf16[1,128,24,4]{1,2,3,0:T(8,128)(2,1)S(1)} %copy.31), channel_id=1, source_target_pairs={{0,1},{2,3},{4,5},{6,7},{8,9},{10,11},{12,13},{14,15},{16,17},{18,... | collective-permute-start | bytes 73736 | tf_op jit(solution)/shard_map/ppermute | solution.py:15
  30.3 5.7 %collective-permute-start.3 = (bf16[1,128,24,4]{1,2,3,0:T(8,128)(2,1)S(1)}, bf16[1,128,24,4]{1,2,3,0:T(8,128)(2,1)S(1)}, u32[]{:S(2)}, u32[]{:S(2)}) collective-permute-start(bf16[1,128,24,4]{1,2,3,0:T(8,128)(2,1)S(1)} %copy.32), channel_id=1, source_target_pairs={{1,0},{3,2},{5,4},{7,6},{9,8},{11,10},{13,12},{15,14},{17,16},{19,... | collective-permute-start | bytes 73736 | tf_op jit(solution)/shard_map/ppermute | solution.py:17
  36.5 2.3 %copy-start = (bf16[1,128,24,4]{3,1,2,0:T(8,128)(2,1)}, bf16[1,128,24,4]{3,1,2,0:T(8,128)(2,1)S(1)}, u32[]{:S(2)}) copy-start(bf16[1,128,24,4]{3,1,2,0:T(8,128)(2,1)S(1)} %copy.34) | copy-start | bytes 73732
  36.5 2.3 %copy-start.3 = (bf16[3,3,64,64]{3,2,1,0:T(8,128)(2,1)S(1)}, bf16[3,3,64,64]{3,2,1,0:T(8,128)(2,1)}, u32[]{:S(2)}) copy-start(bf16[3,3,64,64]{3,2,1,0:T(8,128)(2,1)} %param.6) | copy-start | bytes 221188
  42.8 1.8 copy-start.4
  59.2 2.5 %copy-start.5 = (bf16[1,64,16,256]{3,2,1,0:T(8,128)(2,1)S(1)}, bf16[1,64,16,256]{3,2,1,0:T(8,128)(2,1)}, u32[]{:S(2)}) copy-start(bf16[1,64,16,256]{3,2,1,0:T(8,128)(2,1)} %param.4) | copy-start | bytes 1572868
  65.9 1.4 copy-start.1
  70.8 1.2 copy-start.2
Sparse Core Ops, SparseCore 0:
  72.1 129.1 all-reduce.2
where the time goes:
time: 212 us; the launch traced here: 211 us
  waiting for transfers between devices  141 us (67%)
  matrix products  31.5 us (15%)
  between operations  14.6 us (7%)
  starting transfers between devices  10.9 us (5%)
  other arithmetic  7.62 us (4%)
  local copies, waits for them, and re-layouts  5.49 us (3%)
    psum x1, waiting for transfers between devices, shards(): lax.psum((term_one, term_two), ('dp', 'row', 'col'))  128 us
    dot_general x18, matrix products, convolve(): jnp.einsum('oi,sihw->sohw', kernel[ky, kx], padded[:, :, ky:ky + rows, kx...  11.4 us
    dot_general x18, matrix products, transposed(): jnp.einsum('oi,sohw->sihw', kernel[ky, kx], padded[:, :, 2 - ky:2 - ky +...  10.4 us
    ppermute x2, waiting for transfers between devices, extended(): lax.ppermute(tail, axis, [(i, (i + 1) % count) for i in range(ends)])  9.71 us
    dot_general x18, matrix products, kernel_grad(): jnp.einsum('sohw,sihw->oi', delta, padded[:, :, ky:ky + rows, kx:kx + col...  9.65 us
    ppermute x2, starting transfers between devices, extended(): lax.ppermute(tail, axis, [(i, (i + 1) % count) for i in range(ends)])  8.28 us
  transfers between devices with their start and end apart: 5, of which 3 were waited for; matrix products, arithmetic and copies ran while one was open for 1% of the time, Pallas kernels for 0%

commit v1 on v0

v1 whole, which is shorter than its diff:
```python
import jax
import jax.numpy as jnp
from jax import lax
from jax.experimental import pallas as pl
from jax.experimental.pallas import tpu as pltpu
from jax.sharding import PartitionSpec as P

BF = jnp.bfloat16
F32 = jnp.float32
AXES = ("dp", "row", "col")
LANES = 128
RIM = 16


def pair_exchange(low, high, axis):
    count = lax.axis_size(axis)
    even = lax.axis_index(axis) % 2 == 0
    got = []
    for parity in range(2):
        perm = []
        for i in range(parity, count - 1, 2):
            perm += [(i, i + 1), (i + 1, i)]
        if not perm:
            got.append(jnp.zeros_like(low))
            continue
        up = even if parity == 0 else jnp.logical_not(even)
        got.append(lax.ppermute(jnp.where(up, high, low), axis, perm))
    from_prev = jnp.where(even, got[1], got[0])
    from_next = jnp.where(even, got[0], got[1])
    return from_prev, from_next


def to_pairs(cells):
    _, chans, rows, cols = cells.shape
    part = cells[0].reshape(chans, rows // 2, 2, cols)
    return part.transpose(1, 3, 2, 0).reshape(rows // 2, cols, 2 * chans)


def from_pairs(pairs):
    count, cols, lanes = pairs.shape
    part = pairs.reshape(count, cols, 2, lanes // 2)
    return part.transpose(3, 0, 2, 1).reshape(1, lanes // 2, 2 * count, cols)


def banded(taps):
    chans = taps.shape[2]
    zero = jnp.zeros_like(taps[:1])
    both = jnp.stack([jnp.concatenate([taps, zero]), jnp.concatenate([zero, taps])])
    both = both.reshape(2, 2, 2, 3, chans, chans)
    return both.transpose(1, 3, 2, 4, 0, 5).reshape(12 * chans, 2 * chans)


def sigmoid(value):
    return 0.5 * jnp.tanh(0.5 * value) + 0.5


def store_shifts(value, tmp, out, index):
    wide = value.shape[0]
    tmp[8 : 8 + wide] = value
    tmp[0:8] = value[wide - 8 :]
    tmp[8 + wide :] = value[:8]
    out[index, 0] = tmp[7 : 7 + wide].astype(BF)
    out[index, 1] = value.astype(BF)
    out[index, 2] = tmp[9 : 9 + wide].astype(BF)


def band_dot(shifts, index, weight):
    parts = [shifts[index + p, s] for p in range(2) for s in range(3)]
    return jnp.dot(jnp.concatenate(parts, axis=1), weight[...], preferred_element_type=F32)


def body(f_ref, g_ref, w1, w2, v2, v1, gf_ref, term_ref, fs, hs, ds2, ds1, slope, ht, ft, acc1, acc2, tmp):
    pairs = gf_ref.shape[0]
    cols = gf_ref.shape[1]
    wide = f_ref.shape[1]
    row, col = lax.axis_index("row"), lax.axis_index("col")
    top = (row > 0).astype(F32)
    bottom = (row < lax.axis_size("row") - 1).astype(F32)
    left = (col > 0).astype(F32)
    right = (col < lax.axis_size("col") - 1).astype(F32)
    place = lax.broadcasted_iota(jnp.int32, (RIM, LANES), 0)
    rim_mask = jnp.where(place < RIM // 2, right, left)
    upper = lax.broadcasted_iota(jnp.int32, (1, LANES), 1) < LANES // 2

    def row_mask(first):
        one = jnp.where(first < 0, top, jnp.where(first >= 2 * pairs, bottom, 1.0))
        two = jnp.where(first + 1 < 0, top, jnp.where(first + 1 >= 2 * pairs, bottom, 1.0))
        return jnp.where(upper, one, two)

    def masked(value, first):
        value = value * row_mask(first)
        return jnp.concatenate([value[:cols], value[cols:] * rim_mask], axis=0)

    @pl.loop(0, pairs + 4)
    def _(j):
        store_shifts(f_ref[j].astype(F32), tmp, fs, j)

    @pl.loop(0, pairs + 3)
    def _(j):
        pre = band_dot(fs, j, w1)
        sig = sigmoid(pre)
        act = pre * sig
        slope[j] = sig + act * (1.0 - sig)
        store_shifts(masked(act, 2 * j - 3), tmp, hs, j)

    @pl.loop(0, pairs + 2)
    def _(j):
        pre = band_dot(hs, j, w2)
        sig = sigmoid(pre)
        delta = g_ref[j].astype(F32) * (sig + pre * sig * (1.0 - sig))
        store_shifts(delta, tmp, ds2, j)

    @pl.loop(0, pairs + 1)
    def _(j):
        back = band_dot(ds2, j, v2)
        store_shifts(masked(back * slope[j + 1], 2 * j - 1), tmp, ds1, j)
        ht[j] = hs[j + 1, 1, :cols].T

    acc1[...] = jnp.zeros_like(acc1)
    acc2[...] = jnp.zeros_like(acc2)

    @pl.loop(0, pairs)
    def _(j):
        gf_ref[j] = band_dot(ds1, j, v1)[:cols].astype(BF)
        ft = fs[j + 2, 1, :cols].T
        near = jnp.concatenate([ds1[j + p, s, :cols] for p in range(2) for s in range(3)], axis=1)
        acc1[...] += jnp.dot(ft, near, preferred_element_type=F32)
        both = jnp.concatenate([ht[j], ht[j + 1]], axis=0)
        near = jnp.concatenate([ds2[j + 1, s, :cols] for s in range(3)], axis=1)
        acc2[...] += jnp.dot(both, near, preferred_element_type=F32)

    half = LANES // 2
    for ky in range(3):
        for kx in range(3):
            s = 2 - kx
            one = jnp.zeros((half, half), F32)
            two = jnp.zeros((half, half), F32)
            for a in range(2):
                b = a + 2 - ky
                q, r = b // 2, b % 2
                at = (q * 3 + s) * LANES + r * half
                one = one + acc1[a * half : (a + 1) * half, at : at + half]
                b = a + ky
                at = s * LANES + a * half
                two = two + acc2[b * half : (b + 1) * half, at : at + half]
            at = (ky * 3 + kx) * half
            term_ref[at : at + half] = jnp.concatenate([one, two], axis=1)


def fused(f_ext, g_ext, w1, w2, v2, v1, cols):
    pairs, wide = f_ext.shape[0] - 4, f_ext.shape[1]
    half = LANES // 2
    return pl.pallas_call(
        body,
        out_shape=(
            jax.ShapeDtypeStruct((pairs, cols, LANES), BF),
            jax.ShapeDtypeStruct((9 * half, LANES), F32),
        ),
        scratch_shapes=[
            pltpu.VMEM((pairs + 4, 3, wide, LANES), BF),
            pltpu.VMEM((pairs + 3, 3, wide, LANES), BF),
            pltpu.VMEM((pairs + 2, 3, wide, LANES), BF),
            pltpu.VMEM((pairs + 1, 3, wide, LANES), BF),
            pltpu.VMEM((pairs + 3, wide, LANES), F32),
            pltpu.VMEM((pairs + 1, LANES, cols), BF),
            pltpu.VMEM((pairs, LANES, cols), BF),
            pltpu.VMEM((LANES, 6 * LANES), F32),
            pltpu.VMEM((2 * LANES, 3 * LANES), F32),
            pltpu.VMEM((wide + 16, LANES), F32),
        ],
        compiler_params=pltpu.CompilerParams(vmem_limit_bytes=40 * 2**20),
        name="fused",
    )(f_ext, g_ext, w1, w2, v2, v1)


def reduced(term):
    sizes = [lax.axis_size(axis) for axis in AXES]
    if sizes[0] != 2 or any(size & (size - 1) for size in sizes):
        return lax.psum(term, AXES)
    half = term.shape[0] // 2
    me = lax.axis_index("dp")
    swap = [(0, 1), (1, 0)]
    mine = lax.dynamic_slice_in_dim(term, me * half, half, 0)
    other = lax.dynamic_slice_in_dim(term, (1 - me) * half, half, 0)
    part = mine + lax.ppermute(other, "dp", swap)
    steps = [("col", 1 << b) for b in range(sizes[2].bit_length() - 1)]
    steps += [("row", 1 << b) for b in range(sizes[1].bit_length() - 1)]
    count = len(steps)
    for at in range(count):
        perm = []
        for core in range(2):
            axis, bit = steps[(at + core * (count // 2)) % count]
            for r in range(sizes[1]):
                for c in range(sizes[2]):
                    to_r, to_c = (r ^ bit, c) if axis == "row" else (r, c ^ bit)
                    base = core * sizes[1]
                    perm.append(((base + r) * sizes[2] + c, (base + to_r) * sizes[2] + to_c))
        low = part.astype(BF)
        part = low.astype(F32) + lax.ppermute(low, AXES, perm).astype(F32)
    other = lax.ppermute(part, "dp", swap)
    return jnp.where(me == 0, jnp.concatenate([part, other]), jnp.concatenate([other, part]))


def shards(features, grad_out, kernel_one, kernel_two):
    slides, chans, rows, cols = features.shape
    pairs = rows // 2
    own = jnp.concatenate([to_pairs(features), to_pairs(grad_out)], axis=0)
    from_left, from_right = pair_exchange(own[:, :4], own[:, cols - 4 :], "col")
    filling = jnp.zeros((2 * pairs, RIM - 8, LANES), BF)
    wide = jnp.concatenate([own, from_right, filling, from_left], axis=1)
    feat, grad = wide[:pairs], wide[pairs:]
    low = jnp.concatenate([feat[:2], grad[:1]], axis=0)
    high = jnp.concatenate([feat[pairs - 2 :], grad[pairs - 1 :]], axis=0)
    above, below = pair_exchange(low, high, "row")
    f_ext = jnp.concatenate([above[:2], feat, below[:2]], axis=0)
    g_ext = jnp.concatenate([above[2:], grad, below[2:]], axis=0)
    w1 = banded(kernel_one.transpose(0, 1, 3, 2))
    w2 = banded(kernel_two.transpose(0, 1, 3, 2))
    v2 = banded(kernel_two[::-1, ::-1])
    v1 = banded(kernel_one[::-1, ::-1])
    gf, term = fused(f_ext, g_ext, w1, w2, v2, v1, cols)
    total = reduced(term)
    count = slides * lax.axis_size("dp") * rows * lax.axis_size("row") * cols * lax.axis_size("col")
    total = (total / jnp.sqrt(F32(count))).reshape(3, 3, chans, 2, chans).transpose(3, 0, 1, 4, 2)
    return from_pairs(gf), total[0], total[1]


def solution(mesh):
    return jax.shard_map(
        shards,
        mesh=mesh,
        in_specs=(P("dp", None, "row", "col"), P("dp", None, "row", "col"), P(), P()),
        out_specs=(P("dp", None, "row", "col"), P(), P()),
        check_vma=False,
    )
```

time: 212 us -> 69.8 us (0.33)
  waiting for transfers between devices: 141 us -> 19.9 us
  matrix products: 31.5 us -> 0 us
  Pallas kernels: 0 us -> 14 us
  between operations: 14.6 us -> 1.1 us
  local copies, waits for them, and re-layouts: 5.49 us -> 11.5 us
  starting transfers between devices: 10.9 us -> 16.7 us
    psum x1 -> x0, waiting for transfers between devices: 128 us -> none  [shards(): lax.psum((term_one, term_two), ('dp', 'row', 'col'))]
    dot_general x54 -> x0, matrix products: 31.5 us -> none  [the longest x18 11.4 us: convolve(): jnp.einsum('oi,sihw->sohw', kernel[ky, kx], padded[:, :, ky:ky + rows, kx...]
    pallas_call x0 -> x1, Pallas kernels: none -> 14 us  [fused(): pl.pallas_call(body, out_shape=(jax.ShapeDtypeStruct((pairs, cols, LANES)...]
    ppermute x4 -> x9, waiting for transfers between devices: 13.6 us -> 19.9 us  [the longest x4 10.8 us: reduced(): part = low.astype(F32) + lax.ppermute(low, AXES, perm).astype(F32)]
    ppermute x4 -> x9, starting transfers between devices: 10.9 us -> 16.7 us  [the longest x4 8.38 us: reduced(): part = low.astype(F32) + lax.ppermute(low, AXES, perm).astype(F32)]
    another operation x0 -> x8, local copies, waits for them, and re-layouts: none -> 5.43 us  [banded(): jnp.stack([jnp.concatenate([taps, zero]), jnp.concatenate([zero, taps])])]
    transpose x0 -> x4, other arithmetic: none -> 4.15 us  [banded(): return both.transpose(1, 3, 2, 4, 0, 5).reshape(12 * chans, 2 * chans)]
    mul x2 -> x0, other arithmetic: 3.4 us -> none  [shards(): return (grad_features, summed_one * scale, summed_two * scale)]
  transfers between devices with their start and end apart: 5 -> 9, of which waited for: 3 -> 6; matrix products, arithmetic and copies ran while one was open for 1% -> 18% of each run, Pallas kernels for 0% -> 0%
where the time goes in v1:
time: 69.8 us; the launch traced here: 69.3 us
  waiting for transfers between devices  19.9 us (29%)
  starting transfers between devices  16.7 us (24%)
  Pallas kernels  14 us (20%)
  local copies, waits for them, and re-layouts  11.5 us (16%)
  other arithmetic  6.21 us (9%)
  between operations  1.1 us (2%)
    pallas_call x1, Pallas kernels, fused(): pl.pallas_call(body, out_shape=(jax.ShapeDtypeStruct((pairs, cols, LANES)...  14 us
    ppermute x4, waiting for transfers between devices, reduced(): part = low.astype(F32) + lax.ppermute(low, AXES, perm).astype(F32)  10.8 us
    ppermute x4, starting transfers between devices, reduced(): part = low.astype(F32) + lax.ppermute(low, AXES, perm).astype(F32)  8.38 us
    ppermute x3, starting transfers between devices, pair_exchange(): got.append(lax.ppermute(jnp.where(up, high, low), axis, perm))  8.13 us
    ppermute x3, waiting for transfers between devices, pair_exchange(): got.append(lax.ppermute(jnp.where(up, high, low), axis, perm))  7.65 us
    another operation x8, local copies, waits for them, and re-layouts, banded(): jnp.stack([jnp.concatenate([taps, zero]), jnp.concatenate([zero, taps])])  5.43 us
    transpose x4, other arithmetic, banded(): return both.transpose(1, 3, 2, 4, 0, 5).reshape(12 * chans, 2 * chans)  4.15 us
    unnamed x19, local copies, waits for them, and re-layouts  2.54 us
  transfers between devices with their start and end apart: 9, of which 6 were waited for; matrix products, arithmetic and copies ran while one was open for 18% of the time, Pallas kernels for 0%

profile of v1, /device:TPU:0, one launch (start us, length us, event | category | flops | bytes accessed | tf_op | source)
XLA Modules:
  0.0 69.3 jit_solution(7861672140601848090)
XLA Ops:
  0.7 1.3 %copy.19 = bf16[1,64,16,256]{3,1,2,0:T(8,128)(2,1)S(1)} copy(bf16[1,64,16,256]{3,2,1,0:T(8,128)(2,1)} %param.4) | data formatting | bytes 1048576 | tf_op args[0]
  1.9 0.3 copy.21
  2.2 0.2 copy.20
  2.4 0.3 copy.22
  2.7 0.6 fusion.1
  3.3 2.9 %collective-permute-start = (bf16[16,4,128]{2,1,0:T(4,128)(2,1)}, bf16[16,4,128]{2,1,0:T(4,128)(2,1)}, u32[]{:S(2)}, u32[]{:S(2)}) collective-permute-start(bf16[16,4,128]{2,1,0:T(4,128)(2,1)} %fusion.1), channel_id=1, source_target_pairs={{0,1},{1,0},{2,3},{3,2},{4,5},{5,4},{6,7},{7,6},{8,9},{9,8},{10,11... | collective-permute-start | bytes 49160 | tf_op jit(solution)/shard_map/ppermute | solution.py:27
  6.3 0.2 fusion.5
  6.5 0.3 copy.27
  6.8 0.3 copy.28
  7.2 0.3 copy.29
  7.5 0.3 copy.30
  7.9 0.2 fusion.7
  8.1 1.0 %copy.23 = bf16[1,2,2,3,64,64]{5,0,4,2,3,1:T(2,128)(2,1)} copy(bf16[1,2,2,3,64,64]{4,5,3,2,1,0:T(8,128)(2,1)S(1)} %bitcast.49) | data formatting | bytes 196608 | tf_op jit(solution)/shard_map/stack | solution.py:48
  9.1 1.0 %copy.24 = bf16[1,2,2,3,64,64]{5,0,4,2,3,1:T(2,128)(2,1)} copy(bf16[1,2,2,3,64,64]{4,5,3,2,1,0:T(8,128)(2,1)S(1)} %bitcast.48) | data formatting | bytes 196608 | tf_op jit(solution)/shard_map/stack | solution.py:48
  10.1 1.0 %copy.25 = bf16[1,2,2,3,64,64]{5,0,4,2,3,1:T(2,128)(2,1)} copy(bf16[1,2,2,3,64,64]{4,5,3,2,1,0:T(8,128)(2,1)S(1)} %bitcast.47) | data formatting | bytes 196608 | tf_op jit(solution)/shard_map/stack | solution.py:48
  11.1 1.0 %copy.26 = bf16[1,2,2,3,64,64]{5,0,4,2,3,1:T(2,128)(2,1)} copy(bf16[1,2,2,3,64,64]{4,5,3,2,1,0:T(8,128)(2,1)S(1)} %bitcast.45) | data formatting | bytes 196608 | tf_op jit(solution)/shard_map/stack | solution.py:48
  12.1 1.0 %maximum_bitcast_fusion.2 = bf16[2,3,2,64,2,64]{5,4,3,2,1,0:T(2,128)(2,1)S(1)} fusion(bf16[1,2,2,3,64,64]{5,0,4,2,3,1:T(2,128)(2,1)S(1)} %copy.28, bf16[1,2,2,3,64,64]{5,0,4,2,3,1:T(2,128)(2,1)S(1)} %copy.27), kind=kLoop, calls=%fused_computation.5 | loop fusion | flops 393216 | bytes 393216 | tf_op jit(solution)/shard_map/transpose | solution.py:50
  13.2 1.0 %maximum_bitcast_fusion.3 = bf16[2,3,2,64,2,64]{5,4,3,2,1,0:T(2,128)(2,1)S(1)} fusion(bf16[1,2,2,3,64,64]{5,0,4,2,3,1:T(2,128)(2,1)S(1)} %copy.30, bf16[1,2,2,3,64,64]{5,0,4,2,3,1:T(2,128)(2,1)S(1)} %copy.29), kind=kLoop, calls=%fused_computation.6 | loop fusion | flops 393216 | bytes 393216 | tf_op jit(solution)/shard_map/transpose | solution.py:50
  14.2 1.0 %maximum_bitcast_fusion = bf16[2,3,2,64,2,64]{5,4,3,2,1,0:T(2,128)(2,1)S(1)} fusion(bf16[1,2,2,3,64,64]{5,0,4,2,3,1:T(2,128)(2,1)S(1)} %copy-done.1, bf16[1,2,2,3,64,64]{5,0,4,2,3,1:T(2,128)(2,1)S(1)} %copy-done), kind=kLoop, calls=%fused_computation.3 | loop fusion | flops 393216 | bytes 393216 | tf_op jit(solution)/shard_map/transpose | solution.py:50
  15.3 1.0 %maximum_bitcast_fusion.1 = bf16[2,3,2,64,2,64]{5,4,3,2,1,0:T(2,128)(2,1)S(1)} fusion(bf16[1,2,2,3,64,64]{5,0,4,2,3,1:T(2,128)(2,1)S(1)} %copy-done.3, bf16[1,2,2,3,64,64]{5,0,4,2,3,1:T(2,128)(2,1)S(1)} %copy-done.2), kind=kLoop, calls=%fused_computation.4 | loop fusion | flops 393216 | bytes 393216 | tf_op jit(solution)/shard_map/transpose | solution.py:50
  16.4 0.2 reshape.61.v2
  16.6 0.2 reshape.62.v1
  16.8 0.2 reshape.59.w1
  17.0 0.2 reshape.60.w2
  17.2 0.1 pad.33.clone
  17.3 0.7 %broadcast_select_fusion.5 = (bf16[16,4,128]{2,1,0:T(4,128)(2,1)S(1)}, bf16[16,4,128]{2,1,0:T(4,128)(2,1)S(1)}) fusion(bf16[16,4,128]{2,1,0:T(4,128)(2,1)} %collective-permute-done, pred[]{:T(512)S(6)} %eq.13), kind=kLoop, calls=%fused_computation.25 | loop fusion | flops 16384 | bytes 49153 | tf_op jit(solution)/shard_map/jit(_where)/select_n | solution.py:29
  18.0 0.3 pad_maximum_fusion
  18.4 0.9 %collective-permute-start.1 = (bf16[3,272,128]{2,1,0:T(8,128)(2,1)S(1)}, bf16[3,272,128]{2,1,0:T(8,128)(2,1)S(1)}, u32[]{:S(2)}, u32[]{:S(2)}) collective-permute-start(bf16[3,272,128]{2,1,0:T(8,128)(2,1)S(1)} %get-tuple-element.20), channel_id=1, source_target_pairs={{2,4},{4,2},{6,8},{8,6},{10,12},{12,10},{3,5},{5,3},{7,9},{9,7},{1... | collective-permute-start | bytes 626696 | tf_op jit(solution)/shard_map/ppermute | solution.py:27
  19.3 4.3 %collective-permute-start.2 = (bf16[3,272,128]{2,1,0:T(8,128)(2,1)S(1)}, bf16[3,272,128]{2,1,0:T(8,128)(2,1)S(1)}, u32[]{:S(2)}, u32[]{:S(2)}) collective-permute-start(bf16[3,272,128]{2,1,0:T(8,128)(2,1)S(1)} %get-tuple-element.21), channel_id=1, source_target_pairs={{0,2},{2,0},{4,6},{6,4},{8,10},{10,8},{12,14},{14,12},{1,3},{3,1},... | collective-permute-start | bytes 626696 | tf_op jit(solution)/shard_map/ppermute | solution.py:27
  23.7 7.6 %collective-permute-done.2 = bf16[3,272,128]{2,1,0:T(8,128)(2,1)S(1)} collective-permute-done((bf16[3,272,128]{2,1,0:T(8,128)(2,1)S(1)}, bf16[3,272,128]{2,1,0:T(8,128)(2,1)S(1)}, u32[]{:S(2)}, u32[]{:S(2)}) %collective-permute-start.2) | collective-permute-done | bytes 208928 | tf_op jit(solution)/shard_map/ppermute | solution.py:27
  31.4 0.1 pad_maximum_fusion.2.g_ref
  31.5 0.1 pad_maximum_fusion.1.f_ref
  31.7 14.0 %fused.1 = (bf16[8,256,128]{2,1,0:T(8,128)(2,1)S(1)}, f32[576,128]{1,0:T(8,128)S(1)}) custom-call(bf16[12,272,128]{2,1,0:T(8,128)(2,1)S(1)} %pad_maximum_fusion.1.f_ref, bf16[10,272,128]{2,1,0:T(8,128)(2,1)S(1)} %pad_maximum_fusion.2.g_ref, bf16[768,128]{1,0:T(8,128)(2,1)S(1)} %reshape.59.w1, bf16[768,128]{1,0:T(8,128)(2,1)S(1)} %reshape.60.w2, ...), custom_call_target="tpu_custom_call" | custom-call | tf_op jit(solution)/shard_map/fused/pallas_call | solution.py:153
  45.6 0.1 collective-permute-start.3
  45.7 1.4 %collective-permute-done.3 = f32[288,128]{1,0:T(8,128)S(1)} collective-permute-done((f32[288,128]{1,0:T(8,128)S(1)}, f32[288,128]{1,0:T(8,128)S(1)}, u32[]{:S(2)}, u32[]{:S(2)}) %collective-permute-start.3) | collective-permute-done | bytes 147488 | tf_op jit(solution)/shard_map/ppermute | solution.py:185
  47.1 0.6 collective-permute-start.4
  47.7 3.8 %collective-permute-done.4 = bf16[288,128]{1,0:T(8,128)(2,1)S(1)} collective-permute-done((bf16[288,128]{1,0:T(8,128)(2,1)S(1)}, bf16[288,128]{1,0:T(8,128)(2,1)S(1)}, u32[]{:S(2)}, u32[]{:S(2)}) %collective-permute-start.4) | collective-permute-done | bytes 73760 | tf_op jit(solution)/shard_map/ppermute | solution.py:199
  51.6 2.5 %collective-permute-start.5 = (bf16[288,128]{1,0:T(8,128)(2,1)S(1)}, bf16[288,128]{1,0:T(8,128)(2,1)S(1)}, u32[]{:S(2)}, u32[]{:S(2)}) collective-permute-start(bf16[288,128]{1,0:T(8,128)(2,1)S(1)} %add_convert_fusion.2), channel_id=1, source_target_pairs={{0,2},{1,3},{2,0},{3,1},{4,6},{5,7},{6,4},{7,5},{8,10},{9,11},{10,... | collective-permute-start | bytes 221192 | tf_op jit(solution)/shard_map/ppermute | solution.py:199
  54.1 2.3 %collective-permute-done.5 = bf16[288,128]{1,0:T(8,128)(2,1)S(1)} collective-permute-done((bf16[288,128]{1,0:T(8,128)(2,1)S(1)}, bf16[288,128]{1,0:T(8,128)(2,1)S(1)}, u32[]{:S(2)}, u32[]{:S(2)}) %collective-permute-start.5) | collective-permute-done | bytes 73760 | tf_op jit(solution)/shard_map/ppermute | solution.py:199
  56.5 2.1 %collective-permute-start.6 = (bf16[288,128]{1,0:T(8,128)(2,1)S(1)}, bf16[288,128]{1,0:T(8,128)(2,1)S(1)}, u32[]{:S(2)}, u32[]{:S(2)}) collective-permute-start(bf16[288,128]{1,0:T(8,128)(2,1)S(1)} %add_convert_fusion.1), channel_id=1, source_target_pairs={{0,4},{1,5},{2,6},{3,7},{4,0},{5,1},{6,2},{7,3},{8,12},{9,13},{10,... | collective-permute-start | bytes 221192 | tf_op jit(solution)/shard_map/ppermute | solution.py:199
  58.6 2.3 %collective-permute-done.6 = bf16[288,128]{1,0:T(8,128)(2,1)S(1)} collective-permute-done((bf16[288,128]{1,0:T(8,128)(2,1)S(1)}, bf16[288,128]{1,0:T(8,128)(2,1)S(1)}, u32[]{:S(2)}, u32[]{:S(2)}) %collective-permute-start.6) | collective-permute-done | bytes 73760 | tf_op jit(solution)/shard_map/ppermute | solution.py:199
  61.0 3.1 %collective-permute-start.7 = (bf16[288,128]{1,0:T(8,128)(2,1)S(1)}, bf16[288,128]{1,0:T(8,128)(2,1)S(1)}, u32[]{:S(2)}, u32[]{:S(2)}) collective-permute-start(bf16[288,128]{1,0:T(8,128)(2,1)S(1)} %add_convert_fusion), channel_id=1, source_target_pairs={{0,8},{1,9},{2,10},{3,11},{4,12},{5,13},{6,14},{7,15},{8,0},{9,1},... | collective-permute-start | bytes 221192 | tf_op jit(solution)/shard_map/ppermute | solution.py:199
  64.1 2.3 %collective-permute-done.7 = bf16[288,128]{1,0:T(8,128)(2,1)S(1)} collective-permute-done((bf16[288,128]{1,0:T(8,128)(2,1)S(1)}, bf16[288,128]{1,0:T(8,128)(2,1)S(1)}, u32[]{:S(2)}, u32[]{:S(2)}) %collective-permute-start.7) | collective-permute-done | bytes 73760 | tf_op jit(solution)/shard_map/ppermute | solution.py:199
  66.5 0.2 copy.31
  66.7 1.1 %copy.33 = bf16[1,64,16,256]{3,2,1,0:T(8,128)(2,1)} copy(bf16[1,64,16,256]{3,1,2,0:T(8,128)(2,1)S(1)} %bitcast.39) | data formatting | bytes 1048576
  67.9 0.4 div.10
  68.2 0.2 copy.32
  68.5 0.8 %slice_bitcast_fusion = (f32[3,3,64,64]{3,2,1,0:T(8,128)}, f32[3,3,64,64]{3,2,1,0:T(8,128)}) fusion(f32[2,3,3,64,64]{4,3,2,1,0:T(8,128)S(1)} %bitcast.38), kind=kLoop, calls=%fused_computation.7 | loop fusion | bytes 589824 | tf_op jit(solution)/shard_map/squeeze | solution.py:225
  (39 shorter events, 0.6 us)
Async XLA Ops:
  0.6 1.6 %copy-start.7 = (bf16[1,64,16,256]{3,2,1,0:T(8,128)(2,1)S(1)}, bf16[1,64,16,256]{3,2,1,0:T(8,128)(2,1)}, u32[]{:S(2)}) copy-start(bf16[1,64,16,256]{3,2,1,0:T(8,128)(2,1)} %param.5) | copy-start | bytes 1572868
  2.4 3.9 %copy-start.4 = (bf16[3,3,64,64]{3,2,1,0:T(8,128)(2,1)S(1)}, bf16[3,3,64,64]{3,2,1,0:T(8,128)(2,1)}, u32[]{:S(2)}) copy-start(bf16[3,3,64,64]{3,2,1,0:T(8,128)(2,1)} %param.7) | copy-start | bytes 221188
  2.4 3.9 %copy-start.5 = (bf16[3,3,64,64]{3,2,1,0:T(8,128)(2,1)S(1)}, bf16[3,3,64,64]{3,2,1,0:T(8,128)(2,1)}, u32[]{:S(2)}) copy-start(bf16[3,3,64,64]{3,2,1,0:T(8,128)(2,1)} %param.6) | copy-start | bytes 221188
  3.3 14.0 %collective-permute-start = (bf16[16,4,128]{2,1,0:T(4,128)(2,1)}, bf16[16,4,128]{2,1,0:T(4,128)(2,1)}, u32[]{:S(2)}, u32[]{:S(2)}) collective-permute-start(bf16[16,4,128]{2,1,0:T(4,128)(2,1)} %fusion.1), channel_id=1, source_target_pairs={{0,1},{1,0},{2,3},{3,2},{4,5},{5,4},{6,7},{7,6},{8,9},{9,8},{10,11... | collective-permute-start | bytes 49160 | tf_op jit(solution)/shard_map/ppermute | solution.py:27
  6.4 1.4 %copy-start.6 = (bf16[3,3,64,64]{3,2,1,0:T(8,128)(2,1)S(1)}, bf16[3,3,64,64]{3,2,1,0:T(8,128)(2,1)}, u32[]{:S(2)}) copy-start(bf16[3,3,64,64]{3,2,1,0:T(8,128)(2,1)} %param.6) | copy-start | bytes 221188
  12.1 2.1 %copy-start = (bf16[1,2,2,3,64,64]{5,0,4,2,3,1:T(2,128)(2,1)S(1)}, bf16[1,2,2,3,64,64]{5,0,4,2,3,1:T(2,128)(2,1)}, u32[]{:S(2)}) copy-start(bf16[1,2,2,3,64,64]{5,0,4,2,3,1:T(2,128)(2,1)} %copy.23) | copy-start | bytes 294916
  12.1 2.1 %copy-start.1 = (bf16[1,2,2,3,64,64]{5,0,4,2,3,1:T(2,128)(2,1)S(1)}, bf16[1,2,2,3,64,64]{5,0,4,2,3,1:T(2,128)(2,1)}, u32[]{:S(2)}) copy-start(bf16[1,2,2,3,64,64]{5,0,4,2,3,1:T(2,128)(2,1)} %copy.24) | copy-start | bytes 294916
  13.2 2.1 %copy-start.2 = (bf16[1,2,2,3,64,64]{5,0,4,2,3,1:T(2,128)(2,1)S(1)}, bf16[1,2,2,3,64,64]{5,0,4,2,3,1:T(2,128)(2,1)}, u32[]{:S(2)}) copy-start(bf16[1,2,2,3,64,64]{5,0,4,2,3,1:T(2,128)(2,1)} %copy.25) | copy-start | bytes 294916
  13.2 2.1 %copy-start.3 = (bf16[1,2,2,3,64,64]{5,0,4,2,3,1:T(2,128)(2,1)S(1)}, bf16[1,2,2,3,64,64]{5,0,4,2,3,1:T(2,128)(2,1)}, u32[]{:S(2)}) copy-start(bf16[1,2,2,3,64,64]{5,0,4,2,3,1:T(2,128)(2,1)} %copy.26) | copy-start | bytes 294916
  18.4 5.3 %collective-permute-start.1 = (bf16[3,272,128]{2,1,0:T(8,128)(2,1)S(1)}, bf16[3,272,128]{2,1,0:T(8,128)(2,1)S(1)}, u32[]{:S(2)}, u32[]{:S(2)}) collective-permute-start(bf16[3,272,128]{2,1,0:T(8,128)(2,1)S(1)} %get-tuple-element.20), channel_id=1, source_target_pairs={{2,4},{4,2},{6,8},{8,6},{10,12},{12,10},{3,5},{5,3},{7,9},{9,7},{1... | collective-permute-start | bytes 626696 | tf_op jit(solution)/shard_map/ppermute | solution.py:27
  19.3 12.1 %collective-permute-start.2 = (bf16[3,272,128]{2,1,0:T(8,128)(2,1)S(1)}, bf16[3,272,128]{2,1,0:T(8,128)(2,1)S(1)}, u32[]{:S(2)}, u32[]{:S(2)}) collective-permute-start(bf16[3,272,128]{2,1,0:T(8,128)(2,1)S(1)} %get-tuple-element.21), channel_id=1, source_target_pairs={{0,2},{2,0},{4,6},{6,4},{8,10},{10,8},{12,14},{14,12},{1,3},{3,1},... | collective-permute-start | bytes 626696 | tf_op jit(solution)/shard_map/ppermute | solution.py:27
  45.6 1.4 %collective-permute-start.3 = (f32[288,128]{1,0:T(8,128)S(1)}, f32[288,128]{1,0:T(8,128)S(1)}, u32[]{:S(2)}, u32[]{:S(2)}) collective-permute-start(f32[288,128]{1,0:T(8,128)S(1)} %constant_dynamic-slice_fusion), channel_id=1, source_target_pairs={{0,16},{16,0},{1,17},{17,1},{2,18},{18,2},{3,19},{19,3},{4,20},{20... | collective-permute-start | bytes 442376 | tf_op jit(solution)/shard_map/ppermute | solution.py:185
  47.1 4.4 %collective-permute-start.4 = (bf16[288,128]{1,0:T(8,128)(2,1)S(1)}, bf16[288,128]{1,0:T(8,128)(2,1)S(1)}, u32[]{:S(2)}, u32[]{:S(2)}) collective-permute-start(bf16[288,128]{1,0:T(8,128)(2,1)S(1)} %add_convert_fusion.3), channel_id=1, source_target_pairs={{0,1},{1,0},{2,3},{3,2},{4,5},{5,4},{6,7},{7,6},{8,9},{9,8},{10,11... | collective-permute-start | bytes 221192 | tf_op jit(solution)/shard_map/ppermute | solution.py:199
  51.6 4.9 %collective-permute-start.5 = (bf16[288,128]{1,0:T(8,128)(2,1)S(1)}, bf16[288,128]{1,0:T(8,128)(2,1)S(1)}, u32[]{:S(2)}, u32[]{:S(2)}) collective-permute-start(bf16[288,128]{1,0:T(8,128)(2,1)S(1)} %add_convert_fusion.2), channel_id=1, source_target_pairs={{0,2},{1,3},{2,0},{3,1},{4,6},{5,7},{6,4},{7,5},{8,10},{9,11},{10,... | collective-permute-start | bytes 221192 | tf_op jit(solution)/shard_map/ppermute | solution.py:199
  56.5 4.5 %collective-permute-start.6 = (bf16[288,128]{1,0:T(8,128)(2,1)S(1)}, bf16[288,128]{1,0:T(8,128)(2,1)S(1)}, u32[]{:S(2)}, u32[]{:S(2)}) collective-permute-start(bf16[288,128]{1,0:T(8,128)(2,1)S(1)} %add_convert_fusion.1), channel_id=1, source_target_pairs={{0,4},{1,5},{2,6},{3,7},{4,0},{5,1},{6,2},{7,3},{8,12},{9,13},{10,... | collective-permute-start | bytes 221192 | tf_op jit(solution)/shard_map/ppermute | solution.py:199
  61.0 5.4 %collective-permute-start.7 = (bf16[288,128]{1,0:T(8,128)(2,1)S(1)}, bf16[288,128]{1,0:T(8,128)(2,1)S(1)}, u32[]{:S(2)}, u32[]{:S(2)}) collective-permute-start(bf16[288,128]{1,0:T(8,128)(2,1)S(1)} %add_convert_fusion), channel_id=1, source_target_pairs={{0,8},{1,9},{2,10},{3,11},{4,12},{5,13},{6,14},{7,15},{8,0},{9,1},... | collective-permute-start | bytes 221192 | tf_op jit(solution)/shard_map/ppermute | solution.py:199
  66.4 1.4 %collective-permute-start.8 = (f32[288,128]{1,0:T(8,128)S(1)}, f32[288,128]{1,0:T(8,128)S(1)}, u32[]{:S(2)}, u32[]{:S(2)}) collective-permute-start(f32[288,128]{1,0:T(8,128)S(1)} %convert_add_fusion), channel_id=1, source_target_pairs={{0,16},{16,0},{1,17},{17,1},{2,18},{18,2},{3,19},{19,3},{4,20},{20... | collective-permute-start | bytes 442376 | tf_op jit(solution)/shard_map/ppermute | solution.py:200

commit v2 on v1

v2 whole, which is shorter than its diff:
```python
import jax
import jax.numpy as jnp
from jax import lax
from jax.experimental import pallas as pl
from jax.experimental.pallas import tpu as pltpu
from jax.sharding import PartitionSpec as P

BF = jnp.bfloat16
F32 = jnp.float32
AXES = ("dp", "row", "col")
LANES = 128
HALF = LANES // 2
RIM = 16


def neighbours(axis, parity):
    count = lax.axis_size(axis)
    pairs = []
    for i in range(parity, count - 1, 2):
        pairs += [(i, i + 1), (i + 1, i)]
    return pairs


def is_low(axis, parity):
    return lax.axis_index(axis) % 2 == parity


def swap_one(low, high, axis):
    got = []
    for parity in range(2):
        perm = neighbours(axis, parity)
        if perm:
            got.append(lax.ppermute(jnp.where(is_low(axis, parity), high, low), axis, perm))
        else:
            got.append(jnp.zeros_like(low))
    even = is_low(axis, 0)
    return jnp.where(even, got[1], got[0]), jnp.where(even, got[0], got[1])


def swap_corners(corners):
    row_count, col_count = lax.axis_size("row"), lax.axis_size("col")
    got = {}
    for row_parity in range(2):
        for col_parity in range(2):
            perm = [
                (r * col_count + c, to_r * col_count + to_c)
                for r, to_r in neighbours("row", row_parity)
                for c, to_c in neighbours("col", col_parity)
            ]
            if not perm:
                got[row_parity, col_parity] = jnp.zeros_like(corners[0][0])
                continue
            down, right = is_low("row", row_parity), is_low("col", col_parity)
            sent = jnp.where(
                down, jnp.where(right, corners[1][1], corners[1][0]), jnp.where(right, corners[0][1], corners[0][0])
            )
            got[row_parity, col_parity] = lax.ppermute(sent, ("row", "col"), perm)
    even_row, even_col = is_low("row", 0), is_low("col", 0)

    def pick(row_parity, col_parity):
        across = [jnp.where(even_col, got[p, col_parity], got[p, 1 - col_parity]) for p in range(2)]
        return jnp.where(even_row, across[row_parity], across[1 - row_parity])

    return [[pick(1, 1), pick(1, 0)], [pick(0, 1), pick(0, 0)]]


def to_pairs(cells):
    _, chans, rows, cols = cells.shape
    part = cells[0].reshape(chans, rows // 2, 2, cols)
    return part.transpose(1, 3, 2, 0).reshape(rows // 2, cols, 2 * chans)


def from_pairs(pairs):
    count, cols, lanes = pairs.shape
    part = pairs.reshape(count, cols, 2, lanes // 2)
    return part.transpose(3, 0, 2, 1).reshape(1, lanes // 2, 2 * count, cols)


def weights_body(k1, k2, w1, w2, v2, v1):
    zero = jnp.zeros((HALF, HALF), BF)
    for taps, forward, backward in ((k1, w1, v1), (k2, w2, v2)):
        flat = {(ky, kx): taps[ky, kx] for ky in range(3) for kx in range(3)}
        turned = {at: flat[at].astype(F32).T.astype(BF) for at in flat}
        for p in range(2):
            for kx in range(3):
                for r in range(2):
                    at = ((p * 3 + kx) * 2 + r) * HALF
                    kys = [2 * p + r - a for a in range(2)]
                    forward[at : at + HALF] = jnp.concatenate([turned.get((ky, kx), zero) for ky in kys], axis=1)
                    backward[at : at + HALF] = jnp.concatenate([flat.get((2 - ky, 2 - kx), zero) for ky in kys], axis=1)


def make_weights(kernel_one, kernel_two):
    shape = jax.ShapeDtypeStruct((12 * HALF, LANES), BF)
    return pl.pallas_call(weights_body, out_shape=(shape,) * 4, name="weights")(kernel_one, kernel_two)


def sigmoid(value):
    return 0.5 * jnp.tanh(0.5 * value) + 0.5


def with_rim(own, right, left):
    own, right, left = own.astype(F32), right.astype(F32), left.astype(F32)
    return jnp.concatenate([own, right[: RIM // 2], left[RIM // 2 :]], axis=0)


def store_shifts(value, tmp, out, index):
    wide = value.shape[0]
    tmp[8 : 8 + wide] = value
    tmp[0:8] = value[wide - 8 :]
    tmp[8 + wide :] = value[:8]
    out[index, 0] = tmp[7 : 7 + wide].astype(BF)
    out[index, 1] = value.astype(BF)
    out[index, 2] = tmp[9 : 9 + wide].astype(BF)


def band_dot(first, second, weight):
    parts = [ref[index, s] for ref, index in (first, second) for s in range(3)]
    return jnp.dot(jnp.concatenate(parts, axis=1), weight[...], preferred_element_type=F32)


def edge_masks():
    row, col = lax.axis_index("row"), lax.axis_index("col")
    top = (row > 0).astype(F32)
    bottom = (row < lax.axis_size("row") - 1).astype(F32)
    left = (col > 0).astype(F32)
    right = (col < lax.axis_size("col") - 1).astype(F32)
    place = lax.broadcasted_iota(jnp.int32, (RIM, LANES), 0)
    rim = jnp.where(place < RIM // 2, right, left)
    return top, bottom, rim


def rim_masked(value, rim):
    own = value.shape[0] - RIM
    return jnp.concatenate([value[:own], value[own:] * rim], axis=0)


def add_one(acc, feat_t, pieces):
    near = jnp.concatenate(pieces, axis=1)
    acc[...] += jnp.dot(feat_t, near, preferred_element_type=F32)


def inner_body(f, g, c_left, c_right, w1, w2, v2, hs_edge, ds2_edge, slope_edge, ds1, acc1, acc2, fs, hs, ds2, slope, ht, tmp):
    pairs, cols = f.shape[:2]
    _, _, rim = edge_masks()

    @pl.loop(0, pairs)
    def _(j):
        store_shifts(with_rim(f[j], c_right[j], c_left[j]), tmp, fs, j)

    @pl.loop(0, pairs - 1)
    def _(j):
        pre = band_dot((fs, j), (fs, j + 1), w1)
        sig = sigmoid(pre)
        act = pre * sig
        slope[j] = sig + act * (1.0 - sig)
        store_shifts(rim_masked(act, rim), tmp, hs, j)
        ht[j] = hs[j, 1, :cols].T

    @pl.loop(0, pairs - 2)
    def _(j):
        pre = band_dot((hs, j), (hs, j + 1), w2)
        sig = sigmoid(pre)
        grad = with_rim(g[j + 1], c_right[pairs + j + 1], c_left[pairs + j + 1])
        delta = grad * (sig + pre * sig * (1.0 - sig))
        store_shifts(delta, tmp, ds2, j)

    @pl.loop(0, pairs - 3)
    def _(j):
        back = band_dot((ds2, j), (ds2, j + 1), v2)
        store_shifts(rim_masked(back * slope[j + 1], rim), tmp, ds1, j)

    acc1[...] = jnp.zeros_like(acc1)
    acc2[...] = jnp.zeros_like(acc2)

    @pl.loop(0, pairs - 2)
    def _(j):
        both = jnp.concatenate([ht[j], ht[j + 1]], axis=0)
        add_one(acc2, both, [ds2[j, s, :cols] for s in range(3)])

    @pl.loop(0, pairs - 4)
    def _(j):
        feat_t = fs[j + 2, 1, :cols].T
        add_one(acc1, feat_t, [ds1[j + p, s, :cols] for p in range(2) for s in range(3)])

    for side, at in ((0, 0), (1, pairs - 2)):
        hs_edge[side] = hs[at]
        slope_edge[side] = slope[at]
    for side, at in ((0, 0), (1, pairs - 3)):
        ds2_edge[side] = ds2[at]


def rim_body(
    f, g, c_left, c_right, above, below, c_above, c_below, w1, w2, v2, hs_edge, ds2_edge, slope_edge, ds1_in, acc1_in, acc2_in,
    ds1, term, fs, hs, ds2, slope, acc1, acc2, tmp,
):
    pairs, cols = f.shape[:2]
    top, bottom, rim = edge_masks()
    upper = lax.broadcasted_iota(jnp.int32, (1, LANES), 1) < HALF
    acc1[...] = acc1_in[...]
    acc2[...] = acc2_in[...]

    def own(ref, base, j):
        return with_rim(ref[j], c_right[base + j], c_left[base + j])

    def far(side, j):
        halo, corner = (above, c_above) if side == 0 else (below, c_below)
        return with_rim(halo[j], corner[1, j], corner[0, j])

    for side in range(2):
        flag = (top, bottom)[side]
        outer = jnp.where(upper, flag, 1.0) if side == 0 else jnp.where(upper, 1.0, flag)
        scratch = tmp.at[side]
        ends = (0, 1) if side == 0 else (1, 0)
        feats = [far(side, ends[0]), far(side, ends[1]), own(f, 0, 0 if side == 0 else pairs - 1)]
        for k in range(3):
            store_shifts(feats[k], scratch, fs.at[side], k)

        def order(one, two):
            return (one, two) if side == 0 else (two, one)

        for k in range(2):
            pre = band_dot(*order((fs.at[side], k), (fs.at[side], k + 1)), w1)
            sig = sigmoid(pre)
            act = pre * sig
            if k == 1:
                slope[side] = sig + act * (1.0 - sig)
            act = act * (flag if k == 0 else outer)
            store_shifts(rim_masked(act, rim), scratch, hs.at[side], k)
        for k in range(2):
            grad = far(side, 2) if k == 0 else own(g, pairs, 0 if side == 0 else pairs - 1)
            inward = (hs.at[side], 1) if k == 0 else (hs_edge, side)
            pre = band_dot(*order((hs.at[side], k), inward), w2)
            sig = sigmoid(pre)
            delta = grad * (sig + pre * sig * (1.0 - sig))
            store_shifts(delta, scratch, ds2.at[side], k)
        for k in range(2):
            inward = (ds2.at[side], 1) if k == 0 else (ds2_edge, side)
            back = band_dot(*order((ds2.at[side], k), inward), v2)
            if k == 0:
                value = back * slope[side] * outer
            else:
                value = back * slope_edge[side]
            at = k if side == 0 else pairs - k
            store_shifts(rim_masked(value, rim), scratch, ds1, at)

    for j in range(2, pairs - 1):
        ds1[j] = ds1_in[j - 2]
    for side in range(2):
        near, inward = hs[side, 1, 1, :cols].T, hs_edge[side, 1, :cols].T
        both = [near, inward] if side == 0 else [inward, near]
        add_one(acc2, jnp.concatenate(both, axis=0), [ds2[side, 1, s, :cols] for s in range(3)])
    for j in (0, 1, pairs - 2, pairs - 1):
        add_one(acc1, f[j].T, [ds1[j + p, s, :cols] for p in range(2) for s in range(3)])

    for ky in range(3):
        for kx in range(3):
            s = 2 - kx
            one = jnp.zeros((HALF, HALF), F32)
            two = jnp.zeros((HALF, HALF), F32)
            for a in range(2):
                b = a + 2 - ky
                at = (b // 2 * 3 + s) * LANES + b % 2 * HALF
                one = one + acc1[a * HALF : (a + 1) * HALF, at : at + HALF]
                b = a + ky
                at = s * LANES + a * HALF
                two = two + acc2[b * HALF : (b + 1) * HALF, at : at + HALF]
            at = (ky * 3 + kx) * HALF
            term[at : at + HALF] = jnp.concatenate([one, two], axis=1)


def last_body(ds1, v1, gf):
    pairs, cols = gf.shape[:2]

    @pl.loop(0, pairs)
    def _(j):
        gf[j] = band_dot((ds1, j), (ds1, j + 1), v1)[:cols].astype(BF)


def cost(pair_count):
    return pl.CostEstimate(flops=pair_count * 272 * 768 * 128 * 2, bytes_accessed=4 * 2**20, transcendentals=0)


PARAMS = pltpu.CompilerParams(vmem_limit_bytes=32 * 2**20)


def inner(f, g, c_left, c_right, w1, w2, v2):
    pairs, cols = f.shape[:2]
    wide = cols + RIM

    def shifts(count):
        return (count, 3, wide, LANES)

    return pl.pallas_call(
        inner_body,
        out_shape=(
            jax.ShapeDtypeStruct(shifts(2), BF),
            jax.ShapeDtypeStruct(shifts(2), BF),
            jax.ShapeDtypeStruct((2, wide, LANES), F32),
            jax.ShapeDtypeStruct(shifts(pairs - 3), BF),
            jax.ShapeDtypeStruct((LANES, 6 * LANES), F32),
            jax.ShapeDtypeStruct((2 * LANES, 3 * LANES), F32),
        ),
        scratch_shapes=[
            pltpu.VMEM(shifts(pairs), BF),
            pltpu.VMEM(shifts(pairs - 1), BF),
            pltpu.VMEM(shifts(pairs - 2), BF),
            pltpu.VMEM((pairs - 1, wide, LANES), F32),
            pltpu.VMEM((pairs - 1, LANES, cols), BF),
            pltpu.VMEM((wide + 16, LANES), F32),
        ],
        compiler_params=PARAMS,
        cost_estimate=cost(22),
        name="inner",
    )(f, g, c_left, c_right, w1, w2, v2)


def outer(f, *rest):
    pairs, cols = f.shape[:2]
    wide = cols + RIM

    def shifts(*count):
        return (*count, 3, wide, LANES)

    return pl.pallas_call(
        rim_body,
        out_shape=(
            jax.ShapeDtypeStruct(shifts(pairs + 1), BF),
            jax.ShapeDtypeStruct((9 * HALF, LANES), F32),
        ),
        scratch_shapes=[
            pltpu.VMEM(shifts(2, 3), BF),
            pltpu.VMEM(shifts(2, 2), BF),
            pltpu.VMEM(shifts(2, 2), BF),
            pltpu.VMEM((2, wide, LANES), F32),
            pltpu.VMEM((LANES, 6 * LANES), F32),
            pltpu.VMEM((2 * LANES, 3 * LANES), F32),
            pltpu.VMEM((2, wide + 16, LANES), F32),
        ],
        compiler_params=PARAMS,
        cost_estimate=cost(14),
        name="outer",
    )(f, *rest)


def last(ds1, v1, cols):
    return pl.pallas_call(
        last_body,
        out_shape=jax.ShapeDtypeStruct((ds1.shape[0] - 1, cols, LANES), BF),
        compiler_params=PARAMS,
        cost_estimate=cost(8),
        name="last",
    )(ds1, v1)


def reduced(term):
    sizes = [lax.axis_size(axis) for axis in AXES]
    if sizes[0] != 2 or any(size & (size - 1) for size in sizes):
        return lax.psum(term, AXES)
    half = term.shape[0] // 2
    me = lax.axis_index("dp")
    swap = [(0, 1), (1, 0)]
    mine = lax.dynamic_slice_in_dim(term, me * half, half, 0)
    other = lax.dynamic_slice_in_dim(term, (1 - me) * half, half, 0)
    part = mine + lax.ppermute(other, "dp", swap)
    across = [(0, 1 << b) for b in range(sizes[2].bit_length() - 1)]
    down = [(1 << b, 0) for b in range(sizes[1].bit_length() - 1)]
    bits = []
    while across or down:
        bits += down[:1] + across[:1]
        down, across = down[1:], across[1:]
    groups = [bits[at : at + 2] for at in range(0, len(bits), 2)]
    for at in range(len(groups)):
        mine = [groups[at], groups[(at + len(groups) // 2) % len(groups)]]
        if len(mine[0]) != len(mine[1]):
            mine[1] = mine[0]
        low = part.astype(BF)
        got = []
        for member in range(1, 1 << len(mine[0])):
            perm = []
            for core in range(2):
                flips = [flip for k, flip in enumerate(mine[core]) if member >> k & 1]
                for r in range(sizes[1]):
                    for c in range(sizes[2]):
                        to_r, to_c = r, c
                        for flip in flips:
                            to_r, to_c = to_r ^ flip[0], to_c ^ flip[1]
                        base = core * sizes[1]
                        perm.append(((base + r) * sizes[2] + c, (base + to_r) * sizes[2] + to_c))
            got.append(lax.ppermute(low, AXES, perm).astype(F32))
        part = low.astype(F32) + got[0]
        if len(got) > 1:
            part = part + (got[1] + got[2])
    other = lax.ppermute(part, "dp", swap)
    return jnp.where(me == 0, jnp.concatenate([part, other]), jnp.concatenate([other, part]))


def shards(features, grad_out, kernel_one, kernel_two):
    slides, chans, rows, cols = features.shape
    pairs = rows // 2
    feat, grad = to_pairs(features), to_pairs(grad_out)
    own = jnp.concatenate([feat, grad], axis=0)
    starts, ends = own[:, :RIM], own[:, cols - RIM :]
    c_left, c_right = swap_one(starts, ends, "col")
    low = jnp.concatenate([feat[:2], grad[:1]], axis=0)
    high = jnp.concatenate([feat[pairs - 2 :], grad[pairs - 1 :]], axis=0)
    above, below = swap_one(low, high, "row")
    corners = [[edge[:, :RIM], edge[:, cols - RIM :]] for edge in (low, high)]
    corners = swap_corners(corners)
    c_above, c_below = jnp.stack(corners[0]), jnp.stack(corners[1])
    w1, w2, v2, v1 = make_weights(kernel_one, kernel_two)
    state = inner(feat, grad, c_left, c_right, w1, w2, v2)
    ds1, term = outer(feat, grad, c_left, c_right, above, below, c_above, c_below, w1, w2, v2, *state)
    total = reduced(term)
    gf = last(ds1, v1, cols)
    count = slides * lax.axis_size("dp") * rows * lax.axis_size("row") * cols * lax.axis_size("col")
    total = (total / jnp.sqrt(F32(count))).reshape(3, 3, chans, 2, chans).transpose(3, 0, 1, 4, 2)
    return from_pairs(gf), total[0], total[1]


def solution(mesh):
    return jax.shard_map(
        shards,
        mesh=mesh,
        in_specs=(P("dp", None, "row", "col"), P("dp", None, "row", "col"), P(), P()),
        out_specs=(P("dp", None, "row", "col"), P(), P()),
        check_vma=False,
    )
```

time: 69.8 us -> 56 us (0.80)
  waiting for transfers between devices: 19.9 us -> 8.83 us
  other arithmetic: 6.21 us -> 0.28 us
  starting transfers between devices: 16.7 us -> 21.6 us
  local copies, waits for them, and re-layouts: 11.5 us -> 7.99 us
  Pallas kernels: 14 us -> 16 us
    ppermute x7 -> x11, waiting for transfers between devices: 18.5 us -> 7.48 us  [the longest x6 7.46 us: reduced(): got.append(lax.ppermute(low, AXES, perm).astype(F32))]
    another operation x8 -> x0, local copies, waits for them, and re-layouts: 5.43 us -> none  [banded(): jnp.stack([jnp.concatenate([taps, zero]), jnp.concatenate([zero, taps])])]
    ppermute x7 -> x11, starting transfers between devices: 16.5 us -> 21.5 us  [the longest x3 8.02 us: swap_one(): lax.ppermute(jnp.where(is_low(axis, parity), high, low), axis, perm)]
    transpose x4 -> x0, other arithmetic: 4.15 us -> none  [banded(): return both.transpose(1, 3, 2, 4, 0, 5).reshape(12 * chans, 2 * chans)]
    unnamed x19 -> x13, local copies, waits for them, and re-layouts: 2.54 us -> 5.28 us
    pallas_call x1 -> x4, Pallas kernels: 14 us -> 16 us  [the longest x1 8.75 us: inner(): pl.pallas_call(inner_body, out_shape=(jax.ShapeDtypeStruct(shifts(2), BF)...]
    select_n x4 -> x6, other arithmetic: 1.44 us -> 0.13 us  [the longest x2 0.06 us: swap_one(): jnp.where(is_low(axis, parity), high, low)]
    reshape x4 -> x0, local copies, waits for them, and re-layouts: 0.79 us -> none  [banded(): return both.transpose(1, 3, 2, 4, 0, 5).reshape(12 * chans, 2 * chans)]
  transfers between devices with their start and end apart: 9 -> 13, of which waited for: 6 -> 7; matrix products, arithmetic and copies ran while one was open for 18% -> 3% of each run, Pallas kernels for 0% -> 23%
where the time goes in v2:
time: 56 us; the launch traced here: 55.7 us
  starting transfers between devices  21.6 us (39%)
  Pallas kernels  16 us (29%)
  waiting for transfers between devices  8.83 us (16%)
  local copies, waits for them, and re-layouts  7.99 us (14%)
  between operations  0.93 us (2%)
    pallas_call x1, Pallas kernels, inner(): pl.pallas_call(inner_body, out_shape=(jax.ShapeDtypeStruct(shifts(2), BF)...  8.75 us
    ppermute x3, starting transfers between devices, swap_one(): lax.ppermute(jnp.where(is_low(axis, parity), high, low), axis, perm)  8.02 us
    ppermute x6, starting transfers between devices, reduced(): got.append(lax.ppermute(low, AXES, perm).astype(F32))  7.55 us
    ppermute x6, waiting for transfers between devices, reduced(): got.append(lax.ppermute(low, AXES, perm).astype(F32))  7.46 us
    ppermute x2, starting transfers between devices, swap_corners(): got[row_parity, col_parity] = lax.ppermute(sent, ('row', 'col'), perm)  5.91 us
    unnamed x13, local copies, waits for them, and re-layouts  5.28 us
    pallas_call x1, Pallas kernels, outer(): pl.pallas_call(rim_body, out_shape=(jax.ShapeDtypeStruct(shifts(pairs + 1...  2.96 us
    pallas_call x1, Pallas kernels, last(): pl.pallas_call(last_body, out_shape=jax.ShapeDtypeStruct((ds1.shape[0] -...  2.22 us
  transfers between devices with their start and end apart: 13, of which 7 were waited for; matrix products, arithmetic and copies ran while one was open for 3% of the time, Pallas kernels for 23%

profile of v2, /device:TPU:0, one launch (start us, length us, event | category | flops | bytes accessed | tf_op | source)
XLA Modules:
  0.0 55.7 jit_solution(6981264554376992327)
XLA Ops:
  0.7 1.3 %copy.11 = bf16[1,64,16,256]{3,1,2,0:T(8,128)(2,1)S(1)} copy(bf16[1,64,16,256]{3,2,1,0:T(8,128)(2,1)} %param.4) | data formatting | bytes 1048576 | tf_op args[0]
  1.9 0.3 copy.21.f
  2.2 0.0 copy-done.4
  2.2 0.2 copy.12
  2.4 0.3 copy.22.g
  2.7 3.0 %collective-permute-start = (bf16[16,16,128]{2,1,0:T(8,128)(2,1)S(1)}, bf16[16,16,128]{2,1,0:T(8,128)(2,1)S(1)}, u32[]{:S(2)}, u32[]{:S(2)}) collective-permute-start(bf16[16,16,128]{2,1,0:T(8,128)(2,1)S(1)} %fusion.1), channel_id=1, source_target_pairs={{0,1},{1,0},{2,3},{3,2},{4,5},{5,4},{6,7},{7,6},{8,9},{9,8},{10,11... | collective-permute-start | bytes 196616 | tf_op jit(solution)/shard_map/ppermute | solution.py:33
  5.7 0.1 copy.15
  5.8 0.1 copy.17
  6.0 0.1 copy.16
  6.1 0.1 copy.18
  6.2 0.7 %collective-permute-start.3 = (bf16[3,16,128]{2,1,0:T(8,128)(2,1)S(1)}, bf16[3,16,128]{2,1,0:T(8,128)(2,1)S(1)}, u32[]{:S(2)}, u32[]{:S(2)}) collective-permute-start(bf16[3,16,128]{2,1,0:T(8,128)(2,1)S(1)} %broadcast_select_fusion.6), channel_id=1, source_target_pairs={{2,5},{3,4},{4,3},{5,2},{6,9},{7,8},{8,7},{9,6},{10,13},{11,12},{1... | collective-permute-start | bytes 36872 | tf_op jit(solution)/shard_map/ppermute | solution.py:57
  6.9 5.2 %collective-permute-start.4 = (bf16[3,16,128]{2,1,0:T(8,128)(2,1)S(1)}, bf16[3,16,128]{2,1,0:T(8,128)(2,1)S(1)}, u32[]{:S(2)}, u32[]{:S(2)}) collective-permute-start(bf16[3,16,128]{2,1,0:T(8,128)(2,1)S(1)} %get-tuple-element.30), channel_id=1, source_target_pairs={{0,3},{1,2},{2,1},{3,0},{4,7},{5,6},{6,5},{7,4},{8,11},{9,10},{10,... | collective-permute-start | bytes 36872 | tf_op jit(solution)/shard_map/ppermute | solution.py:57
  12.2 0.7 %collective-permute-start.1 = (bf16[3,256,128]{2,1,0:T(8,128)(2,1)S(1)}, bf16[3,256,128]{2,1,0:T(8,128)(2,1)S(1)}, u32[]{:S(2)}, u32[]{:S(2)}) collective-permute-start(bf16[3,256,128]{2,1,0:T(8,128)(2,1)S(1)} %get-tuple-element.42), channel_id=1, source_target_pairs={{2,4},{4,2},{6,8},{8,6},{10,12},{12,10},{3,5},{5,3},{7,9},{9,7},{1... | collective-permute-start | bytes 589832 | tf_op jit(solution)/shard_map/ppermute | solution.py:33
  12.9 4.3 %collective-permute-start.2 = (bf16[3,256,128]{2,1,0:T(8,128)(2,1)S(1)}, bf16[3,256,128]{2,1,0:T(8,128)(2,1)S(1)}, u32[]{:S(2)}, u32[]{:S(2)}) collective-permute-start(bf16[3,256,128]{2,1,0:T(8,128)(2,1)S(1)} %get-tuple-element.41), channel_id=1, source_target_pairs={{0,2},{2,0},{4,6},{6,4},{8,10},{10,8},{12,14},{14,12},{1,3},{3,1},... | collective-permute-start | bytes 589832 | tf_op jit(solution)/shard_map/ppermute | solution.py:33
  17.2 2.1 %weights.1 = (bf16[768,128]{1,0:T(8,128)(2,1)}, bf16[768,128]{1,0:T(8,128)(2,1)}, bf16[768,128]{1,0:T(8,128)(2,1)}, bf16[768,128]{1,0:T(8,128)(2,1)}) custom-call(bf16[3,3,64,64]{3,2,1,0:T(8,128)(2,1)} %k1.1, bf16[3,3,64,64]{3,2,1,0:T(8,128)(2,1)} %k2.1), custom_call_target="tpu_custom_call" | custom-call | tf_op jit(solution)/shard_map/weights/pallas_call | solution.py:95
  19.3 0.0 collective-permute-done.3
  19.3 0.0 collective-permute-done.4
  19.4 0.0 collective-permute-done
  19.4 0.0 copy-start
  19.4 0.9 %copy-done = bf16[768,128]{1,0:T(8,128)(2,1)S(1)} copy-done((bf16[768,128]{1,0:T(8,128)(2,1)S(1)}, bf16[768,128]{1,0:T(8,128)(2,1)}, u32[]{:S(2)}) %copy-start) | copy-done | bytes 196632
  20.3 0.9 %copy-done.1 = bf16[768,128]{1,0:T(8,128)(2,1)S(1)} copy-done((bf16[768,128]{1,0:T(8,128)(2,1)S(1)}, bf16[768,128]{1,0:T(8,128)(2,1)}, u32[]{:S(2)}) %copy-start.1) | copy-done | bytes 196632
  21.3 0.9 %copy-done.2 = bf16[768,128]{1,0:T(8,128)(2,1)S(1)} copy-done((bf16[768,128]{1,0:T(8,128)(2,1)S(1)}, bf16[768,128]{1,0:T(8,128)(2,1)}, u32[]{:S(2)}) %copy-start.2) | copy-done | bytes 196632
  22.2 8.8 %inner.1 = (bf16[2,3,272,128]{3,2,1,0:T(8,128)(2,1)S(1)}, bf16[2,3,272,128]{3,2,1,0:T(8,128)(2,1)S(1)}, f32[2,272,128]{2,1,0:T(8,128)S(1)}, bf16[5,3,272,128]{3,...) custom-call(bf16[8,256,128]{2,1,0:T(8,128)(2,1)S(1)} %copy.21.f, ...), custom_call_target="tpu_custom_call" | custom-call | flops 1176502272 | bytes 4194304 | tf_op jit(solution)/shard_map/inner/pallas_call | solution.py:294
  30.9 0.0 collective-permute-done.1
  30.9 0.0 collective-permute-done.2
  31.0 3.0 %outer.1 = (bf16[9,3,272,128]{3,2,1,0:T(8,128)(2,1)S(1)}, f32[576,128]{1,0:T(8,128)S(1)}) custom-call(bf16[8,256,128]{2,1,0:T(8,128)(2,1)S(1)} %copy.21.f, bf16[8,256,128]{2,1,0:T(8,128)(2,1)S(1)} %copy.22.g, bf16[16,16,128]{2,1,0:T(8,128)(2,1)S(1)} %get-tuple-element.44.c_left, bf16[16,16,128]{2,1,0:T(8,128)(2,1)S(1)} %get-tuple-element.43.c_right, ...), custom_call_target="tpu_custom_call" | custom-call | flops 748683264 | bytes 4194304 | tf_op jit(solution)/shard_map/outer/pallas_call | solution.py:325
  34.0 0.1 collective-permute-start.5
  34.1 1.4 %collective-permute-done.5 = f32[288,128]{1,0:T(8,128)S(1)} collective-permute-done((f32[288,128]{1,0:T(8,128)S(1)}, f32[288,128]{1,0:T(8,128)S(1)}, u32[]{:S(2)}, u32[]{:S(2)}) %collective-permute-start.5) | collective-permute-done | bytes 147488 | tf_op jit(solution)/shard_map/ppermute | solution.py:365
  35.5 0.1 collective-permute-start.6
  35.5 0.6 %collective-permute-start.7 = (bf16[288,128]{1,0:T(8,128)(2,1)S(1)}, bf16[288,128]{1,0:T(8,128)(2,1)S(1)}, u32[]{:S(2)}, u32[]{:S(2)}) collective-permute-start(bf16[288,128]{1,0:T(8,128)(2,1)S(1)} %add_convert_fusion.1), channel_id=1, source_target_pairs={{0,1},{1,0},{2,3},{3,2},{4,5},{5,4},{6,7},{7,6},{8,9},{9,8},{10,11... | collective-permute-start | bytes 221192 | tf_op jit(solution)/shard_map/ppermute | solution.py:390
  36.1 2.9 %collective-permute-start.8 = (bf16[288,128]{1,0:T(8,128)(2,1)S(1)}, bf16[288,128]{1,0:T(8,128)(2,1)S(1)}, u32[]{:S(2)}, u32[]{:S(2)}) collective-permute-start(bf16[288,128]{1,0:T(8,128)(2,1)S(1)} %add_convert_fusion.1), channel_id=1, source_target_pairs={{0,3},{1,2},{2,1},{3,0},{4,7},{5,6},{6,5},{7,4},{8,11},{9,10},{10,... | collective-permute-start | bytes 221192 | tf_op jit(solution)/shard_map/ppermute | solution.py:390
  39.0 0.9 %collective-permute-done.6 = bf16[288,128]{1,0:T(8,128)(2,1)S(1)} collective-permute-done((bf16[288,128]{1,0:T(8,128)(2,1)S(1)}, bf16[288,128]{1,0:T(8,128)(2,1)S(1)}, u32[]{:S(2)}, u32[]{:S(2)}) %collective-permute-start.6) | collective-permute-done | bytes 73760 | tf_op jit(solution)/shard_map/ppermute | solution.py:390
  39.9 0.1 collective-permute-done.7
  40.0 2.2 %collective-permute-done.8 = bf16[288,128]{1,0:T(8,128)(2,1)S(1)} collective-permute-done((bf16[288,128]{1,0:T(8,128)(2,1)S(1)}, bf16[288,128]{1,0:T(8,128)(2,1)S(1)}, u32[]{:S(2)}, u32[]{:S(2)}) %collective-permute-start.8) | collective-permute-done | bytes 73760 | tf_op jit(solution)/shard_map/ppermute | solution.py:390
  42.2 1.1 %collective-permute-start.10 = (bf16[288,128]{1,0:T(8,128)(2,1)S(1)}, bf16[288,128]{1,0:T(8,128)(2,1)S(1)}, u32[]{:S(2)}, u32[]{:S(2)}) collective-permute-start(bf16[288,128]{1,0:T(8,128)(2,1)S(1)} %add_convert_fusion), channel_id=1, source_target_pairs={{0,8},{1,9},{2,10},{3,11},{4,12},{5,13},{6,14},{7,15},{8,0},{9,1},... | collective-permute-start | bytes 221192 | tf_op jit(solution)/shard_map/ppermute | solution.py:390
  43.3 2.9 %collective-permute-start.11 = (bf16[288,128]{1,0:T(8,128)(2,1)S(1)}, bf16[288,128]{1,0:T(8,128)(2,1)S(1)}, u32[]{:S(2)}, u32[]{:S(2)}) collective-permute-start(bf16[288,128]{1,0:T(8,128)(2,1)S(1)} %add_convert_fusion), channel_id=1, source_target_pairs={{0,12},{1,13},{2,14},{3,15},{4,8},{5,9},{6,10},{7,11},{8,4},{9,5},... | collective-permute-start | bytes 221192 | tf_op jit(solution)/shard_map/ppermute | solution.py:390
  46.2 0.0 collective-permute-start.9
  46.2 1.3 %collective-permute-done.10 = bf16[288,128]{1,0:T(8,128)(2,1)S(1)} collective-permute-done((bf16[288,128]{1,0:T(8,128)(2,1)S(1)}, bf16[288,128]{1,0:T(8,128)(2,1)S(1)}, u32[]{:S(2)}, u32[]{:S(2)}) %collective-permute-start.10) | collective-permute-done | bytes 73760 | tf_op jit(solution)/shard_map/ppermute | solution.py:390
  47.5 2.0 %collective-permute-done.11 = bf16[288,128]{1,0:T(8,128)(2,1)S(1)} collective-permute-done((bf16[288,128]{1,0:T(8,128)(2,1)S(1)}, bf16[288,128]{1,0:T(8,128)(2,1)S(1)}, u32[]{:S(2)}, u32[]{:S(2)}) %collective-permute-start.11) | collective-permute-done | bytes 73760 | tf_op jit(solution)/shard_map/ppermute | solution.py:390
  49.5 1.1 %collective-permute-done.9 = bf16[288,128]{1,0:T(8,128)(2,1)S(1)} collective-permute-done((bf16[288,128]{1,0:T(8,128)(2,1)S(1)}, bf16[288,128]{1,0:T(8,128)(2,1)S(1)}, u32[]{:S(2)}, u32[]{:S(2)}) %collective-permute-start.9) | collective-permute-done | bytes 73760 | tf_op jit(solution)/shard_map/ppermute | solution.py:390
  50.6 0.1 collective-permute-start.12
  50.7 2.2 %last.1 = bf16[8,256,128]{2,1,0:T(8,128)(2,1)S(1)} custom-call(bf16[9,3,272,128]{3,2,1,0:T(8,128)(2,1)S(1)} %get-tuple-element.24.ds1, bf16[768,128]{1,0:T(8,128)(2,1)S(1)} %copy-done.3), custom_call_target="tpu_custom_call" | custom-call | flops 427819008 | bytes 4194304 | tf_op jit(solution)/shard_map/last/pallas_call | solution.py:347
  52.9 0.2 copy.23
  53.1 1.1 %copy.25 = bf16[1,64,16,256]{3,2,1,0:T(8,128)(2,1)} copy(bf16[1,64,16,256]{3,1,2,0:T(8,128)(2,1)S(1)} %bitcast.37) | data formatting | bytes 1048576
  54.2 0.0 collective-permute-done.12
  54.2 0.4 div.10
  54.6 0.2 copy.24
  54.8 0.8 %slice_bitcast_fusion = (f32[3,3,64,64]{3,2,1,0:T(8,128)}, f32[3,3,64,64]{3,2,1,0:T(8,128)}) fusion(f32[2,3,3,64,64]{4,3,2,1,0:T(8,128)S(1)} %bitcast.36), kind=kLoop, calls=%fused_computation | loop fusion | bytes 589824 | tf_op jit(solution)/shard_map/squeeze | solution.py:418
  (20 shorter events, 0.3 us)
Async XLA Ops:
  0.6 1.6 %copy-start.4 = (bf16[1,64,16,256]{3,2,1,0:T(8,128)(2,1)S(1)}, bf16[1,64,16,256]{3,2,1,0:T(8,128)(2,1)}, u32[]{:S(2)}) copy-start(bf16[1,64,16,256]{3,2,1,0:T(8,128)(2,1)} %param.5) | copy-start | bytes 1572868
  2.7 16.7 %collective-permute-start = (bf16[16,16,128]{2,1,0:T(8,128)(2,1)S(1)}, bf16[16,16,128]{2,1,0:T(8,128)(2,1)S(1)}, u32[]{:S(2)}, u32[]{:S(2)}) collective-permute-start(bf16[16,16,128]{2,1,0:T(8,128)(2,1)S(1)} %fusion.1), channel_id=1, source_target_pairs={{0,1},{1,0},{2,3},{3,2},{4,5},{5,4},{6,7},{7,6},{8,9},{9,8},{10,11... | collective-permute-start | bytes 196616 | tf_op jit(solution)/shard_map/ppermute | solution.py:33
  6.2 13.1 %collective-permute-start.3 = (bf16[3,16,128]{2,1,0:T(8,128)(2,1)S(1)}, bf16[3,16,128]{2,1,0:T(8,128)(2,1)S(1)}, u32[]{:S(2)}, u32[]{:S(2)}) collective-permute-start(bf16[3,16,128]{2,1,0:T(8,128)(2,1)S(1)} %broadcast_select_fusion.6), channel_id=1, source_target_pairs={{2,5},{3,4},{4,3},{5,2},{6,9},{7,8},{8,7},{9,6},{10,13},{11,12},{1... | collective-permute-start | bytes 36872 | tf_op jit(solution)/shard_map/ppermute | solution.py:57
  6.9 12.4 %collective-permute-start.4 = (bf16[3,16,128]{2,1,0:T(8,128)(2,1)S(1)}, bf16[3,16,128]{2,1,0:T(8,128)(2,1)S(1)}, u32[]{:S(2)}, u32[]{:S(2)}) collective-permute-start(bf16[3,16,128]{2,1,0:T(8,128)(2,1)S(1)} %get-tuple-element.30), channel_id=1, source_target_pairs={{0,3},{1,2},{2,1},{3,0},{4,7},{5,6},{6,5},{7,4},{8,11},{9,10},{10,... | collective-permute-start | bytes 36872 | tf_op jit(solution)/shard_map/ppermute | solution.py:57
  12.2 18.7 %collective-permute-start.1 = (bf16[3,256,128]{2,1,0:T(8,128)(2,1)S(1)}, bf16[3,256,128]{2,1,0:T(8,128)(2,1)S(1)}, u32[]{:S(2)}, u32[]{:S(2)}) collective-permute-start(bf16[3,256,128]{2,1,0:T(8,128)(2,1)S(1)} %get-tuple-element.42), channel_id=1, source_target_pairs={{2,4},{4,2},{6,8},{8,6},{10,12},{12,10},{3,5},{5,3},{7,9},{9,7},{1... | collective-permute-start | bytes 589832 | tf_op jit(solution)/shard_map/ppermute | solution.py:33
  12.9 18.1 %collective-permute-start.2 = (bf16[3,256,128]{2,1,0:T(8,128)(2,1)S(1)}, bf16[3,256,128]{2,1,0:T(8,128)(2,1)S(1)}, u32[]{:S(2)}, u32[]{:S(2)}) collective-permute-start(bf16[3,256,128]{2,1,0:T(8,128)(2,1)S(1)} %get-tuple-element.41), channel_id=1, source_target_pairs={{0,2},{2,0},{4,6},{6,4},{8,10},{10,8},{12,14},{14,12},{1,3},{3,1},... | collective-permute-start | bytes 589832 | tf_op jit(solution)/shard_map/ppermute | solution.py:33
  19.4 0.9 %copy-start = (bf16[768,128]{1,0:T(8,128)(2,1)S(1)}, bf16[768,128]{1,0:T(8,128)(2,1)}, u32[]{:S(2)}) copy-start(bf16[768,128]{1,0:T(8,128)(2,1)} %get-tuple-element.15.w1) | copy-start | bytes 589828
  20.3 0.9 %copy-start.1 = (bf16[768,128]{1,0:T(8,128)(2,1)S(1)}, bf16[768,128]{1,0:T(8,128)(2,1)}, u32[]{:S(2)}) copy-start(bf16[768,128]{1,0:T(8,128)(2,1)} %get-tuple-element.16.w2) | copy-start | bytes 589828
  21.3 0.9 %copy-start.2 = (bf16[768,128]{1,0:T(8,128)(2,1)S(1)}, bf16[768,128]{1,0:T(8,128)(2,1)}, u32[]{:S(2)}) copy-start(bf16[768,128]{1,0:T(8,128)(2,1)} %get-tuple-element.17.v2) | copy-start | bytes 589828
  31.0 19.7 %copy-start.3 = (bf16[768,128]{1,0:T(8,128)(2,1)S(1)}, bf16[768,128]{1,0:T(8,128)(2,1)}, u32[]{:S(2)}) copy-start(bf16[768,128]{1,0:T(8,128)(2,1)} %get-tuple-element.25.v1) | copy-start | bytes 589828
  34.0 1.4 %collective-permute-start.5 = (f32[288,128]{1,0:T(8,128)S(1)}, f32[288,128]{1,0:T(8,128)S(1)}, u32[]{:S(2)}, u32[]{:S(2)}) collective-permute-start(f32[288,128]{1,0:T(8,128)S(1)} %constant_dynamic-slice_fusion), channel_id=1, source_target_pairs={{0,16},{16,0},{1,17},{17,1},{2,18},{18,2},{3,19},{19,3},{4,20},{20... | collective-permute-start | bytes 442376 | tf_op jit(solution)/shard_map/ppermute | solution.py:365
  35.5 4.4 %collective-permute-start.6 = (bf16[288,128]{1,0:T(8,128)(2,1)S(1)}, bf16[288,128]{1,0:T(8,128)(2,1)S(1)}, u32[]{:S(2)}, u32[]{:S(2)}) collective-permute-start(bf16[288,128]{1,0:T(8,128)(2,1)S(1)} %add_convert_fusion.1), channel_id=1, source_target_pairs={{0,2},{1,3},{2,0},{3,1},{4,6},{5,7},{6,4},{7,5},{8,10},{9,11},{10,... | collective-permute-start | bytes 221192 | tf_op jit(solution)/shard_map/ppermute | solution.py:390
  35.5 4.4 %collective-permute-start.7 = (bf16[288,128]{1,0:T(8,128)(2,1)S(1)}, bf16[288,128]{1,0:T(8,128)(2,1)S(1)}, u32[]{:S(2)}, u32[]{:S(2)}) collective-permute-start(bf16[288,128]{1,0:T(8,128)(2,1)S(1)} %add_convert_fusion.1), channel_id=1, source_target_pairs={{0,1},{1,0},{2,3},{3,2},{4,5},{5,4},{6,7},{7,6},{8,9},{9,8},{10,11... | collective-permute-start | bytes 221192 | tf_op jit(solution)/shard_map/ppermute | solution.py:390
  36.1 6.0 %collective-permute-start.8 = (bf16[288,128]{1,0:T(8,128)(2,1)S(1)}, bf16[288,128]{1,0:T(8,128)(2,1)S(1)}, u32[]{:S(2)}, u32[]{:S(2)}) collective-permute-start(bf16[288,128]{1,0:T(8,128)(2,1)S(1)} %add_convert_fusion.1), channel_id=1, source_target_pairs={{0,3},{1,2},{2,1},{3,0},{4,7},{5,6},{6,5},{7,4},{8,11},{9,10},{10,... | collective-permute-start | bytes 221192 | tf_op jit(solution)/shard_map/ppermute | solution.py:390
  42.2 5.3 %collective-permute-start.10 = (bf16[288,128]{1,0:T(8,128)(2,1)S(1)}, bf16[288,128]{1,0:T(8,128)(2,1)S(1)}, u32[]{:S(2)}, u32[]{:S(2)}) collective-permute-start(bf16[288,128]{1,0:T(8,128)(2,1)S(1)} %add_convert_fusion), channel_id=1, source_target_pairs={{0,8},{1,9},{2,10},{3,11},{4,12},{5,13},{6,14},{7,15},{8,0},{9,1},... | collective-permute-start | bytes 221192 | tf_op jit(solution)/shard_map/ppermute | solution.py:390
  43.3 6.2 %collective-permute-start.11 = (bf16[288,128]{1,0:T(8,128)(2,1)S(1)}, bf16[288,128]{1,0:T(8,128)(2,1)S(1)}, u32[]{:S(2)}, u32[]{:S(2)}) collective-permute-start(bf16[288,128]{1,0:T(8,128)(2,1)S(1)} %add_convert_fusion), channel_id=1, source_target_pairs={{0,12},{1,13},{2,14},{3,15},{4,8},{5,9},{6,10},{7,11},{8,4},{9,5},... | collective-permute-start | bytes 221192 | tf_op jit(solution)/shard_map/ppermute | solution.py:390
  46.2 4.4 %collective-permute-start.9 = (bf16[288,128]{1,0:T(8,128)(2,1)S(1)}, bf16[288,128]{1,0:T(8,128)(2,1)S(1)}, u32[]{:S(2)}, u32[]{:S(2)}) collective-permute-start(bf16[288,128]{1,0:T(8,128)(2,1)S(1)} %add_convert_fusion), channel_id=1, source_target_pairs={{0,4},{1,5},{2,6},{3,7},{4,0},{5,1},{6,2},{7,3},{8,12},{9,13},{10,... | collective-permute-start | bytes 221192 | tf_op jit(solution)/shard_map/ppermute | solution.py:390
  50.6 3.6 %collective-permute-start.12 = (f32[288,128]{1,0:T(8,128)S(1)}, f32[288,128]{1,0:T(8,128)S(1)}, u32[]{:S(2)}, u32[]{:S(2)}) collective-permute-start(f32[288,128]{1,0:T(8,128)S(1)} %add_add_fusion), channel_id=1, source_target_pairs={{0,16},{16,0},{1,17},{17,1},{2,18},{18,2},{3,19},{19,3},{4,20},{20... | collective-permute-start | bytes 442376 | tf_op jit(solution)/shard_map/ppermute | solution.py:394

commit v3 on v2

--- a/solution.py
+++ b/solution.py
@@ -1,3 +1,5 @@
+import functools
+
 import jax
 import jax.numpy as jnp
 from jax import lax
@@ -35,33 +37,6 @@
             got.append(jnp.zeros_like(low))
     even = is_low(axis, 0)
     return jnp.where(even, got[1], got[0]), jnp.where(even, got[0], got[1])
-
-
-def swap_corners(corners):
-    row_count, col_count = lax.axis_size("row"), lax.axis_size("col")
-    got = {}
-    for row_parity in range(2):
-        for col_parity in range(2):
-            perm = [
-                (r * col_count + c, to_r * col_count + to_c)
-                for r, to_r in neighbours("row", row_parity)
-                for c, to_c in neighbours("col", col_parity)
-            ]
-            if not perm:
-                got[row_parity, col_parity] = jnp.zeros_like(corners[0][0])
-                continue
-            down, right = is_low("row", row_parity), is_low("col", col_parity)
-            sent = jnp.where(
-                down, jnp.where(right, corners[1][1], corners[1][0]), jnp.where(right, corners[0][1], corners[0][0])
-            )
-            got[row_parity, col_parity] = lax.ppermute(sent, ("row", "col"), perm)
-    even_row, even_col = is_low("row", 0), is_low("col", 0)
-
-    def pick(row_parity, col_parity):
-        across = [jnp.where(even_col, got[p, col_parity], got[p, 1 - col_parity]) for p in range(2)]
-        return jnp.where(even_row, across[row_parity], across[1 - row_parity])
-
-    return [[pick(1, 1), pick(1, 0)], [pick(0, 1), pick(0, 0)]]
 
 
 def to_pairs(cells):
@@ -92,16 +67,21 @@
 
 def make_weights(kernel_one, kernel_two):
     shape = jax.ShapeDtypeStruct((12 * HALF, LANES), BF)
-    return pl.pallas_call(weights_body, out_shape=(shape,) * 4, name="weights")(kernel_one, kernel_two)
+    return pl.pallas_call(
+        weights_body,
+        out_shape=(shape,) * 4,
+        compiler_params=pltpu.CompilerParams(vmem_limit_bytes=8 * 2**20),
+        cost_estimate=cost(2),
+        name="weights",
+    )(kernel_one, kernel_two)
 
 
 def sigmoid(value):
     return 0.5 * jnp.tanh(0.5 * value) + 0.5
 
 
-def with_rim(own, right, left):
-    own, right, left = own.astype(F32), right.astype(F32), left.astype(F32)
-    return jnp.concatenate([own, right[: RIM // 2], left[RIM // 2 :]], axis=0)
+def with_rim(own, rim):
+    return jnp.concatenate([own.astype(F32), rim.astype(F32)], axis=0)
 
 
 def store_shifts(value, tmp, out, index):
@@ -140,13 +120,13 @@
     acc[...] += jnp.dot(feat_t, near, preferred_element_type=F32)
 
 
-def inner_body(f, g, c_left, c_right, w1, w2, v2, hs_edge, ds2_edge, slope_edge, ds1, acc1, acc2, fs, hs, ds2, slope, ht, tmp):
+def inner_body(f, g, edge, w1, w2, v2, hs_edge, ds2_edge, slope_edge, ds1, acc1, acc2, fs, hs, ds2, slope, ht, tmp):
     pairs, cols = f.shape[:2]
     _, _, rim = edge_masks()
 
     @pl.loop(0, pairs)
     def _(j):
-        store_shifts(with_rim(f[j], c_right[j], c_left[j]), tmp, fs, j)
+        store_shifts(with_rim(f[j], edge[j]), tmp, fs, j)
 
     @pl.loop(0, pairs - 1)
     def _(j):
@@ -161,7 +141,7 @@
     def _(j):
         pre = band_dot((hs, j), (hs, j + 1), w2)
         sig = sigmoid(pre)
-        grad = with_rim(g[j + 1], c_right[pairs + j + 1], c_left[pairs + j + 1])
+        grad = with_rim(g[j + 1], edge[pairs + j + 1])
         delta = grad * (sig + pre * sig * (1.0 - sig))
         store_shifts(delta, tmp, ds2, j)
 
@@ -191,7 +171,7 @@
 
 
 def rim_body(
-    f, g, c_left, c_right, above, below, c_above, c_below, w1, w2, v2, hs_edge, ds2_edge, slope_edge, ds1_in, acc1_in, acc2_in,
+    f, g, edge, above, below, w1, w2, v2, hs_edge, ds2_edge, slope_edge, ds1_in, acc1_in, acc2_in,
     ds1, term, fs, hs, ds2, slope, acc1, acc2, tmp,
 ):
     pairs, cols = f.shape[:2]
@@ -201,11 +181,10 @@
     acc2[...] = acc2_in[...]
 
     def own(ref, base, j):
-        return with_rim(ref[j], c_right[base + j], c_left[base + j])
+        return with_rim(ref[j], edge[base + j])
 
     def far(side, j):
-        halo, corner = (above, c_above) if side == 0 else (below, c_below)
-        return with_rim(halo[j], corner[1, j], corner[0, j])
+        return (above, below)[side][j].astype(F32)
 
     for side in range(2):
         flag = (top, bottom)[side]
@@ -269,8 +248,9 @@
             term[at : at + HALF] = jnp.concatenate([one, two], axis=1)
 
 
-def last_body(ds1, v1, gf):
+def last_body(ds1, v1, gf, done):
     pairs, cols = gf.shape[:2]
+    done[...] = jnp.zeros_like(done)
 
     @pl.loop(0, pairs)
     def _(j):
@@ -284,7 +264,7 @@
 PARAMS = pltpu.CompilerParams(vmem_limit_bytes=32 * 2**20)
 
 
-def inner(f, g, c_left, c_right, w1, w2, v2):
+def inner(f, g, edge, w1, w2, v2):
     pairs, cols = f.shape[:2]
     wide = cols + RIM
 
@@ -312,7 +292,7 @@
         compiler_params=PARAMS,
         cost_estimate=cost(22),
         name="inner",
-    )(f, g, c_left, c_right, w1, w2, v2)
+    )(f, g, edge, w1, w2, v2)
 
 
 def outer(f, *rest):
@@ -346,17 +326,62 @@
 def last(ds1, v1, cols):
     return pl.pallas_call(
         last_body,
-        out_shape=jax.ShapeDtypeStruct((ds1.shape[0] - 1, cols, LANES), BF),
+        out_shape=(
+            jax.ShapeDtypeStruct((ds1.shape[0] - 1, cols, LANES), BF),
+            jax.ShapeDtypeStruct((8, LANES), F32),
+        ),
         compiler_params=PARAMS,
         cost_estimate=cost(8),
         name="last",
     )(ds1, v1)
 
 
-def reduced(term):
+def four_body(own, one, two, three, done, out):
+    low = [ref[...].astype(F32) for ref in (own, one, two, three)]
+    out[...] = ((low[0] + low[1]) + (low[2] + low[3])).astype(BF)
+
+
+def sum_four(own, got, done):
+    return pl.pallas_call(
+        four_body,
+        out_shape=jax.ShapeDtypeStruct(own.shape, BF),
+        compiler_params=pltpu.CompilerParams(vmem_limit_bytes=4 * 2**20),
+        name="sum_four",
+    )(own, *got, done)
+
+
+def finish_body(part, other, one, two, *, scale):
+    half = part.shape[0]
+    first = lax.axis_index("dp") == 0
+    for tap in range(9):
+        rows = []
+        for at in range(tap * HALF, (tap + 1) * HALF, HALF // 2):
+            side, at = (0, at) if at < half else (1, at - half)
+            mine, theirs = part[at : at + HALF // 2], other[at : at + HALF // 2]
+            rows.append(jnp.where(first, mine, theirs) if side == 0 else jnp.where(first, theirs, mine))
+        both = jnp.concatenate(rows, axis=0).T * scale
+        one[tap // 3, tap % 3] = both[:HALF]
+        two[tap // 3, tap % 3] = both[HALF:]
+
+
+def finish(part, other, scale):
+    shape = jax.ShapeDtypeStruct((3, 3, HALF, HALF), F32)
+    return pl.pallas_call(
+        functools.partial(finish_body, scale=scale),
+        out_shape=(shape, shape),
+        compiler_params=pltpu.CompilerParams(vmem_limit_bytes=4 * 2**20),
+        name="finish",
+    )(part, other)
+
+
+def reduced(term, done):
     sizes = [lax.axis_size(axis) for axis in AXES]
     if sizes[0] != 2 or any(size & (size - 1) for size in sizes):
-        return lax.psum(term, AXES)
+        total = lax.psum(term, AXES)
+        half = term.shape[0] // 2
+        both = total[:half], total[half:]
+        core = lax.axis_index("dp") == 0
+        return jnp.where(core, *both), jnp.where(core, both[1], both[0])
     half = term.shape[0] // 2
     me = lax.axis_index("dp")
     swap = [(0, 1), (1, 0)]
@@ -387,12 +412,15 @@
                             to_r, to_c = to_r ^ flip[0], to_c ^ flip[1]
                         base = core * sizes[1]
                         perm.append(((base + r) * sizes[2] + c, (base + to_r) * sizes[2] + to_c))
-            got.append(lax.ppermute(low, AXES, perm).astype(F32))
+            got.append(lax.ppermute(low, AXES, perm))
+        if at == 0 and len(got) > 1 and len(groups) > 1:
+            part = sum_four(low, got, done)
+            continue
+        got = [one.astype(F32) for one in got]
         part = low.astype(F32) + got[0]
         if len(got) > 1:
             part = part + (got[1] + got[2])
-    other = lax.ppermute(part, "dp", swap)
-    return jnp.where(me == 0, jnp.concatenate([part, other]), jnp.concatenate([other, part]))
+    return part, lax.ppermute(part, "dp", swap)
 
 
 def shards(features, grad_out, kernel_one, kernel_two):
@@ -400,22 +428,22 @@
     pairs = rows // 2
     feat, grad = to_pairs(features), to_pairs(grad_out)
     own = jnp.concatenate([feat, grad], axis=0)
-    starts, ends = own[:, :RIM], own[:, cols - RIM :]
-    c_left, c_right = swap_one(starts, ends, "col")
+    from_left, from_right = swap_one(own[:, : RIM // 2], own[:, cols - RIM // 2 :], "col")
+    edge = jnp.concatenate([from_right, from_left], axis=1)
+    w1, w2, v2, v1 = make_weights(kernel_one, kernel_two)
     low = jnp.concatenate([feat[:2], grad[:1]], axis=0)
     high = jnp.concatenate([feat[pairs - 2 :], grad[pairs - 1 :]], axis=0)
+    low_edge = jnp.concatenate([edge[:2], edge[pairs : pairs + 1]], axis=0)
+    high_edge = jnp.concatenate([edge[pairs - 2 : pairs], edge[2 * pairs - 1 :]], axis=0)
+    low, high = jnp.concatenate([low, low_edge], axis=1), jnp.concatenate([high, high_edge], axis=1)
     above, below = swap_one(low, high, "row")
-    corners = [[edge[:, :RIM], edge[:, cols - RIM :]] for edge in (low, high)]
-    corners = swap_corners(corners)
-    c_above, c_below = jnp.stack(corners[0]), jnp.stack(corners[1])
-    w1, w2, v2, v1 = make_weights(kernel_one, kernel_two)
-    state = inner(feat, grad, c_left, c_right, w1, w2, v2)
-    ds1, term = outer(feat, grad, c_left, c_right, above, below, c_above, c_below, w1, w2, v2, *state)
-    total = reduced(term)
-    gf = last(ds1, v1, cols)
+    state = inner(feat, grad, edge, w1, w2, v2)
+    ds1, term = outer(feat, grad, edge, above, below, w1, w2, v2, *state)
+    gf, done = last(ds1, v1, cols)
+    part, other = reduced(term, done)
     count = slides * lax.axis_size("dp") * rows * lax.axis_size("row") * cols * lax.axis_size("col")
-    total = (total / jnp.sqrt(F32(count))).reshape(3, 3, chans, 2, chans).transpose(3, 0, 1, 4, 2)
-    return from_pairs(gf), total[0], total[1]
+    grad_one, grad_two = finish(part, other, float(count) ** -0.5)
+    return from_pairs(gf), grad_one, grad_two
 
 
 def solution(mesh):

time: 56 us -> 46.9 us (0.84)
  starting transfers between devices: 21.6 us -> 16.7 us
  local copies, waits for them, and re-layouts: 7.99 us -> 3.8 us
  waiting for transfers between devices: 8.83 us -> 9.74 us
  Pallas kernels: 16 us -> 15.3 us
    ppermute x9 -> x7, starting transfers between devices: 13.5 us -> 8.08 us  [the longest x6 8.01 us: reduced(): got.append(lax.ppermute(low, AXES, perm))]
    unnamed x13 -> x9, local copies, waits for them, and re-layouts: 5.28 us -> 2.52 us
    ppermute x3, waiting for transfers between devices: 0.01 us -> 1 us  [swap_one(): lax.ppermute(jnp.where(is_low(axis, parity), high, low), axis, perm)]
    squeeze x1 -> x0, local copies, waits for them, and re-layouts: 0.85 us -> none  [shards(): return (from_pairs(gf), total[0], total[1])]
    pallas_call x2 -> x4, Pallas kernels: 4.31 us -> 3.61 us  [the longest x1 2.22 us: last(): pl.pallas_call(last_body, out_shape=(jax.ShapeDtypeStruct((ds1.shape[0] -...]
    div x2 -> x0, local copies, waits for them, and re-layouts: 0.58 us -> none  [shards(): total / jnp.sqrt(F32(count))]
    ppermute x9 -> x7, waiting for transfers between devices: 7.47 us -> 7.39 us  [the longest x6 7.33 us: reduced(): got.append(lax.ppermute(low, AXES, perm))]
  transfers between devices with their start and end apart: 13 -> 11, of which waited for: 7 -> 6; matrix products, arithmetic and copies ran while one was open for 3% -> 4% of each run, Pallas kernels for 23% -> 24%
where the time goes in v3:
time: 46.9 us; the launch traced here: 46.7 us
  starting transfers between devices  16.7 us (36%)
  Pallas kernels  15.3 us (33%)
  waiting for transfers between devices  9.74 us (21%)
  local copies, waits for them, and re-layouts  3.8 us (8%)
  between operations  0.91 us (2%)
    pallas_call x1, Pallas kernels, inner(): pl.pallas_call(inner_body, out_shape=(jax.ShapeDtypeStruct(shifts(2), BF)...  8.76 us
    ppermute x3, starting transfers between devices, swap_one(): lax.ppermute(jnp.where(is_low(axis, parity), high, low), axis, perm)  8.55 us
    ppermute x6, starting transfers between devices, reduced(): got.append(lax.ppermute(low, AXES, perm))  8.01 us
    ppermute x6, waiting for transfers between devices, reduced(): got.append(lax.ppermute(low, AXES, perm))  7.33 us
    pallas_call x1, Pallas kernels, outer(): pl.pallas_call(rim_body, out_shape=(jax.ShapeDtypeStruct(shifts(pairs + 1...  2.94 us
    unnamed x9, local copies, waits for them, and re-layouts  2.52 us
    pallas_call x1, Pallas kernels, last(): pl.pallas_call(last_body, out_shape=(jax.ShapeDtypeStruct((ds1.shape[0] -...  2.22 us
    ppermute x1, waiting for transfers between devices, reduced(): part = mine + lax.ppermute(other, 'dp', swap)  1.35 us
  transfers between devices with their start and end apart: 11, of which 6 were waited for; matrix products, arithmetic and copies ran while one was open for 4% of the time, Pallas kernels for 24%

profile of v3, /device:TPU:0, one launch (start us, length us, event | category | flops | bytes accessed | tf_op | source)
XLA Modules:
  0.0 46.7 jit_solution(7247371445414315520)
XLA Ops:
  0.6 0.0 copy-start.2
  0.7 1.3 %copy.10 = bf16[1,64,16,256]{3,1,2,0:T(8,128)(2,1)S(1)} copy(bf16[1,64,16,256]{3,2,1,0:T(8,128)(2,1)} %param.4) | data formatting | bytes 1048576 | tf_op args[0]
  1.9 0.3 copy.20.f
  2.2 0.0 copy-done.2
  2.2 0.2 copy.11
  2.4 0.0 copy-start
  2.4 0.0 copy-start.1
  2.4 0.3 copy.21.g
  2.7 3.0 %collective-permute-start = (bf16[16,8,128]{2,1,0:T(8,128)(2,1)S(1)}, bf16[16,8,128]{2,1,0:T(8,128)(2,1)S(1)}, u32[]{:S(2)}, u32[]{:S(2)}) collective-permute-start(bf16[16,8,128]{2,1,0:T(8,128)(2,1)S(1)} %fusion), channel_id=1, source_target_pairs={{0,1},{1,0},{2,3},{3,2},{4,5},{5,4},{6,7},{7,6},{8,9},{9,8},{10,11... | collective-permute-start | bytes 98312 | tf_op jit(solution)/shard_map/ppermute | solution.py:35
  5.7 0.1 copy.14
  5.9 0.1 copy.16
  6.0 0.1 copy.15
  6.1 0.1 copy.17
  6.3 0.0 copy-done
  6.3 0.0 copy-done.1
  6.3 0.3 weights.1
  6.6 1.0 %collective-permute-done = bf16[16,8,128]{2,1,0:T(8,128)(2,1)S(1)} collective-permute-done((bf16[16,8,128]{2,1,0:T(8,128)(2,1)S(1)}, bf16[16,8,128]{2,1,0:T(8,128)(2,1)S(1)}, u32[]{:S(2)}, u32[]{:S(2)}) %collective-permute-start) | collective-permute-done | bytes 32800 | tf_op jit(solution)/shard_map/ppermute | solution.py:35
  7.6 0.1 broadcast_select_fusion.3
  7.7 0.7 %collective-permute-start.1 = (bf16[3,272,128]{2,1,0:T(8,128)(2,1)S(1)}, bf16[3,272,128]{2,1,0:T(8,128)(2,1)S(1)}, u32[]{:S(2)}, u32[]{:S(2)}) collective-permute-start(bf16[3,272,128]{2,1,0:T(8,128)(2,1)S(1)} %get-tuple-element.45), channel_id=1, source_target_pairs={{2,4},{4,2},{6,8},{8,6},{10,12},{12,10},{3,5},{5,3},{7,9},{9,7},{1... | collective-permute-start | bytes 626696 | tf_op jit(solution)/shard_map/ppermute | solution.py:35
  8.4 4.9 %collective-permute-start.2 = (bf16[3,272,128]{2,1,0:T(8,128)(2,1)S(1)}, bf16[3,272,128]{2,1,0:T(8,128)(2,1)S(1)}, u32[]{:S(2)}, u32[]{:S(2)}) collective-permute-start(bf16[3,272,128]{2,1,0:T(8,128)(2,1)S(1)} %get-tuple-element.44), channel_id=1, source_target_pairs={{0,2},{2,0},{4,6},{6,4},{8,10},{10,8},{12,14},{14,12},{1,3},{3,1},... | collective-permute-start | bytes 626696 | tf_op jit(solution)/shard_map/ppermute | solution.py:35
  13.3 8.8 %inner.1 = (bf16[2,3,272,128]{3,2,1,0:T(8,128)(2,1)S(1)}, bf16[2,3,272,128]{3,2,1,0:T(8,128)(2,1)S(1)}, f32[2,272,128]{2,1,0:T(8,128)S(1)}, bf16[5,3,272,128]{3,...) custom-call(bf16[8,256,128]{2,1,0:T(8,128)(2,1)S(1)} %copy.20.f, ...), custom_call_target="tpu_custom_call" | custom-call | flops 1176502272 | bytes 4194304 | tf_op jit(solution)/shard_map/inner/pallas_call | solution.py:274
  22.1 0.0 collective-permute-done.1
  22.1 0.0 collective-permute-done.2
  22.1 0.1 broadcast_select_fusion.1
  22.1 2.9 %outer.1 = (bf16[9,3,272,128]{3,2,1,0:T(8,128)(2,1)S(1)}, f32[576,128]{1,0:T(8,128)S(1)}) custom-call(bf16[8,256,128]{2,1,0:T(8,128)(2,1)S(1)} %copy.20.f, bf16[8,256,128]{2,1,0:T(8,128)(2,1)S(1)} %copy.21.g, bf16[16,16,128]{2,1,0:T(8,128)(2,1)S(1)} %pad_maximum_fusion.edge, bf16[3,272,128]{2,1,0:T(8,128)(2,1)S(1)} %get-tuple-element.43.above, ...), custom_call_target="tpu_custom_call" | custom-call | flops 748683264 | bytes 4194304 | tf_op jit(solution)/shard_map/outer/pallas_call | solution.py:305
  25.1 0.1 collective-permute-start.3
  25.2 1.4 %collective-permute-done.3 = f32[288,128]{1,0:T(8,128)S(1)} collective-permute-done((f32[288,128]{1,0:T(8,128)S(1)}, f32[288,128]{1,0:T(8,128)S(1)}, u32[]{:S(2)}, u32[]{:S(2)}) %collective-permute-start.3) | collective-permute-done | bytes 147488 | tf_op jit(solution)/shard_map/ppermute | solution.py:390
  26.6 0.8 %collective-permute-start.4 = (bf16[288,128]{1,0:T(8,128)(2,1)S(1)}, bf16[288,128]{1,0:T(8,128)(2,1)S(1)}, u32[]{:S(2)}, u32[]{:S(2)}) collective-permute-start(bf16[288,128]{1,0:T(8,128)(2,1)S(1)} %add_convert_fusion.own), channel_id=1, source_target_pairs={{0,2},{1,3},{2,0},{3,1},{4,6},{5,7},{6,4},{7,5},{8,10},{9,11},{10,... | collective-permute-start | bytes 221192 | tf_op jit(solution)/shard_map/ppermute | solution.py:415
  27.4 1.5 %collective-permute-start.5 = (bf16[288,128]{1,0:T(8,128)(2,1)S(1)}, bf16[288,128]{1,0:T(8,128)(2,1)S(1)}, u32[]{:S(2)}, u32[]{:S(2)}) collective-permute-start(bf16[288,128]{1,0:T(8,128)(2,1)S(1)} %add_convert_fusion.own), channel_id=1, source_target_pairs={{0,1},{1,0},{2,3},{3,2},{4,5},{5,4},{6,7},{7,6},{8,9},{9,8},{10,11... | collective-permute-start | bytes 221192 | tf_op jit(solution)/shard_map/ppermute | solution.py:415
  28.8 1.3 %collective-permute-start.6 = (bf16[288,128]{1,0:T(8,128)(2,1)S(1)}, bf16[288,128]{1,0:T(8,128)(2,1)S(1)}, u32[]{:S(2)}, u32[]{:S(2)}) collective-permute-start(bf16[288,128]{1,0:T(8,128)(2,1)S(1)} %add_convert_fusion.own), channel_id=1, source_target_pairs={{0,3},{1,2},{2,1},{3,0},{4,7},{5,6},{6,5},{7,4},{8,11},{9,10},{10,... | collective-permute-start | bytes 221192 | tf_op jit(solution)/shard_map/ppermute | solution.py:415
  30.1 2.2 %last.1 = (bf16[8,256,128]{2,1,0:T(8,128)(2,1)S(1)}, f32[8,128]{1,0:T(8,128)S(1)}) custom-call(bf16[9,3,272,128]{3,2,1,0:T(8,128)(2,1)S(1)} %get-tuple-element.28.ds1, bf16[768,128]{1,0:T(8,128)(2,1)S(1)} %get-tuple-element.29.v1), custom_call_target="tpu_custom_call" | custom-call | flops 427819008 | bytes 4194304 | tf_op jit(solution)/shard_map/last/pallas_call | solution.py:327
  32.3 0.0 collective-permute-done.4.one
  32.4 0.0 collective-permute-done.5.two
  32.4 1.7 %collective-permute-done.6.three = bf16[288,128]{1,0:T(8,128)(2,1)S(1)} collective-permute-done((bf16[288,128]{1,0:T(8,128)(2,1)S(1)}, bf16[288,128]{1,0:T(8,128)(2,1)S(1)}, u32[]{:S(2)}, u32[]{:S(2)}) %collective-permute-start.6) | collective-permute-done | bytes 73760 | tf_op jit(solution)/shard_map/ppermute | solution.py:415
  34.1 1.6 %collective-permute-start.7 = (bf16[288,128]{1,0:T(8,128)(2,1)S(1)}, bf16[288,128]{1,0:T(8,128)(2,1)S(1)}, u32[]{:S(2)}, u32[]{:S(2)}) collective-permute-start(bf16[288,128]{1,0:T(8,128)(2,1)S(1)} %sum_four.1), channel_id=1, source_target_pairs={{0,4},{1,5},{2,6},{3,7},{4,0},{5,1},{6,2},{7,3},{8,12},{9,13},{10,... | collective-permute-start | bytes 221192 | tf_op jit(solution)/shard_map/ppermute | solution.py:415
  35.8 2.3 %collective-permute-start.8 = (bf16[288,128]{1,0:T(8,128)(2,1)S(1)}, bf16[288,128]{1,0:T(8,128)(2,1)S(1)}, u32[]{:S(2)}, u32[]{:S(2)}) collective-permute-start(bf16[288,128]{1,0:T(8,128)(2,1)S(1)} %sum_four.1), channel_id=1, source_target_pairs={{0,8},{1,9},{2,10},{3,11},{4,12},{5,13},{6,14},{7,15},{8,0},{9,1},... | collective-permute-start | bytes 221192 | tf_op jit(solution)/shard_map/ppermute | solution.py:415
  38.0 0.6 %collective-permute-start.9 = (bf16[288,128]{1,0:T(8,128)(2,1)S(1)}, bf16[288,128]{1,0:T(8,128)(2,1)S(1)}, u32[]{:S(2)}, u32[]{:S(2)}) collective-permute-start(bf16[288,128]{1,0:T(8,128)(2,1)S(1)} %sum_four.1), channel_id=1, source_target_pairs={{0,12},{1,13},{2,14},{3,15},{4,8},{5,9},{6,10},{7,11},{8,4},{9,5},... | collective-permute-start | bytes 221192 | tf_op jit(solution)/shard_map/ppermute | solution.py:415
  38.6 0.0 collective-permute-done.7
  38.6 3.2 %collective-permute-done.8 = bf16[288,128]{1,0:T(8,128)(2,1)S(1)} collective-permute-done((bf16[288,128]{1,0:T(8,128)(2,1)S(1)}, bf16[288,128]{1,0:T(8,128)(2,1)S(1)}, u32[]{:S(2)}, u32[]{:S(2)}) %collective-permute-start.8) | collective-permute-done | bytes 73760 | tf_op jit(solution)/shard_map/ppermute | solution.py:415
  41.8 2.4 %collective-permute-done.9 = bf16[288,128]{1,0:T(8,128)(2,1)S(1)} collective-permute-done((bf16[288,128]{1,0:T(8,128)(2,1)S(1)}, bf16[288,128]{1,0:T(8,128)(2,1)S(1)}, u32[]{:S(2)}, u32[]{:S(2)}) %collective-permute-start.9) | collective-permute-done | bytes 73760 | tf_op jit(solution)/shard_map/ppermute | solution.py:415
  44.2 0.1 collective-permute-start.10
  44.3 0.2 copy.22
  44.5 1.1 %copy.23 = bf16[1,64,16,256]{3,2,1,0:T(8,128)(2,1)} copy(bf16[1,64,16,256]{3,1,2,0:T(8,128)(2,1)S(1)} %bitcast.23) | data formatting | bytes 1048576
  45.6 0.1 collective-permute-done.10.other
  45.7 1.0 %finish.1 = (f32[3,3,64,64]{3,2,1,0:T(8,128)}, f32[3,3,64,64]{3,2,1,0:T(8,128)}) custom-call(f32[288,128]{1,0:T(8,128)S(1)} %add_add_fusion.part, f32[288,128]{1,0:T(8,128)S(1)} %collective-permute-done.10.other), custom_call_target="tpu_custom_call" | custom-call | tf_op jit(solution)/shard_map/finish/pallas_call | solution.py:369
  (11 shorter events, 0.2 us)
Async XLA Ops:
  0.6 1.6 %copy-start.2 = (bf16[1,64,16,256]{3,2,1,0:T(8,128)(2,1)S(1)}, bf16[1,64,16,256]{3,2,1,0:T(8,128)(2,1)}, u32[]{:S(2)}) copy-start(bf16[1,64,16,256]{3,2,1,0:T(8,128)(2,1)} %param.5) | copy-start | bytes 1572868
  2.4 3.9 %copy-start = (bf16[3,3,64,64]{3,2,1,0:T(8,128)(2,1)S(1)}, bf16[3,3,64,64]{3,2,1,0:T(8,128)(2,1)}, u32[]{:S(2)}) copy-start(bf16[3,3,64,64]{3,2,1,0:T(8,128)(2,1)} %k1.1) | copy-start | bytes 221188
  2.4 3.9 %copy-start.1 = (bf16[3,3,64,64]{3,2,1,0:T(8,128)(2,1)S(1)}, bf16[3,3,64,64]{3,2,1,0:T(8,128)(2,1)}, u32[]{:S(2)}) copy-start(bf16[3,3,64,64]{3,2,1,0:T(8,128)(2,1)} %k2.1) | copy-start | bytes 221188
  2.7 4.9 %collective-permute-start = (bf16[16,8,128]{2,1,0:T(8,128)(2,1)S(1)}, bf16[16,8,128]{2,1,0:T(8,128)(2,1)S(1)}, u32[]{:S(2)}, u32[]{:S(2)}) collective-permute-start(bf16[16,8,128]{2,1,0:T(8,128)(2,1)S(1)} %fusion), channel_id=1, source_target_pairs={{0,1},{1,0},{2,3},{3,2},{4,5},{5,4},{6,7},{7,6},{8,9},{9,8},{10,11... | collective-permute-start | bytes 98312 | tf_op jit(solution)/shard_map/ppermute | solution.py:35
  7.7 14.3 %collective-permute-start.1 = (bf16[3,272,128]{2,1,0:T(8,128)(2,1)S(1)}, bf16[3,272,128]{2,1,0:T(8,128)(2,1)S(1)}, u32[]{:S(2)}, u32[]{:S(2)}) collective-permute-start(bf16[3,272,128]{2,1,0:T(8,128)(2,1)S(1)} %get-tuple-element.45), channel_id=1, source_target_pairs={{2,4},{4,2},{6,8},{8,6},{10,12},{12,10},{3,5},{5,3},{7,9},{9,7},{1... | collective-permute-start | bytes 626696 | tf_op jit(solution)/shard_map/ppermute | solution.py:35
  8.4 13.7 %collective-permute-start.2 = (bf16[3,272,128]{2,1,0:T(8,128)(2,1)S(1)}, bf16[3,272,128]{2,1,0:T(8,128)(2,1)S(1)}, u32[]{:S(2)}, u32[]{:S(2)}) collective-permute-start(bf16[3,272,128]{2,1,0:T(8,128)(2,1)S(1)} %get-tuple-element.44), channel_id=1, source_target_pairs={{0,2},{2,0},{4,6},{6,4},{8,10},{10,8},{12,14},{14,12},{1,3},{3,1},... | collective-permute-start | bytes 626696 | tf_op jit(solution)/shard_map/ppermute | solution.py:35
  25.1 1.4 %collective-permute-start.3 = (f32[288,128]{1,0:T(8,128)S(1)}, f32[288,128]{1,0:T(8,128)S(1)}, u32[]{:S(2)}, u32[]{:S(2)}) collective-permute-start(f32[288,128]{1,0:T(8,128)S(1)} %constant_dynamic-slice_fusion), channel_id=1, source_target_pairs={{0,16},{16,0},{1,17},{17,1},{2,18},{18,2},{3,19},{19,3},{4,20},{20... | collective-permute-start | bytes 442376 | tf_op jit(solution)/shard_map/ppermute | solution.py:390
  26.6 5.8 %collective-permute-start.4 = (bf16[288,128]{1,0:T(8,128)(2,1)S(1)}, bf16[288,128]{1,0:T(8,128)(2,1)S(1)}, u32[]{:S(2)}, u32[]{:S(2)}) collective-permute-start(bf16[288,128]{1,0:T(8,128)(2,1)S(1)} %add_convert_fusion.own), channel_id=1, source_target_pairs={{0,2},{1,3},{2,0},{3,1},{4,6},{5,7},{6,4},{7,5},{8,10},{9,11},{10,... | collective-permute-start | bytes 221192 | tf_op jit(solution)/shard_map/ppermute | solution.py:415
  27.4 5.0 %collective-permute-start.5 = (bf16[288,128]{1,0:T(8,128)(2,1)S(1)}, bf16[288,128]{1,0:T(8,128)(2,1)S(1)}, u32[]{:S(2)}, u32[]{:S(2)}) collective-permute-start(bf16[288,128]{1,0:T(8,128)(2,1)S(1)} %add_convert_fusion.own), channel_id=1, source_target_pairs={{0,1},{1,0},{2,3},{3,2},{4,5},{5,4},{6,7},{7,6},{8,9},{9,8},{10,11... | collective-permute-start | bytes 221192 | tf_op jit(solution)/shard_map/ppermute | solution.py:415
  28.8 5.3 %collective-permute-start.6 = (bf16[288,128]{1,0:T(8,128)(2,1)S(1)}, bf16[288,128]{1,0:T(8,128)(2,1)S(1)}, u32[]{:S(2)}, u32[]{:S(2)}) collective-permute-start(bf16[288,128]{1,0:T(8,128)(2,1)S(1)} %add_convert_fusion.own), channel_id=1, source_target_pairs={{0,3},{1,2},{2,1},{3,0},{4,7},{5,6},{6,5},{7,4},{8,11},{9,10},{10,... | collective-permute-start | bytes 221192 | tf_op jit(solution)/shard_map/ppermute | solution.py:415
  34.1 4.5 %collective-permute-start.7 = (bf16[288,128]{1,0:T(8,128)(2,1)S(1)}, bf16[288,128]{1,0:T(8,128)(2,1)S(1)}, u32[]{:S(2)}, u32[]{:S(2)}) collective-permute-start(bf16[288,128]{1,0:T(8,128)(2,1)S(1)} %sum_four.1), channel_id=1, source_target_pairs={{0,4},{1,5},{2,6},{3,7},{4,0},{5,1},{6,2},{7,3},{8,12},{9,13},{10,... | collective-permute-start | bytes 221192 | tf_op jit(solution)/shard_map/ppermute | solution.py:415
  35.8 6.0 %collective-permute-start.8 = (bf16[288,128]{1,0:T(8,128)(2,1)S(1)}, bf16[288,128]{1,0:T(8,128)(2,1)S(1)}, u32[]{:S(2)}, u32[]{:S(2)}) collective-permute-start(bf16[288,128]{1,0:T(8,128)(2,1)S(1)} %sum_four.1), channel_id=1, source_target_pairs={{0,8},{1,9},{2,10},{3,11},{4,12},{5,13},{6,14},{7,15},{8,0},{9,1},... | collective-permute-start | bytes 221192 | tf_op jit(solution)/shard_map/ppermute | solution.py:415
  38.0 6.2 %collective-permute-start.9 = (bf16[288,128]{1,0:T(8,128)(2,1)S(1)}, bf16[288,128]{1,0:T(8,128)(2,1)S(1)}, u32[]{:S(2)}, u32[]{:S(2)}) collective-permute-start(bf16[288,128]{1,0:T(8,128)(2,1)S(1)} %sum_four.1), channel_id=1, source_target_pairs={{0,12},{1,13},{2,14},{3,15},{4,8},{5,9},{6,10},{7,11},{8,4},{9,5},... | collective-permute-start | bytes 221192 | tf_op jit(solution)/shard_map/ppermute | solution.py:415
  44.2 1.4 %collective-permute-start.10 = (f32[288,128]{1,0:T(8,128)S(1)}, f32[288,128]{1,0:T(8,128)S(1)}, u32[]{:S(2)}, u32[]{:S(2)}) collective-permute-start(f32[288,128]{1,0:T(8,128)S(1)} %add_add_fusion.part), channel_id=1, source_target_pairs={{0,16},{16,0},{1,17},{17,1},{2,18},{18,2},{3,19},{19,3},{4,20},{20... | collective-permute-start | bytes 442376 | tf_op jit(solution)/shard_map/ppermute | solution.py:423

commit v4 on v3

--- a/solution.py
+++ b/solution.py
@@ -84,14 +84,10 @@
     return jnp.concatenate([own.astype(F32), rim.astype(F32)], axis=0)
 
 
-def store_shifts(value, tmp, out, index):
-    wide = value.shape[0]
-    tmp[8 : 8 + wide] = value
-    tmp[0:8] = value[wide - 8 :]
-    tmp[8 + wide :] = value[:8]
-    out[index, 0] = tmp[7 : 7 + wide].astype(BF)
+def store_shifts(value, out, index):
+    out[index, 0] = pltpu.roll(value, 1, 0).astype(BF)
     out[index, 1] = value.astype(BF)
-    out[index, 2] = tmp[9 : 9 + wide].astype(BF)
+    out[index, 2] = pltpu.roll(value, value.shape[0] - 1, 0).astype(BF)
 
 
 def band_dot(first, second, weight):
@@ -120,45 +116,45 @@
     acc[...] += jnp.dot(feat_t, near, preferred_element_type=F32)
 
 
-def inner_body(f, g, edge, w1, w2, v2, hs_edge, ds2_edge, slope_edge, ds1, acc1, acc2, fs, hs, ds2, slope, ht, tmp):
+def inner_body(f, g, edge, w1, w2, v2, hs_edge, ds2_edge, slope_edge, ds1, acc1, acc2, fs, hs, ds2, slope, ht):
     pairs, cols = f.shape[:2]
     _, _, rim = edge_masks()
 
-    @pl.loop(0, pairs)
-    def _(j):
-        store_shifts(with_rim(f[j], edge[j]), tmp, fs, j)
-
-    @pl.loop(0, pairs - 1)
+    @pl.loop(0, pairs, unroll=True)
+    def _(j):
+        store_shifts(with_rim(f[j], edge[j]), fs, j)
+
+    @pl.loop(0, pairs - 1, unroll=True)
     def _(j):
         pre = band_dot((fs, j), (fs, j + 1), w1)
         sig = sigmoid(pre)
         act = pre * sig
         slope[j] = sig + act * (1.0 - sig)
-        store_shifts(rim_masked(act, rim), tmp, hs, j)
+        store_shifts(rim_masked(act, rim), hs, j)
         ht[j] = hs[j, 1, :cols].T
 
-    @pl.loop(0, pairs - 2)
+    @pl.loop(0, pairs - 2, unroll=True)
     def _(j):
         pre = band_dot((hs, j), (hs, j + 1), w2)
         sig = sigmoid(pre)
         grad = with_rim(g[j + 1], edge[pairs + j + 1])
         delta = grad * (sig + pre * sig * (1.0 - sig))
-        store_shifts(delta, tmp, ds2, j)
-
-    @pl.loop(0, pairs - 3)
+        store_shifts(delta, ds2, j)
+
+    @pl.loop(0, pairs - 3, unroll=True)
     def _(j):
         back = band_dot((ds2, j), (ds2, j + 1), v2)
-        store_shifts(rim_masked(back * slope[j + 1], rim), tmp, ds1, j)
+        store_shifts(rim_masked(back * slope[j + 1], rim), ds1, j)
 
     acc1[...] = jnp.zeros_like(acc1)
     acc2[...] = jnp.zeros_like(acc2)
 
-    @pl.loop(0, pairs - 2)
+    @pl.loop(0, pairs - 2, unroll=True)
     def _(j):
         both = jnp.concatenate([ht[j], ht[j + 1]], axis=0)
         add_one(acc2, both, [ds2[j, s, :cols] for s in range(3)])
 
-    @pl.loop(0, pairs - 4)
+    @pl.loop(0, pairs - 4, unroll=True)
     def _(j):
         feat_t = fs[j + 2, 1, :cols].T
         add_one(acc1, feat_t, [ds1[j + p, s, :cols] for p in range(2) for s in range(3)])
@@ -172,7 +168,7 @@
 
 def rim_body(
     f, g, edge, above, below, w1, w2, v2, hs_edge, ds2_edge, slope_edge, ds1_in, acc1_in, acc2_in,
-    ds1, term, fs, hs, ds2, slope, acc1, acc2, tmp,
+    ds1, term, fs, hs, ds2, slope, acc1, acc2,
 ):
     pairs, cols = f.shape[:2]
     top, bottom, rim = edge_masks()
@@ -186,42 +182,42 @@
     def far(side, j):
         return (above, below)[side][j].astype(F32)
 
-    for side in range(2):
-        flag = (top, bottom)[side]
-        outer = jnp.where(upper, flag, 1.0) if side == 0 else jnp.where(upper, 1.0, flag)
-        scratch = tmp.at[side]
-        ends = (0, 1) if side == 0 else (1, 0)
-        feats = [far(side, ends[0]), far(side, ends[1]), own(f, 0, 0 if side == 0 else pairs - 1)]
-        for k in range(3):
-            store_shifts(feats[k], scratch, fs.at[side], k)
-
-        def order(one, two):
-            return (one, two) if side == 0 else (two, one)
-
-        for k in range(2):
-            pre = band_dot(*order((fs.at[side], k), (fs.at[side], k + 1)), w1)
+    flags = (top, bottom)
+    outers = (jnp.where(upper, top, 1.0), jnp.where(upper, 1.0, bottom))
+    ends = ((0, 1), (1, 0))
+    near = (0, pairs - 1)
+
+    def order(side, one, two):
+        return (one, two) if side == 0 else (two, one)
+
+    for k in range(3):
+        for side in range(2):
+            feat = far(side, ends[side][k]) if k < 2 else own(f, 0, near[side])
+            store_shifts(feat, fs.at[side], k)
+    for k in range(2):
+        for side in range(2):
+            pre = band_dot(*order(side, (fs.at[side], k), (fs.at[side], k + 1)), w1)
             sig = sigmoid(pre)
             act = pre * sig
             if k == 1:
                 slope[side] = sig + act * (1.0 - sig)
-            act = act * (flag if k == 0 else outer)
-            store_shifts(rim_masked(act, rim), scratch, hs.at[side], k)
-        for k in range(2):
-            grad = far(side, 2) if k == 0 else own(g, pairs, 0 if side == 0 else pairs - 1)
+            act = act * (flags[side] if k == 0 else outers[side])
+            store_shifts(rim_masked(act, rim), hs.at[side], k)
+    for k in (1, 0):
+        for side in range(2):
+            grad = far(side, 2) if k == 0 else own(g, pairs, near[side])
             inward = (hs.at[side], 1) if k == 0 else (hs_edge, side)
-            pre = band_dot(*order((hs.at[side], k), inward), w2)
+            pre = band_dot(*order(side, (hs.at[side], k), inward), w2)
             sig = sigmoid(pre)
             delta = grad * (sig + pre * sig * (1.0 - sig))
-            store_shifts(delta, scratch, ds2.at[side], k)
-        for k in range(2):
+            store_shifts(delta, ds2.at[side], k)
+    for k in (1, 0):
+        for side in range(2):
             inward = (ds2.at[side], 1) if k == 0 else (ds2_edge, side)
-            back = band_dot(*order((ds2.at[side], k), inward), v2)
-            if k == 0:
-                value = back * slope[side] * outer
-            else:
-                value = back * slope_edge[side]
+            back = band_dot(*order(side, (ds2.at[side], k), inward), v2)
+            value = back * slope[side] * outers[side] if k == 0 else back * slope_edge[side]
             at = k if side == 0 else pairs - k
-            store_shifts(rim_masked(value, rim), scratch, ds1, at)
+            store_shifts(rim_masked(value, rim), ds1, at)
 
     for j in range(2, pairs - 1):
         ds1[j] = ds1_in[j - 2]
@@ -252,7 +248,7 @@
     pairs, cols = gf.shape[:2]
     done[...] = jnp.zeros_like(done)
 
-    @pl.loop(0, pairs)
+    @pl.loop(0, pairs, unroll=True)
     def _(j):
         gf[j] = band_dot((ds1, j), (ds1, j + 1), v1)[:cols].astype(BF)
 
@@ -287,7 +283,6 @@
             pltpu.VMEM(shifts(pairs - 2), BF),
             pltpu.VMEM((pairs - 1, wide, LANES), F32),
             pltpu.VMEM((pairs - 1, LANES, cols), BF),
-            pltpu.VMEM((wide + 16, LANES), F32),
         ],
         compiler_params=PARAMS,
         cost_estimate=cost(22),
@@ -315,7 +310,6 @@
             pltpu.VMEM((2, wide, LANES), F32),
             pltpu.VMEM((LANES, 6 * LANES), F32),
             pltpu.VMEM((2 * LANES, 3 * LANES), F32),
-            pltpu.VMEM((2, wide + 16, LANES), F32),
         ],
         compiler_params=PARAMS,
         cost_estimate=cost(14),

time: 46.9 us -> 45.3 us (0.966)
  Pallas kernels: 15.3 us -> 7.96 us
  waiting for transfers between devices: 9.74 us -> 15.1 us
  starting transfers between devices: 16.7 us -> 17.2 us
    pallas_call x1, Pallas kernels: 8.76 us -> 3.1 us  [inner(): pl.pallas_call(inner_body, out_shape=(jax.ShapeDtypeStruct(shifts(2), BF)...]
    ppermute x3, waiting for transfers between devices: 1 us -> 4.91 us  [swap_one(): lax.ppermute(jnp.where(is_low(axis, parity), high, low), axis, perm)]
    ppermute x6, waiting for transfers between devices: 7.33 us -> 8.74 us  [reduced(): got.append(lax.ppermute(low, AXES, perm))]
    pallas_call x1, Pallas kernels: 2.22 us -> 1.03 us  [last(): pl.pallas_call(last_body, out_shape=(jax.ShapeDtypeStruct((ds1.shape[0] -...]
    ppermute x6, starting transfers between devices: 8.01 us -> 8.54 us  [reduced(): got.append(lax.ppermute(low, AXES, perm))]
    pallas_call x1, Pallas kernels: 2.94 us -> 2.44 us  [outer(): pl.pallas_call(rim_body, out_shape=(jax.ShapeDtypeStruct(shifts(pairs + 1...]
  transfers between devices with their start and end apart: 11 -> 11, of which waited for: 6 -> 8; matrix products, arithmetic and copies ran while one was open for 4% -> 4% of each run, Pallas kernels for 24% -> 10%
where the time goes in v4:
time: 45.3 us; the launch traced here: 45.2 us
  starting transfers between devices  17.2 us (38%)
  waiting for transfers between devices  15.1 us (33%)
  Pallas kernels  7.96 us (18%)
  local copies, waits for them, and re-layouts  3.8 us (8%)
  between operations  0.89 us (2%)
    ppermute x6, waiting for transfers between devices, reduced(): got.append(lax.ppermute(low, AXES, perm))  8.74 us
    ppermute x3, starting transfers between devices, swap_one(): lax.ppermute(jnp.where(is_low(axis, parity), high, low), axis, perm)  8.55 us
    ppermute x6, starting transfers between devices, reduced(): got.append(lax.ppermute(low, AXES, perm))  8.54 us
    ppermute x3, waiting for transfers between devices, swap_one(): lax.ppermute(jnp.where(is_low(axis, parity), high, low), axis, perm)  4.91 us
    pallas_call x1, Pallas kernels, inner(): pl.pallas_call(inner_body, out_shape=(jax.ShapeDtypeStruct(shifts(2), BF)...  3.1 us
    unnamed x9, local copies, waits for them, and re-layouts  2.52 us
    pallas_call x1, Pallas kernels, outer(): pl.pallas_call(rim_body, out_shape=(jax.ShapeDtypeStruct(shifts(pairs + 1...  2.44 us
    ppermute x1, waiting for transfers between devices, reduced(): part = mine + lax.ppermute(other, 'dp', swap)  1.35 us
  transfers between devices with their start and end apart: 11, of which 8 were waited for; matrix products, arithmetic and copies ran while one was open for 4% of the time, Pallas kernels for 10%

profile of v4, /device:TPU:0, one launch (start us, length us, event | category | flops | bytes accessed | tf_op | source)
XLA Modules:
  0.0 45.2 jit_solution(1108495944654673783)
XLA Ops:
  0.6 0.0 copy-start.2
  0.7 1.3 %copy.10 = bf16[1,64,16,256]{3,1,2,0:T(8,128)(2,1)S(1)} copy(bf16[1,64,16,256]{3,2,1,0:T(8,128)(2,1)} %param.4) | data formatting | bytes 1048576 | tf_op args[0]
  1.9 0.3 copy.20.f
  2.2 0.0 copy-done.2
  2.2 0.2 copy.11
  2.4 0.0 copy-start
  2.4 0.0 copy-start.1
  2.4 0.3 copy.21.g
  2.7 3.0 %collective-permute-start = (bf16[16,8,128]{2,1,0:T(8,128)(2,1)S(1)}, bf16[16,8,128]{2,1,0:T(8,128)(2,1)S(1)}, u32[]{:S(2)}, u32[]{:S(2)}) collective-permute-start(bf16[16,8,128]{2,1,0:T(8,128)(2,1)S(1)} %fusion), channel_id=1, source_target_pairs={{0,1},{1,0},{2,3},{3,2},{4,5},{5,4},{6,7},{7,6},{8,9},{9,8},{10,11... | collective-permute-start | bytes 98312 | tf_op jit(solution)/shard_map/ppermute | solution.py:35
  5.7 0.1 copy.14
  5.9 0.1 copy.16
  6.0 0.1 copy.15
  6.1 0.1 copy.17
  6.3 0.0 copy-done
  6.3 0.0 copy-done.1
  6.3 0.3 weights.1
  6.6 1.0 %collective-permute-done = bf16[16,8,128]{2,1,0:T(8,128)(2,1)S(1)} collective-permute-done((bf16[16,8,128]{2,1,0:T(8,128)(2,1)S(1)}, bf16[16,8,128]{2,1,0:T(8,128)(2,1)S(1)}, u32[]{:S(2)}, u32[]{:S(2)}) %collective-permute-start) | collective-permute-done | bytes 32800 | tf_op jit(solution)/shard_map/ppermute | solution.py:35
  7.6 0.1 broadcast_select_fusion.3
  7.7 0.7 %collective-permute-start.1 = (bf16[3,272,128]{2,1,0:T(8,128)(2,1)S(1)}, bf16[3,272,128]{2,1,0:T(8,128)(2,1)S(1)}, u32[]{:S(2)}, u32[]{:S(2)}) collective-permute-start(bf16[3,272,128]{2,1,0:T(8,128)(2,1)S(1)} %get-tuple-element.45), channel_id=1, source_target_pairs={{2,4},{4,2},{6,8},{8,6},{10,12},{12,10},{3,5},{5,3},{7,9},{9,7},{1... | collective-permute-start | bytes 626696 | tf_op jit(solution)/shard_map/ppermute | solution.py:35
  8.4 4.9 %collective-permute-start.2 = (bf16[3,272,128]{2,1,0:T(8,128)(2,1)S(1)}, bf16[3,272,128]{2,1,0:T(8,128)(2,1)S(1)}, u32[]{:S(2)}, u32[]{:S(2)}) collective-permute-start(bf16[3,272,128]{2,1,0:T(8,128)(2,1)S(1)} %get-tuple-element.44), channel_id=1, source_target_pairs={{0,2},{2,0},{4,6},{6,4},{8,10},{10,8},{12,14},{14,12},{1,3},{3,1},... | collective-permute-start | bytes 626696 | tf_op jit(solution)/shard_map/ppermute | solution.py:35
  13.3 3.1 %inner.1 = (bf16[2,3,272,128]{3,2,1,0:T(8,128)(2,1)S(1)}, bf16[2,3,272,128]{3,2,1,0:T(8,128)(2,1)S(1)}, f32[2,272,128]{2,1,0:T(8,128)S(1)}, bf16[5,3,272,128]{3,...) custom-call(bf16[8,256,128]{2,1,0:T(8,128)(2,1)S(1)} %copy.20.f, ...), custom_call_target="tpu_custom_call" | custom-call | flops 1176502272 | bytes 4194304 | tf_op jit(solution)/shard_map/inner/pallas_call | solution.py:270
  16.4 0.0 collective-permute-done.1
  16.4 3.9 %collective-permute-done.2 = bf16[3,272,128]{2,1,0:T(8,128)(2,1)S(1)} collective-permute-done((bf16[3,272,128]{2,1,0:T(8,128)(2,1)S(1)}, bf16[3,272,128]{2,1,0:T(8,128)(2,1)S(1)}, u32[]{:S(2)}, u32[]{:S(2)}) %collective-permute-start.2) | collective-permute-done | bytes 208928 | tf_op jit(solution)/shard_map/ppermute | solution.py:35
  20.3 0.1 broadcast_select_fusion.1
  20.4 2.4 %outer.1 = (bf16[9,3,272,128]{3,2,1,0:T(8,128)(2,1)S(1)}, f32[576,128]{1,0:T(8,128)S(1)}) custom-call(bf16[8,256,128]{2,1,0:T(8,128)(2,1)S(1)} %copy.20.f, bf16[8,256,128]{2,1,0:T(8,128)(2,1)S(1)} %copy.21.g, bf16[16,16,128]{2,1,0:T(8,128)(2,1)S(1)} %pad_maximum_fusion.edge, bf16[3,272,128]{2,1,0:T(8,128)(2,1)S(1)} %get-tuple-element.43.above, ...), custom_call_target="tpu_custom_call" | custom-call | flops 748683264 | bytes 4194304 | tf_op jit(solution)/shard_map/outer/pallas_call | solution.py:300
  22.8 0.1 collective-permute-start.3
  22.9 1.4 %collective-permute-done.3 = f32[288,128]{1,0:T(8,128)S(1)} collective-permute-done((f32[288,128]{1,0:T(8,128)S(1)}, f32[288,128]{1,0:T(8,128)S(1)}, u32[]{:S(2)}, u32[]{:S(2)}) %collective-permute-start.3) | collective-permute-done | bytes 147488 | tf_op jit(solution)/shard_map/ppermute | solution.py:384
  24.3 2.5 %collective-permute-start.4 = (bf16[288,128]{1,0:T(8,128)(2,1)S(1)}, bf16[288,128]{1,0:T(8,128)(2,1)S(1)}, u32[]{:S(2)}, u32[]{:S(2)}) collective-permute-start(bf16[288,128]{1,0:T(8,128)(2,1)S(1)} %add_convert_fusion.own), channel_id=1, source_target_pairs={{0,2},{1,3},{2,0},{3,1},{4,6},{5,7},{6,4},{7,5},{8,10},{9,11},{10,... | collective-permute-start | bytes 221192 | tf_op jit(solution)/shard_map/ppermute | solution.py:409
  26.8 1.5 %collective-permute-start.5 = (bf16[288,128]{1,0:T(8,128)(2,1)S(1)}, bf16[288,128]{1,0:T(8,128)(2,1)S(1)}, u32[]{:S(2)}, u32[]{:S(2)}) collective-permute-start(bf16[288,128]{1,0:T(8,128)(2,1)S(1)} %add_convert_fusion.own), channel_id=1, source_target_pairs={{0,1},{1,0},{2,3},{3,2},{4,5},{5,4},{6,7},{7,6},{8,9},{9,8},{10,11... | collective-permute-start | bytes 221192 | tf_op jit(solution)/shard_map/ppermute | solution.py:409
  28.3 0.1 collective-permute-start.6
  28.4 1.0 %last.1 = (bf16[8,256,128]{2,1,0:T(8,128)(2,1)S(1)}, f32[8,128]{1,0:T(8,128)S(1)}) custom-call(bf16[9,3,272,128]{3,2,1,0:T(8,128)(2,1)S(1)} %get-tuple-element.28.ds1, bf16[768,128]{1,0:T(8,128)(2,1)S(1)} %get-tuple-element.29.v1), custom_call_target="tpu_custom_call" | custom-call | flops 427819008 | bytes 4194304 | tf_op jit(solution)/shard_map/last/pallas_call | solution.py:321
  29.4 0.0 collective-permute-done.4.one
  29.4 1.8 %collective-permute-done.5.two = bf16[288,128]{1,0:T(8,128)(2,1)S(1)} collective-permute-done((bf16[288,128]{1,0:T(8,128)(2,1)S(1)}, bf16[288,128]{1,0:T(8,128)(2,1)S(1)}, u32[]{:S(2)}, u32[]{:S(2)}) %collective-permute-start.5) | collective-permute-done | bytes 73760 | tf_op jit(solution)/shard_map/ppermute | solution.py:409
  31.2 2.4 %collective-permute-done.6.three = bf16[288,128]{1,0:T(8,128)(2,1)S(1)} collective-permute-done((bf16[288,128]{1,0:T(8,128)(2,1)S(1)}, bf16[288,128]{1,0:T(8,128)(2,1)S(1)}, u32[]{:S(2)}, u32[]{:S(2)}) %collective-permute-start.6) | collective-permute-done | bytes 73760 | tf_op jit(solution)/shard_map/ppermute | solution.py:409
  33.6 1.6 %collective-permute-start.7 = (bf16[288,128]{1,0:T(8,128)(2,1)S(1)}, bf16[288,128]{1,0:T(8,128)(2,1)S(1)}, u32[]{:S(2)}, u32[]{:S(2)}) collective-permute-start(bf16[288,128]{1,0:T(8,128)(2,1)S(1)} %sum_four.1), channel_id=1, source_target_pairs={{0,4},{1,5},{2,6},{3,7},{4,0},{5,1},{6,2},{7,3},{8,12},{9,13},{10,... | collective-permute-start | bytes 221192 | tf_op jit(solution)/shard_map/ppermute | solution.py:409
  35.3 1.1 %collective-permute-start.8 = (bf16[288,128]{1,0:T(8,128)(2,1)S(1)}, bf16[288,128]{1,0:T(8,128)(2,1)S(1)}, u32[]{:S(2)}, u32[]{:S(2)}) collective-permute-start(bf16[288,128]{1,0:T(8,128)(2,1)S(1)} %sum_four.1), channel_id=1, source_target_pairs={{0,8},{1,9},{2,10},{3,11},{4,12},{5,13},{6,14},{7,15},{8,0},{9,1},... | collective-permute-start | bytes 221192 | tf_op jit(solution)/shard_map/ppermute | solution.py:409
  36.4 1.7 %collective-permute-start.9 = (bf16[288,128]{1,0:T(8,128)(2,1)S(1)}, bf16[288,128]{1,0:T(8,128)(2,1)S(1)}, u32[]{:S(2)}, u32[]{:S(2)}) collective-permute-start(bf16[288,128]{1,0:T(8,128)(2,1)S(1)} %sum_four.1), channel_id=1, source_target_pairs={{0,12},{1,13},{2,14},{3,15},{4,8},{5,9},{6,10},{7,11},{8,4},{9,5},... | collective-permute-start | bytes 221192 | tf_op jit(solution)/shard_map/ppermute | solution.py:409
  38.1 0.0 collective-permute-done.7
  38.1 3.2 %collective-permute-done.8 = bf16[288,128]{1,0:T(8,128)(2,1)S(1)} collective-permute-done((bf16[288,128]{1,0:T(8,128)(2,1)S(1)}, bf16[288,128]{1,0:T(8,128)(2,1)S(1)}, u32[]{:S(2)}, u32[]{:S(2)}) %collective-permute-start.8) | collective-permute-done | bytes 73760 | tf_op jit(solution)/shard_map/ppermute | solution.py:409
  41.3 1.4 %collective-permute-done.9 = bf16[288,128]{1,0:T(8,128)(2,1)S(1)} collective-permute-done((bf16[288,128]{1,0:T(8,128)(2,1)S(1)}, bf16[288,128]{1,0:T(8,128)(2,1)S(1)}, u32[]{:S(2)}, u32[]{:S(2)}) %collective-permute-start.9) | collective-permute-done | bytes 73760 | tf_op jit(solution)/shard_map/ppermute | solution.py:409
  42.7 0.1 collective-permute-start.10
  42.8 0.2 copy.22
  43.0 1.1 %copy.23 = bf16[1,64,16,256]{3,2,1,0:T(8,128)(2,1)} copy(bf16[1,64,16,256]{3,1,2,0:T(8,128)(2,1)S(1)} %bitcast.23) | data formatting | bytes 1048576
  44.1 0.1 collective-permute-done.10.other
  44.2 1.0 %finish.1 = (f32[3,3,64,64]{3,2,1,0:T(8,128)}, f32[3,3,64,64]{3,2,1,0:T(8,128)}) custom-call(f32[288,128]{1,0:T(8,128)S(1)} %add_add_fusion.part, f32[288,128]{1,0:T(8,128)S(1)} %collective-permute-done.10.other), custom_call_target="tpu_custom_call" | custom-call | tf_op jit(solution)/shard_map/finish/pallas_call | solution.py:363
  (11 shorter events, 0.2 us)
Async XLA Ops:
  0.6 1.6 %copy-start.2 = (bf16[1,64,16,256]{3,2,1,0:T(8,128)(2,1)S(1)}, bf16[1,64,16,256]{3,2,1,0:T(8,128)(2,1)}, u32[]{:S(2)}) copy-start(bf16[1,64,16,256]{3,2,1,0:T(8,128)(2,1)} %param.5) | copy-start | bytes 1572868
  2.4 3.9 %copy-start = (bf16[3,3,64,64]{3,2,1,0:T(8,128)(2,1)S(1)}, bf16[3,3,64,64]{3,2,1,0:T(8,128)(2,1)}, u32[]{:S(2)}) copy-start(bf16[3,3,64,64]{3,2,1,0:T(8,128)(2,1)} %k1.1) | copy-start | bytes 221188
  2.4 3.9 %copy-start.1 = (bf16[3,3,64,64]{3,2,1,0:T(8,128)(2,1)S(1)}, bf16[3,3,64,64]{3,2,1,0:T(8,128)(2,1)}, u32[]{:S(2)}) copy-start(bf16[3,3,64,64]{3,2,1,0:T(8,128)(2,1)} %k2.1) | copy-start | bytes 221188
  2.7 4.9 %collective-permute-start = (bf16[16,8,128]{2,1,0:T(8,128)(2,1)S(1)}, bf16[16,8,128]{2,1,0:T(8,128)(2,1)S(1)}, u32[]{:S(2)}, u32[]{:S(2)}) collective-permute-start(bf16[16,8,128]{2,1,0:T(8,128)(2,1)S(1)} %fusion), channel_id=1, source_target_pairs={{0,1},{1,0},{2,3},{3,2},{4,5},{5,4},{6,7},{7,6},{8,9},{9,8},{10,11... | collective-permute-start | bytes 98312 | tf_op jit(solution)/shard_map/ppermute | solution.py:35
  7.7 8.7 %collective-permute-start.1 = (bf16[3,272,128]{2,1,0:T(8,128)(2,1)S(1)}, bf16[3,272,128]{2,1,0:T(8,128)(2,1)S(1)}, u32[]{:S(2)}, u32[]{:S(2)}) collective-permute-start(bf16[3,272,128]{2,1,0:T(8,128)(2,1)S(1)} %get-tuple-element.45), channel_id=1, source_target_pairs={{2,4},{4,2},{6,8},{8,6},{10,12},{12,10},{3,5},{5,3},{7,9},{9,7},{1... | collective-permute-start | bytes 626696 | tf_op jit(solution)/shard_map/ppermute | solution.py:35
  8.4 11.9 %collective-permute-start.2 = (bf16[3,272,128]{2,1,0:T(8,128)(2,1)S(1)}, bf16[3,272,128]{2,1,0:T(8,128)(2,1)S(1)}, u32[]{:S(2)}, u32[]{:S(2)}) collective-permute-start(bf16[3,272,128]{2,1,0:T(8,128)(2,1)S(1)} %get-tuple-element.44), channel_id=1, source_target_pairs={{0,2},{2,0},{4,6},{6,4},{8,10},{10,8},{12,14},{14,12},{1,3},{3,1},... | collective-permute-start | bytes 626696 | tf_op jit(solution)/shard_map/ppermute | solution.py:35
  22.8 1.4 %collective-permute-start.3 = (f32[288,128]{1,0:T(8,128)S(1)}, f32[288,128]{1,0:T(8,128)S(1)}, u32[]{:S(2)}, u32[]{:S(2)}) collective-permute-start(f32[288,128]{1,0:T(8,128)S(1)} %constant_dynamic-slice_fusion), channel_id=1, source_target_pairs={{0,16},{16,0},{1,17},{17,1},{2,18},{18,2},{3,19},{19,3},{4,20},{20... | collective-permute-start | bytes 442376 | tf_op jit(solution)/shard_map/ppermute | solution.py:384
  24.3 5.1 %collective-permute-start.4 = (bf16[288,128]{1,0:T(8,128)(2,1)S(1)}, bf16[288,128]{1,0:T(8,128)(2,1)S(1)}, u32[]{:S(2)}, u32[]{:S(2)}) collective-permute-start(bf16[288,128]{1,0:T(8,128)(2,1)S(1)} %add_convert_fusion.own), channel_id=1, source_target_pairs={{0,2},{1,3},{2,0},{3,1},{4,6},{5,7},{6,4},{7,5},{8,10},{9,11},{10,... | collective-permute-start | bytes 221192 | tf_op jit(solution)/shard_map/ppermute | solution.py:409
  26.8 4.4 %collective-permute-start.5 = (bf16[288,128]{1,0:T(8,128)(2,1)S(1)}, bf16[288,128]{1,0:T(8,128)(2,1)S(1)}, u32[]{:S(2)}, u32[]{:S(2)}) collective-permute-start(bf16[288,128]{1,0:T(8,128)(2,1)S(1)} %add_convert_fusion.own), channel_id=1, source_target_pairs={{0,1},{1,0},{2,3},{3,2},{4,5},{5,4},{6,7},{7,6},{8,9},{9,8},{10,11... | collective-permute-start | bytes 221192 | tf_op jit(solution)/shard_map/ppermute | solution.py:409
  28.3 5.3 %collective-permute-start.6 = (bf16[288,128]{1,0:T(8,128)(2,1)S(1)}, bf16[288,128]{1,0:T(8,128)(2,1)S(1)}, u32[]{:S(2)}, u32[]{:S(2)}) collective-permute-start(bf16[288,128]{1,0:T(8,128)(2,1)S(1)} %add_convert_fusion.own), channel_id=1, source_target_pairs={{0,3},{1,2},{2,1},{3,0},{4,7},{5,6},{6,5},{7,4},{8,11},{9,10},{10,... | collective-permute-start | bytes 221192 | tf_op jit(solution)/shard_map/ppermute | solution.py:409
  33.6 4.5 %collective-permute-start.7 = (bf16[288,128]{1,0:T(8,128)(2,1)S(1)}, bf16[288,128]{1,0:T(8,128)(2,1)S(1)}, u32[]{:S(2)}, u32[]{:S(2)}) collective-permute-start(bf16[288,128]{1,0:T(8,128)(2,1)S(1)} %sum_four.1), channel_id=1, source_target_pairs={{0,4},{1,5},{2,6},{3,7},{4,0},{5,1},{6,2},{7,3},{8,12},{9,13},{10,... | collective-permute-start | bytes 221192 | tf_op jit(solution)/shard_map/ppermute | solution.py:409
  35.3 6.0 %collective-permute-start.8 = (bf16[288,128]{1,0:T(8,128)(2,1)S(1)}, bf16[288,128]{1,0:T(8,128)(2,1)S(1)}, u32[]{:S(2)}, u32[]{:S(2)}) collective-permute-start(bf16[288,128]{1,0:T(8,128)(2,1)S(1)} %sum_four.1), channel_id=1, source_target_pairs={{0,8},{1,9},{2,10},{3,11},{4,12},{5,13},{6,14},{7,15},{8,0},{9,1},... | collective-permute-start | bytes 221192 | tf_op jit(solution)/shard_map/ppermute | solution.py:409
  36.4 6.3 %collective-permute-start.9 = (bf16[288,128]{1,0:T(8,128)(2,1)S(1)}, bf16[288,128]{1,0:T(8,128)(2,1)S(1)}, u32[]{:S(2)}, u32[]{:S(2)}) collective-permute-start(bf16[288,128]{1,0:T(8,128)(2,1)S(1)} %sum_four.1), channel_id=1, source_target_pairs={{0,12},{1,13},{2,14},{3,15},{4,8},{5,9},{6,10},{7,11},{8,4},{9,5},... | collective-permute-start | bytes 221192 | tf_op jit(solution)/shard_map/ppermute | solution.py:409
  42.7 1.4 %collective-permute-start.10 = (f32[288,128]{1,0:T(8,128)S(1)}, f32[288,128]{1,0:T(8,128)S(1)}, u32[]{:S(2)}, u32[]{:S(2)}) collective-permute-start(f32[288,128]{1,0:T(8,128)S(1)} %add_add_fusion.part), channel_id=1, source_target_pairs={{0,16},{16,0},{1,17},{17,1},{2,18},{18,2},{3,19},{19,3},{4,20},{20... | collective-permute-start | bytes 442376 | tf_op jit(solution)/shard_map/ppermute | solution.py:417

commit v5 on v4

--- a/solution.py
+++ b/solution.py
@@ -25,6 +25,12 @@
 
 def is_low(axis, parity):
     return lax.axis_index(axis) % 2 == parity
+
+
+def shift_both(low, high, axis):
+    ends = lax.axis_size(axis) - 1
+    from_prev = lax.ppermute(high, axis, [(i, i + 1) for i in range(ends)])
+    return from_prev, lax.ppermute(low, axis, [(i + 1, i) for i in range(ends)])
 
 
 def swap_one(low, high, axis):
@@ -116,7 +122,7 @@
     acc[...] += jnp.dot(feat_t, near, preferred_element_type=F32)
 
 
-def inner_body(f, g, edge, w1, w2, v2, hs_edge, ds2_edge, slope_edge, ds1, acc1, acc2, fs, hs, ds2, slope, ht):
+def inner_body(f, g, edge, w1, w2, v2, hs_edge, ds2_edge, slope_edge, ds1, acc1, acc2, fs, hs, ds2, slope, ht, ft):
     pairs, cols = f.shape[:2]
     _, _, rim = edge_masks()
 
@@ -154,10 +160,14 @@
         both = jnp.concatenate([ht[j], ht[j + 1]], axis=0)
         add_one(acc2, both, [ds2[j, s, :cols] for s in range(3)])
 
-    @pl.loop(0, pairs - 4, unroll=True)
-    def _(j):
-        feat_t = fs[j + 2, 1, :cols].T
-        add_one(acc1, feat_t, [ds1[j + p, s, :cols] for p in range(2) for s in range(3)])
+    @pl.loop(1, pairs - 1, unroll=True)
+    def _(j):
+        ft[j] = f[j].T
+
+    @pl.loop(0, pairs - 3, unroll=True)
+    def _(j):
+        both = jnp.concatenate([ft[j + 1], ft[j + 2]], axis=0)
+        add_one(acc1, both, [ds1[j, s, :cols] for s in range(3)])
 
     for side, at in ((0, 0), (1, pairs - 2)):
         hs_edge[side] = hs[at]
@@ -166,91 +176,102 @@
         ds2_edge[side] = ds2[at]
 
 
+def take_terms(acc1, acc2, term):
+    for ky in range(3):
+        for kx in range(3):
+            at = (2 - kx) * LANES
+            sums = []
+            for acc in (acc1, acc2):
+                first = acc[ky * HALF : (ky + 1) * HALF, at : at + HALF]
+                sums.append(first + acc[(ky + 1) * HALF : (ky + 2) * HALF, at + HALF : at + LANES])
+            at = (ky * 3 + kx) * HALF
+            term[at : at + HALF] = jnp.concatenate(sums, axis=1)
+
+
+def half_lanes(side):
+    upper = lax.broadcasted_iota(jnp.int32, (1, LANES), 1) >= HALF
+    return upper == (side == 1)
+
+
 def rim_body(
-    f, g, edge, above, below, w1, w2, v2, hs_edge, ds2_edge, slope_edge, ds1_in, acc1_in, acc2_in,
-    ds1, term, fs, hs, ds2, slope, acc1, acc2,
+    f, g, edge, halo, w1, w2, v2, hs_edge, ds2_edge, slope_edge, acc1_in, acc2_in, ds1, row, acc1, acc2, *rest, side
 ):
+    if side == 0:
+        fs, hs, ds2, slope = rest
+    else:
+        term, fs, hs, ds2, slope = rest
     pairs, cols = f.shape[:2]
     top, bottom, rim = edge_masks()
-    upper = lax.broadcasted_iota(jnp.int32, (1, LANES), 1) < HALF
+    flag = (top, bottom)[side]
+    beyond = half_lanes(side)
+    outer = jnp.where(beyond, flag, 1.0)
+    near, next_near = (0, 1) if side == 0 else (pairs - 1, pairs - 2)
+    mixed = halo[1].astype(F32)
+
+    def order(one, two):
+        return (one, two) if side == 0 else (two, one)
+
+    store_shifts(jnp.where(beyond, 0.0, mixed), fs, 0)
+    store_shifts(halo[0].astype(F32), fs, 1)
+    store_shifts(with_rim(f[near], edge[near]), fs, 2)
+    for k in (1, 0):
+        pre = band_dot(*order((fs, k), (fs, k + 1)), w1)
+        sig = sigmoid(pre)
+        act = pre * sig
+        if k == 1:
+            slope[...] = sig + act * (1.0 - sig)
+        act = act * (flag if k == 0 else outer)
+        store_shifts(rim_masked(act, rim), hs, k)
+    far_grad = jnp.where(beyond, 0.0, pltpu.roll(mixed, HALF, 1))
+    for k in (1, 0):
+        grad = far_grad if k == 0 else with_rim(g[near], edge[pairs + near])
+        inward = (hs, 1) if k == 0 else (hs_edge, side)
+        pre = band_dot(*order((hs, k), inward), w2)
+        sig = sigmoid(pre)
+        delta = grad * (sig + pre * sig * (1.0 - sig))
+        store_shifts(delta, ds2, k)
+    for k in (1, 0):
+        inward = (ds2, 1) if k == 0 else (ds2_edge, side)
+        back = band_dot(*order((ds2, k), inward), v2)
+        value = back * slope[...] if k == 0 else back * slope_edge[side]
+        if k == 0:
+            value = jnp.where(beyond, 0.0, value)
+        value = rim_masked(value, rim)
+        store_shifts(value, ds1, k)
+        if k == 0:
+            first, second = value[: row.shape[0]], value[value.shape[0] - row.shape[0] :]
+            turned = (first, second)[side]
+            turned = pltpu.roll(turned, HALF, 1)
+            row[...] = ((turned + second) if side == 0 else (first + turned)).astype(BF)
+
     acc1[...] = acc1_in[...]
     acc2[...] = acc2_in[...]
-
-    def own(ref, base, j):
-        return with_rim(ref[j], edge[base + j])
-
-    def far(side, j):
-        return (above, below)[side][j].astype(F32)
-
-    flags = (top, bottom)
-    outers = (jnp.where(upper, top, 1.0), jnp.where(upper, 1.0, bottom))
-    ends = ((0, 1), (1, 0))
-    near = (0, pairs - 1)
-
-    def order(side, one, two):
-        return (one, two) if side == 0 else (two, one)
-
-    for k in range(3):
-        for side in range(2):
-            feat = far(side, ends[side][k]) if k < 2 else own(f, 0, near[side])
-            store_shifts(feat, fs.at[side], k)
+    hid = order(hs[1, 1, :cols].T, hs_edge[side, 1, :cols].T)
+    add_one(acc2, jnp.concatenate(hid, axis=0), [ds2[1, s, :cols] for s in range(3)])
+    own = f[near].T
     for k in range(2):
-        for side in range(2):
-            pre = band_dot(*order(side, (fs.at[side], k), (fs.at[side], k + 1)), w1)
-            sig = sigmoid(pre)
-            act = pre * sig
-            if k == 1:
-                slope[side] = sig + act * (1.0 - sig)
-            act = act * (flags[side] if k == 0 else outers[side])
-            store_shifts(rim_masked(act, rim), hs.at[side], k)
-    for k in (1, 0):
-        for side in range(2):
-            grad = far(side, 2) if k == 0 else own(g, pairs, near[side])
-            inward = (hs.at[side], 1) if k == 0 else (hs_edge, side)
-            pre = band_dot(*order(side, (hs.at[side], k), inward), w2)
-            sig = sigmoid(pre)
-            delta = grad * (sig + pre * sig * (1.0 - sig))
-            store_shifts(delta, ds2.at[side], k)
-    for k in (1, 0):
-        for side in range(2):
-            inward = (ds2.at[side], 1) if k == 0 else (ds2_edge, side)
-            back = band_dot(*order(side, (ds2.at[side], k), inward), v2)
-            value = back * slope[side] * outers[side] if k == 0 else back * slope_edge[side]
-            at = k if side == 0 else pairs - k
-            store_shifts(rim_masked(value, rim), ds1, at)
-
-    for j in range(2, pairs - 1):
-        ds1[j] = ds1_in[j - 2]
-    for side in range(2):
-        near, inward = hs[side, 1, 1, :cols].T, hs_edge[side, 1, :cols].T
-        both = [near, inward] if side == 0 else [inward, near]
-        add_one(acc2, jnp.concatenate(both, axis=0), [ds2[side, 1, s, :cols] for s in range(3)])
-    for j in (0, 1, pairs - 2, pairs - 1):
-        add_one(acc1, f[j].T, [ds1[j + p, s, :cols] for p in range(2) for s in range(3)])
-
-    for ky in range(3):
-        for kx in range(3):
-            s = 2 - kx
-            one = jnp.zeros((HALF, HALF), F32)
-            two = jnp.zeros((HALF, HALF), F32)
-            for a in range(2):
-                b = a + 2 - ky
-                at = (b // 2 * 3 + s) * LANES + b % 2 * HALF
-                one = one + acc1[a * HALF : (a + 1) * HALF, at : at + HALF]
-                b = a + ky
-                at = s * LANES + a * HALF
-                two = two + acc2[b * HALF : (b + 1) * HALF, at : at + HALF]
-            at = (ky * 3 + kx) * HALF
-            term[at : at + HALF] = jnp.concatenate([one, two], axis=1)
-
-
-def last_body(ds1, v1, gf, done):
+        feat = order(halo[0, :cols].T, own) if k == 0 else order(own, f[next_near].T)
+        add_one(acc1, jnp.concatenate(feat, axis=0), [ds1[k, s, :cols] for s in range(3)])
+    if side == 1:
+        take_terms(acc1, acc2, term)
+
+
+def with_row(center, row, side):
+    turned = pltpu.roll(row, HALF, 1)
+    first, second = (row, turned) if side == 0 else (turned, row)
+    cols = center.shape[0] - row.shape[0]
+    full = jnp.concatenate([first[:cols], second], axis=0)
+    return jnp.where(half_lanes(side), full, center)
+
+
+def last_body(ds1_top, ds1, ds1_bottom, prev_row, next_row, v1, gf, done, ends):
     pairs, cols = gf.shape[:2]
     done[...] = jnp.zeros_like(done)
-
-    @pl.loop(0, pairs, unroll=True)
-    def _(j):
-        gf[j] = band_dot((ds1, j), (ds1, j + 1), v1)[:cols].astype(BF)
+    store_shifts(with_row(ds1_top[0, 1].astype(F32), prev_row[...].astype(F32), 0), ends, 0)
+    store_shifts(with_row(ds1_bottom[0, 1].astype(F32), next_row[...].astype(F32), 1), ends, 1)
+    places = [(ends, 0), (ds1_top, 1)] + [(ds1, j) for j in range(pairs - 3)] + [(ds1_bottom, 1), (ends, 1)]
+    for j in range(pairs):
+        gf[j] = band_dot(places[j], places[j + 1], v1)[:cols].astype(BF)
 
 
 def cost(pair_count):
@@ -274,7 +295,7 @@
             jax.ShapeDtypeStruct(shifts(2), BF),
             jax.ShapeDtypeStruct((2, wide, LANES), F32),
             jax.ShapeDtypeStruct(shifts(pairs - 3), BF),
-            jax.ShapeDtypeStruct((LANES, 6 * LANES), F32),
+            jax.ShapeDtypeStruct((2 * LANES, 3 * LANES), F32),
             jax.ShapeDtypeStruct((2 * LANES, 3 * LANES), F32),
         ),
         scratch_shapes=[
@@ -283,6 +304,7 @@
             pltpu.VMEM(shifts(pairs - 2), BF),
             pltpu.VMEM((pairs - 1, wide, LANES), F32),
             pltpu.VMEM((pairs - 1, LANES, cols), BF),
+            pltpu.VMEM((pairs - 1, LANES, cols), BF),
         ],
         compiler_params=PARAMS,
         cost_estimate=cost(22),
@@ -290,55 +312,60 @@
     )(f, g, edge, w1, w2, v2)
 
 
-def outer(f, *rest):
-    pairs, cols = f.shape[:2]
-    wide = cols + RIM
-
-    def shifts(*count):
-        return (*count, 3, wide, LANES)
-
-    return pl.pallas_call(
-        rim_body,
-        out_shape=(
-            jax.ShapeDtypeStruct(shifts(pairs + 1), BF),
-            jax.ShapeDtypeStruct((9 * HALF, LANES), F32),
-        ),
+def outer(side, f, *rest):
+    wide = f.shape[1] + RIM
+    acc = jax.ShapeDtypeStruct((2 * LANES, 3 * LANES), F32)
+
+    def shifts(count):
+        return (count, 3, wide, LANES)
+
+    out_shape = [
+        jax.ShapeDtypeStruct(shifts(2), BF),
+        jax.ShapeDtypeStruct((wide // 2 + RIM // 2, LANES), BF),
+        acc,
+        acc,
+    ]
+    if side == 1:
+        out_shape.append(jax.ShapeDtypeStruct((9 * HALF, LANES), F32))
+    return pl.pallas_call(
+        functools.partial(rim_body, side=side),
+        out_shape=out_shape,
         scratch_shapes=[
-            pltpu.VMEM(shifts(2, 3), BF),
-            pltpu.VMEM(shifts(2, 2), BF),
-            pltpu.VMEM(shifts(2, 2), BF),
-            pltpu.VMEM((2, wide, LANES), F32),
-            pltpu.VMEM((LANES, 6 * LANES), F32),
-            pltpu.VMEM((2 * LANES, 3 * LANES), F32),
+            pltpu.VMEM(shifts(3), BF),
+            pltpu.VMEM(shifts(2), BF),
+            pltpu.VMEM(shifts(2), BF),
+            pltpu.VMEM((wide, LANES), F32),
         ],
         compiler_params=PARAMS,
-        cost_estimate=cost(14),
-        name="outer",
+        cost_estimate=cost(8),
+        name=("upper", "lower")[side],
     )(f, *rest)
 
 
-def last(ds1, v1, cols):
+def last(ds1_top, ds1, ds1_bottom, prev_row, next_row, v1, cols):
+    pairs = ds1.shape[0] + 3
     return pl.pallas_call(
         last_body,
         out_shape=(
-            jax.ShapeDtypeStruct((ds1.shape[0] - 1, cols, LANES), BF),
+            jax.ShapeDtypeStruct((pairs, cols, LANES), BF),
             jax.ShapeDtypeStruct((8, LANES), F32),
         ),
+        scratch_shapes=[pltpu.VMEM((2, 3, cols + RIM, LANES), BF)],
         compiler_params=PARAMS,
         cost_estimate=cost(8),
         name="last",
-    )(ds1, v1)
+    )(ds1_top, ds1, ds1_bottom, prev_row, next_row, v1)
 
 
 def four_body(own, one, two, three, done, out):
     low = [ref[...].astype(F32) for ref in (own, one, two, three)]
-    out[...] = ((low[0] + low[1]) + (low[2] + low[3])).astype(BF)
+    out[...] = (low[0] + low[1]) + (low[2] + low[3])
 
 
 def sum_four(own, got, done):
     return pl.pallas_call(
         four_body,
-        out_shape=jax.ShapeDtypeStruct(own.shape, BF),
+        out_shape=jax.ShapeDtypeStruct(own.shape, F32),
         compiler_params=pltpu.CompilerParams(vmem_limit_bytes=4 * 2**20),
         name="sum_four",
     )(own, *got, done)
@@ -407,7 +434,7 @@
                         base = core * sizes[1]
                         perm.append(((base + r) * sizes[2] + c, (base + to_r) * sizes[2] + to_c))
             got.append(lax.ppermute(low, AXES, perm))
-        if at == 0 and len(got) > 1 and len(groups) > 1:
+        if at == 1 and len(got) > 1:
             part = sum_four(low, got, done)
             continue
         got = [one.astype(F32) for one in got]
@@ -425,15 +452,19 @@
     from_left, from_right = swap_one(own[:, : RIM // 2], own[:, cols - RIM // 2 :], "col")
     edge = jnp.concatenate([from_right, from_left], axis=1)
     w1, w2, v2, v1 = make_weights(kernel_one, kernel_two)
-    low = jnp.concatenate([feat[:2], grad[:1]], axis=0)
-    high = jnp.concatenate([feat[pairs - 2 :], grad[pairs - 1 :]], axis=0)
-    low_edge = jnp.concatenate([edge[:2], edge[pairs : pairs + 1]], axis=0)
-    high_edge = jnp.concatenate([edge[pairs - 2 : pairs], edge[2 * pairs - 1 :]], axis=0)
+    low = jnp.stack([feat[0], jnp.concatenate([feat[1, :, :HALF], grad[0, :, :HALF]], axis=1)])
+    high = jnp.stack([feat[-1], jnp.concatenate([grad[-1, :, HALF:], feat[-2, :, HALF:]], axis=1)])
+    feat_edge, grad_edge = edge[:pairs], edge[pairs:]
+    low_edge = jnp.stack([feat_edge[0], jnp.concatenate([feat_edge[1, :, :HALF], grad_edge[0, :, :HALF]], axis=1)])
+    high_edge = jnp.stack([feat_edge[-1], jnp.concatenate([grad_edge[-1, :, HALF:], feat_edge[-2, :, HALF:]], axis=1)])
     low, high = jnp.concatenate([low, low_edge], axis=1), jnp.concatenate([high, high_edge], axis=1)
-    above, below = swap_one(low, high, "row")
-    state = inner(feat, grad, edge, w1, w2, v2)
-    ds1, term = outer(feat, grad, edge, above, below, w1, w2, v2, *state)
-    gf, done = last(ds1, v1, cols)
+    above, below = shift_both(low, high, "row")
+    hs_edge, ds2_edge, slope_edge, ds1, acc1, acc2 = inner(feat, grad, edge, w1, w2, v2)
+    shared = (w1, w2, v2, hs_edge, ds2_edge, slope_edge)
+    ds1_top, low_row, acc1, acc2 = outer(0, feat, grad, edge, above, *shared, acc1, acc2)
+    ds1_bottom, high_row, _, _, term = outer(1, feat, grad, edge, below, *shared, acc1, acc2)
+    prev_row, next_row = shift_both(low_row, high_row, "row")
+    gf, done = last(ds1_top, ds1, ds1_bottom, prev_row, next_row, v1, cols)
     part, other = reduced(term, done)
     count = slides * lax.axis_size("dp") * rows * lax.axis_size("row") * cols * lax.axis_size("col")
     grad_one, grad_two = finish(part, other, float(count) ** -0.5)

time: 45.3 us -> 48 us (1.060)
  waiting for transfers between devices: 15.1 us -> 7.56 us
  starting transfers between devices: 17.2 us -> 24.2 us
  Pallas kernels: 7.96 us -> 9.52 us
  local copies, waits for them, and re-layouts: 3.8 us -> 4.99 us
    ppermute x0 -> x4, starting transfers between devices: none -> 10.4 us  [the longest x2 7.77 us: shift_both(): from_prev = lax.ppermute(high, axis, [(i, i + 1) for i in range(ends)])]
    ppermute x3 -> x1, starting transfers between devices: 8.55 us -> 3 us  [swap_one(): lax.ppermute(jnp.where(is_low(axis, parity), high, low), axis, perm)]
    ppermute x3 -> x1, waiting for transfers between devices: 4.91 us -> 0.31 us  [swap_one(): lax.ppermute(jnp.where(is_low(axis, parity), high, low), axis, perm)]
    ppermute x6, waiting for transfers between devices: 8.74 us -> 5.06 us  [reduced(): got.append(lax.ppermute(low, AXES, perm))]
    ppermute x6, starting transfers between devices: 8.54 us -> 10.7 us  [reduced(): got.append(lax.ppermute(low, AXES, perm))]
    pallas_call x3 -> x4, Pallas kernels: 3.51 us -> 4.91 us  [the longest x2 3.81 us: outer(): pl.pallas_call(functools.partial(rim_body, side=side), out_shape=out_shap...]
    unnamed x9, local copies, waits for them, and re-layouts: 2.52 us -> 3.88 us
    ppermute x0 -> x4, waiting for transfers between devices: none -> 0.78 us  [the longest x2 0.77 us: shift_both(): lax.ppermute(low, axis, [(i + 1, i) for i in range(ends)])]
  transfers between devices with their start and end apart: 11 -> 13, of which waited for: 8 -> 6; matrix products, arithmetic and copies ran while one was open for 4% -> 4% of each run, Pallas kernels for 10% -> 13%
where the time goes in v5:
time: 48 us; the launch traced here: 47.7 us
  starting transfers between devices  24.2 us (50%)
  Pallas kernels  9.52 us (20%)
  waiting for transfers between devices  7.56 us (16%)
  local copies, waits for them, and re-layouts  4.99 us (10%)
  between operations  0.91 us (2%)
  other arithmetic  0.55 us (1%)
    ppermute x6, starting transfers between devices, reduced(): got.append(lax.ppermute(low, AXES, perm))  10.7 us
    ppermute x2, starting transfers between devices, shift_both(): from_prev = lax.ppermute(high, axis, [(i, i + 1) for i in range(ends)])  7.77 us
    ppermute x6, waiting for transfers between devices, reduced(): got.append(lax.ppermute(low, AXES, perm))  5.06 us
    unnamed x9, local copies, waits for them, and re-layouts  3.88 us
    pallas_call x2, Pallas kernels, outer(): pl.pallas_call(functools.partial(rim_body, side=side), out_shape=out_shap...  3.81 us
    pallas_call x1, Pallas kernels, inner(): pl.pallas_call(inner_body, out_shape=(jax.ShapeDtypeStruct(shifts(2), BF)...  3.26 us
    ppermute x1, starting transfers between devices, swap_one(): lax.ppermute(jnp.where(is_low(axis, parity), high, low), axis, perm)  3 us
    ppermute x2, starting transfers between devices, shift_both(): lax.ppermute(low, axis, [(i + 1, i) for i in range(ends)])  2.58 us
  transfers between devices with their start and end apart: 13, of which 6 were waited for; matrix products, arithmetic and copies ran while one was open for 4% of the time, Pallas kernels for 13%

profile of v5, /device:TPU:0, one launch (start us, length us, event | category | flops | bytes accessed | tf_op | source)
XLA Modules:
  0.0 47.7 jit_solution(17931694604971987065)
XLA Ops:
  0.6 1.2 %copy.10 = bf16[1,64,16,256]{3,1,2,0:T(8,128)(2,1)S(1)} copy(bf16[1,64,16,256]{3,2,1,0:T(8,128)(2,1)} %param.4) | data formatting | bytes 1048576 | tf_op args[0]
  1.8 0.0 copy-start.2
  1.9 0.3 copy.19.f
  2.1 0.8 %copy-done.2 = bf16[1,64,16,256]{3,2,1,0:T(8,128)(2,1)S(1)} copy-done((bf16[1,64,16,256]{3,2,1,0:T(8,128)(2,1)S(1)}, bf16[1,64,16,256]{3,2,1,0:T(8,128)(2,1)}, u32[]{:S(2)}) %copy-start.2) | copy-done | bytes 524312
  2.9 0.2 copy.11
  3.0 0.3 copy.20.g
  3.4 3.0 %collective-permute-start = (bf16[16,8,128]{2,1,0:T(8,128)(2,1)S(1)}, bf16[16,8,128]{2,1,0:T(8,128)(2,1)S(1)}, u32[]{:S(2)}, u32[]{:S(2)}) collective-permute-start(bf16[16,8,128]{2,1,0:T(8,128)(2,1)S(1)} %fusion), channel_id=1, source_target_pairs={{0,1},{1,0},{2,3},{3,2},{4,5},{5,4},{6,7},{7,6},{8,9},{9,8},{10,11... | collective-permute-start | bytes 98312 | tf_op jit(solution)/shard_map/ppermute | solution.py:41
  6.4 0.1 slice_bitcast_fusion
  6.5 0.1 maximum_bitcast_fusion
  6.6 0.0 copy-start.1
  6.6 0.1 maximum_bitcast_fusion.1
  6.7 0.0 copy-start
  6.7 0.1 copy.16
  6.8 0.1 copy.23
  7.0 0.5 %copy-done.1 = bf16[3,3,64,64]{3,2,1,0:T(8,128)(2,1)S(1)} copy-done((bf16[3,3,64,64]{3,2,1,0:T(8,128)(2,1)S(1)}, bf16[3,3,64,64]{3,2,1,0:T(8,128)(2,1)}, u32[]{:S(2)}) %copy-start.1) | copy-done | bytes 73752
  7.5 0.1 copy-done
  7.6 0.3 weights.1
  7.9 0.3 collective-permute-done
  8.3 0.1 fusion.8
  8.4 0.1 maximum_bitcast_fusion.2
  8.4 4.0 %collective-permute-start.1 = (bf16[2,272,128]{2,1,0:T(8,128)(2,1)S(1)}, bf16[2,272,128]{2,1,0:T(8,128)(2,1)S(1)}, u32[]{:S(2)}, u32[]{:S(2)}) collective-permute-start(bf16[2,272,128]{2,1,0:T(8,128)(2,1)S(1)} %maximum_maximum_fusion), channel_id=1, source_target_pairs={{0,2},{2,4},{4,6},{6,8},{8,10},{10,12},{12,14},{1,3},{3,5},{5,7},{... | collective-permute-start | bytes 417800 | tf_op jit(solution)/shard_map/ppermute | solution.py:32
  12.4 0.1 maximum_bitcast_fusion.3
  12.5 1.3 %collective-permute-start.2 = (bf16[2,272,128]{2,1,0:T(8,128)(2,1)S(1)}, bf16[2,272,128]{2,1,0:T(8,128)(2,1)S(1)}, u32[]{:S(2)}, u32[]{:S(2)}) collective-permute-start(bf16[2,272,128]{2,1,0:T(8,128)(2,1)S(1)} %maximum_maximum_fusion.1), channel_id=1, source_target_pairs={{2,0},{4,2},{6,4},{8,6},{10,8},{12,10},{14,12},{3,1},{5,3},{7,5},{... | collective-permute-start | bytes 417800 | tf_op jit(solution)/shard_map/ppermute | solution.py:33
  13.8 3.3 %inner.1 = (bf16[2,3,272,128]{3,2,1,0:T(8,128)(2,1)S(1)}, bf16[2,3,272,128]{3,2,1,0:T(8,128)(2,1)S(1)}, f32[2,272,128]{2,1,0:T(8,128)S(1)}, bf16[5,3,272,128]{3,...) custom-call(bf16[8,256,128]{2,1,0:T(8,128)(2,1)S(1)} %copy.19.f, ...), custom_call_target="tpu_custom_call" | custom-call | flops 1176502272 | bytes 4194304 | tf_op jit(solution)/shard_map/inner/pallas_call | solution.py:291
  17.1 1.6 %upper.1 = (bf16[2,3,272,128]{3,2,1,0:T(8,128)(2,1)S(1)}, bf16[144,128]{1,0:T(8,128)(2,1)S(1)}, f32[256,384]{1,0:T(8,128)S(1)}, f32[256,384]{1,0:T(8,128)S(1)}) custom-call(bf16[8,256,128]{2,1,0:T(8,128)(2,1)S(1)} %copy.19.f, bf16[8,256,128]{2,1,0:T(8,128)(2,1)S(1)} %copy.20.g, bf16[16,16,128]{2,1,0:T(8,128)(2,1)S(1)} %pad_maximum_fusion.edge, ...), custom_call_target="tpu_custom_call" | custom-call | flops 427819008 | bytes 4194304 | tf_op jit(solution)/shard_map/upper/pallas_call | solution.py:330
  18.7 0.8 %collective-permute-done.2.halo = bf16[2,272,128]{2,1,0:T(8,128)(2,1)S(1)} collective-permute-done((bf16[2,272,128]{2,1,0:T(8,128)(2,1)S(1)}, bf16[2,272,128]{2,1,0:T(8,128)(2,1)S(1)}, u32[]{:S(2)}, u32[]{:S(2)}) %collective-permute-start.2) | collective-permute-done | bytes 139296 | tf_op jit(solution)/shard_map/ppermute | solution.py:33
  19.5 2.2 %lower.1 = (bf16[2,3,272,128]{3,2,1,0:T(8,128)(2,1)S(1)}, bf16[144,128]{1,0:T(8,128)(2,1)S(1)}, f32[256,384]{1,0:T(8,128)}, f32[256,384]{1,0:T(8,128)}, f32[576,128]{1,0:T(8,128)S(1)}) custom-call(bf16[8,256,128]{2,1,0:T(8,128)(2,1)S(1)} %copy.19.f, bf16[8,256,128]{2,1,0:T(8,128)(2,1)S(1)} %copy.20.g, bf16[16,16,128]{2,1,0:T(8,128)(2,1)S(1)} %pad_maximum_fusion.edge, ...), custom_call_target="tpu_custom_call" | custom-call | flops 427819008 | bytes 4194304 | tf_op jit(solution)/shard_map/lower/pallas_call | solution.py:330
  21.7 0.1 collective-permute-start.5
  21.8 1.4 %collective-permute-done.5 = f32[288,128]{1,0:T(8,128)S(1)} collective-permute-done((f32[288,128]{1,0:T(8,128)S(1)}, f32[288,128]{1,0:T(8,128)S(1)}, u32[]{:S(2)}, u32[]{:S(2)}) %collective-permute-start.5) | collective-permute-done | bytes 147488 | tf_op jit(solution)/shard_map/ppermute | solution.py:411
  23.2 3.4 %collective-permute-start.8 = (bf16[288,128]{1,0:T(8,128)(2,1)S(1)}, bf16[288,128]{1,0:T(8,128)(2,1)S(1)}, u32[]{:S(2)}, u32[]{:S(2)}) collective-permute-start(bf16[288,128]{1,0:T(8,128)(2,1)S(1)} %add_convert_fusion.1), channel_id=1, source_target_pairs={{0,3},{1,2},{2,1},{3,0},{4,7},{5,6},{6,5},{7,4},{8,11},{9,10},{10,... | collective-permute-start | bytes 221192 | tf_op jit(solution)/shard_map/ppermute | solution.py:436
  26.6 0.5 %collective-permute-start.7 = (bf16[288,128]{1,0:T(8,128)(2,1)S(1)}, bf16[288,128]{1,0:T(8,128)(2,1)S(1)}, u32[]{:S(2)}, u32[]{:S(2)}) collective-permute-start(bf16[288,128]{1,0:T(8,128)(2,1)S(1)} %add_convert_fusion.1), channel_id=1, source_target_pairs={{0,1},{1,0},{2,3},{3,2},{4,5},{5,4},{6,7},{7,6},{8,9},{9,8},{10,11... | collective-permute-start | bytes 221192 | tf_op jit(solution)/shard_map/ppermute | solution.py:436
  27.1 0.1 collective-permute-start.6
  27.2 3.8 %collective-permute-start.3 = (bf16[144,128]{1,0:T(8,128)(2,1)S(1)}, bf16[144,128]{1,0:T(8,128)(2,1)S(1)}, u32[]{:S(2)}, u32[]{:S(2)}) collective-permute-start(bf16[144,128]{1,0:T(8,128)(2,1)S(1)} %get-tuple-element.37), channel_id=1, source_target_pairs={{0,2},{2,4},{4,6},{6,8},{8,10},{10,12},{12,14},{1,3},{3,5},{5,7},{... | collective-permute-start | bytes 110600 | tf_op jit(solution)/shard_map/ppermute | solution.py:32
  31.0 1.3 %collective-permute-start.4 = (bf16[144,128]{1,0:T(8,128)(2,1)S(1)}, bf16[144,128]{1,0:T(8,128)(2,1)S(1)}, u32[]{:S(2)}, u32[]{:S(2)}) collective-permute-start(bf16[144,128]{1,0:T(8,128)(2,1)S(1)} %get-tuple-element.38), channel_id=1, source_target_pairs={{2,0},{4,2},{6,4},{8,6},{10,8},{12,10},{14,12},{3,1},{5,3},{7,5},{... | collective-permute-start | bytes 110600 | tf_op jit(solution)/shard_map/ppermute | solution.py:33
  32.3 0.0 collective-permute-done.8
  32.3 0.0 collective-permute-done.6
  32.4 4.0 %collective-permute-start.9 = (bf16[288,128]{1,0:T(8,128)(2,1)S(1)}, bf16[288,128]{1,0:T(8,128)(2,1)S(1)}, u32[]{:S(2)}, u32[]{:S(2)}) collective-permute-start(bf16[288,128]{1,0:T(8,128)(2,1)S(1)} %add_convert_fusion.own), channel_id=1, source_target_pairs={{0,4},{1,5},{2,6},{3,7},{4,0},{5,1},{6,2},{7,3},{8,12},{9,13},{10,... | collective-permute-start | bytes 221192 | tf_op jit(solution)/shard_map/ppermute | solution.py:436
  36.4 2.6 %collective-permute-start.10 = (bf16[288,128]{1,0:T(8,128)(2,1)S(1)}, bf16[288,128]{1,0:T(8,128)(2,1)S(1)}, u32[]{:S(2)}, u32[]{:S(2)}) collective-permute-start(bf16[288,128]{1,0:T(8,128)(2,1)S(1)} %add_convert_fusion.own), channel_id=1, source_target_pairs={{0,8},{1,9},{2,10},{3,11},{4,12},{5,13},{6,14},{7,15},{8,0},{9,1},... | collective-permute-start | bytes 221192 | tf_op jit(solution)/shard_map/ppermute | solution.py:436
  39.0 0.0 collective-permute-start.11
  39.0 0.0 collective-permute-done.3.prev_row
  39.0 1.1 %last.1 = (bf16[8,256,128]{2,1,0:T(8,128)(2,1)S(1)}, f32[8,128]{1,0:T(8,128)S(1)}) custom-call(bf16[2,3,272,128]{3,2,1,0:T(8,128)(2,1)S(1)} %get-tuple-element.32.ds1_top, bf16[5,3,272,128]{3,2,1,0:T(8,128)(2,1)S(1)} %get-tuple-element.33.ds1, bf16[2,3,272,128]{3,2,1,0:T(8,128)(2,1)S(1)} %get-tuple-element.36.ds1_bottom, ...), custom_call_target="tpu_custom_call" | custom-call | flops 427819008 | bytes 4194304 | tf_op jit(solution)/shard_map/last/pallas_call | solution.py:347
  40.1 2.4 %collective-permute-done.10.two = bf16[288,128]{1,0:T(8,128)(2,1)S(1)} collective-permute-done((bf16[288,128]{1,0:T(8,128)(2,1)S(1)}, bf16[288,128]{1,0:T(8,128)(2,1)S(1)}, u32[]{:S(2)}, u32[]{:S(2)}) %collective-permute-start.10) | collective-permute-done | bytes 73760 | tf_op jit(solution)/shard_map/ppermute | solution.py:436
  42.5 2.7 %collective-permute-done.11.three = bf16[288,128]{1,0:T(8,128)(2,1)S(1)} collective-permute-done((bf16[288,128]{1,0:T(8,128)(2,1)S(1)}, bf16[288,128]{1,0:T(8,128)(2,1)S(1)}, u32[]{:S(2)}, u32[]{:S(2)}) %collective-permute-start.11) | collective-permute-done | bytes 73760 | tf_op jit(solution)/shard_map/ppermute | solution.py:436
  45.2 0.1 collective-permute-start.12
  45.3 0.2 copy.26
  45.5 1.1 %copy.27 = bf16[1,64,16,256]{3,2,1,0:T(8,128)(2,1)} copy(bf16[1,64,16,256]{3,1,2,0:T(8,128)(2,1)S(1)} %bitcast.43) | data formatting | bytes 1048576
  46.6 0.1 collective-permute-done.12.other
  46.6 1.0 %finish.1 = (f32[3,3,64,64]{3,2,1,0:T(8,128)}, f32[3,3,64,64]{3,2,1,0:T(8,128)}) custom-call(f32[288,128]{1,0:T(8,128)S(1)} %sum_four.1.part, f32[288,128]{1,0:T(8,128)S(1)} %collective-permute-done.12.other), custom_call_target="tpu_custom_call" | custom-call | tf_op jit(solution)/shard_map/finish/pallas_call | solution.py:390
  (15 shorter events, 0.2 us)
Async XLA Ops:
  1.8 1.0 %copy-start.2 = (bf16[1,64,16,256]{3,2,1,0:T(8,128)(2,1)S(1)}, bf16[1,64,16,256]{3,2,1,0:T(8,128)(2,1)}, u32[]{:S(2)}) copy-start(bf16[1,64,16,256]{3,2,1,0:T(8,128)(2,1)} %param.5) | copy-start | bytes 1572868
  3.4 4.9 %collective-permute-start = (bf16[16,8,128]{2,1,0:T(8,128)(2,1)S(1)}, bf16[16,8,128]{2,1,0:T(8,128)(2,1)S(1)}, u32[]{:S(2)}, u32[]{:S(2)}) collective-permute-start(bf16[16,8,128]{2,1,0:T(8,128)(2,1)S(1)} %fusion), channel_id=1, source_target_pairs={{0,1},{1,0},{2,3},{3,2},{4,5},{5,4},{6,7},{7,6},{8,9},{9,8},{10,11... | collective-permute-start | bytes 98312 | tf_op jit(solution)/shard_map/ppermute | solution.py:41
  6.6 0.9 %copy-start.1 = (bf16[3,3,64,64]{3,2,1,0:T(8,128)(2,1)S(1)}, bf16[3,3,64,64]{3,2,1,0:T(8,128)(2,1)}, u32[]{:S(2)}) copy-start(bf16[3,3,64,64]{3,2,1,0:T(8,128)(2,1)} %k2.1) | copy-start | bytes 221188
  6.7 0.9 %copy-start = (bf16[3,3,64,64]{3,2,1,0:T(8,128)(2,1)S(1)}, bf16[3,3,64,64]{3,2,1,0:T(8,128)(2,1)}, u32[]{:S(2)}) copy-start(bf16[3,3,64,64]{3,2,1,0:T(8,128)(2,1)} %k1.1) | copy-start | bytes 221188
  8.4 8.6 %collective-permute-start.1 = (bf16[2,272,128]{2,1,0:T(8,128)(2,1)S(1)}, bf16[2,272,128]{2,1,0:T(8,128)(2,1)S(1)}, u32[]{:S(2)}, u32[]{:S(2)}) collective-permute-start(bf16[2,272,128]{2,1,0:T(8,128)(2,1)S(1)} %maximum_maximum_fusion), channel_id=1, source_target_pairs={{0,2},{2,4},{4,6},{6,8},{8,10},{10,12},{12,14},{1,3},{3,5},{5,7},{... | collective-permute-start | bytes 417800 | tf_op jit(solution)/shard_map/ppermute | solution.py:32
  12.5 6.9 %collective-permute-start.2 = (bf16[2,272,128]{2,1,0:T(8,128)(2,1)S(1)}, bf16[2,272,128]{2,1,0:T(8,128)(2,1)S(1)}, u32[]{:S(2)}, u32[]{:S(2)}) collective-permute-start(bf16[2,272,128]{2,1,0:T(8,128)(2,1)S(1)} %maximum_maximum_fusion.1), channel_id=1, source_target_pairs={{2,0},{4,2},{6,4},{8,6},{10,8},{12,10},{14,12},{3,1},{5,3},{7,5},{... | collective-permute-start | bytes 417800 | tf_op jit(solution)/shard_map/ppermute | solution.py:33
  21.7 1.4 %collective-permute-start.5 = (f32[288,128]{1,0:T(8,128)S(1)}, f32[288,128]{1,0:T(8,128)S(1)}, u32[]{:S(2)}, u32[]{:S(2)}) collective-permute-start(f32[288,128]{1,0:T(8,128)S(1)} %constant_dynamic-slice_fusion), channel_id=1, source_target_pairs={{0,16},{16,0},{1,17},{17,1},{2,18},{18,2},{3,19},{19,3},{4,20},{20... | collective-permute-start | bytes 442376 | tf_op jit(solution)/shard_map/ppermute | solution.py:411
  23.2 9.2 %collective-permute-start.8 = (bf16[288,128]{1,0:T(8,128)(2,1)S(1)}, bf16[288,128]{1,0:T(8,128)(2,1)S(1)}, u32[]{:S(2)}, u32[]{:S(2)}) collective-permute-start(bf16[288,128]{1,0:T(8,128)(2,1)S(1)} %add_convert_fusion.1), channel_id=1, source_target_pairs={{0,3},{1,2},{2,1},{3,0},{4,7},{5,6},{6,5},{7,4},{8,11},{9,10},{10,... | collective-permute-start | bytes 221192 | tf_op jit(solution)/shard_map/ppermute | solution.py:436
  26.6 5.8 %collective-permute-start.7 = (bf16[288,128]{1,0:T(8,128)(2,1)S(1)}, bf16[288,128]{1,0:T(8,128)(2,1)S(1)}, u32[]{:S(2)}, u32[]{:S(2)}) collective-permute-start(bf16[288,128]{1,0:T(8,128)(2,1)S(1)} %add_convert_fusion.1), channel_id=1, source_target_pairs={{0,1},{1,0},{2,3},{3,2},{4,5},{5,4},{6,7},{7,6},{8,9},{9,8},{10,11... | collective-permute-start | bytes 221192 | tf_op jit(solution)/shard_map/ppermute | solution.py:436
  27.1 5.3 %collective-permute-start.6 = (bf16[288,128]{1,0:T(8,128)(2,1)S(1)}, bf16[288,128]{1,0:T(8,128)(2,1)S(1)}, u32[]{:S(2)}, u32[]{:S(2)}) collective-permute-start(bf16[288,128]{1,0:T(8,128)(2,1)S(1)} %add_convert_fusion.1), channel_id=1, source_target_pairs={{0,2},{1,3},{2,0},{3,1},{4,6},{5,7},{6,4},{7,5},{8,10},{9,11},{10,... | collective-permute-start | bytes 221192 | tf_op jit(solution)/shard_map/ppermute | solution.py:436
  27.2 11.8 %collective-permute-start.3 = (bf16[144,128]{1,0:T(8,128)(2,1)S(1)}, bf16[144,128]{1,0:T(8,128)(2,1)S(1)}, u32[]{:S(2)}, u32[]{:S(2)}) collective-permute-start(bf16[144,128]{1,0:T(8,128)(2,1)S(1)} %get-tuple-element.37), channel_id=1, source_target_pairs={{0,2},{2,4},{4,6},{6,8},{8,10},{10,12},{12,14},{1,3},{3,5},{5,7},{... | collective-permute-start | bytes 110600 | tf_op jit(solution)/shard_map/ppermute | solution.py:32
  31.0 8.0 %collective-permute-start.4 = (bf16[144,128]{1,0:T(8,128)(2,1)S(1)}, bf16[144,128]{1,0:T(8,128)(2,1)S(1)}, u32[]{:S(2)}, u32[]{:S(2)}) collective-permute-start(bf16[144,128]{1,0:T(8,128)(2,1)S(1)} %get-tuple-element.38), channel_id=1, source_target_pairs={{2,0},{4,2},{6,4},{8,6},{10,8},{12,10},{14,12},{3,1},{5,3},{7,5},{... | collective-permute-start | bytes 110600 | tf_op jit(solution)/shard_map/ppermute | solution.py:33
  32.4 7.7 %collective-permute-start.9 = (bf16[288,128]{1,0:T(8,128)(2,1)S(1)}, bf16[288,128]{1,0:T(8,128)(2,1)S(1)}, u32[]{:S(2)}, u32[]{:S(2)}) collective-permute-start(bf16[288,128]{1,0:T(8,128)(2,1)S(1)} %add_convert_fusion.own), channel_id=1, source_target_pairs={{0,4},{1,5},{2,6},{3,7},{4,0},{5,1},{6,2},{7,3},{8,12},{9,13},{10,... | collective-permute-start | bytes 221192 | tf_op jit(solution)/shard_map/ppermute | solution.py:436
  36.4 6.0 %collective-permute-start.10 = (bf16[288,128]{1,0:T(8,128)(2,1)S(1)}, bf16[288,128]{1,0:T(8,128)(2,1)S(1)}, u32[]{:S(2)}, u32[]{:S(2)}) collective-permute-start(bf16[288,128]{1,0:T(8,128)(2,1)S(1)} %add_convert_fusion.own), channel_id=1, source_target_pairs={{0,8},{1,9},{2,10},{3,11},{4,12},{5,13},{6,14},{7,15},{8,0},{9,1},... | collective-permute-start | bytes 221192 | tf_op jit(solution)/shard_map/ppermute | solution.py:436
  39.0 6.2 %collective-permute-start.11 = (bf16[288,128]{1,0:T(8,128)(2,1)S(1)}, bf16[288,128]{1,0:T(8,128)(2,1)S(1)}, u32[]{:S(2)}, u32[]{:S(2)}) collective-permute-start(bf16[288,128]{1,0:T(8,128)(2,1)S(1)} %add_convert_fusion.own), channel_id=1, source_target_pairs={{0,12},{1,13},{2,14},{3,15},{4,8},{5,9},{6,10},{7,11},{8,4},{9,5},... | collective-permute-start | bytes 221192 | tf_op jit(solution)/shard_map/ppermute | solution.py:436
  45.2 1.4 %collective-permute-start.12 = (f32[288,128]{1,0:T(8,128)S(1)}, f32[288,128]{1,0:T(8,128)S(1)}, u32[]{:S(2)}, u32[]{:S(2)}) collective-permute-start(f32[288,128]{1,0:T(8,128)S(1)} %sum_four.1.part), channel_id=1, source_target_pairs={{0,16},{16,0},{1,17},{17,1},{2,18},{18,2},{3,19},{19,3},{4,20},{20... | collective-permute-start | bytes 442376 | tf_op jit(solution)/shard_map/ppermute | solution.py:444

commit v6 on v5

--- a/solution.py
+++ b/solution.py
@@ -25,12 +25,6 @@
 
 def is_low(axis, parity):
     return lax.axis_index(axis) % 2 == parity
-
-
-def shift_both(low, high, axis):
-    ends = lax.axis_size(axis) - 1
-    from_prev = lax.ppermute(high, axis, [(i, i + 1) for i in range(ends)])
-    return from_prev, lax.ppermute(low, axis, [(i + 1, i) for i in range(ends)])
 
 
 def swap_one(low, high, axis):
@@ -194,66 +188,73 @@
 
 
 def rim_body(
-    f, g, edge, halo, w1, w2, v2, hs_edge, ds2_edge, slope_edge, acc1_in, acc2_in, ds1, row, acc1, acc2, *rest, side
+    f, g, edge, above, below, w1, w2, v2, hs_edge, ds2_edge, slope_edge, acc1_in, acc2_in,
+    ds1_top, ds1_bottom, row_top, row_bottom, term, fs, hs, ds2, slope, acc1, acc2,
 ):
-    if side == 0:
-        fs, hs, ds2, slope = rest
-    else:
-        term, fs, hs, ds2, slope = rest
     pairs, cols = f.shape[:2]
     top, bottom, rim = edge_masks()
-    flag = (top, bottom)[side]
-    beyond = half_lanes(side)
-    outer = jnp.where(beyond, flag, 1.0)
-    near, next_near = (0, 1) if side == 0 else (pairs - 1, pairs - 2)
-    mixed = halo[1].astype(F32)
-
-    def order(one, two):
+    flags = (top, bottom)
+    beyond = [half_lanes(side) for side in range(2)]
+    halo, ds1, rows = (above, below), (ds1_top, ds1_bottom), (row_top, row_bottom)
+    near, next_near = (0, pairs - 1), (1, pairs - 2)
+    mixed = [ref[1].astype(F32) for ref in halo]
+    sides = range(2)
+
+    def order(side, one, two):
         return (one, two) if side == 0 else (two, one)
 
-    store_shifts(jnp.where(beyond, 0.0, mixed), fs, 0)
-    store_shifts(halo[0].astype(F32), fs, 1)
-    store_shifts(with_rim(f[near], edge[near]), fs, 2)
+    for side in sides:
+        store_shifts(jnp.where(beyond[side], 0.0, mixed[side]), fs.at[side], 0)
+        store_shifts(halo[side][0].astype(F32), fs.at[side], 1)
+        store_shifts(with_rim(f[near[side]], edge[near[side]]), fs.at[side], 2)
     for k in (1, 0):
-        pre = band_dot(*order((fs, k), (fs, k + 1)), w1)
-        sig = sigmoid(pre)
-        act = pre * sig
-        if k == 1:
-            slope[...] = sig + act * (1.0 - sig)
-        act = act * (flag if k == 0 else outer)
-        store_shifts(rim_masked(act, rim), hs, k)
-    far_grad = jnp.where(beyond, 0.0, pltpu.roll(mixed, HALF, 1))
+        for side in sides:
+            pre = band_dot(*order(side, (fs.at[side], k), (fs.at[side], k + 1)), w1)
+            sig = sigmoid(pre)
+            act = pre * sig
+            if k == 1:
+                slope[side] = sig + act * (1.0 - sig)
+            act = act * (flags[side] if k == 0 else jnp.where(beyond[side], flags[side], 1.0))
+            store_shifts(rim_masked(act, rim), hs.at[side], k)
     for k in (1, 0):
-        grad = far_grad if k == 0 else with_rim(g[near], edge[pairs + near])
-        inward = (hs, 1) if k == 0 else (hs_edge, side)
-        pre = band_dot(*order((hs, k), inward), w2)
-        sig = sigmoid(pre)
-        delta = grad * (sig + pre * sig * (1.0 - sig))
-        store_shifts(delta, ds2, k)
+        for side in sides:
+            if k == 0:
+                grad = jnp.where(beyond[side], 0.0, pltpu.roll(mixed[side], HALF, 1))
+            else:
+                grad = with_rim(g[near[side]], edge[pairs + near[side]])
+            inward = (hs.at[side], 1) if k == 0 else (hs_edge, side)
+            pre = band_dot(*order(side, (hs.at[side], k), inward), w2)
+            sig = sigmoid(pre)
+            delta = grad * (sig + pre * sig * (1.0 - sig))
+            store_shifts(delta, ds2.at[side], k)
     for k in (1, 0):
-        inward = (ds2, 1) if k == 0 else (ds2_edge, side)
-        back = band_dot(*order((ds2, k), inward), v2)
-        value = back * slope[...] if k == 0 else back * slope_edge[side]
-        if k == 0:
-            value = jnp.where(beyond, 0.0, value)
-        value = rim_masked(value, rim)
-        store_shifts(value, ds1, k)
-        if k == 0:
-            first, second = value[: row.shape[0]], value[value.shape[0] - row.shape[0] :]
-            turned = (first, second)[side]
-            turned = pltpu.roll(turned, HALF, 1)
-            row[...] = ((turned + second) if side == 0 else (first + turned)).astype(BF)
+        for side in sides:
+            inward = (ds2.at[side], 1) if k == 0 else (ds2_edge, side)
+            back = band_dot(*order(side, (ds2.at[side], k), inward), v2)
+            value = back * slope[side] if k == 0 else back * slope_edge[side]
+            if k == 0:
+                value = jnp.where(beyond[side], 0.0, value)
+            value = rim_masked(value, rim)
+            store_shifts(value, ds1[side], k)
+            if k == 0:
+                tall = rows[side].shape[0]
+                first, second = value[:tall], value[value.shape[0] - tall :]
+                if side == 0:
+                    first = pltpu.roll(first, HALF, 1)
+                else:
+                    second = pltpu.roll(second, HALF, 1)
+                rows[side][...] = (first + second).astype(BF)
 
     acc1[...] = acc1_in[...]
     acc2[...] = acc2_in[...]
-    hid = order(hs[1, 1, :cols].T, hs_edge[side, 1, :cols].T)
-    add_one(acc2, jnp.concatenate(hid, axis=0), [ds2[1, s, :cols] for s in range(3)])
-    own = f[near].T
-    for k in range(2):
-        feat = order(halo[0, :cols].T, own) if k == 0 else order(own, f[next_near].T)
-        add_one(acc1, jnp.concatenate(feat, axis=0), [ds1[k, s, :cols] for s in range(3)])
-    if side == 1:
-        take_terms(acc1, acc2, term)
+    for side in sides:
+        hid = order(side, hs[side, 1, 1, :cols].T, hs_edge[side, 1, :cols].T)
+        add_one(acc2, jnp.concatenate(hid, axis=0), [ds2[side, 1, s, :cols] for s in range(3)])
+        own = f[near[side]].T
+        for k in (1, 0):
+            feat = order(side, halo[side][0, :cols].T, own) if k == 0 else order(side, own, f[next_near[side]].T)
+            add_one(acc1, jnp.concatenate(feat, axis=0), [ds1[side][k, s, :cols] for s in range(3)])
+    take_terms(acc1, acc2, term)
 
 
 def with_row(center, row, side):
@@ -312,33 +313,33 @@
     )(f, g, edge, w1, w2, v2)
 
 
-def outer(side, f, *rest):
+def outer(f, *rest):
     wide = f.shape[1] + RIM
-    acc = jax.ShapeDtypeStruct((2 * LANES, 3 * LANES), F32)
-
-    def shifts(count):
-        return (count, 3, wide, LANES)
-
-    out_shape = [
-        jax.ShapeDtypeStruct(shifts(2), BF),
-        jax.ShapeDtypeStruct((wide // 2 + RIM // 2, LANES), BF),
-        acc,
-        acc,
-    ]
-    if side == 1:
-        out_shape.append(jax.ShapeDtypeStruct((9 * HALF, LANES), F32))
-    return pl.pallas_call(
-        functools.partial(rim_body, side=side),
-        out_shape=out_shape,
+
+    def shifts(*count):
+        return (*count, 3, wide, LANES)
+
+    row = jax.ShapeDtypeStruct((wide // 2 + RIM // 2, LANES), BF)
+    return pl.pallas_call(
+        rim_body,
+        out_shape=(
+            jax.ShapeDtypeStruct(shifts(2), BF),
+            jax.ShapeDtypeStruct(shifts(2), BF),
+            row,
+            row,
+            jax.ShapeDtypeStruct((9 * HALF, LANES), F32),
+        ),
         scratch_shapes=[
-            pltpu.VMEM(shifts(3), BF),
-            pltpu.VMEM(shifts(2), BF),
-            pltpu.VMEM(shifts(2), BF),
-            pltpu.VMEM((wide, LANES), F32),
+            pltpu.VMEM(shifts(2, 3), BF),
+            pltpu.VMEM(shifts(2, 2), BF),
+            pltpu.VMEM(shifts(2, 2), BF),
+            pltpu.VMEM((2, wide, LANES), F32),
+            pltpu.VMEM((2 * LANES, 3 * LANES), F32),
+            pltpu.VMEM((2 * LANES, 3 * LANES), F32),
         ],
         compiler_params=PARAMS,
-        cost_estimate=cost(8),
-        name=("upper", "lower")[side],
+        cost_estimate=cost(14),
+        name="outer",
     )(f, *rest)
 
 
@@ -458,12 +459,12 @@
     low_edge = jnp.stack([feat_edge[0], jnp.concatenate([feat_edge[1, :, :HALF], grad_edge[0, :, :HALF]], axis=1)])
     high_edge = jnp.stack([feat_edge[-1], jnp.concatenate([grad_edge[-1, :, HALF:], feat_edge[-2, :, HALF:]], axis=1)])
     low, high = jnp.concatenate([low, low_edge], axis=1), jnp.concatenate([high, high_edge], axis=1)
-    above, below = shift_both(low, high, "row")
+    above, below = swap_one(low, high, "row")
     hs_edge, ds2_edge, slope_edge, ds1, acc1, acc2 = inner(feat, grad, edge, w1, w2, v2)
-    shared = (w1, w2, v2, hs_edge, ds2_edge, slope_edge)
-    ds1_top, low_row, acc1, acc2 = outer(0, feat, grad, edge, above, *shared, acc1, acc2)
-    ds1_bottom, high_row, _, _, term = outer(1, feat, grad, edge, below, *shared, acc1, acc2)
-    prev_row, next_row = shift_both(low_row, high_row, "row")
+    ds1_top, ds1_bottom, low_row, high_row, term = outer(
+        feat, grad, edge, above, below, w1, w2, v2, hs_edge, ds2_edge, slope_edge, acc1, acc2
+    )
+    prev_row, next_row = swap_one(low_row, high_row, "row")
     gf, done = last(ds1_top, ds1, ds1_bottom, prev_row, next_row, v1, cols)
     part, other = reduced(term, done)
     count = slides * lax.axis_size("dp") * rows * lax.axis_size("row") * cols * lax.axis_size("col")

time: 48 us -> 43.4 us (0.904)
  starting transfers between devices: 24.2 us -> 22.2 us
  Pallas kernels: 9.52 us -> 7.81 us
  waiting for transfers between devices: 7.56 us -> 6.62 us
    ppermute x1 -> x5, starting transfers between devices: 3 us -> 14 us  [swap_one(): lax.ppermute(jnp.where(is_low(axis, parity), high, low), axis, perm)]
    ppermute x4 -> x0, starting transfers between devices: 10.4 us -> none  [the longest x2 7.77 us: shift_both(): from_prev = lax.ppermute(high, axis, [(i, i + 1) for i in range(ends)])]
    ppermute x6, starting transfers between devices: 10.7 us -> 8.1 us  [reduced(): got.append(lax.ppermute(low, AXES, perm))]
    pallas_call x2 -> x1, Pallas kernels: 3.81 us -> 2.12 us  [outer(): pl.pallas_call(rim_body, out_shape=(jax.ShapeDtypeStruct(shifts(2), BF),...]
    ppermute x6, waiting for transfers between devices: 5.06 us -> 4.04 us  [reduced(): got.append(lax.ppermute(low, AXES, perm))]
    ppermute x1 -> x5, waiting for transfers between devices: 0.31 us -> 1.17 us  [swap_one(): lax.ppermute(jnp.where(is_low(axis, parity), high, low), axis, perm)]
    ppermute x4 -> x0, waiting for transfers between devices: 0.78 us -> none  [the longest x2 0.77 us: shift_both(): lax.ppermute(low, axis, [(i + 1, i) for i in range(ends)])]
  transfers between devices with their start and end apart: 13 -> 13, of which waited for: 6 -> 7; matrix products, arithmetic and copies ran while one was open for 4% -> 4% of each run, Pallas kernels for 13% -> 11%
where the time goes in v6:
time: 43.4 us; the launch traced here: 43.1 us
  starting transfers between devices  22.2 us (51%)
  Pallas kernels  7.81 us (18%)
  waiting for transfers between devices  6.62 us (15%)
  local copies, waits for them, and re-layouts  5.1 us (12%)
  between operations  0.89 us (2%)
  other arithmetic  0.48 us (1%)
    ppermute x5, starting transfers between devices, swap_one(): lax.ppermute(jnp.where(is_low(axis, parity), high, low), axis, perm)  14 us
    ppermute x6, starting transfers between devices, reduced(): got.append(lax.ppermute(low, AXES, perm))  8.1 us
    ppermute x6, waiting for transfers between devices, reduced(): got.append(lax.ppermute(low, AXES, perm))  4.04 us
    unnamed x9, local copies, waits for them, and re-layouts  3.92 us
    pallas_call x1, Pallas kernels, inner(): pl.pallas_call(inner_body, out_shape=(jax.ShapeDtypeStruct(shifts(2), BF)...  3.22 us
    pallas_call x1, Pallas kernels, outer(): pl.pallas_call(rim_body, out_shape=(jax.ShapeDtypeStruct(shifts(2), BF),...  2.12 us
    ppermute x1, waiting for transfers between devices, reduced(): part = mine + lax.ppermute(other, 'dp', swap)  1.35 us
    ppermute x5, waiting for transfers between devices, swap_one(): lax.ppermute(jnp.where(is_low(axis, parity), high, low), axis, perm)  1.17 us
  transfers between devices with their start and end apart: 13, of which 7 were waited for; matrix products, arithmetic and copies ran while one was open for 4% of the time, Pallas kernels for 11%

profile of v6, /device:TPU:0, one launch (start us, length us, event | category | flops | bytes accessed | tf_op | source)
XLA Modules:
  0.0 43.1 jit_solution(5421982616954645862)
XLA Ops:
  0.6 1.2 %copy.10 = bf16[1,64,16,256]{3,1,2,0:T(8,128)(2,1)S(1)} copy(bf16[1,64,16,256]{3,2,1,0:T(8,128)(2,1)} %param.4) | data formatting | bytes 1048576 | tf_op args[0]
  1.8 0.0 copy-start.2
  1.9 0.3 copy.22.f
  2.1 0.8 %copy-done.2 = bf16[1,64,16,256]{3,2,1,0:T(8,128)(2,1)S(1)} copy-done((bf16[1,64,16,256]{3,2,1,0:T(8,128)(2,1)S(1)}, bf16[1,64,16,256]{3,2,1,0:T(8,128)(2,1)}, u32[]{:S(2)}) %copy-start.2) | copy-done | bytes 524312
  2.9 0.2 copy.11
  3.1 0.3 copy.23.g
  3.4 3.0 %collective-permute-start = (bf16[16,8,128]{2,1,0:T(8,128)(2,1)S(1)}, bf16[16,8,128]{2,1,0:T(8,128)(2,1)S(1)}, u32[]{:S(2)}, u32[]{:S(2)}) collective-permute-start(bf16[16,8,128]{2,1,0:T(8,128)(2,1)S(1)} %fusion), channel_id=1, source_target_pairs={{0,1},{1,0},{2,3},{3,2},{4,5},{5,4},{6,7},{7,6},{8,9},{9,8},{10,11... | collective-permute-start | bytes 98312 | tf_op jit(solution)/shard_map/ppermute | solution.py:35
  6.4 0.1 slice_bitcast_fusion.2
  6.4 0.1 slice_bitcast_fusion.3
  6.6 0.1 maximum_bitcast_fusion
  6.7 0.0 copy-start
  6.7 0.0 copy-start.1
  6.7 0.1 copy.16
  6.8 0.1 copy.19
  7.0 0.6 %copy-done = bf16[3,3,64,64]{3,2,1,0:T(8,128)(2,1)S(1)} copy-done((bf16[3,3,64,64]{3,2,1,0:T(8,128)(2,1)S(1)}, bf16[3,3,64,64]{3,2,1,0:T(8,128)(2,1)}, u32[]{:S(2)}) %copy-start) | copy-done | bytes 73752
  7.6 0.1 copy-done.1
  7.7 0.3 weights.1
  8.0 0.3 collective-permute-done
  8.3 0.1 fusion.10
  8.4 0.1 maximum_bitcast_fusion.2
  8.4 0.1 broadcast_select_fusion.3
  8.5 0.7 %collective-permute-start.1 = (bf16[2,272,128]{2,1,0:T(8,128)(2,1)S(1)}, bf16[2,272,128]{2,1,0:T(8,128)(2,1)S(1)}, u32[]{:S(2)}, u32[]{:S(2)}) collective-permute-start(bf16[2,272,128]{2,1,0:T(8,128)(2,1)S(1)} %get-tuple-element.53), channel_id=1, source_target_pairs={{2,4},{4,2},{6,8},{8,6},{10,12},{12,10},{3,5},{5,3},{7,9},{9,7},{1... | collective-permute-start | bytes 417800 | tf_op jit(solution)/shard_map/ppermute | solution.py:35
  9.2 4.9 %collective-permute-start.2 = (bf16[2,272,128]{2,1,0:T(8,128)(2,1)S(1)}, bf16[2,272,128]{2,1,0:T(8,128)(2,1)S(1)}, u32[]{:S(2)}, u32[]{:S(2)}) collective-permute-start(bf16[2,272,128]{2,1,0:T(8,128)(2,1)S(1)} %get-tuple-element.52), channel_id=1, source_target_pairs={{0,2},{2,0},{4,6},{6,4},{8,10},{10,8},{12,14},{14,12},{1,3},{3,1},... | collective-permute-start | bytes 417800 | tf_op jit(solution)/shard_map/ppermute | solution.py:35
  14.1 3.2 %inner.1 = (bf16[2,3,272,128]{3,2,1,0:T(8,128)(2,1)S(1)}, bf16[2,3,272,128]{3,2,1,0:T(8,128)(2,1)S(1)}, f32[2,272,128]{2,1,0:T(8,128)S(1)}, bf16[5,3,272,128]{3,...) custom-call(bf16[8,256,128]{2,1,0:T(8,128)(2,1)S(1)} %copy.22.f, ...), custom_call_target="tpu_custom_call" | custom-call | flops 1176502272 | bytes 4194304 | tf_op jit(solution)/shard_map/inner/pallas_call | solution.py:292
  17.3 0.0 collective-permute-done.1
  17.3 0.9 %collective-permute-done.2 = bf16[2,272,128]{2,1,0:T(8,128)(2,1)S(1)} collective-permute-done((bf16[2,272,128]{2,1,0:T(8,128)(2,1)S(1)}, bf16[2,272,128]{2,1,0:T(8,128)(2,1)S(1)}, u32[]{:S(2)}, u32[]{:S(2)}) %collective-permute-start.2) | collective-permute-done | bytes 139296 | tf_op jit(solution)/shard_map/ppermute | solution.py:35
  18.2 2.1 %outer.1 = (bf16[2,3,272,128]{3,2,1,0:T(8,128)(2,1)S(1)}, bf16[2,3,272,128]{3,2,1,0:T(8,128)(2,1)S(1)}, bf16[144,128]{1,0:T(8,128)(2,1)S(1)}, bf16[144,128]{1,0:T(8,128)(2,1)S(1)}, f32[576,128]{1,0:T(8,128)S(1)}) custom-call(bf16[8,256,128]{2,1,0:T(8,128)(2,1)S(1)} %copy.22.f, bf16[8,256,128]{2,1,0:T(8,128)(2,1)S(1)} %copy.23.g, ...), custom_call_target="tpu_custom_call" | custom-call | flops 748683264 | bytes 4194304 | tf_op jit(solution)/shard_map/outer/pallas_call | solution.py:323
  20.4 0.1 collective-permute-start.5
  20.5 1.4 %collective-permute-done.5 = f32[288,128]{1,0:T(8,128)S(1)} collective-permute-done((f32[288,128]{1,0:T(8,128)S(1)}, f32[288,128]{1,0:T(8,128)S(1)}, u32[]{:S(2)}, u32[]{:S(2)}) %collective-permute-start.5) | collective-permute-done | bytes 147488 | tf_op jit(solution)/shard_map/ppermute | solution.py:412
  21.8 2.6 %collective-permute-start.6 = (bf16[288,128]{1,0:T(8,128)(2,1)S(1)}, bf16[288,128]{1,0:T(8,128)(2,1)S(1)}, u32[]{:S(2)}, u32[]{:S(2)}) collective-permute-start(bf16[288,128]{1,0:T(8,128)(2,1)S(1)} %add_convert_fusion.1), channel_id=1, source_target_pairs={{0,2},{1,3},{2,0},{3,1},{4,6},{5,7},{6,4},{7,5},{8,10},{9,11},{10,... | collective-permute-start | bytes 221192 | tf_op jit(solution)/shard_map/ppermute | solution.py:437
  24.4 1.4 %collective-permute-start.7 = (bf16[288,128]{1,0:T(8,128)(2,1)S(1)}, bf16[288,128]{1,0:T(8,128)(2,1)S(1)}, u32[]{:S(2)}, u32[]{:S(2)}) collective-permute-start(bf16[288,128]{1,0:T(8,128)(2,1)S(1)} %add_convert_fusion.1), channel_id=1, source_target_pairs={{0,1},{1,0},{2,3},{3,2},{4,5},{5,4},{6,7},{7,6},{8,9},{9,8},{10,11... | collective-permute-start | bytes 221192 | tf_op jit(solution)/shard_map/ppermute | solution.py:437
  25.8 0.1 collective-permute-start.8
  25.9 0.7 %collective-permute-start.3 = (bf16[144,128]{1,0:T(8,128)(2,1)S(1)}, bf16[144,128]{1,0:T(8,128)(2,1)S(1)}, u32[]{:S(2)}, u32[]{:S(2)}) collective-permute-start(bf16[144,128]{1,0:T(8,128)(2,1)S(1)} %get-tuple-element.57), channel_id=1, source_target_pairs={{2,4},{4,2},{6,8},{8,6},{10,12},{12,10},{3,5},{5,3},{7,9},{9,7},{1... | collective-permute-start | bytes 110600 | tf_op jit(solution)/shard_map/ppermute | solution.py:35
  26.6 4.8 %collective-permute-start.4 = (bf16[144,128]{1,0:T(8,128)(2,1)S(1)}, bf16[144,128]{1,0:T(8,128)(2,1)S(1)}, u32[]{:S(2)}, u32[]{:S(2)}) collective-permute-start(bf16[144,128]{1,0:T(8,128)(2,1)S(1)} %get-tuple-element.56), channel_id=1, source_target_pairs={{0,2},{2,0},{4,6},{6,4},{8,10},{10,8},{12,14},{14,12},{1,3},{3,1},... | collective-permute-start | bytes 110600 | tf_op jit(solution)/shard_map/ppermute | solution.py:35
  31.5 2.7 %collective-permute-start.10 = (bf16[288,128]{1,0:T(8,128)(2,1)S(1)}, bf16[288,128]{1,0:T(8,128)(2,1)S(1)}, u32[]{:S(2)}, u32[]{:S(2)}) collective-permute-start(bf16[288,128]{1,0:T(8,128)(2,1)S(1)} %add_convert_fusion.own), channel_id=1, source_target_pairs={{0,8},{1,9},{2,10},{3,11},{4,12},{5,13},{6,14},{7,15},{8,0},{9,1},... | collective-permute-start | bytes 221192 | tf_op jit(solution)/shard_map/ppermute | solution.py:437
  34.1 1.3 %collective-permute-start.11 = (bf16[288,128]{1,0:T(8,128)(2,1)S(1)}, bf16[288,128]{1,0:T(8,128)(2,1)S(1)}, u32[]{:S(2)}, u32[]{:S(2)}) collective-permute-start(bf16[288,128]{1,0:T(8,128)(2,1)S(1)} %add_convert_fusion.own), channel_id=1, source_target_pairs={{0,12},{1,13},{2,14},{3,15},{4,8},{5,9},{6,10},{7,11},{8,4},{9,5},... | collective-permute-start | bytes 221192 | tf_op jit(solution)/shard_map/ppermute | solution.py:437
  35.5 0.0 collective-permute-start.9
  35.5 0.0 collective-permute-done.3
  35.5 0.0 collective-permute-done.4
  35.5 1.1 %last.1 = (bf16[8,256,128]{2,1,0:T(8,128)(2,1)S(1)}, f32[8,128]{1,0:T(8,128)S(1)}) custom-call(bf16[2,3,272,128]{3,2,1,0:T(8,128)(2,1)S(1)} %get-tuple-element.30.ds1_top, bf16[5,3,272,128]{3,2,1,0:T(8,128)(2,1)S(1)} %get-tuple-element.31.ds1, bf16[2,3,272,128]{3,2,1,0:T(8,128)(2,1)S(1)} %get-tuple-element.32.ds1_bottom, ...), custom_call_target="tpu_custom_call" | custom-call | flops 427819008 | bytes 4194304 | tf_op jit(solution)/shard_map/last/pallas_call | solution.py:348
  36.6 0.2 collective-permute-done.10.two
  36.8 3.6 %collective-permute-done.11.three = bf16[288,128]{1,0:T(8,128)(2,1)S(1)} collective-permute-done((bf16[288,128]{1,0:T(8,128)(2,1)S(1)}, bf16[288,128]{1,0:T(8,128)(2,1)S(1)}, u32[]{:S(2)}, u32[]{:S(2)}) %collective-permute-start.11) | collective-permute-done | bytes 73760 | tf_op jit(solution)/shard_map/ppermute | solution.py:437
  40.4 0.2 collective-permute-done.9.one
  40.6 0.1 collective-permute-start.12
  40.7 0.2 copy.24
  40.9 1.1 %copy.25 = bf16[1,64,16,256]{3,2,1,0:T(8,128)(2,1)} copy(bf16[1,64,16,256]{3,1,2,0:T(8,128)(2,1)S(1)} %bitcast.43) | data formatting | bytes 1048576
  42.0 0.1 collective-permute-done.12.other
  42.1 1.0 %finish.1 = (f32[3,3,64,64]{3,2,1,0:T(8,128)}, f32[3,3,64,64]{3,2,1,0:T(8,128)}) custom-call(f32[288,128]{1,0:T(8,128)S(1)} %sum_four.1.part, f32[288,128]{1,0:T(8,128)S(1)} %collective-permute-done.12.other), custom_call_target="tpu_custom_call" | custom-call | tf_op jit(solution)/shard_map/finish/pallas_call | solution.py:391
  (15 shorter events, 0.2 us)
Async XLA Ops:
  1.8 1.0 %copy-start.2 = (bf16[1,64,16,256]{3,2,1,0:T(8,128)(2,1)S(1)}, bf16[1,64,16,256]{3,2,1,0:T(8,128)(2,1)}, u32[]{:S(2)}) copy-start(bf16[1,64,16,256]{3,2,1,0:T(8,128)(2,1)} %param.5) | copy-start | bytes 1572868
  3.4 4.9 %collective-permute-start = (bf16[16,8,128]{2,1,0:T(8,128)(2,1)S(1)}, bf16[16,8,128]{2,1,0:T(8,128)(2,1)S(1)}, u32[]{:S(2)}, u32[]{:S(2)}) collective-permute-start(bf16[16,8,128]{2,1,0:T(8,128)(2,1)S(1)} %fusion), channel_id=1, source_target_pairs={{0,1},{1,0},{2,3},{3,2},{4,5},{5,4},{6,7},{7,6},{8,9},{9,8},{10,11... | collective-permute-start | bytes 98312 | tf_op jit(solution)/shard_map/ppermute | solution.py:35
  6.7 0.9 %copy-start = (bf16[3,3,64,64]{3,2,1,0:T(8,128)(2,1)S(1)}, bf16[3,3,64,64]{3,2,1,0:T(8,128)(2,1)}, u32[]{:S(2)}) copy-start(bf16[3,3,64,64]{3,2,1,0:T(8,128)(2,1)} %k1.1) | copy-start | bytes 221188
  6.7 1.0 %copy-start.1 = (bf16[3,3,64,64]{3,2,1,0:T(8,128)(2,1)S(1)}, bf16[3,3,64,64]{3,2,1,0:T(8,128)(2,1)}, u32[]{:S(2)}) copy-start(bf16[3,3,64,64]{3,2,1,0:T(8,128)(2,1)} %k2.1) | copy-start | bytes 221188
  8.5 8.8 %collective-permute-start.1 = (bf16[2,272,128]{2,1,0:T(8,128)(2,1)S(1)}, bf16[2,272,128]{2,1,0:T(8,128)(2,1)S(1)}, u32[]{:S(2)}, u32[]{:S(2)}) collective-permute-start(bf16[2,272,128]{2,1,0:T(8,128)(2,1)S(1)} %get-tuple-element.53), channel_id=1, source_target_pairs={{2,4},{4,2},{6,8},{8,6},{10,12},{12,10},{3,5},{5,3},{7,9},{9,7},{1... | collective-permute-start | bytes 417800 | tf_op jit(solution)/shard_map/ppermute | solution.py:35
  9.2 9.0 %collective-permute-start.2 = (bf16[2,272,128]{2,1,0:T(8,128)(2,1)S(1)}, bf16[2,272,128]{2,1,0:T(8,128)(2,1)S(1)}, u32[]{:S(2)}, u32[]{:S(2)}) collective-permute-start(bf16[2,272,128]{2,1,0:T(8,128)(2,1)S(1)} %get-tuple-element.52), channel_id=1, source_target_pairs={{0,2},{2,0},{4,6},{6,4},{8,10},{10,8},{12,14},{14,12},{1,3},{3,1},... | collective-permute-start | bytes 417800 | tf_op jit(solution)/shard_map/ppermute | solution.py:35
  20.4 1.4 %collective-permute-start.5 = (f32[288,128]{1,0:T(8,128)S(1)}, f32[288,128]{1,0:T(8,128)S(1)}, u32[]{:S(2)}, u32[]{:S(2)}) collective-permute-start(f32[288,128]{1,0:T(8,128)S(1)} %constant_dynamic-slice_fusion), channel_id=1, source_target_pairs={{0,16},{16,0},{1,17},{17,1},{2,18},{18,2},{3,19},{19,3},{4,20},{20... | collective-permute-start | bytes 442376 | tf_op jit(solution)/shard_map/ppermute | solution.py:412
  21.8 9.6 %collective-permute-start.6 = (bf16[288,128]{1,0:T(8,128)(2,1)S(1)}, bf16[288,128]{1,0:T(8,128)(2,1)S(1)}, u32[]{:S(2)}, u32[]{:S(2)}) collective-permute-start(bf16[288,128]{1,0:T(8,128)(2,1)S(1)} %add_convert_fusion.1), channel_id=1, source_target_pairs={{0,2},{1,3},{2,0},{3,1},{4,6},{5,7},{6,4},{7,5},{8,10},{9,11},{10,... | collective-permute-start | bytes 221192 | tf_op jit(solution)/shard_map/ppermute | solution.py:437
  24.4 7.0 %collective-permute-start.7 = (bf16[288,128]{1,0:T(8,128)(2,1)S(1)}, bf16[288,128]{1,0:T(8,128)(2,1)S(1)}, u32[]{:S(2)}, u32[]{:S(2)}) collective-permute-start(bf16[288,128]{1,0:T(8,128)(2,1)S(1)} %add_convert_fusion.1), channel_id=1, source_target_pairs={{0,1},{1,0},{2,3},{3,2},{4,5},{5,4},{6,7},{7,6},{8,9},{9,8},{10,11... | collective-permute-start | bytes 221192 | tf_op jit(solution)/shard_map/ppermute | solution.py:437
  25.8 5.6 %collective-permute-start.8 = (bf16[288,128]{1,0:T(8,128)(2,1)S(1)}, bf16[288,128]{1,0:T(8,128)(2,1)S(1)}, u32[]{:S(2)}, u32[]{:S(2)}) collective-permute-start(bf16[288,128]{1,0:T(8,128)(2,1)S(1)} %add_convert_fusion.1), channel_id=1, source_target_pairs={{0,3},{1,2},{2,1},{3,0},{4,7},{5,6},{6,5},{7,4},{8,11},{9,10},{10,... | collective-permute-start | bytes 221192 | tf_op jit(solution)/shard_map/ppermute | solution.py:437
  25.9 9.5 %collective-permute-start.3 = (bf16[144,128]{1,0:T(8,128)(2,1)S(1)}, bf16[144,128]{1,0:T(8,128)(2,1)S(1)}, u32[]{:S(2)}, u32[]{:S(2)}) collective-permute-start(bf16[144,128]{1,0:T(8,128)(2,1)S(1)} %get-tuple-element.57), channel_id=1, source_target_pairs={{2,4},{4,2},{6,8},{8,6},{10,12},{12,10},{3,5},{5,3},{7,9},{9,7},{1... | collective-permute-start | bytes 110600 | tf_op jit(solution)/shard_map/ppermute | solution.py:35
  26.6 8.8 %collective-permute-start.4 = (bf16[144,128]{1,0:T(8,128)(2,1)S(1)}, bf16[144,128]{1,0:T(8,128)(2,1)S(1)}, u32[]{:S(2)}, u32[]{:S(2)}) collective-permute-start(bf16[144,128]{1,0:T(8,128)(2,1)S(1)} %get-tuple-element.56), channel_id=1, source_target_pairs={{0,2},{2,0},{4,6},{6,4},{8,10},{10,8},{12,14},{14,12},{1,3},{3,1},... | collective-permute-start | bytes 110600 | tf_op jit(solution)/shard_map/ppermute | solution.py:35
  31.5 5.3 %collective-permute-start.10 = (bf16[288,128]{1,0:T(8,128)(2,1)S(1)}, bf16[288,128]{1,0:T(8,128)(2,1)S(1)}, u32[]{:S(2)}, u32[]{:S(2)}) collective-permute-start(bf16[288,128]{1,0:T(8,128)(2,1)S(1)} %add_convert_fusion.own), channel_id=1, source_target_pairs={{0,8},{1,9},{2,10},{3,11},{4,12},{5,13},{6,14},{7,15},{8,0},{9,1},... | collective-permute-start | bytes 221192 | tf_op jit(solution)/shard_map/ppermute | solution.py:437
  34.1 6.3 %collective-permute-start.11 = (bf16[288,128]{1,0:T(8,128)(2,1)S(1)}, bf16[288,128]{1,0:T(8,128)(2,1)S(1)}, u32[]{:S(2)}, u32[]{:S(2)}) collective-permute-start(bf16[288,128]{1,0:T(8,128)(2,1)S(1)} %add_convert_fusion.own), channel_id=1, source_target_pairs={{0,12},{1,13},{2,14},{3,15},{4,8},{5,9},{6,10},{7,11},{8,4},{9,5},... | collective-permute-start | bytes 221192 | tf_op jit(solution)/shard_map/ppermute | solution.py:437
  35.5 5.1 %collective-permute-start.9 = (bf16[288,128]{1,0:T(8,128)(2,1)S(1)}, bf16[288,128]{1,0:T(8,128)(2,1)S(1)}, u32[]{:S(2)}, u32[]{:S(2)}) collective-permute-start(bf16[288,128]{1,0:T(8,128)(2,1)S(1)} %add_convert_fusion.own), channel_id=1, source_target_pairs={{0,4},{1,5},{2,6},{3,7},{4,0},{5,1},{6,2},{7,3},{8,12},{9,13},{10,... | collective-permute-start | bytes 221192 | tf_op jit(solution)/shard_map/ppermute | solution.py:437
  40.6 1.4 %collective-permute-start.12 = (f32[288,128]{1,0:T(8,128)S(1)}, f32[288,128]{1,0:T(8,128)S(1)}, u32[]{:S(2)}, u32[]{:S(2)}) collective-permute-start(f32[288,128]{1,0:T(8,128)S(1)} %sum_four.1.part), channel_id=1, source_target_pairs={{0,16},{16,0},{1,17},{17,1},{2,18},{18,2},{3,19},{19,3},{4,20},{20... | collective-permute-start | bytes 442376 | tf_op jit(solution)/shard_map/ppermute | solution.py:445

commit v7 on v6

--- a/solution.py
+++ b/solution.py
@@ -35,8 +35,8 @@
             got.append(lax.ppermute(jnp.where(is_low(axis, parity), high, low), axis, perm))
         else:
             got.append(jnp.zeros_like(low))
-    even = is_low(axis, 0)
-    return jnp.where(even, got[1], got[0]), jnp.where(even, got[0], got[1])
+    odd = is_low(axis, 1)
+    return jnp.where(odd, got[0], got[1]), jnp.where(odd, got[1], got[0])
 
 
 def to_pairs(cells):

time: 43.4 us -> 41.4 us (0.954)
  starting transfers between devices: 22.2 us -> 18.6 us
  waiting for transfers between devices: 6.62 us -> 8.24 us
    ppermute x5, starting transfers between devices: 14 us -> 8.37 us  [swap_one(): lax.ppermute(jnp.where(is_low(axis, parity), high, low), axis, perm)]
    ppermute x6, waiting for transfers between devices: 4.04 us -> 6.37 us  [reduced(): got.append(lax.ppermute(low, AXES, perm))]
    ppermute x6, starting transfers between devices: 8.1 us -> 10.1 us  [reduced(): got.append(lax.ppermute(low, AXES, perm))]
    ppermute x5, waiting for transfers between devices: 1.17 us -> 0.46 us  [swap_one(): lax.ppermute(jnp.where(is_low(axis, parity), high, low), axis, perm)]
  transfers between devices with their start and end apart: 13 -> 13, of which waited for: 7 -> 8; matrix products, arithmetic and copies ran while one was open for 4% -> 5% of each run, Pallas kernels for 11% -> 11%
where the time goes in v7:
time: 41.4 us; the launch traced here: 41.1 us
  starting transfers between devices  18.6 us (45%)
  waiting for transfers between devices  8.24 us (20%)
  Pallas kernels  7.81 us (19%)
  local copies, waits for them, and re-layouts  5.1 us (12%)
  between operations  0.9 us (2%)
  other arithmetic  0.47 us (1%)
    ppermute x6, starting transfers between devices, reduced(): got.append(lax.ppermute(low, AXES, perm))  10.1 us
    ppermute x5, starting transfers between devices, swap_one(): lax.ppermute(jnp.where(is_low(axis, parity), high, low), axis, perm)  8.37 us
    ppermute x6, waiting for transfers between devices, reduced(): got.append(lax.ppermute(low, AXES, perm))  6.37 us
    unnamed x9, local copies, waits for them, and re-layouts  3.92 us
    pallas_call x1, Pallas kernels, inner(): pl.pallas_call(inner_body, out_shape=(jax.ShapeDtypeStruct(shifts(2), BF)...  3.22 us
    pallas_call x1, Pallas kernels, outer(): pl.pallas_call(rim_body, out_shape=(jax.ShapeDtypeStruct(shifts(2), BF),...  2.13 us
    ppermute x1, waiting for transfers between devices, reduced(): part = mine + lax.ppermute(other, 'dp', swap)  1.35 us
    pallas_call x1, Pallas kernels, last(): pl.pallas_call(last_body, out_shape=(jax.ShapeDtypeStruct((pairs, cols, L...  1.07 us
  transfers between devices with their start and end apart: 13, of which 8 were waited for; matrix products, arithmetic and copies ran while one was open for 5% of the time, Pallas kernels for 11%

profile of v7, /device:TPU:0, one launch (start us, length us, event | category | flops | bytes accessed | tf_op | source)
XLA Modules:
  0.0 41.1 jit_solution(8701091661406085683)
XLA Ops:
  0.6 1.2 %copy.10 = bf16[1,64,16,256]{3,1,2,0:T(8,128)(2,1)S(1)} copy(bf16[1,64,16,256]{3,2,1,0:T(8,128)(2,1)} %param.4) | data formatting | bytes 1048576 | tf_op args[0]
  1.8 0.0 copy-start.2
  1.9 0.3 copy.22.f
  2.1 0.8 %copy-done.2 = bf16[1,64,16,256]{3,2,1,0:T(8,128)(2,1)S(1)} copy-done((bf16[1,64,16,256]{3,2,1,0:T(8,128)(2,1)S(1)}, bf16[1,64,16,256]{3,2,1,0:T(8,128)(2,1)}, u32[]{:S(2)}) %copy-start.2) | copy-done | bytes 524312
  2.9 0.2 copy.11
  3.1 0.3 copy.23.g
  3.4 3.0 %collective-permute-start = (bf16[16,8,128]{2,1,0:T(8,128)(2,1)S(1)}, bf16[16,8,128]{2,1,0:T(8,128)(2,1)S(1)}, u32[]{:S(2)}, u32[]{:S(2)}) collective-permute-start(bf16[16,8,128]{2,1,0:T(8,128)(2,1)S(1)} %fusion), channel_id=1, source_target_pairs={{0,1},{1,0},{2,3},{3,2},{4,5},{5,4},{6,7},{7,6},{8,9},{9,8},{10,11... | collective-permute-start | bytes 98312 | tf_op jit(solution)/shard_map/ppermute | solution.py:35
  6.4 0.1 slice_bitcast_fusion.2
  6.4 0.1 slice_bitcast_fusion.3
  6.6 0.1 maximum_bitcast_fusion
  6.7 0.0 copy-start
  6.7 0.0 copy-start.1
  6.7 0.1 copy.16
  6.8 0.1 copy.19
  7.0 0.6 %copy-done = bf16[3,3,64,64]{3,2,1,0:T(8,128)(2,1)S(1)} copy-done((bf16[3,3,64,64]{3,2,1,0:T(8,128)(2,1)S(1)}, bf16[3,3,64,64]{3,2,1,0:T(8,128)(2,1)}, u32[]{:S(2)}) %copy-start) | copy-done | bytes 73752
  7.6 0.1 copy-done.1
  7.7 0.3 weights.1
  8.0 0.3 collective-permute-done
  8.3 0.1 fusion.10
  8.4 0.1 maximum_bitcast_fusion.2
  8.4 0.1 broadcast_select_fusion.3
  8.5 2.1 %collective-permute-start.1 = (bf16[2,272,128]{2,1,0:T(8,128)(2,1)S(1)}, bf16[2,272,128]{2,1,0:T(8,128)(2,1)S(1)}, u32[]{:S(2)}, u32[]{:S(2)}) collective-permute-start(bf16[2,272,128]{2,1,0:T(8,128)(2,1)S(1)} %get-tuple-element.53), channel_id=1, source_target_pairs={{0,2},{2,0},{4,6},{6,4},{8,10},{10,8},{12,14},{14,12},{1,3},{3,1},... | collective-permute-start | bytes 417800 | tf_op jit(solution)/shard_map/ppermute | solution.py:35
  10.6 0.7 %collective-permute-start.2 = (bf16[2,272,128]{2,1,0:T(8,128)(2,1)S(1)}, bf16[2,272,128]{2,1,0:T(8,128)(2,1)S(1)}, u32[]{:S(2)}, u32[]{:S(2)}) collective-permute-start(bf16[2,272,128]{2,1,0:T(8,128)(2,1)S(1)} %get-tuple-element.52), channel_id=1, source_target_pairs={{2,4},{4,2},{6,8},{8,6},{10,12},{12,10},{3,5},{5,3},{7,9},{9,7},{1... | collective-permute-start | bytes 417800 | tf_op jit(solution)/shard_map/ppermute | solution.py:35
  11.3 3.2 %inner.1 = (bf16[2,3,272,128]{3,2,1,0:T(8,128)(2,1)S(1)}, bf16[2,3,272,128]{3,2,1,0:T(8,128)(2,1)S(1)}, f32[2,272,128]{2,1,0:T(8,128)S(1)}, bf16[5,3,272,128]{3,...) custom-call(bf16[8,256,128]{2,1,0:T(8,128)(2,1)S(1)} %copy.22.f, ...), custom_call_target="tpu_custom_call" | custom-call | flops 1176502272 | bytes 4194304 | tf_op jit(solution)/shard_map/inner/pallas_call | solution.py:292
  14.5 0.2 collective-permute-done.1
  14.7 0.0 collective-permute-done.2
  14.7 2.1 %outer.1 = (bf16[2,3,272,128]{3,2,1,0:T(8,128)(2,1)S(1)}, bf16[2,3,272,128]{3,2,1,0:T(8,128)(2,1)S(1)}, bf16[144,128]{1,0:T(8,128)(2,1)S(1)}, bf16[144,128]{1,0:T(8,128)(2,1)S(1)}, f32[576,128]{1,0:T(8,128)S(1)}) custom-call(bf16[8,256,128]{2,1,0:T(8,128)(2,1)S(1)} %copy.22.f, bf16[8,256,128]{2,1,0:T(8,128)(2,1)S(1)} %copy.23.g, ...), custom_call_target="tpu_custom_call" | custom-call | flops 748683264 | bytes 4194304 | tf_op jit(solution)/shard_map/outer/pallas_call | solution.py:323
  16.9 0.1 collective-permute-start.5
  17.0 1.4 %collective-permute-done.5 = f32[288,128]{1,0:T(8,128)S(1)} collective-permute-done((f32[288,128]{1,0:T(8,128)S(1)}, f32[288,128]{1,0:T(8,128)S(1)}, u32[]{:S(2)}, u32[]{:S(2)}) %collective-permute-start.5) | collective-permute-done | bytes 147488 | tf_op jit(solution)/shard_map/ppermute | solution.py:412
  18.4 4.2 %collective-permute-start.6 = (bf16[288,128]{1,0:T(8,128)(2,1)S(1)}, bf16[288,128]{1,0:T(8,128)(2,1)S(1)}, u32[]{:S(2)}, u32[]{:S(2)}) collective-permute-start(bf16[288,128]{1,0:T(8,128)(2,1)S(1)} %add_convert_fusion.1), channel_id=1, source_target_pairs={{0,2},{1,3},{2,0},{3,1},{4,6},{5,7},{6,4},{7,5},{8,10},{9,11},{10,... | collective-permute-start | bytes 221192 | tf_op jit(solution)/shard_map/ppermute | solution.py:437
  22.6 1.6 %collective-permute-start.7 = (bf16[288,128]{1,0:T(8,128)(2,1)S(1)}, bf16[288,128]{1,0:T(8,128)(2,1)S(1)}, u32[]{:S(2)}, u32[]{:S(2)}) collective-permute-start(bf16[288,128]{1,0:T(8,128)(2,1)S(1)} %add_convert_fusion.1), channel_id=1, source_target_pairs={{0,1},{1,0},{2,3},{3,2},{4,5},{5,4},{6,7},{7,6},{8,9},{9,8},{10,11... | collective-permute-start | bytes 221192 | tf_op jit(solution)/shard_map/ppermute | solution.py:437
  24.2 0.0 collective-permute-start.8
  24.2 1.9 %collective-permute-start.3 = (bf16[144,128]{1,0:T(8,128)(2,1)S(1)}, bf16[144,128]{1,0:T(8,128)(2,1)S(1)}, u32[]{:S(2)}, u32[]{:S(2)}) collective-permute-start(bf16[144,128]{1,0:T(8,128)(2,1)S(1)} %get-tuple-element.57), channel_id=1, source_target_pairs={{0,2},{2,0},{4,6},{6,4},{8,10},{10,8},{12,14},{14,12},{1,3},{3,1},... | collective-permute-start | bytes 110600 | tf_op jit(solution)/shard_map/ppermute | solution.py:35
  26.1 0.7 %collective-permute-start.4 = (bf16[144,128]{1,0:T(8,128)(2,1)S(1)}, bf16[144,128]{1,0:T(8,128)(2,1)S(1)}, u32[]{:S(2)}, u32[]{:S(2)}) collective-permute-start(bf16[144,128]{1,0:T(8,128)(2,1)S(1)} %get-tuple-element.56), channel_id=1, source_target_pairs={{2,4},{4,2},{6,8},{8,6},{10,12},{12,10},{3,5},{5,3},{7,9},{9,7},{1... | collective-permute-start | bytes 110600 | tf_op jit(solution)/shard_map/ppermute | solution.py:35
  26.8 0.1 collective-permute-done.7
  26.9 2.6 %collective-permute-done.8 = bf16[288,128]{1,0:T(8,128)(2,1)S(1)} collective-permute-done((bf16[288,128]{1,0:T(8,128)(2,1)S(1)}, bf16[288,128]{1,0:T(8,128)(2,1)S(1)}, u32[]{:S(2)}, u32[]{:S(2)}) %collective-permute-start.8) | collective-permute-done | bytes 73760 | tf_op jit(solution)/shard_map/ppermute | solution.py:437
  29.6 2.7 %collective-permute-start.10 = (bf16[288,128]{1,0:T(8,128)(2,1)S(1)}, bf16[288,128]{1,0:T(8,128)(2,1)S(1)}, u32[]{:S(2)}, u32[]{:S(2)}) collective-permute-start(bf16[288,128]{1,0:T(8,128)(2,1)S(1)} %add_convert_fusion.own), channel_id=1, source_target_pairs={{0,8},{1,9},{2,10},{3,11},{4,12},{5,13},{6,14},{7,15},{8,0},{9,1},... | collective-permute-start | bytes 221192 | tf_op jit(solution)/shard_map/ppermute | solution.py:437
  32.3 1.2 %collective-permute-start.11 = (bf16[288,128]{1,0:T(8,128)(2,1)S(1)}, bf16[288,128]{1,0:T(8,128)(2,1)S(1)}, u32[]{:S(2)}, u32[]{:S(2)}) collective-permute-start(bf16[288,128]{1,0:T(8,128)(2,1)S(1)} %add_convert_fusion.own), channel_id=1, source_target_pairs={{0,12},{1,13},{2,14},{3,15},{4,8},{5,9},{6,10},{7,11},{8,4},{9,5},... | collective-permute-start | bytes 221192 | tf_op jit(solution)/shard_map/ppermute | solution.py:437
  33.5 0.4 collective-permute-start.9
  33.9 0.0 collective-permute-done.4
  33.9 1.1 %last.1 = (bf16[8,256,128]{2,1,0:T(8,128)(2,1)S(1)}, f32[8,128]{1,0:T(8,128)S(1)}) custom-call(bf16[2,3,272,128]{3,2,1,0:T(8,128)(2,1)S(1)} %get-tuple-element.30.ds1_top, bf16[5,3,272,128]{3,2,1,0:T(8,128)(2,1)S(1)} %get-tuple-element.31.ds1, bf16[2,3,272,128]{3,2,1,0:T(8,128)(2,1)S(1)} %get-tuple-element.32.ds1_bottom, ...), custom_call_target="tpu_custom_call" | custom-call | flops 427819008 | bytes 4194304 | tf_op jit(solution)/shard_map/last/pallas_call | solution.py:348
  35.0 3.6 %collective-permute-done.11.three = bf16[288,128]{1,0:T(8,128)(2,1)S(1)} collective-permute-done((bf16[288,128]{1,0:T(8,128)(2,1)S(1)}, bf16[288,128]{1,0:T(8,128)(2,1)S(1)}, u32[]{:S(2)}, u32[]{:S(2)}) %collective-permute-start.11) | collective-permute-done | bytes 73760 | tf_op jit(solution)/shard_map/ppermute | solution.py:437
  38.5 0.1 collective-permute-done.9.one
  38.7 0.1 collective-permute-start.12
  38.7 0.2 copy.24
  39.0 1.1 %copy.25 = bf16[1,64,16,256]{3,2,1,0:T(8,128)(2,1)} copy(bf16[1,64,16,256]{3,1,2,0:T(8,128)(2,1)S(1)} %bitcast.43) | data formatting | bytes 1048576
  40.0 0.1 collective-permute-done.12.other
  40.1 1.0 %finish.1 = (f32[3,3,64,64]{3,2,1,0:T(8,128)}, f32[3,3,64,64]{3,2,1,0:T(8,128)}) custom-call(f32[288,128]{1,0:T(8,128)S(1)} %sum_four.1.part, f32[288,128]{1,0:T(8,128)S(1)} %collective-permute-done.12.other), custom_call_target="tpu_custom_call" | custom-call | tf_op jit(solution)/shard_map/finish/pallas_call | solution.py:391
  (15 shorter events, 0.2 us)
Async XLA Ops:
  1.8 1.0 %copy-start.2 = (bf16[1,64,16,256]{3,2,1,0:T(8,128)(2,1)S(1)}, bf16[1,64,16,256]{3,2,1,0:T(8,128)(2,1)}, u32[]{:S(2)}) copy-start(bf16[1,64,16,256]{3,2,1,0:T(8,128)(2,1)} %param.5) | copy-start | bytes 1572868
  3.4 4.9 %collective-permute-start = (bf16[16,8,128]{2,1,0:T(8,128)(2,1)S(1)}, bf16[16,8,128]{2,1,0:T(8,128)(2,1)S(1)}, u32[]{:S(2)}, u32[]{:S(2)}) collective-permute-start(bf16[16,8,128]{2,1,0:T(8,128)(2,1)S(1)} %fusion), channel_id=1, source_target_pairs={{0,1},{1,0},{2,3},{3,2},{4,5},{5,4},{6,7},{7,6},{8,9},{9,8},{10,11... | collective-permute-start | bytes 98312 | tf_op jit(solution)/shard_map/ppermute | solution.py:35
  6.7 0.9 %copy-start = (bf16[3,3,64,64]{3,2,1,0:T(8,128)(2,1)S(1)}, bf16[3,3,64,64]{3,2,1,0:T(8,128)(2,1)}, u32[]{:S(2)}) copy-start(bf16[3,3,64,64]{3,2,1,0:T(8,128)(2,1)} %k1.1) | copy-start | bytes 221188
  6.7 1.0 %copy-start.1 = (bf16[3,3,64,64]{3,2,1,0:T(8,128)(2,1)S(1)}, bf16[3,3,64,64]{3,2,1,0:T(8,128)(2,1)}, u32[]{:S(2)}) copy-start(bf16[3,3,64,64]{3,2,1,0:T(8,128)(2,1)} %k2.1) | copy-start | bytes 221188
  8.5 6.2 %collective-permute-start.1 = (bf16[2,272,128]{2,1,0:T(8,128)(2,1)S(1)}, bf16[2,272,128]{2,1,0:T(8,128)(2,1)S(1)}, u32[]{:S(2)}, u32[]{:S(2)}) collective-permute-start(bf16[2,272,128]{2,1,0:T(8,128)(2,1)S(1)} %get-tuple-element.53), channel_id=1, source_target_pairs={{0,2},{2,0},{4,6},{6,4},{8,10},{10,8},{12,14},{14,12},{1,3},{3,1},... | collective-permute-start | bytes 417800 | tf_op jit(solution)/shard_map/ppermute | solution.py:35
  10.6 4.1 %collective-permute-start.2 = (bf16[2,272,128]{2,1,0:T(8,128)(2,1)S(1)}, bf16[2,272,128]{2,1,0:T(8,128)(2,1)S(1)}, u32[]{:S(2)}, u32[]{:S(2)}) collective-permute-start(bf16[2,272,128]{2,1,0:T(8,128)(2,1)S(1)} %get-tuple-element.52), channel_id=1, source_target_pairs={{2,4},{4,2},{6,8},{8,6},{10,12},{12,10},{3,5},{5,3},{7,9},{9,7},{1... | collective-permute-start | bytes 417800 | tf_op jit(solution)/shard_map/ppermute | solution.py:35
  16.9 1.4 %collective-permute-start.5 = (f32[288,128]{1,0:T(8,128)S(1)}, f32[288,128]{1,0:T(8,128)S(1)}, u32[]{:S(2)}, u32[]{:S(2)}) collective-permute-start(f32[288,128]{1,0:T(8,128)S(1)} %constant_dynamic-slice_fusion), channel_id=1, source_target_pairs={{0,16},{16,0},{1,17},{17,1},{2,18},{18,2},{3,19},{19,3},{4,20},{20... | collective-permute-start | bytes 442376 | tf_op jit(solution)/shard_map/ppermute | solution.py:412
  18.4 8.4 %collective-permute-start.6 = (bf16[288,128]{1,0:T(8,128)(2,1)S(1)}, bf16[288,128]{1,0:T(8,128)(2,1)S(1)}, u32[]{:S(2)}, u32[]{:S(2)}) collective-permute-start(bf16[288,128]{1,0:T(8,128)(2,1)S(1)} %add_convert_fusion.1), channel_id=1, source_target_pairs={{0,2},{1,3},{2,0},{3,1},{4,6},{5,7},{6,4},{7,5},{8,10},{9,11},{10,... | collective-permute-start | bytes 221192 | tf_op jit(solution)/shard_map/ppermute | solution.py:437
  22.6 4.4 %collective-permute-start.7 = (bf16[288,128]{1,0:T(8,128)(2,1)S(1)}, bf16[288,128]{1,0:T(8,128)(2,1)S(1)}, u32[]{:S(2)}, u32[]{:S(2)}) collective-permute-start(bf16[288,128]{1,0:T(8,128)(2,1)S(1)} %add_convert_fusion.1), channel_id=1, source_target_pairs={{0,1},{1,0},{2,3},{3,2},{4,5},{5,4},{6,7},{7,6},{8,9},{9,8},{10,11... | collective-permute-start | bytes 221192 | tf_op jit(solution)/shard_map/ppermute | solution.py:437
  24.2 5.4 %collective-permute-start.8 = (bf16[288,128]{1,0:T(8,128)(2,1)S(1)}, bf16[288,128]{1,0:T(8,128)(2,1)S(1)}, u32[]{:S(2)}, u32[]{:S(2)}) collective-permute-start(bf16[288,128]{1,0:T(8,128)(2,1)S(1)} %add_convert_fusion.1), channel_id=1, source_target_pairs={{0,3},{1,2},{2,1},{3,0},{4,7},{5,6},{6,5},{7,4},{8,11},{9,10},{10,... | collective-permute-start | bytes 221192 | tf_op jit(solution)/shard_map/ppermute | solution.py:437
  24.2 9.7 %collective-permute-start.3 = (bf16[144,128]{1,0:T(8,128)(2,1)S(1)}, bf16[144,128]{1,0:T(8,128)(2,1)S(1)}, u32[]{:S(2)}, u32[]{:S(2)}) collective-permute-start(bf16[144,128]{1,0:T(8,128)(2,1)S(1)} %get-tuple-element.57), channel_id=1, source_target_pairs={{0,2},{2,0},{4,6},{6,4},{8,10},{10,8},{12,14},{14,12},{1,3},{3,1},... | collective-permute-start | bytes 110600 | tf_op jit(solution)/shard_map/ppermute | solution.py:35
  26.1 7.8 %collective-permute-start.4 = (bf16[144,128]{1,0:T(8,128)(2,1)S(1)}, bf16[144,128]{1,0:T(8,128)(2,1)S(1)}, u32[]{:S(2)}, u32[]{:S(2)}) collective-permute-start(bf16[144,128]{1,0:T(8,128)(2,1)S(1)} %get-tuple-element.56), channel_id=1, source_target_pairs={{2,4},{4,2},{6,8},{8,6},{10,12},{12,10},{3,5},{5,3},{7,9},{9,7},{1... | collective-permute-start | bytes 110600 | tf_op jit(solution)/shard_map/ppermute | solution.py:35
  29.6 5.4 %collective-permute-start.10 = (bf16[288,128]{1,0:T(8,128)(2,1)S(1)}, bf16[288,128]{1,0:T(8,128)(2,1)S(1)}, u32[]{:S(2)}, u32[]{:S(2)}) collective-permute-start(bf16[288,128]{1,0:T(8,128)(2,1)S(1)} %add_convert_fusion.own), channel_id=1, source_target_pairs={{0,8},{1,9},{2,10},{3,11},{4,12},{5,13},{6,14},{7,15},{8,0},{9,1},... | collective-permute-start | bytes 221192 | tf_op jit(solution)/shard_map/ppermute | solution.py:437
  32.3 6.3 %collective-permute-start.11 = (bf16[288,128]{1,0:T(8,128)(2,1)S(1)}, bf16[288,128]{1,0:T(8,128)(2,1)S(1)}, u32[]{:S(2)}, u32[]{:S(2)}) collective-permute-start(bf16[288,128]{1,0:T(8,128)(2,1)S(1)} %add_convert_fusion.own), channel_id=1, source_target_pairs={{0,12},{1,13},{2,14},{3,15},{4,8},{5,9},{6,10},{7,11},{8,4},{9,5},... | collective-permute-start | bytes 221192 | tf_op jit(solution)/shard_map/ppermute | solution.py:437
  33.5 5.1 %collective-permute-start.9 = (bf16[288,128]{1,0:T(8,128)(2,1)S(1)}, bf16[288,128]{1,0:T(8,128)(2,1)S(1)}, u32[]{:S(2)}, u32[]{:S(2)}) collective-permute-start(bf16[288,128]{1,0:T(8,128)(2,1)S(1)} %add_convert_fusion.own), channel_id=1, source_target_pairs={{0,4},{1,5},{2,6},{3,7},{4,0},{5,1},{6,2},{7,3},{8,12},{9,13},{10,... | collective-permute-start | bytes 221192 | tf_op jit(solution)/shard_map/ppermute | solution.py:437
  38.7 1.4 %collective-permute-start.12 = (f32[288,128]{1,0:T(8,128)S(1)}, f32[288,128]{1,0:T(8,128)S(1)}, u32[]{:S(2)}, u32[]{:S(2)}) collective-permute-start(f32[288,128]{1,0:T(8,128)S(1)} %sum_four.1.part), channel_id=1, source_target_pairs={{0,16},{16,0},{1,17},{17,1},{2,18},{18,2},{3,19},{19,3},{4,20},{20... | collective-permute-start | bytes 442376 | tf_op jit(solution)/shard_map/ppermute | solution.py:445

commit v8 on v7

--- a/solution.py
+++ b/solution.py
@@ -27,7 +27,7 @@
     return lax.axis_index(axis) % 2 == parity
 
 
-def swap_one(low, high, axis):
+def swap(low, high, axis):
     got = []
     for parity in range(2):
         perm = neighbours(axis, parity)
@@ -39,6 +39,10 @@
     return jnp.where(odd, got[0], got[1]), jnp.where(odd, got[1], got[0])
 
 
+def odd_place(axis):
+    return lax.rem(lax.axis_index(axis), 2) == 1
+
+
 def to_pairs(cells):
     _, chans, rows, cols = cells.shape
     part = cells[0].reshape(chans, rows // 2, 2, cols)
@@ -51,7 +55,7 @@
     return part.transpose(3, 0, 2, 1).reshape(1, lanes // 2, 2 * count, cols)
 
 
-def weights_body(k1, k2, w1, w2, v2, v1):
+def make_weights(k1, k2, w1, w2, v2, v1):
     zero = jnp.zeros((HALF, HALF), BF)
     for taps, forward, backward in ((k1, w1, v1), (k2, w2, v2)):
         flat = {(ky, kx): taps[ky, kx] for ky in range(3) for kx in range(3)}
@@ -65,15 +69,56 @@
                     backward[at : at + HALF] = jnp.concatenate([flat.get((2 - ky, 2 - kx), zero) for ky in kys], axis=1)
 
 
-def make_weights(kernel_one, kernel_two):
-    shape = jax.ShapeDtypeStruct((12 * HALF, LANES), BF)
-    return pl.pallas_call(
-        weights_body,
-        out_shape=(shape,) * 4,
+def outer_units(feats, grads, high):
+    pairs = feats.shape[0]
+    near = jnp.where(high, pairs - 1, 0)
+    then = feats[jnp.where(high, pairs - 2, 1)].astype(F32)
+    grad = pltpu.roll(grads[near].astype(F32), HALF, 1)
+    lane = lax.broadcasted_iota(jnp.int32, then.shape, 1)
+    own = (lane >= HALF).astype(jnp.int32) == jnp.where(high, 1, 0)
+    return feats[near], jnp.where(own, then, grad).astype(BF), jnp.where(own, grad, then).astype(BF)
+
+
+def prep_body(f, g, k1, k2, weights, sent_near, sent_far):
+    make_weights(k1, k2, *(weights.at[at] for at in range(4)))
+    odd = odd_place("row")
+    for sent, high in ((sent_near, jnp.logical_not(odd)), (sent_far, odd)):
+        units = outer_units(f, g, high)
+        for at in range(sent.shape[0]):
+            sent[at] = units[at]
+
+
+def prep(feat, grad, kernel_one, kernel_two):
+    shape = jax.ShapeDtypeStruct((4, 12 * HALF, LANES), BF)
+    sent = [jax.ShapeDtypeStruct((units, *feat.shape[1:]), BF) for units in (3, 2)]
+    return pl.pallas_call(
+        prep_body,
+        out_shape=(shape, *sent),
+        compiler_params=pltpu.CompilerParams(vmem_limit_bytes=12 * 2**20),
+        cost_estimate=cost(2),
+        name="prep",
+    )(feat, grad, kernel_one, kernel_two)
+
+
+def frame_body(own_near, own_far, edge, sent_near, sent_far):
+    pairs, cols = edge.shape[0] // 2, own_near.shape[1]
+    odd = odd_place("row")
+    feats, grads = edge.at[:pairs], edge.at[pairs:]
+    for own, sent, high in ((own_near, sent_near, jnp.logical_not(odd)), (own_far, sent_far, odd)):
+        units = outer_units(feats, grads, high)
+        for at in range(sent.shape[0]):
+            sent[at, :cols] = own[at]
+            sent[at, cols:] = units[at]
+
+
+def frame(own_near, own_far, edge):
+    wide = own_near.shape[1] + RIM
+    return pl.pallas_call(
+        frame_body,
+        out_shape=[jax.ShapeDtypeStruct((own.shape[0], wide, LANES), BF) for own in (own_near, own_far)],
         compiler_params=pltpu.CompilerParams(vmem_limit_bytes=8 * 2**20),
-        cost_estimate=cost(2),
-        name="weights",
-    )(kernel_one, kernel_two)
+        name="frame",
+    )(own_near, own_far, edge)
 
 
 def sigmoid(value):
@@ -116,7 +161,8 @@
     acc[...] += jnp.dot(feat_t, near, preferred_element_type=F32)
 
 
-def inner_body(f, g, edge, w1, w2, v2, hs_edge, ds2_edge, slope_edge, ds1, acc1, acc2, fs, hs, ds2, slope, ht, ft):
+def inner_body(f, g, edge, weights, hs_edge, ds2_edge, slope_edge, ds1, acc1, acc2, fs, hs, ds2, slope, ht, ft):
+    w1, w2, v2 = (weights.at[at] for at in range(3))
     pairs, cols = f.shape[:2]
     _, _, rim = edge_masks()
 
@@ -170,7 +216,8 @@
         ds2_edge[side] = ds2[at]
 
 
-def take_terms(acc1, acc2, term):
+def take_terms(acc1, acc2, mine, other):
+    blocks = []
     for ky in range(3):
         for kx in range(3):
             at = (2 - kx) * LANES
@@ -178,8 +225,13 @@
             for acc in (acc1, acc2):
                 first = acc[ky * HALF : (ky + 1) * HALF, at : at + HALF]
                 sums.append(first + acc[(ky + 1) * HALF : (ky + 2) * HALF, at + HALF : at + LANES])
-            at = (ky * 3 + kx) * HALF
-            term[at : at + HALF] = jnp.concatenate(sums, axis=1)
+            blocks.append(jnp.concatenate(sums, axis=1))
+    half = HALF // 2
+    second = lax.axis_index("dp") == 1
+    for tap in range(9):
+        one, two = blocks[tap][:half], blocks[tap][half:]
+        mine[tap * half : (tap + 1) * half] = jnp.where(second, two, one)
+        other[tap * half : (tap + 1) * half] = jnp.where(second, one, two)
 
 
 def half_lanes(side):
@@ -188,24 +240,27 @@
 
 
 def rim_body(
-    f, g, edge, above, below, w1, w2, v2, hs_edge, ds2_edge, slope_edge, acc1_in, acc2_in,
-    ds1_top, ds1_bottom, row_top, row_bottom, term, fs, hs, ds2, slope, acc1, acc2,
+    f, g, edge, above, below, weights, hs_edge, ds2_edge, slope_edge, acc1_in, acc2_in,
+    ds1_next, end, row, mine, other, fs, hs, ds2, slope, ds1, acc1, acc2,
 ):
     pairs, cols = f.shape[:2]
     top, bottom, rim = edge_masks()
     flags = (top, bottom)
     beyond = [half_lanes(side) for side in range(2)]
-    halo, ds1, rows = (above, below), (ds1_top, ds1_bottom), (row_top, row_bottom)
+    w1, w2, v2 = (weights.at[at] for at in range(3))
+    rows = []
+    odd = odd_place("row")
+    known = jnp.where(odd, top, 0.0), jnp.where(odd, 0.0, bottom)
+    halo, mixed, more = ([ref[at].astype(F32) for ref in (above, below)] for at in range(3))
     near, next_near = (0, pairs - 1), (1, pairs - 2)
-    mixed = [ref[1].astype(F32) for ref in halo]
     sides = range(2)
 
     def order(side, one, two):
         return (one, two) if side == 0 else (two, one)
 
     for side in sides:
-        store_shifts(jnp.where(beyond[side], 0.0, mixed[side]), fs.at[side], 0)
-        store_shifts(halo[side][0].astype(F32), fs.at[side], 1)
+        store_shifts(jnp.where(beyond[side], more[side], mixed[side]), fs.at[side], 0)
+        store_shifts(halo[side], fs.at[side], 1)
         store_shifts(with_rim(f[near[side]], edge[near[side]]), fs.at[side], 2)
     for k in (1, 0):
         for side in sides:
@@ -219,7 +274,7 @@
     for k in (1, 0):
         for side in sides:
             if k == 0:
-                grad = jnp.where(beyond[side], 0.0, pltpu.roll(mixed[side], HALF, 1))
+                grad = pltpu.roll(jnp.where(beyond[side], mixed[side], more[side]), HALF, 1)
             else:
                 grad = with_rim(g[near[side]], edge[pairs + near[side]])
             inward = (hs.at[side], 1) if k == 0 else (hs_edge, side)
@@ -232,18 +287,23 @@
             inward = (ds2.at[side], 1) if k == 0 else (ds2_edge, side)
             back = band_dot(*order(side, (ds2.at[side], k), inward), v2)
             value = back * slope[side] if k == 0 else back * slope_edge[side]
+            value = rim_masked(value, rim)
             if k == 0:
+                end[side] = jnp.where(beyond[side], value * known[side], value).astype(BF)
                 value = jnp.where(beyond[side], 0.0, value)
-            value = rim_masked(value, rim)
-            store_shifts(value, ds1[side], k)
+            store_shifts(value, ds1.at[side], k)
+            if k == 1:
+                for s in range(3):
+                    ds1_next[side, s] = ds1[side, 1, s]
             if k == 0:
-                tall = rows[side].shape[0]
+                tall = row.shape[0]
                 first, second = value[:tall], value[value.shape[0] - tall :]
                 if side == 0:
                     first = pltpu.roll(first, HALF, 1)
                 else:
                     second = pltpu.roll(second, HALF, 1)
-                rows[side][...] = (first + second).astype(BF)
+                rows.append(first + second)
+    row[...] = jnp.where(odd, rows[1], rows[0]).astype(BF)
 
     acc1[...] = acc1_in[...]
     acc2[...] = acc2_in[...]
@@ -252,9 +312,9 @@
         add_one(acc2, jnp.concatenate(hid, axis=0), [ds2[side, 1, s, :cols] for s in range(3)])
         own = f[near[side]].T
         for k in (1, 0):
-            feat = order(side, halo[side][0, :cols].T, own) if k == 0 else order(side, own, f[next_near[side]].T)
-            add_one(acc1, jnp.concatenate(feat, axis=0), [ds1[side][k, s, :cols] for s in range(3)])
-    take_terms(acc1, acc2, term)
+            feat = order(side, fs[side, 1, 1, :cols].T, own) if k == 0 else order(side, own, f[next_near[side]].T)
+            add_one(acc1, jnp.concatenate(feat, axis=0), [ds1[side, k, s, :cols] for s in range(3)])
+    take_terms(acc1, acc2, mine, other)
 
 
 def with_row(center, row, side):
@@ -262,17 +322,20 @@
     first, second = (row, turned) if side == 0 else (turned, row)
     cols = center.shape[0] - row.shape[0]
     full = jnp.concatenate([first[:cols], second], axis=0)
-    return jnp.where(half_lanes(side), full, center)
-
-
-def last_body(ds1_top, ds1, ds1_bottom, prev_row, next_row, v1, gf, done, ends):
+    return center + jnp.where(half_lanes(side), full, 0.0)
+
+
+def last_body(end, ds1_next, ds1, row, weights, gf, done, ends):
     pairs, cols = gf.shape[:2]
     done[...] = jnp.zeros_like(done)
-    store_shifts(with_row(ds1_top[0, 1].astype(F32), prev_row[...].astype(F32), 0), ends, 0)
-    store_shifts(with_row(ds1_bottom[0, 1].astype(F32), next_row[...].astype(F32), 1), ends, 1)
-    places = [(ends, 0), (ds1_top, 1)] + [(ds1, j) for j in range(pairs - 3)] + [(ds1_bottom, 1), (ends, 1)]
+    odd = odd_place("row")
+    from_prev = jnp.where(odd, 0.0, row[...].astype(F32))
+    from_next = jnp.where(odd, row[...].astype(F32), 0.0)
+    store_shifts(with_row(end[0].astype(F32), from_prev, 0), ends, 0)
+    store_shifts(with_row(end[1].astype(F32), from_next, 1), ends, 1)
+    places = [(ends, 0), (ds1_next, 0)] + [(ds1, j) for j in range(pairs - 3)] + [(ds1_next, 1), (ends, 1)]
     for j in range(pairs):
-        gf[j] = band_dot(places[j], places[j + 1], v1)[:cols].astype(BF)
+        gf[j] = band_dot(places[j], places[j + 1], weights.at[3])[:cols].astype(BF)
 
 
 def cost(pair_count):
@@ -282,7 +345,7 @@
 PARAMS = pltpu.CompilerParams(vmem_limit_bytes=32 * 2**20)
 
 
-def inner(f, g, edge, w1, w2, v2):
+def inner(f, g, edge, weights):
     pairs, cols = f.shape[:2]
     wide = cols + RIM
 
@@ -310,7 +373,7 @@
         compiler_params=PARAMS,
         cost_estimate=cost(22),
         name="inner",
-    )(f, g, edge, w1, w2, v2)
+    )(f, g, edge, weights)
 
 
 def outer(f, *rest):
@@ -324,16 +387,17 @@
         rim_body,
         out_shape=(
             jax.ShapeDtypeStruct(shifts(2), BF),
-            jax.ShapeDtypeStruct(shifts(2), BF),
+            jax.ShapeDtypeStruct((2, wide, LANES), BF),
             row,
-            row,
-            jax.ShapeDtypeStruct((9 * HALF, LANES), F32),
+            jax.ShapeDtypeStruct((9 * HALF // 2, LANES), F32),
+            jax.ShapeDtypeStruct((9 * HALF // 2, LANES), F32),
         ),
         scratch_shapes=[
             pltpu.VMEM(shifts(2, 3), BF),
             pltpu.VMEM(shifts(2, 2), BF),
             pltpu.VMEM(shifts(2, 2), BF),
             pltpu.VMEM((2, wide, LANES), F32),
+            pltpu.VMEM(shifts(2, 2), BF),
             pltpu.VMEM((2 * LANES, 3 * LANES), F32),
             pltpu.VMEM((2 * LANES, 3 * LANES), F32),
         ],
@@ -343,7 +407,7 @@
     )(f, *rest)
 
 
-def last(ds1_top, ds1, ds1_bottom, prev_row, next_row, v1, cols):
+def last(end, ds1_next, ds1, row, weights, cols):
     pairs = ds1.shape[0] + 3
     return pl.pallas_call(
         last_body,
@@ -355,7 +419,7 @@
         compiler_params=PARAMS,
         cost_estimate=cost(8),
         name="last",
-    )(ds1_top, ds1, ds1_bottom, prev_row, next_row, v1)
+    )(end, ds1_next, ds1, row, weights)
 
 
 def four_body(own, one, two, three, done, out):
@@ -373,14 +437,11 @@
 
 
 def finish_body(part, other, one, two, *, scale):
-    half = part.shape[0]
-    first = lax.axis_index("dp") == 0
+    half = HALF // 2
+    second = lax.axis_index("dp") == 1
     for tap in range(9):
-        rows = []
-        for at in range(tap * HALF, (tap + 1) * HALF, HALF // 2):
-            side, at = (0, at) if at < half else (1, at - half)
-            mine, theirs = part[at : at + HALF // 2], other[at : at + HALF // 2]
-            rows.append(jnp.where(first, mine, theirs) if side == 0 else jnp.where(first, theirs, mine))
+        mine, theirs = (ref[tap * half : (tap + 1) * half] for ref in (part, other))
+        rows = [jnp.where(second, theirs, mine), jnp.where(second, mine, theirs)]
         both = jnp.concatenate(rows, axis=0).T * scale
         one[tap // 3, tap % 3] = both[:HALF]
         two[tap // 3, tap % 3] = both[HALF:]
@@ -396,20 +457,14 @@
     )(part, other)
 
 
-def reduced(term, done):
+def reduced(mine, other, done):
     sizes = [lax.axis_size(axis) for axis in AXES]
+    swap_cores = [(0, 1), (1, 0)]
     if sizes[0] != 2 or any(size & (size - 1) for size in sizes):
-        total = lax.psum(term, AXES)
-        half = term.shape[0] // 2
-        both = total[:half], total[half:]
-        core = lax.axis_index("dp") == 0
-        return jnp.where(core, *both), jnp.where(core, both[1], both[0])
-    half = term.shape[0] // 2
-    me = lax.axis_index("dp")
-    swap = [(0, 1), (1, 0)]
-    mine = lax.dynamic_slice_in_dim(term, me * half, half, 0)
-    other = lax.dynamic_slice_in_dim(term, (1 - me) * half, half, 0)
-    part = mine + lax.ppermute(other, "dp", swap)
+        first = lax.axis_index("dp") == 0
+        both = lax.psum([jnp.where(first, mine, other), jnp.where(first, other, mine)], AXES)
+        return jnp.where(first, *both), jnp.where(first, both[1], both[0])
+    part = mine + lax.ppermute(other, "dp", swap_cores)
     across = [(0, 1 << b) for b in range(sizes[2].bit_length() - 1)]
     down = [(1 << b, 0) for b in range(sizes[1].bit_length() - 1)]
     bits = []
@@ -442,7 +497,7 @@
         part = low.astype(F32) + got[0]
         if len(got) > 1:
             part = part + (got[1] + got[2])
-    return part, lax.ppermute(part, "dp", swap)
+    return part, lax.ppermute(part, "dp", swap_cores)
 
 
 def shards(features, grad_out, kernel_one, kernel_two):
@@ -450,23 +505,23 @@
     pairs = rows // 2
     feat, grad = to_pairs(features), to_pairs(grad_out)
     own = jnp.concatenate([feat, grad], axis=0)
-    from_left, from_right = swap_one(own[:, : RIM // 2], own[:, cols - RIM // 2 :], "col")
+    from_left, from_right = swap(own[:, : RIM // 2], own[:, cols - RIM // 2 :], "col")
     edge = jnp.concatenate([from_right, from_left], axis=1)
-    w1, w2, v2, v1 = make_weights(kernel_one, kernel_two)
-    low = jnp.stack([feat[0], jnp.concatenate([feat[1, :, :HALF], grad[0, :, :HALF]], axis=1)])
-    high = jnp.stack([feat[-1], jnp.concatenate([grad[-1, :, HALF:], feat[-2, :, HALF:]], axis=1)])
-    feat_edge, grad_edge = edge[:pairs], edge[pairs:]
-    low_edge = jnp.stack([feat_edge[0], jnp.concatenate([feat_edge[1, :, :HALF], grad_edge[0, :, :HALF]], axis=1)])
-    high_edge = jnp.stack([feat_edge[-1], jnp.concatenate([grad_edge[-1, :, HALF:], feat_edge[-2, :, HALF:]], axis=1)])
-    low, high = jnp.concatenate([low, low_edge], axis=1), jnp.concatenate([high, high_edge], axis=1)
-    above, below = swap_one(low, high, "row")
-    hs_edge, ds2_edge, slope_edge, ds1, acc1, acc2 = inner(feat, grad, edge, w1, w2, v2)
-    ds1_top, ds1_bottom, low_row, high_row, term = outer(
-        feat, grad, edge, above, below, w1, w2, v2, hs_edge, ds2_edge, slope_edge, acc1, acc2
+    weights, own_near, own_far = prep(feat, grad, kernel_one, kernel_two)
+    sent_near, sent_far = frame(own_near, own_far, edge)
+    got_near = lax.ppermute(sent_near, "row", neighbours("row", 0))
+    got_far = lax.ppermute(sent_far, "row", neighbours("row", 1))
+    odd = is_low("row", 1)
+    one, more = got_near[:2], got_near[2:]
+    above = jnp.concatenate([jnp.where(odd, one, got_far), jnp.where(odd, more, jnp.zeros_like(more))])
+    below = jnp.concatenate([jnp.where(odd, got_far, one), jnp.where(odd, jnp.zeros_like(more), more)])
+    hs_edge, ds2_edge, slope_edge, ds1, acc1, acc2 = inner(feat, grad, edge, weights)
+    ds1_next, end, row, mine, other = outer(
+        feat, grad, edge, above, below, weights, hs_edge, ds2_edge, slope_edge, acc1, acc2
     )
-    prev_row, next_row = swap_one(low_row, high_row, "row")
-    gf, done = last(ds1_top, ds1, ds1_bottom, prev_row, next_row, v1, cols)
-    part, other = reduced(term, done)
+    row = lax.ppermute(row, "row", neighbours("row", 1))
+    gf, done = last(end, ds1_next, ds1, row, weights, cols)
+    part, other = reduced(mine, other, done)
     count = slides * lax.axis_size("dp") * rows * lax.axis_size("row") * cols * lax.axis_size("col")
     grad_one, grad_two = finish(part, other, float(count) ** -0.5)
     return from_pairs(gf), grad_one, grad_two

time: 41.4 us -> 40.4 us (0.976)
  waiting for transfers between devices: 8.24 us -> 12.1 us
  starting transfers between devices: 18.6 us -> 15.1 us
  local copies, waits for them, and re-layouts: 5.1 us -> 3.97 us
    ppermute x7 -> x6, waiting for transfers between devices: 1.86 us -> 5.35 us  [the longest x1 2.4 us: shards(): got_near = lax.ppermute(sent_near, 'row', neighbours('row', 0))]
    ppermute x7 -> x6, starting transfers between devices: 8.51 us -> 6.51 us  [the longest x1 3 us: swap(): lax.ppermute(jnp.where(is_low(axis, parity), high, low), axis, perm)]
    ppermute x6, starting transfers between devices: 10.1 us -> 8.57 us  [reduced(): got.append(lax.ppermute(low, AXES, perm))]
    unnamed x9, local copies, waits for them, and re-layouts: 3.92 us -> 3.22 us
  transfers between devices with their start and end apart: 13 -> 12, of which waited for: 8 -> 9; matrix products, arithmetic and copies ran while one was open for 5% -> 3% of each run, Pallas kernels for 11% -> 12%
where the time goes in v8:
time: 40.4 us; the launch traced here: 40.2 us
  starting transfers between devices  15.1 us (37%)
  waiting for transfers between devices  12.1 us (30%)
  Pallas kernels  8.02 us (20%)
  local copies, waits for them, and re-layouts  3.97 us (10%)
  between operations  0.81 us (2%)
    ppermute x6, starting transfers between devices, reduced(): got.append(lax.ppermute(low, AXES, perm))  8.57 us
    ppermute x6, waiting for transfers between devices, reduced(): got.append(lax.ppermute(low, AXES, perm))  6.75 us
    pallas_call x1, Pallas kernels, inner(): pl.pallas_call(inner_body, out_shape=(jax.ShapeDtypeStruct(shifts(2), BF)...  3.24 us
    unnamed x9, local copies, waits for them, and re-layouts  3.22 us
    ppermute x1, starting transfers between devices, swap(): lax.ppermute(jnp.where(is_low(axis, parity), high, low), axis, perm)  3 us
    ppermute x1, waiting for transfers between devices, shards(): got_near = lax.ppermute(sent_near, 'row', neighbours('row', 0))  2.4 us
    pallas_call x1, Pallas kernels, outer(): pl.pallas_call(rim_body, out_shape=(jax.ShapeDtypeStruct(shifts(2), BF),...  2.18 us
    ppermute x1, starting transfers between devices, shards(): got_near = lax.ppermute(sent_near, 'row', neighbours('row', 0))  2.06 us
  transfers between devices with their start and end apart: 12, of which 9 were waited for; matrix products, arithmetic and copies ran while one was open for 3% of the time, Pallas kernels for 12%

profile of v8, /device:TPU:0, one launch (start us, length us, event | category | flops | bytes accessed | tf_op | source)
XLA Modules:
  0.0 40.2 jit_solution(1813445112490926081)
XLA Ops:
  0.6 1.2 %copy.10 = bf16[1,64,16,256]{3,1,2,0:T(8,128)(2,1)S(1)} copy(bf16[1,64,16,256]{3,2,1,0:T(8,128)(2,1)} %param.4) | data formatting | bytes 1048576 | tf_op args[0]
  1.8 0.0 copy-start.2
  1.9 0.3 copy.18.f
  2.1 0.8 %copy-done.2 = bf16[1,64,16,256]{3,2,1,0:T(8,128)(2,1)S(1)} copy-done((bf16[1,64,16,256]{3,2,1,0:T(8,128)(2,1)S(1)}, bf16[1,64,16,256]{3,2,1,0:T(8,128)(2,1)}, u32[]{:S(2)}) %copy-start.2) | copy-done | bytes 524312
  2.9 0.2 copy.11
  3.1 0.3 copy.19.g
  3.3 0.0 copy-start
  3.3 0.0 copy-start.1
  3.4 3.0 %collective-permute-start = (bf16[16,8,128]{2,1,0:T(8,128)(2,1)S(1)}, bf16[16,8,128]{2,1,0:T(8,128)(2,1)S(1)}, u32[]{:S(2)}, u32[]{:S(2)}) collective-permute-start(bf16[16,8,128]{2,1,0:T(8,128)(2,1)S(1)} %fusion), channel_id=1, source_target_pairs={{0,1},{1,0},{2,3},{3,2},{4,5},{5,4},{6,7},{7,6},{8,9},{9,8},{10,11... | collective-permute-start | bytes 98312 | tf_op jit(solution)/shard_map/ppermute | solution.py:35
  6.4 0.0 copy-done
  6.4 0.0 copy-done.1
  6.4 0.3 prep.1
  6.7 1.5 %collective-permute-done = bf16[16,8,128]{2,1,0:T(8,128)(2,1)S(1)} collective-permute-done((bf16[16,8,128]{2,1,0:T(8,128)(2,1)S(1)}, bf16[16,8,128]{2,1,0:T(8,128)(2,1)S(1)}, u32[]{:S(2)}, u32[]{:S(2)}) %collective-permute-start) | collective-permute-done | bytes 32800 | tf_op jit(solution)/shard_map/ppermute | solution.py:35
  8.3 0.1 frame.1
  8.4 2.1 %collective-permute-start.1 = (bf16[3,272,128]{2,1,0:T(8,128)(2,1)S(1)}, bf16[3,272,128]{2,1,0:T(8,128)(2,1)S(1)}, u32[]{:S(2)}, u32[]{:S(2)}) collective-permute-start(bf16[3,272,128]{2,1,0:T(8,128)(2,1)S(1)} %get-tuple-element.25), channel_id=1, source_target_pairs={{0,2},{2,0},{4,6},{6,4},{8,10},{10,8},{12,14},{14,12},{1,3},{3,1},... | collective-permute-start | bytes 626696 | tf_op jit(solution)/shard_map/ppermute | solution.py:512
  10.5 0.7 %collective-permute-start.2 = (bf16[2,272,128]{2,1,0:T(8,128)(2,1)S(1)}, bf16[2,272,128]{2,1,0:T(8,128)(2,1)S(1)}, u32[]{:S(2)}, u32[]{:S(2)}) collective-permute-start(bf16[2,272,128]{2,1,0:T(8,128)(2,1)S(1)} %get-tuple-element.26), channel_id=1, source_target_pairs={{2,4},{4,2},{6,8},{8,6},{10,12},{12,10},{3,5},{5,3},{7,9},{9,7},{1... | collective-permute-start | bytes 417800 | tf_op jit(solution)/shard_map/ppermute | solution.py:513
  11.1 3.2 %inner.1 = (bf16[2,3,272,128]{3,2,1,0:T(8,128)(2,1)S(1)}, bf16[2,3,272,128]{3,2,1,0:T(8,128)(2,1)S(1)}, f32[2,272,128]{2,1,0:T(8,128)S(1)}, bf16[5,3,272,128]{3,...) custom-call(bf16[8,256,128]{2,1,0:T(8,128)(2,1)S(1)} %copy.18.f, ...), custom_call_target="tpu_custom_call" | custom-call | flops 1176502272 | bytes 4194304 | tf_op jit(solution)/shard_map/inner/pallas_call | solution.py:355
  14.4 2.4 %collective-permute-done.1 = bf16[3,272,128]{2,1,0:T(8,128)(2,1)S(1)} collective-permute-done((bf16[3,272,128]{2,1,0:T(8,128)(2,1)S(1)}, bf16[3,272,128]{2,1,0:T(8,128)(2,1)S(1)}, u32[]{:S(2)}, u32[]{:S(2)}) %collective-permute-start.1) | collective-permute-done | bytes 208928 | tf_op jit(solution)/shard_map/ppermute | solution.py:512
  16.8 0.0 collective-permute-done.2
  16.9 2.2 %outer.1 = (bf16[2,3,272,128]{3,2,1,0:T(8,128)(2,1)S(1)}, bf16[2,272,128]{2,1,0:T(8,128)(2,1)S(1)}, bf16[144,128]{1,0:T(8,128)(2,1)S(1)}, f32[288,128]{1,0:T(8,128)S(1)}, f32[288,128]{1,0:T(8,128)S(1)}) custom-call(bf16[8,256,128]{2,1,0:T(8,128)(2,1)S(1)} %copy.18.f, bf16[8,256,128]{2,1,0:T(8,128)(2,1)S(1)} %copy.19.g, ...), custom_call_target="tpu_custom_call" | custom-call | flops 748683264 | bytes 4194304 | tf_op jit(solution)/shard_map/outer/pallas_call | solution.py:386
  19.1 0.1 collective-permute-start.4
  19.1 1.4 %collective-permute-done.4 = f32[288,128]{1,0:T(8,128)S(1)} collective-permute-done((f32[288,128]{1,0:T(8,128)S(1)}, f32[288,128]{1,0:T(8,128)S(1)}, u32[]{:S(2)}, u32[]{:S(2)}) %collective-permute-start.4) | collective-permute-done | bytes 147488 | tf_op jit(solution)/shard_map/ppermute | solution.py:467
  20.5 3.5 %collective-permute-start.7 = (bf16[288,128]{1,0:T(8,128)(2,1)S(1)}, bf16[288,128]{1,0:T(8,128)(2,1)S(1)}, u32[]{:S(2)}, u32[]{:S(2)}) collective-permute-start(bf16[288,128]{1,0:T(8,128)(2,1)S(1)} %add_convert_fusion.1), channel_id=1, source_target_pairs={{0,3},{1,2},{2,1},{3,0},{4,7},{5,6},{6,5},{7,4},{8,11},{9,10},{10,... | collective-permute-start | bytes 221192 | tf_op jit(solution)/shard_map/ppermute | solution.py:492
  24.0 0.5 %collective-permute-start.6 = (bf16[288,128]{1,0:T(8,128)(2,1)S(1)}, bf16[288,128]{1,0:T(8,128)(2,1)S(1)}, u32[]{:S(2)}, u32[]{:S(2)}) collective-permute-start(bf16[288,128]{1,0:T(8,128)(2,1)S(1)} %add_convert_fusion.1), channel_id=1, source_target_pairs={{0,1},{1,0},{2,3},{3,2},{4,5},{5,4},{6,7},{7,6},{8,9},{9,8},{10,11... | collective-permute-start | bytes 221192 | tf_op jit(solution)/shard_map/ppermute | solution.py:492
  24.5 0.1 collective-permute-start.5
  24.6 0.7 %collective-permute-start.3 = (bf16[144,128]{1,0:T(8,128)(2,1)S(1)}, bf16[144,128]{1,0:T(8,128)(2,1)S(1)}, u32[]{:S(2)}, u32[]{:S(2)}) collective-permute-start(bf16[144,128]{1,0:T(8,128)(2,1)S(1)} %get-tuple-element.36), channel_id=1, source_target_pairs={{2,4},{4,2},{6,8},{8,6},{10,12},{12,10},{3,5},{5,3},{7,9},{9,7},{1... | collective-permute-start | bytes 110600 | tf_op jit(solution)/shard_map/ppermute | solution.py:522
  25.3 1.0 %collective-permute-done.7 = bf16[288,128]{1,0:T(8,128)(2,1)S(1)} collective-permute-done((bf16[288,128]{1,0:T(8,128)(2,1)S(1)}, bf16[288,128]{1,0:T(8,128)(2,1)S(1)}, u32[]{:S(2)}, u32[]{:S(2)}) %collective-permute-start.7) | collective-permute-done | bytes 73760 | tf_op jit(solution)/shard_map/ppermute | solution.py:492
  26.3 2.0 %collective-permute-done.6 = bf16[288,128]{1,0:T(8,128)(2,1)S(1)} collective-permute-done((bf16[288,128]{1,0:T(8,128)(2,1)S(1)}, bf16[288,128]{1,0:T(8,128)(2,1)S(1)}, u32[]{:S(2)}, u32[]{:S(2)}) %collective-permute-start.6) | collective-permute-done | bytes 73760 | tf_op jit(solution)/shard_map/ppermute | solution.py:492
  28.4 0.5 %collective-permute-done.5 = bf16[288,128]{1,0:T(8,128)(2,1)S(1)} collective-permute-done((bf16[288,128]{1,0:T(8,128)(2,1)S(1)}, bf16[288,128]{1,0:T(8,128)(2,1)S(1)}, u32[]{:S(2)}, u32[]{:S(2)}) %collective-permute-start.5) | collective-permute-done | bytes 73760 | tf_op jit(solution)/shard_map/ppermute | solution.py:492
  28.9 3.2 %collective-permute-start.10 = (bf16[288,128]{1,0:T(8,128)(2,1)S(1)}, bf16[288,128]{1,0:T(8,128)(2,1)S(1)}, u32[]{:S(2)}, u32[]{:S(2)}) collective-permute-start(bf16[288,128]{1,0:T(8,128)(2,1)S(1)} %add_convert_fusion.own), channel_id=1, source_target_pairs={{0,12},{1,13},{2,14},{3,15},{4,8},{5,9},{6,10},{7,11},{8,4},{9,5},... | collective-permute-start | bytes 221192 | tf_op jit(solution)/shard_map/ppermute | solution.py:492
  32.1 0.0 collective-permute-start.9
  32.1 1.3 %collective-permute-start.8 = (bf16[288,128]{1,0:T(8,128)(2,1)S(1)}, bf16[288,128]{1,0:T(8,128)(2,1)S(1)}, u32[]{:S(2)}, u32[]{:S(2)}) collective-permute-start(bf16[288,128]{1,0:T(8,128)(2,1)S(1)} %add_convert_fusion.own), channel_id=1, source_target_pairs={{0,4},{1,5},{2,6},{3,7},{4,0},{5,1},{6,2},{7,3},{8,12},{9,13},{10,... | collective-permute-start | bytes 221192 | tf_op jit(solution)/shard_map/ppermute | solution.py:492
  33.4 0.0 collective-permute-done.3.row
  33.4 1.1 %last.1 = (bf16[8,256,128]{2,1,0:T(8,128)(2,1)S(1)}, f32[8,128]{1,0:T(8,128)S(1)}) custom-call(bf16[2,272,128]{2,1,0:T(8,128)(2,1)S(1)} %get-tuple-element.33.end, bf16[2,3,272,128]{3,2,1,0:T(8,128)(2,1)S(1)} %get-tuple-element.34.ds1_next, bf16[5,3,272,128]{3,2,1,0:T(8,128)(2,1)S(1)} %get-tuple-element.35.ds1, ...), custom_call_target="tpu_custom_call" | custom-call | flops 427819008 | bytes 4194304 | tf_op jit(solution)/shard_map/last/pallas_call | solution.py:412
  34.5 0.7 %collective-permute-done.10.three = bf16[288,128]{1,0:T(8,128)(2,1)S(1)} collective-permute-done((bf16[288,128]{1,0:T(8,128)(2,1)S(1)}, bf16[288,128]{1,0:T(8,128)(2,1)S(1)}, u32[]{:S(2)}, u32[]{:S(2)}) %collective-permute-start.10) | collective-permute-done | bytes 73760 | tf_op jit(solution)/shard_map/ppermute | solution.py:492
  35.2 2.5 %collective-permute-done.9.two = bf16[288,128]{1,0:T(8,128)(2,1)S(1)} collective-permute-done((bf16[288,128]{1,0:T(8,128)(2,1)S(1)}, bf16[288,128]{1,0:T(8,128)(2,1)S(1)}, u32[]{:S(2)}, u32[]{:S(2)}) %collective-permute-start.9) | collective-permute-done | bytes 73760 | tf_op jit(solution)/shard_map/ppermute | solution.py:492
  37.6 0.0 collective-permute-done.8.one
  37.7 0.1 collective-permute-start.11
  37.8 0.2 copy.20
  38.0 1.1 %copy.21 = bf16[1,64,16,256]{3,2,1,0:T(8,128)(2,1)} copy(bf16[1,64,16,256]{3,1,2,0:T(8,128)(2,1)S(1)} %bitcast.15) | data formatting | bytes 1048576
  39.1 0.1 collective-permute-done.11.other
  39.1 1.0 %finish.1 = (f32[3,3,64,64]{3,2,1,0:T(8,128)}, f32[3,3,64,64]{3,2,1,0:T(8,128)}) custom-call(f32[288,128]{1,0:T(8,128)S(1)} %sum_four.1.part, f32[288,128]{1,0:T(8,128)S(1)} %collective-permute-done.11.other), custom_call_target="tpu_custom_call" | custom-call | tf_op jit(solution)/shard_map/finish/pallas_call | solution.py:452
  (9 shorter events, 0.2 us)
Async XLA Ops:
  1.8 1.0 %copy-start.2 = (bf16[1,64,16,256]{3,2,1,0:T(8,128)(2,1)S(1)}, bf16[1,64,16,256]{3,2,1,0:T(8,128)(2,1)}, u32[]{:S(2)}) copy-start(bf16[1,64,16,256]{3,2,1,0:T(8,128)(2,1)} %param.5) | copy-start | bytes 1572868
  3.3 3.1 %copy-start = (bf16[3,3,64,64]{3,2,1,0:T(8,128)(2,1)S(1)}, bf16[3,3,64,64]{3,2,1,0:T(8,128)(2,1)}, u32[]{:S(2)}) copy-start(bf16[3,3,64,64]{3,2,1,0:T(8,128)(2,1)} %k1.1) | copy-start | bytes 221188
  3.3 3.0 %copy-start.1 = (bf16[3,3,64,64]{3,2,1,0:T(8,128)(2,1)S(1)}, bf16[3,3,64,64]{3,2,1,0:T(8,128)(2,1)}, u32[]{:S(2)}) copy-start(bf16[3,3,64,64]{3,2,1,0:T(8,128)(2,1)} %k2.1) | copy-start | bytes 221188
  3.4 4.9 %collective-permute-start = (bf16[16,8,128]{2,1,0:T(8,128)(2,1)S(1)}, bf16[16,8,128]{2,1,0:T(8,128)(2,1)S(1)}, u32[]{:S(2)}, u32[]{:S(2)}) collective-permute-start(bf16[16,8,128]{2,1,0:T(8,128)(2,1)S(1)} %fusion), channel_id=1, source_target_pairs={{0,1},{1,0},{2,3},{3,2},{4,5},{5,4},{6,7},{7,6},{8,9},{9,8},{10,11... | collective-permute-start | bytes 98312 | tf_op jit(solution)/shard_map/ppermute | solution.py:35
  8.4 8.4 %collective-permute-start.1 = (bf16[3,272,128]{2,1,0:T(8,128)(2,1)S(1)}, bf16[3,272,128]{2,1,0:T(8,128)(2,1)S(1)}, u32[]{:S(2)}, u32[]{:S(2)}) collective-permute-start(bf16[3,272,128]{2,1,0:T(8,128)(2,1)S(1)} %get-tuple-element.25), channel_id=1, source_target_pairs={{0,2},{2,0},{4,6},{6,4},{8,10},{10,8},{12,14},{14,12},{1,3},{3,1},... | collective-permute-start | bytes 626696 | tf_op jit(solution)/shard_map/ppermute | solution.py:512
  10.5 6.3 %collective-permute-start.2 = (bf16[2,272,128]{2,1,0:T(8,128)(2,1)S(1)}, bf16[2,272,128]{2,1,0:T(8,128)(2,1)S(1)}, u32[]{:S(2)}, u32[]{:S(2)}) collective-permute-start(bf16[2,272,128]{2,1,0:T(8,128)(2,1)S(1)} %get-tuple-element.26), channel_id=1, source_target_pairs={{2,4},{4,2},{6,8},{8,6},{10,12},{12,10},{3,5},{5,3},{7,9},{9,7},{1... | collective-permute-start | bytes 417800 | tf_op jit(solution)/shard_map/ppermute | solution.py:513
  19.1 1.4 %collective-permute-start.4 = (f32[288,128]{1,0:T(8,128)S(1)}, f32[288,128]{1,0:T(8,128)S(1)}, u32[]{:S(2)}, u32[]{:S(2)}) collective-permute-start(f32[288,128]{1,0:T(8,128)S(1)} %get-tuple-element.39), channel_id=1, source_target_pairs={{0,16},{16,0},{1,17},{17,1},{2,18},{18,2},{3,19},{19,3},{4,20},{20... | collective-permute-start | bytes 442376 | tf_op jit(solution)/shard_map/ppermute | solution.py:467
  20.5 5.8 %collective-permute-start.7 = (bf16[288,128]{1,0:T(8,128)(2,1)S(1)}, bf16[288,128]{1,0:T(8,128)(2,1)S(1)}, u32[]{:S(2)}, u32[]{:S(2)}) collective-permute-start(bf16[288,128]{1,0:T(8,128)(2,1)S(1)} %add_convert_fusion.1), channel_id=1, source_target_pairs={{0,3},{1,2},{2,1},{3,0},{4,7},{5,6},{6,5},{7,4},{8,11},{9,10},{10,... | collective-permute-start | bytes 221192 | tf_op jit(solution)/shard_map/ppermute | solution.py:492
  24.0 4.4 %collective-permute-start.6 = (bf16[288,128]{1,0:T(8,128)(2,1)S(1)}, bf16[288,128]{1,0:T(8,128)(2,1)S(1)}, u32[]{:S(2)}, u32[]{:S(2)}) collective-permute-start(bf16[288,128]{1,0:T(8,128)(2,1)S(1)} %add_convert_fusion.1), channel_id=1, source_target_pairs={{0,1},{1,0},{2,3},{3,2},{4,5},{5,4},{6,7},{7,6},{8,9},{9,8},{10,11... | collective-permute-start | bytes 221192 | tf_op jit(solution)/shard_map/ppermute | solution.py:492
  24.5 4.4 %collective-permute-start.5 = (bf16[288,128]{1,0:T(8,128)(2,1)S(1)}, bf16[288,128]{1,0:T(8,128)(2,1)S(1)}, u32[]{:S(2)}, u32[]{:S(2)}) collective-permute-start(bf16[288,128]{1,0:T(8,128)(2,1)S(1)} %add_convert_fusion.1), channel_id=1, source_target_pairs={{0,2},{1,3},{2,0},{3,1},{4,6},{5,7},{6,4},{7,5},{8,10},{9,11},{10,... | collective-permute-start | bytes 221192 | tf_op jit(solution)/shard_map/ppermute | solution.py:492
  24.6 8.8 %collective-permute-start.3 = (bf16[144,128]{1,0:T(8,128)(2,1)S(1)}, bf16[144,128]{1,0:T(8,128)(2,1)S(1)}, u32[]{:S(2)}, u32[]{:S(2)}) collective-permute-start(bf16[144,128]{1,0:T(8,128)(2,1)S(1)} %get-tuple-element.36), channel_id=1, source_target_pairs={{2,4},{4,2},{6,8},{8,6},{10,12},{12,10},{3,5},{5,3},{7,9},{9,7},{1... | collective-permute-start | bytes 110600 | tf_op jit(solution)/shard_map/ppermute | solution.py:522
  28.9 6.2 %collective-permute-start.10 = (bf16[288,128]{1,0:T(8,128)(2,1)S(1)}, bf16[288,128]{1,0:T(8,128)(2,1)S(1)}, u32[]{:S(2)}, u32[]{:S(2)}) collective-permute-start(bf16[288,128]{1,0:T(8,128)(2,1)S(1)} %add_convert_fusion.own), channel_id=1, source_target_pairs={{0,12},{1,13},{2,14},{3,15},{4,8},{5,9},{6,10},{7,11},{8,4},{9,5},... | collective-permute-start | bytes 221192 | tf_op jit(solution)/shard_map/ppermute | solution.py:492
  32.1 5.5 %collective-permute-start.9 = (bf16[288,128]{1,0:T(8,128)(2,1)S(1)}, bf16[288,128]{1,0:T(8,128)(2,1)S(1)}, u32[]{:S(2)}, u32[]{:S(2)}) collective-permute-start(bf16[288,128]{1,0:T(8,128)(2,1)S(1)} %add_convert_fusion.own), channel_id=1, source_target_pairs={{0,8},{1,9},{2,10},{3,11},{4,12},{5,13},{6,14},{7,15},{8,0},{9,1},... | collective-permute-start | bytes 221192 | tf_op jit(solution)/shard_map/ppermute | solution.py:492
  32.1 5.5 %collective-permute-start.8 = (bf16[288,128]{1,0:T(8,128)(2,1)S(1)}, bf16[288,128]{1,0:T(8,128)(2,1)S(1)}, u32[]{:S(2)}, u32[]{:S(2)}) collective-permute-start(bf16[288,128]{1,0:T(8,128)(2,1)S(1)} %add_convert_fusion.own), channel_id=1, source_target_pairs={{0,4},{1,5},{2,6},{3,7},{4,0},{5,1},{6,2},{7,3},{8,12},{9,13},{10,... | collective-permute-start | bytes 221192 | tf_op jit(solution)/shard_map/ppermute | solution.py:492
  37.7 1.4 %collective-permute-start.11 = (f32[288,128]{1,0:T(8,128)S(1)}, f32[288,128]{1,0:T(8,128)S(1)}, u32[]{:S(2)}, u32[]{:S(2)}) collective-permute-start(f32[288,128]{1,0:T(8,128)S(1)} %sum_four.1.part), channel_id=1, source_target_pairs={{0,16},{16,0},{1,17},{17,1},{2,18},{18,2},{3,19},{19,3},{4,20},{20... | collective-permute-start | bytes 442376 | tf_op jit(solution)/shard_map/ppermute | solution.py:500

commit v9 on v8

--- a/solution.py
+++ b/solution.py
@@ -27,14 +27,14 @@
     return lax.axis_index(axis) % 2 == parity
 
 
-def swap(low, high, axis):
+def swap(low, high, axis, turn):
     got = []
     for parity in range(2):
         perm = neighbours(axis, parity)
         if perm:
-            got.append(lax.ppermute(jnp.where(is_low(axis, parity), high, low), axis, perm))
+            got.append(lax.ppermute(turn(low, high, is_low(axis, parity)), axis, perm))
         else:
-            got.append(jnp.zeros_like(low))
+            got.append(jnp.zeros_like(got[0]))
     odd = is_low(axis, 1)
     return jnp.where(odd, got[0], got[1]), jnp.where(odd, got[1], got[0])
 
@@ -47,6 +47,26 @@
     _, chans, rows, cols = cells.shape
     part = cells[0].reshape(chans, rows // 2, 2, cols)
     return part.transpose(1, 3, 2, 0).reshape(rows // 2, cols, 2 * chans)
+
+
+def edges_body(*refs):
+    out = refs[-1]
+    at = 0
+    for cells in refs[:-1]:
+        turned = jnp.swapaxes(cells[0], 0, 1)
+        for pair in range(turned.shape[0] // 2):
+            out[at] = turned[2 * pair : 2 * pair + 2].reshape(2 * turned.shape[1], -1).T
+            at += 1
+
+
+def turn_edges(*parts):
+    pairs = sum(part.shape[2] // 2 for part in parts)
+    return pl.pallas_call(
+        edges_body,
+        out_shape=jax.ShapeDtypeStruct((pairs, parts[0].shape[3], LANES), BF),
+        compiler_params=pltpu.CompilerParams(vmem_limit_bytes=8 * 2**20),
+        name="edges",
+    )(*parts)
 
 
 def from_pairs(pairs):
@@ -504,8 +524,11 @@
     slides, chans, rows, cols = features.shape
     pairs = rows // 2
     feat, grad = to_pairs(features), to_pairs(grad_out)
-    own = jnp.concatenate([feat, grad], axis=0)
-    from_left, from_right = swap(own[:, : RIM // 2], own[:, cols - RIM // 2 :], "col")
+    def turn(low, high, is_lower):
+        return turn_edges(jnp.where(is_lower, high, low))
+
+    both = jnp.concatenate([features, grad_out], axis=2)
+    from_left, from_right = swap(both[..., : RIM // 2], both[..., cols - RIM // 2 :], "col", turn)
     edge = jnp.concatenate([from_right, from_left], axis=1)
     weights, own_near, own_far = prep(feat, grad, kernel_one, kernel_two)
     sent_near, sent_far = frame(own_near, own_far, edge)

time: 40.4 us -> 39.7 us (0.983)
  waiting for transfers between devices: 12.1 us -> 11 us
    ppermute x1, waiting for transfers between devices: 1.53 us -> 0.01 us  [swap(): got.append(lax.ppermute(turn(low, high, is_low(axis, parity)), axis, perm))]
    unnamed x9 -> x12, local copies, waits for them, and re-layouts: 3.22 us -> 3.29 us
  transfers between devices with their start and end apart: 12 -> 12, of which waited for: 9 -> 8; matrix products, arithmetic and copies ran while one was open for 3% -> 6% of each run, Pallas kernels for 12% -> 12%
where the time goes in v9:
time: 39.7 us; the launch traced here: 39.5 us
  starting transfers between devices  14.9 us (38%)
  waiting for transfers between devices  11 us (28%)
  Pallas kernels  8.23 us (21%)
  local copies, waits for them, and re-layouts  4.1 us (10%)
  between operations  0.85 us (2%)
    ppermute x6, starting transfers between devices, reduced(): got.append(lax.ppermute(low, AXES, perm))  8.47 us
    ppermute x6, waiting for transfers between devices, reduced(): got.append(lax.ppermute(low, AXES, perm))  6.85 us
    unnamed x12, local copies, waits for them, and re-layouts  3.29 us
    pallas_call x1, Pallas kernels, inner(): pl.pallas_call(inner_body, out_shape=(jax.ShapeDtypeStruct(shifts(2), BF)...  3.23 us
    ppermute x1, starting transfers between devices, swap(): got.append(lax.ppermute(turn(low, high, is_low(axis, parity)), axis, perm))  2.98 us
    ppermute x1, waiting for transfers between devices, shards(): got_near = lax.ppermute(sent_near, 'row', neighbours('row', 0))  2.78 us
    pallas_call x1, Pallas kernels, outer(): pl.pallas_call(rim_body, out_shape=(jax.ShapeDtypeStruct(shifts(2), BF),...  2.18 us
    ppermute x1, starting transfers between devices, shards(): got_near = lax.ppermute(sent_near, 'row', neighbours('row', 0))  1.99 us
  transfers between devices with their start and end apart: 12, of which 8 were waited for; matrix products, arithmetic and copies ran while one was open for 6% of the time, Pallas kernels for 12%

profile of v9, /device:TPU:0, one launch (start us, length us, event | category | flops | bytes accessed | tf_op | source)
XLA Modules:
  0.0 39.5 jit_solution(4554271108306402096)
XLA Ops:
  0.6 0.0 copy-start.3
  0.7 1.2 %constant_dynamic-update-slice_fusion.1 = bf16[1,64,32,256]{3,2,1,0:T(8,128)(2,1)S(1)} fusion(bf16[1,64,16,256]{3,2,1,0:T(8,128)(2,1)} %param.4), kind=kLoop, calls=%fused_computation.13 | loop fusion | bytes 1048576
  1.8 0.0 copy-done.3
  1.8 0.1 constant_dynamic-update-slice_fusion
  1.9 0.2 slice_select_fusion.refs_0_
  2.1 0.0 copy-start.2
  2.1 0.2 edges.1
  2.4 3.0 %collective-permute-start = (bf16[16,8,128]{2,1,0:T(8,128)(2,1)S(1)}, bf16[16,8,128]{2,1,0:T(8,128)(2,1)S(1)}, u32[]{:S(2)}, u32[]{:S(2)}) collective-permute-start(bf16[16,8,128]{2,1,0:T(8,128)(2,1)S(1)} %edges.1), channel_id=1, source_target_pairs={{0,1},{1,0},{2,3},{3,2},{4,5},{5,4},{6,7},{7,6},{8,9},{9,8},{10,11... | collective-permute-start | bytes 98312 | tf_op jit(solution)/shard_map/ppermute | solution.py:35
  5.3 0.0 copy-done.2
  5.3 0.2 copy.10
  5.5 0.2 copy.11
  5.7 0.3 copy.16.f
  5.9 0.0 copy-start
  6.0 0.0 copy-start.1
  6.0 0.3 copy.17.g
  6.3 0.6 %copy-done = bf16[3,3,64,64]{3,2,1,0:T(8,128)(2,1)S(1)} copy-done((bf16[3,3,64,64]{3,2,1,0:T(8,128)(2,1)S(1)}, bf16[3,3,64,64]{3,2,1,0:T(8,128)(2,1)}, u32[]{:S(2)}) %copy-start) | copy-done | bytes 73752
  6.9 0.1 copy-done.1
  6.9 0.3 prep.1
  7.3 0.0 collective-permute-done
  7.3 0.1 frame.1
  7.4 2.0 %collective-permute-start.1 = (bf16[3,272,128]{2,1,0:T(8,128)(2,1)S(1)}, bf16[3,272,128]{2,1,0:T(8,128)(2,1)S(1)}, u32[]{:S(2)}, u32[]{:S(2)}) collective-permute-start(bf16[3,272,128]{2,1,0:T(8,128)(2,1)S(1)} %get-tuple-element.25), channel_id=1, source_target_pairs={{0,2},{2,0},{4,6},{6,4},{8,10},{10,8},{12,14},{14,12},{1,3},{3,1},... | collective-permute-start | bytes 626696 | tf_op jit(solution)/shard_map/ppermute | solution.py:535
  9.4 0.7 %collective-permute-start.2 = (bf16[2,272,128]{2,1,0:T(8,128)(2,1)S(1)}, bf16[2,272,128]{2,1,0:T(8,128)(2,1)S(1)}, u32[]{:S(2)}, u32[]{:S(2)}) collective-permute-start(bf16[2,272,128]{2,1,0:T(8,128)(2,1)S(1)} %get-tuple-element.26), channel_id=1, source_target_pairs={{2,4},{4,2},{6,8},{8,6},{10,12},{12,10},{3,5},{5,3},{7,9},{9,7},{1... | collective-permute-start | bytes 417800 | tf_op jit(solution)/shard_map/ppermute | solution.py:536
  10.1 3.2 %inner.1 = (bf16[2,3,272,128]{3,2,1,0:T(8,128)(2,1)S(1)}, bf16[2,3,272,128]{3,2,1,0:T(8,128)(2,1)S(1)}, f32[2,272,128]{2,1,0:T(8,128)S(1)}, bf16[5,3,272,128]{3,...) custom-call(bf16[8,256,128]{2,1,0:T(8,128)(2,1)S(1)} %copy.16.f, ...), custom_call_target="tpu_custom_call" | custom-call | flops 1176502272 | bytes 4194304 | tf_op jit(solution)/shard_map/inner/pallas_call | solution.py:375
  13.3 2.8 %collective-permute-done.1 = bf16[3,272,128]{2,1,0:T(8,128)(2,1)S(1)} collective-permute-done((bf16[3,272,128]{2,1,0:T(8,128)(2,1)S(1)}, bf16[3,272,128]{2,1,0:T(8,128)(2,1)S(1)}, u32[]{:S(2)}, u32[]{:S(2)}) %collective-permute-start.1) | collective-permute-done | bytes 208928 | tf_op jit(solution)/shard_map/ppermute | solution.py:535
  16.1 0.0 collective-permute-done.2
  16.2 2.2 %outer.1 = (bf16[2,3,272,128]{3,2,1,0:T(8,128)(2,1)S(1)}, bf16[2,272,128]{2,1,0:T(8,128)(2,1)S(1)}, bf16[144,128]{1,0:T(8,128)(2,1)S(1)}, f32[288,128]{1,0:T(8,128)S(1)}, f32[288,128]{1,0:T(8,128)S(1)}) custom-call(bf16[8,256,128]{2,1,0:T(8,128)(2,1)S(1)} %copy.16.f, bf16[8,256,128]{2,1,0:T(8,128)(2,1)S(1)} %copy.17.g, ...), custom_call_target="tpu_custom_call" | custom-call | flops 748683264 | bytes 4194304 | tf_op jit(solution)/shard_map/outer/pallas_call | solution.py:406
  18.4 0.1 collective-permute-start.4
  18.5 1.4 %collective-permute-done.4 = f32[288,128]{1,0:T(8,128)S(1)} collective-permute-done((f32[288,128]{1,0:T(8,128)S(1)}, f32[288,128]{1,0:T(8,128)S(1)}, u32[]{:S(2)}, u32[]{:S(2)}) %collective-permute-start.4) | collective-permute-done | bytes 147488 | tf_op jit(solution)/shard_map/ppermute | solution.py:487
  19.9 3.1 %collective-permute-start.7 = (bf16[288,128]{1,0:T(8,128)(2,1)S(1)}, bf16[288,128]{1,0:T(8,128)(2,1)S(1)}, u32[]{:S(2)}, u32[]{:S(2)}) collective-permute-start(bf16[288,128]{1,0:T(8,128)(2,1)S(1)} %add_convert_fusion.1), channel_id=1, source_target_pairs={{0,3},{1,2},{2,1},{3,0},{4,7},{5,6},{6,5},{7,4},{8,11},{9,10},{10,... | collective-permute-start | bytes 221192 | tf_op jit(solution)/shard_map/ppermute | solution.py:512
  23.0 0.9 %collective-permute-start.6 = (bf16[288,128]{1,0:T(8,128)(2,1)S(1)}, bf16[288,128]{1,0:T(8,128)(2,1)S(1)}, u32[]{:S(2)}, u32[]{:S(2)}) collective-permute-start(bf16[288,128]{1,0:T(8,128)(2,1)S(1)} %add_convert_fusion.1), channel_id=1, source_target_pairs={{0,1},{1,0},{2,3},{3,2},{4,5},{5,4},{6,7},{7,6},{8,9},{9,8},{10,11... | collective-permute-start | bytes 221192 | tf_op jit(solution)/shard_map/ppermute | solution.py:512
  23.9 0.0 collective-permute-start.5
  23.9 0.7 %collective-permute-start.3 = (bf16[144,128]{1,0:T(8,128)(2,1)S(1)}, bf16[144,128]{1,0:T(8,128)(2,1)S(1)}, u32[]{:S(2)}, u32[]{:S(2)}) collective-permute-start(bf16[144,128]{1,0:T(8,128)(2,1)S(1)} %get-tuple-element.36), channel_id=1, source_target_pairs={{2,4},{4,2},{6,8},{8,6},{10,12},{12,10},{3,5},{5,3},{7,9},{9,7},{1... | collective-permute-start | bytes 110600 | tf_op jit(solution)/shard_map/ppermute | solution.py:545
  24.5 0.8 %collective-permute-done.7 = bf16[288,128]{1,0:T(8,128)(2,1)S(1)} collective-permute-done((bf16[288,128]{1,0:T(8,128)(2,1)S(1)}, bf16[288,128]{1,0:T(8,128)(2,1)S(1)}, u32[]{:S(2)}, u32[]{:S(2)}) %collective-permute-start.7) | collective-permute-done | bytes 73760 | tf_op jit(solution)/shard_map/ppermute | solution.py:512
  25.3 2.0 %collective-permute-done.6 = bf16[288,128]{1,0:T(8,128)(2,1)S(1)} collective-permute-done((bf16[288,128]{1,0:T(8,128)(2,1)S(1)}, bf16[288,128]{1,0:T(8,128)(2,1)S(1)}, u32[]{:S(2)}, u32[]{:S(2)}) %collective-permute-start.6) | collective-permute-done | bytes 73760 | tf_op jit(solution)/shard_map/ppermute | solution.py:512
  27.3 0.9 %collective-permute-done.5 = bf16[288,128]{1,0:T(8,128)(2,1)S(1)} collective-permute-done((bf16[288,128]{1,0:T(8,128)(2,1)S(1)}, bf16[288,128]{1,0:T(8,128)(2,1)S(1)}, u32[]{:S(2)}, u32[]{:S(2)}) %collective-permute-start.5) | collective-permute-done | bytes 73760 | tf_op jit(solution)/shard_map/ppermute | solution.py:512
  28.3 3.2 %collective-permute-start.10 = (bf16[288,128]{1,0:T(8,128)(2,1)S(1)}, bf16[288,128]{1,0:T(8,128)(2,1)S(1)}, u32[]{:S(2)}, u32[]{:S(2)}) collective-permute-start(bf16[288,128]{1,0:T(8,128)(2,1)S(1)} %add_convert_fusion.own), channel_id=1, source_target_pairs={{0,12},{1,13},{2,14},{3,15},{4,8},{5,9},{6,10},{7,11},{8,4},{9,5},... | collective-permute-start | bytes 221192 | tf_op jit(solution)/shard_map/ppermute | solution.py:512
  31.4 0.0 collective-permute-start.9
  31.4 1.3 %collective-permute-start.8 = (bf16[288,128]{1,0:T(8,128)(2,1)S(1)}, bf16[288,128]{1,0:T(8,128)(2,1)S(1)}, u32[]{:S(2)}, u32[]{:S(2)}) collective-permute-start(bf16[288,128]{1,0:T(8,128)(2,1)S(1)} %add_convert_fusion.own), channel_id=1, source_target_pairs={{0,4},{1,5},{2,6},{3,7},{4,0},{5,1},{6,2},{7,3},{8,12},{9,13},{10,... | collective-permute-start | bytes 221192 | tf_op jit(solution)/shard_map/ppermute | solution.py:512
  32.7 0.0 collective-permute-done.3.row
  32.7 1.1 %last.1 = (bf16[8,256,128]{2,1,0:T(8,128)(2,1)S(1)}, f32[8,128]{1,0:T(8,128)S(1)}) custom-call(bf16[2,272,128]{2,1,0:T(8,128)(2,1)S(1)} %get-tuple-element.33.end, bf16[2,3,272,128]{3,2,1,0:T(8,128)(2,1)S(1)} %get-tuple-element.34.ds1_next, bf16[5,3,272,128]{3,2,1,0:T(8,128)(2,1)S(1)} %get-tuple-element.35.ds1, ...), custom_call_target="tpu_custom_call" | custom-call | flops 427819008 | bytes 4194304 | tf_op jit(solution)/shard_map/last/pallas_call | solution.py:432
  33.8 0.7 %collective-permute-done.10.three = bf16[288,128]{1,0:T(8,128)(2,1)S(1)} collective-permute-done((bf16[288,128]{1,0:T(8,128)(2,1)S(1)}, bf16[288,128]{1,0:T(8,128)(2,1)S(1)}, u32[]{:S(2)}, u32[]{:S(2)}) %collective-permute-start.10) | collective-permute-done | bytes 73760 | tf_op jit(solution)/shard_map/ppermute | solution.py:512
  34.5 2.5 %collective-permute-done.9.two = bf16[288,128]{1,0:T(8,128)(2,1)S(1)} collective-permute-done((bf16[288,128]{1,0:T(8,128)(2,1)S(1)}, bf16[288,128]{1,0:T(8,128)(2,1)S(1)}, u32[]{:S(2)}, u32[]{:S(2)}) %collective-permute-start.9) | collective-permute-done | bytes 73760 | tf_op jit(solution)/shard_map/ppermute | solution.py:512
  37.0 0.0 collective-permute-done.8.one
  37.0 0.1 collective-permute-start.11
  37.1 0.2 copy.18
  37.3 1.1 %copy.19 = bf16[1,64,16,256]{3,2,1,0:T(8,128)(2,1)} copy(bf16[1,64,16,256]{3,1,2,0:T(8,128)(2,1)S(1)} %bitcast.17) | data formatting | bytes 1048576
  38.4 0.1 collective-permute-done.11.other
  38.5 1.0 %finish.1 = (f32[3,3,64,64]{3,2,1,0:T(8,128)}, f32[3,3,64,64]{3,2,1,0:T(8,128)}) custom-call(f32[288,128]{1,0:T(8,128)S(1)} %sum_four.1.part, f32[288,128]{1,0:T(8,128)S(1)} %collective-permute-done.11.other), custom_call_target="tpu_custom_call" | custom-call | tf_op jit(solution)/shard_map/finish/pallas_call | solution.py:472
  (8 shorter events, 0.2 us)
Async XLA Ops:
  0.6 1.2 %copy-start.3 = (bf16[1,64,16,256]{3,2,1,0:T(8,128)(2,1)S(1)}, bf16[1,64,16,256]{3,2,1,0:T(8,128)(2,1)}, u32[]{:S(2)}) copy-start(bf16[1,64,16,256]{3,2,1,0:T(8,128)(2,1)} %param.5) | copy-start | bytes 1572868
  2.1 3.2 %copy-start.2 = (bf16[1,64,16,256]{3,2,1,0:T(8,128)(2,1)S(1)}, bf16[1,64,16,256]{3,2,1,0:T(8,128)(2,1)}, u32[]{:S(2)}) copy-start(bf16[1,64,16,256]{3,2,1,0:T(8,128)(2,1)} %param.4) | copy-start | bytes 1572868
  2.4 4.9 %collective-permute-start = (bf16[16,8,128]{2,1,0:T(8,128)(2,1)S(1)}, bf16[16,8,128]{2,1,0:T(8,128)(2,1)S(1)}, u32[]{:S(2)}, u32[]{:S(2)}) collective-permute-start(bf16[16,8,128]{2,1,0:T(8,128)(2,1)S(1)} %edges.1), channel_id=1, source_target_pairs={{0,1},{1,0},{2,3},{3,2},{4,5},{5,4},{6,7},{7,6},{8,9},{9,8},{10,11... | collective-permute-start | bytes 98312 | tf_op jit(solution)/shard_map/ppermute | solution.py:35
  5.9 0.9 %copy-start = (bf16[3,3,64,64]{3,2,1,0:T(8,128)(2,1)S(1)}, bf16[3,3,64,64]{3,2,1,0:T(8,128)(2,1)}, u32[]{:S(2)}) copy-start(bf16[3,3,64,64]{3,2,1,0:T(8,128)(2,1)} %k1.1) | copy-start | bytes 221188
  6.0 1.0 %copy-start.1 = (bf16[3,3,64,64]{3,2,1,0:T(8,128)(2,1)S(1)}, bf16[3,3,64,64]{3,2,1,0:T(8,128)(2,1)}, u32[]{:S(2)}) copy-start(bf16[3,3,64,64]{3,2,1,0:T(8,128)(2,1)} %k2.1) | copy-start | bytes 221188
  7.4 8.7 %collective-permute-start.1 = (bf16[3,272,128]{2,1,0:T(8,128)(2,1)S(1)}, bf16[3,272,128]{2,1,0:T(8,128)(2,1)S(1)}, u32[]{:S(2)}, u32[]{:S(2)}) collective-permute-start(bf16[3,272,128]{2,1,0:T(8,128)(2,1)S(1)} %get-tuple-element.25), channel_id=1, source_target_pairs={{0,2},{2,0},{4,6},{6,4},{8,10},{10,8},{12,14},{14,12},{1,3},{3,1},... | collective-permute-start | bytes 626696 | tf_op jit(solution)/shard_map/ppermute | solution.py:535
  9.4 6.7 %collective-permute-start.2 = (bf16[2,272,128]{2,1,0:T(8,128)(2,1)S(1)}, bf16[2,272,128]{2,1,0:T(8,128)(2,1)S(1)}, u32[]{:S(2)}, u32[]{:S(2)}) collective-permute-start(bf16[2,272,128]{2,1,0:T(8,128)(2,1)S(1)} %get-tuple-element.26), channel_id=1, source_target_pairs={{2,4},{4,2},{6,8},{8,6},{10,12},{12,10},{3,5},{5,3},{7,9},{9,7},{1... | collective-permute-start | bytes 417800 | tf_op jit(solution)/shard_map/ppermute | solution.py:536
  18.4 1.4 %collective-permute-start.4 = (f32[288,128]{1,0:T(8,128)S(1)}, f32[288,128]{1,0:T(8,128)S(1)}, u32[]{:S(2)}, u32[]{:S(2)}) collective-permute-start(f32[288,128]{1,0:T(8,128)S(1)} %get-tuple-element.39), channel_id=1, source_target_pairs={{0,16},{16,0},{1,17},{17,1},{2,18},{18,2},{3,19},{19,3},{4,20},{20... | collective-permute-start | bytes 442376 | tf_op jit(solution)/shard_map/ppermute | solution.py:487
  19.9 5.5 %collective-permute-start.7 = (bf16[288,128]{1,0:T(8,128)(2,1)S(1)}, bf16[288,128]{1,0:T(8,128)(2,1)S(1)}, u32[]{:S(2)}, u32[]{:S(2)}) collective-permute-start(bf16[288,128]{1,0:T(8,128)(2,1)S(1)} %add_convert_fusion.1), channel_id=1, source_target_pairs={{0,3},{1,2},{2,1},{3,0},{4,7},{5,6},{6,5},{7,4},{8,11},{9,10},{10,... | collective-permute-start | bytes 221192 | tf_op jit(solution)/shard_map/ppermute | solution.py:512
  23.0 4.4 %collective-permute-start.6 = (bf16[288,128]{1,0:T(8,128)(2,1)S(1)}, bf16[288,128]{1,0:T(8,128)(2,1)S(1)}, u32[]{:S(2)}, u32[]{:S(2)}) collective-permute-start(bf16[288,128]{1,0:T(8,128)(2,1)S(1)} %add_convert_fusion.1), channel_id=1, source_target_pairs={{0,1},{1,0},{2,3},{3,2},{4,5},{5,4},{6,7},{7,6},{8,9},{9,8},{10,11... | collective-permute-start | bytes 221192 | tf_op jit(solution)/shard_map/ppermute | solution.py:512
  23.9 4.4 %collective-permute-start.5 = (bf16[288,128]{1,0:T(8,128)(2,1)S(1)}, bf16[288,128]{1,0:T(8,128)(2,1)S(1)}, u32[]{:S(2)}, u32[]{:S(2)}) collective-permute-start(bf16[288,128]{1,0:T(8,128)(2,1)S(1)} %add_convert_fusion.1), channel_id=1, source_target_pairs={{0,2},{1,3},{2,0},{3,1},{4,6},{5,7},{6,4},{7,5},{8,10},{9,11},{10,... | collective-permute-start | bytes 221192 | tf_op jit(solution)/shard_map/ppermute | solution.py:512
  23.9 8.9 %collective-permute-start.3 = (bf16[144,128]{1,0:T(8,128)(2,1)S(1)}, bf16[144,128]{1,0:T(8,128)(2,1)S(1)}, u32[]{:S(2)}, u32[]{:S(2)}) collective-permute-start(bf16[144,128]{1,0:T(8,128)(2,1)S(1)} %get-tuple-element.36), channel_id=1, source_target_pairs={{2,4},{4,2},{6,8},{8,6},{10,12},{12,10},{3,5},{5,3},{7,9},{9,7},{1... | collective-permute-start | bytes 110600 | tf_op jit(solution)/shard_map/ppermute | solution.py:545
  28.3 6.2 %collective-permute-start.10 = (bf16[288,128]{1,0:T(8,128)(2,1)S(1)}, bf16[288,128]{1,0:T(8,128)(2,1)S(1)}, u32[]{:S(2)}, u32[]{:S(2)}) collective-permute-start(bf16[288,128]{1,0:T(8,128)(2,1)S(1)} %add_convert_fusion.own), channel_id=1, source_target_pairs={{0,12},{1,13},{2,14},{3,15},{4,8},{5,9},{6,10},{7,11},{8,4},{9,5},... | collective-permute-start | bytes 221192 | tf_op jit(solution)/shard_map/ppermute | solution.py:512
  31.4 5.5 %collective-permute-start.9 = (bf16[288,128]{1,0:T(8,128)(2,1)S(1)}, bf16[288,128]{1,0:T(8,128)(2,1)S(1)}, u32[]{:S(2)}, u32[]{:S(2)}) collective-permute-start(bf16[288,128]{1,0:T(8,128)(2,1)S(1)} %add_convert_fusion.own), channel_id=1, source_target_pairs={{0,8},{1,9},{2,10},{3,11},{4,12},{5,13},{6,14},{7,15},{8,0},{9,1},... | collective-permute-start | bytes 221192 | tf_op jit(solution)/shard_map/ppermute | solution.py:512
  31.4 5.5 %collective-permute-start.8 = (bf16[288,128]{1,0:T(8,128)(2,1)S(1)}, bf16[288,128]{1,0:T(8,128)(2,1)S(1)}, u32[]{:S(2)}, u32[]{:S(2)}) collective-permute-start(bf16[288,128]{1,0:T(8,128)(2,1)S(1)} %add_convert_fusion.own), channel_id=1, source_target_pairs={{0,4},{1,5},{2,6},{3,7},{4,0},{5,1},{6,2},{7,3},{8,12},{9,13},{10,... | collective-permute-start | bytes 221192 | tf_op jit(solution)/shard_map/ppermute | solution.py:512
  37.0 1.4 %collective-permute-start.11 = (f32[288,128]{1,0:T(8,128)S(1)}, f32[288,128]{1,0:T(8,128)S(1)}, u32[]{:S(2)}, u32[]{:S(2)}) collective-permute-start(f32[288,128]{1,0:T(8,128)S(1)} %sum_four.1.part), channel_id=1, source_target_pairs={{0,16},{16,0},{1,17},{17,1},{2,18},{18,2},{3,19},{19,3},{4,20},{20... | collective-permute-start | bytes 442376 | tf_op jit(solution)/shard_map/ppermute | solution.py:520

commit v10 on v9

--- a/solution.py
+++ b/solution.py
@@ -75,18 +75,23 @@
     return part.transpose(3, 0, 2, 1).reshape(1, lanes // 2, 2 * count, cols)
 
 
-def make_weights(k1, k2, w1, w2, v2, v1):
+def make_weights(k1, k2, ahead, back):
     zero = jnp.zeros((HALF, HALF), BF)
-    for taps, forward, backward in ((k1, w1, v1), (k2, w2, v2)):
+    for layer, taps in enumerate((k1, k2)):
         flat = {(ky, kx): taps[ky, kx] for ky in range(3) for kx in range(3)}
         turned = {at: flat[at].astype(F32).T.astype(BF) for at in flat}
         for p in range(2):
-            for kx in range(3):
-                for r in range(2):
-                    at = ((p * 3 + kx) * 2 + r) * HALF
-                    kys = [2 * p + r - a for a in range(2)]
-                    forward[at : at + HALF] = jnp.concatenate([turned.get((ky, kx), zero) for ky in kys], axis=1)
-                    backward[at : at + HALF] = jnp.concatenate([flat.get((2 - ky, 2 - kx), zero) for ky in kys], axis=1)
+            for r in range(2):
+                kys = [2 * p + r - a for a in range(2)]
+                at = (p * 2 + r) * HALF
+                for kx in range(3):
+                    ahead[layer, at : at + HALF, kx * LANES : (kx + 1) * LANES] = jnp.concatenate(
+                        [turned.get((ky, kx), zero) for ky in kys], axis=1
+                    )
+                    to = ((p * 3 + kx) * 2 + r) * HALF
+                    back[layer, to : to + HALF] = jnp.concatenate(
+                        [flat.get((2 - ky, 2 - kx), zero) for ky in kys], axis=1
+                    )
 
 
 def outer_units(feats, grads, high):
@@ -99,8 +104,8 @@
     return feats[near], jnp.where(own, then, grad).astype(BF), jnp.where(own, grad, then).astype(BF)
 
 
-def prep_body(f, g, k1, k2, weights, sent_near, sent_far):
-    make_weights(k1, k2, *(weights.at[at] for at in range(4)))
+def prep_body(f, g, k1, k2, ahead, back, sent_near, sent_far):
+    make_weights(k1, k2, ahead, back)
     odd = odd_place("row")
     for sent, high in ((sent_near, jnp.logical_not(odd)), (sent_far, odd)):
         units = outer_units(f, g, high)
@@ -109,11 +114,11 @@
 
 
 def prep(feat, grad, kernel_one, kernel_two):
-    shape = jax.ShapeDtypeStruct((4, 12 * HALF, LANES), BF)
+    weights = [jax.ShapeDtypeStruct(shape, BF) for shape in ((2, 4 * HALF, 3 * LANES), (2, 12 * HALF, LANES))]
     sent = [jax.ShapeDtypeStruct((units, *feat.shape[1:]), BF) for units in (3, 2)]
     return pl.pallas_call(
         prep_body,
-        out_shape=(shape, *sent),
+        out_shape=(*weights, *sent),
         compiler_params=pltpu.CompilerParams(vmem_limit_bytes=12 * 2**20),
         cost_estimate=cost(2),
         name="prep",
@@ -160,6 +165,13 @@
     return jnp.dot(jnp.concatenate(parts, axis=1), weight[...], preferred_element_type=F32)
 
 
+def row_dot(first, second, weight):
+    three = jnp.dot(jnp.concatenate([first, second], axis=1), weight[...], preferred_element_type=F32)
+    left = pltpu.roll(three[:, :LANES], 1, 0)
+    right = pltpu.roll(three[:, 2 * LANES :], three.shape[0] - 1, 0)
+    return left + three[:, LANES : 2 * LANES] + right
+
+
 def edge_masks():
     row, col = lax.axis_index("row"), lax.axis_index("col")
     top = (row > 0).astype(F32)
@@ -181,27 +193,32 @@
     acc[...] += jnp.dot(feat_t, near, preferred_element_type=F32)
 
 
-def inner_body(f, g, edge, weights, hs_edge, ds2_edge, slope_edge, ds1, acc1, acc2, fs, hs, ds2, slope, ht, ft):
-    w1, w2, v2 = (weights.at[at] for at in range(3))
+def add_dot(acc, lefts, rights):
+    left, right = jnp.concatenate(lefts, axis=1), jnp.concatenate(rights, axis=0)
+    acc[...] += jnp.dot(left, right, preferred_element_type=F32)
+
+
+def inner_body(f, g, edge, ahead, back, hs_edge, ds2_edge, slope_edge, ds1, acc1, acc2, fs, hs, ds2, slope, ht, ft):
+    w1, w2, v2 = ahead.at[0], ahead.at[1], back.at[1]
     pairs, cols = f.shape[:2]
     _, _, rim = edge_masks()
 
     @pl.loop(0, pairs, unroll=True)
     def _(j):
-        store_shifts(with_rim(f[j], edge[j]), fs, j)
+        fs[j] = with_rim(f[j], edge[j]).astype(BF)
 
     @pl.loop(0, pairs - 1, unroll=True)
     def _(j):
-        pre = band_dot((fs, j), (fs, j + 1), w1)
+        pre = row_dot(fs[j], fs[j + 1], w1)
         sig = sigmoid(pre)
         act = pre * sig
         slope[j] = sig + act * (1.0 - sig)
-        store_shifts(rim_masked(act, rim), hs, j)
-        ht[j] = hs[j, 1, :cols].T
+        hs[j] = rim_masked(act, rim).astype(BF)
+        ht[j] = hs[j, :cols].T
 
     @pl.loop(0, pairs - 2, unroll=True)
     def _(j):
-        pre = band_dot((hs, j), (hs, j + 1), w2)
+        pre = row_dot(hs[j], hs[j + 1], w2)
         sig = sigmoid(pre)
         grad = with_rim(g[j + 1], edge[pairs + j + 1])
         delta = grad * (sig + pre * sig * (1.0 - sig))
@@ -209,8 +226,8 @@
 
     @pl.loop(0, pairs - 3, unroll=True)
     def _(j):
-        back = band_dot((ds2, j), (ds2, j + 1), v2)
-        store_shifts(rim_masked(back * slope[j + 1], rim), ds1, j)
+        value = band_dot((ds2, j), (ds2, j + 1), v2)
+        store_shifts(rim_masked(value * slope[j + 1], rim), ds1, j)
 
     acc1[...] = jnp.zeros_like(acc1)
     acc2[...] = jnp.zeros_like(acc2)
@@ -260,14 +277,14 @@
 
 
 def rim_body(
-    f, g, edge, above, below, weights, hs_edge, ds2_edge, slope_edge, acc1_in, acc2_in,
+    f, g, edge, above, below, ahead, back, hs_edge, ds2_edge, slope_edge, acc1_in, acc2_in,
     ds1_next, end, row, mine, other, fs, hs, ds2, slope, ds1, acc1, acc2,
 ):
     pairs, cols = f.shape[:2]
     top, bottom, rim = edge_masks()
     flags = (top, bottom)
     beyond = [half_lanes(side) for side in range(2)]
-    w1, w2, v2 = (weights.at[at] for at in range(3))
+    w1, w2, v2 = ahead.at[0], ahead.at[1], back.at[1]
     rows = []
     odd = odd_place("row")
     known = jnp.where(odd, top, 0.0), jnp.where(odd, 0.0, bottom)
@@ -279,34 +296,34 @@
         return (one, two) if side == 0 else (two, one)
 
     for side in sides:
-        store_shifts(jnp.where(beyond[side], more[side], mixed[side]), fs.at[side], 0)
-        store_shifts(halo[side], fs.at[side], 1)
-        store_shifts(with_rim(f[near[side]], edge[near[side]]), fs.at[side], 2)
+        fs[side, 0] = jnp.where(beyond[side], more[side], mixed[side]).astype(BF)
+        fs[side, 1] = halo[side].astype(BF)
+        fs[side, 2] = with_rim(f[near[side]], edge[near[side]]).astype(BF)
     for k in (1, 0):
         for side in sides:
-            pre = band_dot(*order(side, (fs.at[side], k), (fs.at[side], k + 1)), w1)
+            pre = row_dot(*order(side, fs[side, k], fs[side, k + 1]), w1)
             sig = sigmoid(pre)
             act = pre * sig
             if k == 1:
                 slope[side] = sig + act * (1.0 - sig)
             act = act * (flags[side] if k == 0 else jnp.where(beyond[side], flags[side], 1.0))
-            store_shifts(rim_masked(act, rim), hs.at[side], k)
+            hs[side, k] = rim_masked(act, rim).astype(BF)
     for k in (1, 0):
         for side in sides:
             if k == 0:
                 grad = pltpu.roll(jnp.where(beyond[side], mixed[side], more[side]), HALF, 1)
             else:
                 grad = with_rim(g[near[side]], edge[pairs + near[side]])
-            inward = (hs.at[side], 1) if k == 0 else (hs_edge, side)
-            pre = band_dot(*order(side, (hs.at[side], k), inward), w2)
+            inward = hs[side, 1] if k == 0 else hs_edge[side]
+            pre = row_dot(*order(side, hs[side, k], inward), w2)
             sig = sigmoid(pre)
             delta = grad * (sig + pre * sig * (1.0 - sig))
             store_shifts(delta, ds2.at[side], k)
     for k in (1, 0):
         for side in sides:
             inward = (ds2.at[side], 1) if k == 0 else (ds2_edge, side)
-            back = band_dot(*order(side, (ds2.at[side], k), inward), v2)
-            value = back * slope[side] if k == 0 else back * slope_edge[side]
+            value = band_dot(*order(side, (ds2.at[side], k), inward), v2)
+            value = value * (slope[side] if k == 0 else slope_edge[side])
             value = rim_masked(value, rim)
             if k == 0:
                 end[side] = jnp.where(beyond[side], value * known[side], value).astype(BF)
@@ -327,13 +344,20 @@
 
     acc1[...] = acc1_in[...]
     acc2[...] = acc2_in[...]
+    lefts, rights = [], []
     for side in sides:
-        hid = order(side, hs[side, 1, 1, :cols].T, hs_edge[side, 1, :cols].T)
-        add_one(acc2, jnp.concatenate(hid, axis=0), [ds2[side, 1, s, :cols] for s in range(3)])
+        hid = order(side, hs[side, 1, :cols].T, hs_edge[side, :cols].T)
+        lefts.append(jnp.concatenate(hid, axis=0))
+        rights.append(jnp.concatenate([ds2[side, 1, s, :cols] for s in range(3)], axis=1))
+    add_dot(acc2, lefts, rights)
+    lefts, rights = [], []
+    for side in sides:
         own = f[near[side]].T
         for k in (1, 0):
-            feat = order(side, fs[side, 1, 1, :cols].T, own) if k == 0 else order(side, own, f[next_near[side]].T)
-            add_one(acc1, jnp.concatenate(feat, axis=0), [ds1[side, k, s, :cols] for s in range(3)])
+            feat = order(side, fs[side, 1, :cols].T, own) if k == 0 else order(side, own, f[next_near[side]].T)
+            lefts.append(jnp.concatenate(feat, axis=0))
+            rights.append(jnp.concatenate([ds1[side, k, s, :cols] for s in range(3)], axis=1))
+    add_dot(acc1, lefts, rights)
     take_terms(acc1, acc2, mine, other)
 
 
@@ -345,7 +369,7 @@
     return center + jnp.where(half_lanes(side), full, 0.0)
 
 
-def last_body(end, ds1_next, ds1, row, weights, gf, done, ends):
+def last_body(end, ds1_next, ds1, row, back, gf, done, ends):
     pairs, cols = gf.shape[:2]
     done[...] = jnp.zeros_like(done)
     odd = odd_place("row")
@@ -355,7 +379,7 @@
     store_shifts(with_row(end[1].astype(F32), from_next, 1), ends, 1)
     places = [(ends, 0), (ds1_next, 0)] + [(ds1, j) for j in range(pairs - 3)] + [(ds1_next, 1), (ends, 1)]
     for j in range(pairs):
-        gf[j] = band_dot(places[j], places[j + 1], weights.at[3])[:cols].astype(BF)
+        gf[j] = band_dot(places[j], places[j + 1], back.at[0])[:cols].astype(BF)
 
 
 def cost(pair_count):
@@ -365,7 +389,7 @@
 PARAMS = pltpu.CompilerParams(vmem_limit_bytes=32 * 2**20)
 
 
-def inner(f, g, edge, weights):
+def inner(f, g, edge, ahead, back):
     pairs, cols = f.shape[:2]
     wide = cols + RIM
 
@@ -375,7 +399,7 @@
     return pl.pallas_call(
         inner_body,
         out_shape=(
-            jax.ShapeDtypeStruct(shifts(2), BF),
+            jax.ShapeDtypeStruct((2, wide, LANES), BF),
             jax.ShapeDtypeStruct(shifts(2), BF),
             jax.ShapeDtypeStruct((2, wide, LANES), F32),
             jax.ShapeDtypeStruct(shifts(pairs - 3), BF),
@@ -383,8 +407,8 @@
             jax.ShapeDtypeStruct((2 * LANES, 3 * LANES), F32),
         ),
         scratch_shapes=[
-            pltpu.VMEM(shifts(pairs), BF),
-            pltpu.VMEM(shifts(pairs - 1), BF),
+            pltpu.VMEM((pairs, wide, LANES), BF),
+            pltpu.VMEM((pairs - 1, wide, LANES), BF),
             pltpu.VMEM(shifts(pairs - 2), BF),
             pltpu.VMEM((pairs - 1, wide, LANES), F32),
             pltpu.VMEM((pairs - 1, LANES, cols), BF),
@@ -393,7 +417,7 @@
         compiler_params=PARAMS,
         cost_estimate=cost(22),
         name="inner",
-    )(f, g, edge, weights)
+    )(f, g, edge, ahead, back)
 
 
 def outer(f, *rest):
@@ -413,8 +437,8 @@
             jax.ShapeDtypeStruct((9 * HALF // 2, LANES), F32),
         ),
         scratch_shapes=[
-            pltpu.VMEM(shifts(2, 3), BF),
-            pltpu.VMEM(shifts(2, 2), BF),
+            pltpu.VMEM((2, 3, wide, LANES), BF),
+            pltpu.VMEM((2, 2, wide, LANES), BF),
             pltpu.VMEM(shifts(2, 2), BF),
             pltpu.VMEM((2, wide, LANES), F32),
             pltpu.VMEM(shifts(2, 2), BF),
@@ -427,7 +451,7 @@
     )(f, *rest)
 
 
-def last(end, ds1_next, ds1, row, weights, cols):
+def last(end, ds1_next, ds1, row, back, cols):
     pairs = ds1.shape[0] + 3
     return pl.pallas_call(
         last_body,
@@ -439,7 +463,7 @@
         compiler_params=PARAMS,
         cost_estimate=cost(8),
         name="last",
-    )(end, ds1_next, ds1, row, weights)
+    )(end, ds1_next, ds1, row, back)
 
 
 def four_body(own, one, two, three, done, out):
@@ -530,7 +554,7 @@
     both = jnp.concatenate([features, grad_out], axis=2)
     from_left, from_right = swap(both[..., : RIM // 2], both[..., cols - RIM // 2 :], "col", turn)
     edge = jnp.concatenate([from_right, from_left], axis=1)
-    weights, own_near, own_far = prep(feat, grad, kernel_one, kernel_two)
+    ahead, back, own_near, own_far = prep(feat, grad, kernel_one, kernel_two)
     sent_near, sent_far = frame(own_near, own_far, edge)
     got_near = lax.ppermute(sent_near, "row", neighbours("row", 0))
     got_far = lax.ppermute(sent_far, "row", neighbours("row", 1))
@@ -538,12 +562,12 @@
     one, more = got_near[:2], got_near[2:]
     above = jnp.concatenate([jnp.where(odd, one, got_far), jnp.where(odd, more, jnp.zeros_like(more))])
     below = jnp.concatenate([jnp.where(odd, got_far, one), jnp.where(odd, jnp.zeros_like(more), more)])
-    hs_edge, ds2_edge, slope_edge, ds1, acc1, acc2 = inner(feat, grad, edge, weights)
+    hs_edge, ds2_edge, slope_edge, ds1, acc1, acc2 = inner(feat, grad, edge, ahead, back)
     ds1_next, end, row, mine, other = outer(
-        feat, grad, edge, above, below, weights, hs_edge, ds2_edge, slope_edge, acc1, acc2
+        feat, grad, edge, above, below, ahead, back, hs_edge, ds2_edge, slope_edge, acc1, acc2
     )
     row = lax.ppermute(row, "row", neighbours("row", 1))
-    gf, done = last(end, ds1_next, ds1, row, weights, cols)
+    gf, done = last(end, ds1_next, ds1, row, back, cols)
     part, other = reduced(mine, other, done)
     count = slides * lax.axis_size("dp") * rows * lax.axis_size("row") * cols * lax.axis_size("col")
     grad_one, grad_two = finish(part, other, float(count) ** -0.5)

time: 39.7 us -> 39.4 us (level)
  Pallas kernels: 8.23 us -> 7.47 us
  waiting for transfers between devices: 11 us -> 11.5 us
    pallas_call x2, Pallas kernels: 3.57 us -> 3.15 us  [the longest x1 2.8 us: inner(): pl.pallas_call(inner_body, out_shape=(jax.ShapeDtypeStruct((2, wide, LANE...]
    ppermute x1, waiting for transfers between devices: 2.78 us -> 3.2 us  [shards(): got_near = lax.ppermute(sent_near, 'row', neighbours('row', 0))]
  transfers between devices with their start and end apart: 12 -> 12, of which waited for: 8 -> 8; matrix products, arithmetic and copies ran while one was open for 6% -> 6% of each run, Pallas kernels for 12% -> 11%
where the time goes in v10:
time: 39.4 us; the launch traced here: 39.2 us
  starting transfers between devices  14.9 us (38%)
  waiting for transfers between devices  11.5 us (29%)
  Pallas kernels  7.47 us (19%)
  local copies, waits for them, and re-layouts  4.1 us (10%)
  between operations  0.85 us (2%)
    ppermute x6, starting transfers between devices, reduced(): got.append(lax.ppermute(low, AXES, perm))  8.47 us
    ppermute x6, waiting for transfers between devices, reduced(): got.append(lax.ppermute(low, AXES, perm))  6.84 us
    unnamed x12, local copies, waits for them, and re-layouts  3.29 us
    ppermute x1, waiting for transfers between devices, shards(): got_near = lax.ppermute(sent_near, 'row', neighbours('row', 0))  3.2 us
    ppermute x1, starting transfers between devices, swap(): got.append(lax.ppermute(turn(low, high, is_low(axis, parity)), axis, perm))  2.98 us
    pallas_call x1, Pallas kernels, inner(): pl.pallas_call(inner_body, out_shape=(jax.ShapeDtypeStruct((2, wide, LANE...  2.8 us
    ppermute x1, starting transfers between devices, shards(): got_near = lax.ppermute(sent_near, 'row', neighbours('row', 0))  1.99 us
    pallas_call x1, Pallas kernels, outer(): pl.pallas_call(rim_body, out_shape=(jax.ShapeDtypeStruct(shifts(2), BF),...  1.85 us
  transfers between devices with their start and end apart: 12, of which 8 were waited for; matrix products, arithmetic and copies ran while one was open for 6% of the time, Pallas kernels for 11%

profile of v10, /device:TPU:0, one launch (start us, length us, event | category | flops | bytes accessed | tf_op | source)
XLA Modules:
  0.0 39.2 jit_solution(680530869878579108)
XLA Ops:
  0.6 0.0 copy-start.3
  0.7 1.2 %constant_dynamic-update-slice_fusion.1 = bf16[1,64,32,256]{3,2,1,0:T(8,128)(2,1)S(1)} fusion(bf16[1,64,16,256]{3,2,1,0:T(8,128)(2,1)} %param.4), kind=kLoop, calls=%fused_computation.13 | loop fusion | bytes 1048576
  1.8 0.0 copy-done.3
  1.8 0.1 constant_dynamic-update-slice_fusion
  1.9 0.2 slice_select_fusion.refs_0_
  2.1 0.0 copy-start.2
  2.1 0.2 edges.1
  2.4 3.0 %collective-permute-start = (bf16[16,8,128]{2,1,0:T(8,128)(2,1)S(1)}, bf16[16,8,128]{2,1,0:T(8,128)(2,1)S(1)}, u32[]{:S(2)}, u32[]{:S(2)}) collective-permute-start(bf16[16,8,128]{2,1,0:T(8,128)(2,1)S(1)} %edges.1), channel_id=1, source_target_pairs={{0,1},{1,0},{2,3},{3,2},{4,5},{5,4},{6,7},{7,6},{8,9},{9,8},{10,11... | collective-permute-start | bytes 98312 | tf_op jit(solution)/shard_map/ppermute | solution.py:35
  5.3 0.0 copy-done.2
  5.3 0.2 copy.10
  5.5 0.2 copy.11
  5.7 0.3 copy.16.f
  5.9 0.0 copy-start
  6.0 0.0 copy-start.1
  6.0 0.3 copy.17.g
  6.3 0.6 %copy-done = bf16[3,3,64,64]{3,2,1,0:T(8,128)(2,1)S(1)} copy-done((bf16[3,3,64,64]{3,2,1,0:T(8,128)(2,1)S(1)}, bf16[3,3,64,64]{3,2,1,0:T(8,128)(2,1)}, u32[]{:S(2)}) %copy-start) | copy-done | bytes 73752
  6.9 0.1 copy-done.1
  6.9 0.3 prep.1
  7.3 0.0 collective-permute-done
  7.3 0.1 frame.1
  7.4 2.0 %collective-permute-start.1 = (bf16[3,272,128]{2,1,0:T(8,128)(2,1)S(1)}, bf16[3,272,128]{2,1,0:T(8,128)(2,1)S(1)}, u32[]{:S(2)}, u32[]{:S(2)}) collective-permute-start(bf16[3,272,128]{2,1,0:T(8,128)(2,1)S(1)} %get-tuple-element.26), channel_id=1, source_target_pairs={{0,2},{2,0},{4,6},{6,4},{8,10},{10,8},{12,14},{14,12},{1,3},{3,1},... | collective-permute-start | bytes 626696 | tf_op jit(solution)/shard_map/ppermute | solution.py:559
  9.4 0.7 %collective-permute-start.2 = (bf16[2,272,128]{2,1,0:T(8,128)(2,1)S(1)}, bf16[2,272,128]{2,1,0:T(8,128)(2,1)S(1)}, u32[]{:S(2)}, u32[]{:S(2)}) collective-permute-start(bf16[2,272,128]{2,1,0:T(8,128)(2,1)S(1)} %get-tuple-element.27), channel_id=1, source_target_pairs={{2,4},{4,2},{6,8},{8,6},{10,12},{12,10},{3,5},{5,3},{7,9},{9,7},{1... | collective-permute-start | bytes 417800 | tf_op jit(solution)/shard_map/ppermute | solution.py:560
  10.1 2.8 %inner.1 = (bf16[2,272,128]{2,1,0:T(8,128)(2,1)S(1)}, bf16[2,3,272,128]{3,2,1,0:T(8,128)(2,1)S(1)}, f32[2,272,128]{2,1,0:T(8,128)S(1)}, bf16[5,3,272,128]{3,2,1,...) custom-call(bf16[8,256,128]{2,1,0:T(8,128)(2,1)S(1)} %copy.16.f, bf16[8,256,128]{2,1,0:T(8,128)(2,1)S(1)} %copy.17.g, ...), custom_call_target="tpu_custom_call" | custom-call | flops 1176502272 | bytes 4194304 | tf_op jit(solution)/shard_map/inner/pallas_call | solution.py:399
  12.9 3.2 %collective-permute-done.1 = bf16[3,272,128]{2,1,0:T(8,128)(2,1)S(1)} collective-permute-done((bf16[3,272,128]{2,1,0:T(8,128)(2,1)S(1)}, bf16[3,272,128]{2,1,0:T(8,128)(2,1)S(1)}, u32[]{:S(2)}, u32[]{:S(2)}) %collective-permute-start.1) | collective-permute-done | bytes 208928 | tf_op jit(solution)/shard_map/ppermute | solution.py:559
  16.1 0.0 collective-permute-done.2
  16.2 1.9 %outer.1 = (bf16[2,3,272,128]{3,2,1,0:T(8,128)(2,1)S(1)}, bf16[2,272,128]{2,1,0:T(8,128)(2,1)S(1)}, bf16[144,128]{1,0:T(8,128)(2,1)S(1)}, f32[288,128]{1,0:T(8,128)S(1)}, f32[288,128]{1,0:T(8,128)S(1)}) custom-call(bf16[8,256,128]{2,1,0:T(8,128)(2,1)S(1)} %copy.16.f, bf16[8,256,128]{2,1,0:T(8,128)(2,1)S(1)} %copy.17.g, ...), custom_call_target="tpu_custom_call" | custom-call | flops 748683264 | bytes 4194304 | tf_op jit(solution)/shard_map/outer/pallas_call | solution.py:430
  18.1 0.1 collective-permute-start.4
  18.1 1.4 %collective-permute-done.4 = f32[288,128]{1,0:T(8,128)S(1)} collective-permute-done((f32[288,128]{1,0:T(8,128)S(1)}, f32[288,128]{1,0:T(8,128)S(1)}, u32[]{:S(2)}, u32[]{:S(2)}) %collective-permute-start.4) | collective-permute-done | bytes 147488 | tf_op jit(solution)/shard_map/ppermute | solution.py:511
  19.5 3.1 %collective-permute-start.7 = (bf16[288,128]{1,0:T(8,128)(2,1)S(1)}, bf16[288,128]{1,0:T(8,128)(2,1)S(1)}, u32[]{:S(2)}, u32[]{:S(2)}) collective-permute-start(bf16[288,128]{1,0:T(8,128)(2,1)S(1)} %add_convert_fusion.1), channel_id=1, source_target_pairs={{0,3},{1,2},{2,1},{3,0},{4,7},{5,6},{6,5},{7,4},{8,11},{9,10},{10,... | collective-permute-start | bytes 221192 | tf_op jit(solution)/shard_map/ppermute | solution.py:536
  22.6 0.9 %collective-permute-start.6 = (bf16[288,128]{1,0:T(8,128)(2,1)S(1)}, bf16[288,128]{1,0:T(8,128)(2,1)S(1)}, u32[]{:S(2)}, u32[]{:S(2)}) collective-permute-start(bf16[288,128]{1,0:T(8,128)(2,1)S(1)} %add_convert_fusion.1), channel_id=1, source_target_pairs={{0,1},{1,0},{2,3},{3,2},{4,5},{5,4},{6,7},{7,6},{8,9},{9,8},{10,11... | collective-permute-start | bytes 221192 | tf_op jit(solution)/shard_map/ppermute | solution.py:536
  23.5 0.0 collective-permute-start.5
  23.5 0.7 %collective-permute-start.3 = (bf16[144,128]{1,0:T(8,128)(2,1)S(1)}, bf16[144,128]{1,0:T(8,128)(2,1)S(1)}, u32[]{:S(2)}, u32[]{:S(2)}) collective-permute-start(bf16[144,128]{1,0:T(8,128)(2,1)S(1)} %get-tuple-element.38), channel_id=1, source_target_pairs={{2,4},{4,2},{6,8},{8,6},{10,12},{12,10},{3,5},{5,3},{7,9},{9,7},{1... | collective-permute-start | bytes 110600 | tf_op jit(solution)/shard_map/ppermute | solution.py:569
  24.2 0.8 %collective-permute-done.7 = bf16[288,128]{1,0:T(8,128)(2,1)S(1)} collective-permute-done((bf16[288,128]{1,0:T(8,128)(2,1)S(1)}, bf16[288,128]{1,0:T(8,128)(2,1)S(1)}, u32[]{:S(2)}, u32[]{:S(2)}) %collective-permute-start.7) | collective-permute-done | bytes 73760 | tf_op jit(solution)/shard_map/ppermute | solution.py:536
  25.0 2.0 %collective-permute-done.6 = bf16[288,128]{1,0:T(8,128)(2,1)S(1)} collective-permute-done((bf16[288,128]{1,0:T(8,128)(2,1)S(1)}, bf16[288,128]{1,0:T(8,128)(2,1)S(1)}, u32[]{:S(2)}, u32[]{:S(2)}) %collective-permute-start.6) | collective-permute-done | bytes 73760 | tf_op jit(solution)/shard_map/ppermute | solution.py:536
  27.0 0.9 %collective-permute-done.5 = bf16[288,128]{1,0:T(8,128)(2,1)S(1)} collective-permute-done((bf16[288,128]{1,0:T(8,128)(2,1)S(1)}, bf16[288,128]{1,0:T(8,128)(2,1)S(1)}, u32[]{:S(2)}, u32[]{:S(2)}) %collective-permute-start.5) | collective-permute-done | bytes 73760 | tf_op jit(solution)/shard_map/ppermute | solution.py:536
  27.9 3.2 %collective-permute-start.10 = (bf16[288,128]{1,0:T(8,128)(2,1)S(1)}, bf16[288,128]{1,0:T(8,128)(2,1)S(1)}, u32[]{:S(2)}, u32[]{:S(2)}) collective-permute-start(bf16[288,128]{1,0:T(8,128)(2,1)S(1)} %add_convert_fusion.own), channel_id=1, source_target_pairs={{0,12},{1,13},{2,14},{3,15},{4,8},{5,9},{6,10},{7,11},{8,4},{9,5},... | collective-permute-start | bytes 221192 | tf_op jit(solution)/shard_map/ppermute | solution.py:536
  31.1 0.0 collective-permute-start.9
  31.1 1.3 %collective-permute-start.8 = (bf16[288,128]{1,0:T(8,128)(2,1)S(1)}, bf16[288,128]{1,0:T(8,128)(2,1)S(1)}, u32[]{:S(2)}, u32[]{:S(2)}) collective-permute-start(bf16[288,128]{1,0:T(8,128)(2,1)S(1)} %add_convert_fusion.own), channel_id=1, source_target_pairs={{0,4},{1,5},{2,6},{3,7},{4,0},{5,1},{6,2},{7,3},{8,12},{9,13},{10,... | collective-permute-start | bytes 221192 | tf_op jit(solution)/shard_map/ppermute | solution.py:536
  32.4 0.0 collective-permute-done.3.row
  32.4 1.1 %last.1 = (bf16[8,256,128]{2,1,0:T(8,128)(2,1)S(1)}, f32[8,128]{1,0:T(8,128)S(1)}) custom-call(bf16[2,272,128]{2,1,0:T(8,128)(2,1)S(1)} %get-tuple-element.35.end, bf16[2,3,272,128]{3,2,1,0:T(8,128)(2,1)S(1)} %get-tuple-element.36.ds1_next, bf16[5,3,272,128]{3,2,1,0:T(8,128)(2,1)S(1)} %get-tuple-element.37.ds1, ...), custom_call_target="tpu_custom_call" | custom-call | flops 427819008 | bytes 4194304 | tf_op jit(solution)/shard_map/last/pallas_call | solution.py:456
  33.5 0.7 %collective-permute-done.10.three = bf16[288,128]{1,0:T(8,128)(2,1)S(1)} collective-permute-done((bf16[288,128]{1,0:T(8,128)(2,1)S(1)}, bf16[288,128]{1,0:T(8,128)(2,1)S(1)}, u32[]{:S(2)}, u32[]{:S(2)}) %collective-permute-start.10) | collective-permute-done | bytes 73760 | tf_op jit(solution)/shard_map/ppermute | solution.py:536
  34.2 2.5 %collective-permute-done.9.two = bf16[288,128]{1,0:T(8,128)(2,1)S(1)} collective-permute-done((bf16[288,128]{1,0:T(8,128)(2,1)S(1)}, bf16[288,128]{1,0:T(8,128)(2,1)S(1)}, u32[]{:S(2)}, u32[]{:S(2)}) %collective-permute-start.9) | collective-permute-done | bytes 73760 | tf_op jit(solution)/shard_map/ppermute | solution.py:536
  36.6 0.0 collective-permute-done.8.one
  36.7 0.1 collective-permute-start.11
  36.8 0.2 copy.18
  37.0 1.1 %copy.19 = bf16[1,64,16,256]{3,2,1,0:T(8,128)(2,1)} copy(bf16[1,64,16,256]{3,1,2,0:T(8,128)(2,1)S(1)} %bitcast.17) | data formatting | bytes 1048576
  38.1 0.1 collective-permute-done.11.other
  38.1 1.0 %finish.1 = (f32[3,3,64,64]{3,2,1,0:T(8,128)}, f32[3,3,64,64]{3,2,1,0:T(8,128)}) custom-call(f32[288,128]{1,0:T(8,128)S(1)} %sum_four.1.part, f32[288,128]{1,0:T(8,128)S(1)} %collective-permute-done.11.other), custom_call_target="tpu_custom_call" | custom-call | tf_op jit(solution)/shard_map/finish/pallas_call | solution.py:496
  (8 shorter events, 0.2 us)
Async XLA Ops:
  0.6 1.2 %copy-start.3 = (bf16[1,64,16,256]{3,2,1,0:T(8,128)(2,1)S(1)}, bf16[1,64,16,256]{3,2,1,0:T(8,128)(2,1)}, u32[]{:S(2)}) copy-start(bf16[1,64,16,256]{3,2,1,0:T(8,128)(2,1)} %param.5) | copy-start | bytes 1572868
  2.1 3.2 %copy-start.2 = (bf16[1,64,16,256]{3,2,1,0:T(8,128)(2,1)S(1)}, bf16[1,64,16,256]{3,2,1,0:T(8,128)(2,1)}, u32[]{:S(2)}) copy-start(bf16[1,64,16,256]{3,2,1,0:T(8,128)(2,1)} %param.4) | copy-start | bytes 1572868
  2.4 4.9 %collective-permute-start = (bf16[16,8,128]{2,1,0:T(8,128)(2,1)S(1)}, bf16[16,8,128]{2,1,0:T(8,128)(2,1)S(1)}, u32[]{:S(2)}, u32[]{:S(2)}) collective-permute-start(bf16[16,8,128]{2,1,0:T(8,128)(2,1)S(1)} %edges.1), channel_id=1, source_target_pairs={{0,1},{1,0},{2,3},{3,2},{4,5},{5,4},{6,7},{7,6},{8,9},{9,8},{10,11... | collective-permute-start | bytes 98312 | tf_op jit(solution)/shard_map/ppermute | solution.py:35
  5.9 0.9 %copy-start = (bf16[3,3,64,64]{3,2,1,0:T(8,128)(2,1)S(1)}, bf16[3,3,64,64]{3,2,1,0:T(8,128)(2,1)}, u32[]{:S(2)}) copy-start(bf16[3,3,64,64]{3,2,1,0:T(8,128)(2,1)} %k1.1) | copy-start | bytes 221188
  6.0 1.0 %copy-start.1 = (bf16[3,3,64,64]{3,2,1,0:T(8,128)(2,1)S(1)}, bf16[3,3,64,64]{3,2,1,0:T(8,128)(2,1)}, u32[]{:S(2)}) copy-start(bf16[3,3,64,64]{3,2,1,0:T(8,128)(2,1)} %k2.1) | copy-start | bytes 221188
  7.4 8.7 %collective-permute-start.1 = (bf16[3,272,128]{2,1,0:T(8,128)(2,1)S(1)}, bf16[3,272,128]{2,1,0:T(8,128)(2,1)S(1)}, u32[]{:S(2)}, u32[]{:S(2)}) collective-permute-start(bf16[3,272,128]{2,1,0:T(8,128)(2,1)S(1)} %get-tuple-element.26), channel_id=1, source_target_pairs={{0,2},{2,0},{4,6},{6,4},{8,10},{10,8},{12,14},{14,12},{1,3},{3,1},... | collective-permute-start | bytes 626696 | tf_op jit(solution)/shard_map/ppermute | solution.py:559
  9.4 6.7 %collective-permute-start.2 = (bf16[2,272,128]{2,1,0:T(8,128)(2,1)S(1)}, bf16[2,272,128]{2,1,0:T(8,128)(2,1)S(1)}, u32[]{:S(2)}, u32[]{:S(2)}) collective-permute-start(bf16[2,272,128]{2,1,0:T(8,128)(2,1)S(1)} %get-tuple-element.27), channel_id=1, source_target_pairs={{2,4},{4,2},{6,8},{8,6},{10,12},{12,10},{3,5},{5,3},{7,9},{9,7},{1... | collective-permute-start | bytes 417800 | tf_op jit(solution)/shard_map/ppermute | solution.py:560
  18.1 1.4 %collective-permute-start.4 = (f32[288,128]{1,0:T(8,128)S(1)}, f32[288,128]{1,0:T(8,128)S(1)}, u32[]{:S(2)}, u32[]{:S(2)}) collective-permute-start(f32[288,128]{1,0:T(8,128)S(1)} %get-tuple-element.41), channel_id=1, source_target_pairs={{0,16},{16,0},{1,17},{17,1},{2,18},{18,2},{3,19},{19,3},{4,20},{20... | collective-permute-start | bytes 442376 | tf_op jit(solution)/shard_map/ppermute | solution.py:511
  19.5 5.4 %collective-permute-start.7 = (bf16[288,128]{1,0:T(8,128)(2,1)S(1)}, bf16[288,128]{1,0:T(8,128)(2,1)S(1)}, u32[]{:S(2)}, u32[]{:S(2)}) collective-permute-start(bf16[288,128]{1,0:T(8,128)(2,1)S(1)} %add_convert_fusion.1), channel_id=1, source_target_pairs={{0,3},{1,2},{2,1},{3,0},{4,7},{5,6},{6,5},{7,4},{8,11},{9,10},{10,... | collective-permute-start | bytes 221192 | tf_op jit(solution)/shard_map/ppermute | solution.py:536
  22.6 4.4 %collective-permute-start.6 = (bf16[288,128]{1,0:T(8,128)(2,1)S(1)}, bf16[288,128]{1,0:T(8,128)(2,1)S(1)}, u32[]{:S(2)}, u32[]{:S(2)}) collective-permute-start(bf16[288,128]{1,0:T(8,128)(2,1)S(1)} %add_convert_fusion.1), channel_id=1, source_target_pairs={{0,1},{1,0},{2,3},{3,2},{4,5},{5,4},{6,7},{7,6},{8,9},{9,8},{10,11... | collective-permute-start | bytes 221192 | tf_op jit(solution)/shard_map/ppermute | solution.py:536
  23.5 4.4 %collective-permute-start.5 = (bf16[288,128]{1,0:T(8,128)(2,1)S(1)}, bf16[288,128]{1,0:T(8,128)(2,1)S(1)}, u32[]{:S(2)}, u32[]{:S(2)}) collective-permute-start(bf16[288,128]{1,0:T(8,128)(2,1)S(1)} %add_convert_fusion.1), channel_id=1, source_target_pairs={{0,2},{1,3},{2,0},{3,1},{4,6},{5,7},{6,4},{7,5},{8,10},{9,11},{10,... | collective-permute-start | bytes 221192 | tf_op jit(solution)/shard_map/ppermute | solution.py:536
  23.5 8.9 %collective-permute-start.3 = (bf16[144,128]{1,0:T(8,128)(2,1)S(1)}, bf16[144,128]{1,0:T(8,128)(2,1)S(1)}, u32[]{:S(2)}, u32[]{:S(2)}) collective-permute-start(bf16[144,128]{1,0:T(8,128)(2,1)S(1)} %get-tuple-element.38), channel_id=1, source_target_pairs={{2,4},{4,2},{6,8},{8,6},{10,12},{12,10},{3,5},{5,3},{7,9},{9,7},{1... | collective-permute-start | bytes 110600 | tf_op jit(solution)/shard_map/ppermute | solution.py:569
  27.9 6.2 %collective-permute-start.10 = (bf16[288,128]{1,0:T(8,128)(2,1)S(1)}, bf16[288,128]{1,0:T(8,128)(2,1)S(1)}, u32[]{:S(2)}, u32[]{:S(2)}) collective-permute-start(bf16[288,128]{1,0:T(8,128)(2,1)S(1)} %add_convert_fusion.own), channel_id=1, source_target_pairs={{0,12},{1,13},{2,14},{3,15},{4,8},{5,9},{6,10},{7,11},{8,4},{9,5},... | collective-permute-start | bytes 221192 | tf_op jit(solution)/shard_map/ppermute | solution.py:536
  31.1 5.5 %collective-permute-start.9 = (bf16[288,128]{1,0:T(8,128)(2,1)S(1)}, bf16[288,128]{1,0:T(8,128)(2,1)S(1)}, u32[]{:S(2)}, u32[]{:S(2)}) collective-permute-start(bf16[288,128]{1,0:T(8,128)(2,1)S(1)} %add_convert_fusion.own), channel_id=1, source_target_pairs={{0,8},{1,9},{2,10},{3,11},{4,12},{5,13},{6,14},{7,15},{8,0},{9,1},... | collective-permute-start | bytes 221192 | tf_op jit(solution)/shard_map/ppermute | solution.py:536
  31.1 5.5 %collective-permute-start.8 = (bf16[288,128]{1,0:T(8,128)(2,1)S(1)}, bf16[288,128]{1,0:T(8,128)(2,1)S(1)}, u32[]{:S(2)}, u32[]{:S(2)}) collective-permute-start(bf16[288,128]{1,0:T(8,128)(2,1)S(1)} %add_convert_fusion.own), channel_id=1, source_target_pairs={{0,4},{1,5},{2,6},{3,7},{4,0},{5,1},{6,2},{7,3},{8,12},{9,13},{10,... | collective-permute-start | bytes 221192 | tf_op jit(solution)/shard_map/ppermute | solution.py:536
  36.7 1.4 %collective-permute-start.11 = (f32[288,128]{1,0:T(8,128)S(1)}, f32[288,128]{1,0:T(8,128)S(1)}, u32[]{:S(2)}, u32[]{:S(2)}) collective-permute-start(f32[288,128]{1,0:T(8,128)S(1)} %sum_four.1.part), channel_id=1, source_target_pairs={{0,16},{16,0},{1,17},{17,1},{2,18},{18,2},{3,19},{19,3},{4,20},{20... | collective-permute-start | bytes 442376 | tf_op jit(solution)/shard_map/ppermute | solution.py:544

commit v11 on v10

--- a/solution.py
+++ b/solution.py
@@ -520,6 +520,7 @@
         mine = [groups[at], groups[(at + len(groups) // 2) % len(groups)]]
         if len(mine[0]) != len(mine[1]):
             mine[1] = mine[0]
+        mine.reverse()
         low = part.astype(BF)
         got = []
         for member in range(1, 1 << len(mine[0])):

time: 39.4 us -> 38.6 us (0.980)
  waiting for transfers between devices: 11.5 us -> 10.1 us
  starting transfers between devices: 14.9 us -> 15.4 us
    ppermute x6, waiting for transfers between devices: 6.84 us -> 5.52 us  [reduced(): got.append(lax.ppermute(low, AXES, perm))]
    ppermute x6, starting transfers between devices: 8.47 us -> 8.99 us  [reduced(): got.append(lax.ppermute(low, AXES, perm))]
where the time goes in v11:
time: 38.6 us; the launch traced here: 38.4 us
  starting transfers between devices  15.4 us (40%)
  waiting for transfers between devices  10.1 us (26%)
  Pallas kernels  7.47 us (19%)
  local copies, waits for them, and re-layouts  4.1 us (11%)
  between operations  0.85 us (2%)
  other arithmetic  0.39 us (1%)
    ppermute x6, starting transfers between devices, reduced(): got.append(lax.ppermute(low, AXES, perm))  8.99 us
    ppermute x6, waiting for transfers between devices, reduced(): got.append(lax.ppermute(low, AXES, perm))  5.52 us
    unnamed x12, local copies, waits for them, and re-layouts  3.29 us
    ppermute x1, waiting for transfers between devices, shards(): got_near = lax.ppermute(sent_near, 'row', neighbours('row', 0))  3.2 us
    ppermute x1, starting transfers between devices, swap(): got.append(lax.ppermute(turn(low, high, is_low(axis, parity)), axis, perm))  2.98 us
    pallas_call x1, Pallas kernels, inner(): pl.pallas_call(inner_body, out_shape=(jax.ShapeDtypeStruct((2, wide, LANE...  2.8 us
    ppermute x1, starting transfers between devices, shards(): got_near = lax.ppermute(sent_near, 'row', neighbours('row', 0))  1.99 us
    pallas_call x1, Pallas kernels, outer(): pl.pallas_call(rim_body, out_shape=(jax.ShapeDtypeStruct(shifts(2), BF),...  1.85 us
  transfers between devices with their start and end apart: 12, of which 8 were waited for; matrix products, arithmetic and copies ran while one was open for 6% of the time, Pallas kernels for 11%

profile of v11, /device:TPU:0, one launch (start us, length us, event | category | flops | bytes accessed | tf_op | source)
XLA Modules:
  0.0 38.4 jit_solution(1083035048216655248)
XLA Ops:
  0.6 0.0 copy-start.3
  0.7 1.2 %constant_dynamic-update-slice_fusion.1 = bf16[1,64,32,256]{3,2,1,0:T(8,128)(2,1)S(1)} fusion(bf16[1,64,16,256]{3,2,1,0:T(8,128)(2,1)} %param.4), kind=kLoop, calls=%fused_computation.13 | loop fusion | bytes 1048576
  1.8 0.0 copy-done.3
  1.8 0.1 constant_dynamic-update-slice_fusion
  1.9 0.2 slice_select_fusion.refs_0_
  2.1 0.0 copy-start.2
  2.1 0.2 edges.1
  2.4 3.0 %collective-permute-start = (bf16[16,8,128]{2,1,0:T(8,128)(2,1)S(1)}, bf16[16,8,128]{2,1,0:T(8,128)(2,1)S(1)}, u32[]{:S(2)}, u32[]{:S(2)}) collective-permute-start(bf16[16,8,128]{2,1,0:T(8,128)(2,1)S(1)} %edges.1), channel_id=1, source_target_pairs={{0,1},{1,0},{2,3},{3,2},{4,5},{5,4},{6,7},{7,6},{8,9},{9,8},{10,11... | collective-permute-start | bytes 98312 | tf_op jit(solution)/shard_map/ppermute | solution.py:35
  5.3 0.0 copy-done.2
  5.3 0.2 copy.10
  5.5 0.2 copy.11
  5.7 0.3 copy.16.f
  5.9 0.0 copy-start
  6.0 0.0 copy-start.1
  6.0 0.3 copy.17.g
  6.3 0.6 %copy-done = bf16[3,3,64,64]{3,2,1,0:T(8,128)(2,1)S(1)} copy-done((bf16[3,3,64,64]{3,2,1,0:T(8,128)(2,1)S(1)}, bf16[3,3,64,64]{3,2,1,0:T(8,128)(2,1)}, u32[]{:S(2)}) %copy-start) | copy-done | bytes 73752
  6.9 0.1 copy-done.1
  6.9 0.3 prep.1
  7.3 0.0 collective-permute-done
  7.3 0.1 frame.1
  7.4 2.0 %collective-permute-start.1 = (bf16[3,272,128]{2,1,0:T(8,128)(2,1)S(1)}, bf16[3,272,128]{2,1,0:T(8,128)(2,1)S(1)}, u32[]{:S(2)}, u32[]{:S(2)}) collective-permute-start(bf16[3,272,128]{2,1,0:T(8,128)(2,1)S(1)} %get-tuple-element.26), channel_id=1, source_target_pairs={{0,2},{2,0},{4,6},{6,4},{8,10},{10,8},{12,14},{14,12},{1,3},{3,1},... | collective-permute-start | bytes 626696 | tf_op jit(solution)/shard_map/ppermute | solution.py:560
  9.4 0.7 %collective-permute-start.2 = (bf16[2,272,128]{2,1,0:T(8,128)(2,1)S(1)}, bf16[2,272,128]{2,1,0:T(8,128)(2,1)S(1)}, u32[]{:S(2)}, u32[]{:S(2)}) collective-permute-start(bf16[2,272,128]{2,1,0:T(8,128)(2,1)S(1)} %get-tuple-element.27), channel_id=1, source_target_pairs={{2,4},{4,2},{6,8},{8,6},{10,12},{12,10},{3,5},{5,3},{7,9},{9,7},{1... | collective-permute-start | bytes 417800 | tf_op jit(solution)/shard_map/ppermute | solution.py:561
  10.1 2.8 %inner.1 = (bf16[2,272,128]{2,1,0:T(8,128)(2,1)S(1)}, bf16[2,3,272,128]{3,2,1,0:T(8,128)(2,1)S(1)}, f32[2,272,128]{2,1,0:T(8,128)S(1)}, bf16[5,3,272,128]{3,2,1,...) custom-call(bf16[8,256,128]{2,1,0:T(8,128)(2,1)S(1)} %copy.16.f, bf16[8,256,128]{2,1,0:T(8,128)(2,1)S(1)} %copy.17.g, ...), custom_call_target="tpu_custom_call" | custom-call | flops 1176502272 | bytes 4194304 | tf_op jit(solution)/shard_map/inner/pallas_call | solution.py:399
  12.9 3.2 %collective-permute-done.1 = bf16[3,272,128]{2,1,0:T(8,128)(2,1)S(1)} collective-permute-done((bf16[3,272,128]{2,1,0:T(8,128)(2,1)S(1)}, bf16[3,272,128]{2,1,0:T(8,128)(2,1)S(1)}, u32[]{:S(2)}, u32[]{:S(2)}) %collective-permute-start.1) | collective-permute-done | bytes 208928 | tf_op jit(solution)/shard_map/ppermute | solution.py:560
  16.1 0.0 collective-permute-done.2
  16.2 1.9 %outer.1 = (bf16[2,3,272,128]{3,2,1,0:T(8,128)(2,1)S(1)}, bf16[2,272,128]{2,1,0:T(8,128)(2,1)S(1)}, bf16[144,128]{1,0:T(8,128)(2,1)S(1)}, f32[288,128]{1,0:T(8,128)S(1)}, f32[288,128]{1,0:T(8,128)S(1)}) custom-call(bf16[8,256,128]{2,1,0:T(8,128)(2,1)S(1)} %copy.16.f, bf16[8,256,128]{2,1,0:T(8,128)(2,1)S(1)} %copy.17.g, ...), custom_call_target="tpu_custom_call" | custom-call | flops 748683264 | bytes 4194304 | tf_op jit(solution)/shard_map/outer/pallas_call | solution.py:430
  18.1 0.1 collective-permute-start.4
  18.1 1.4 %collective-permute-done.4 = f32[288,128]{1,0:T(8,128)S(1)} collective-permute-done((f32[288,128]{1,0:T(8,128)S(1)}, f32[288,128]{1,0:T(8,128)S(1)}, u32[]{:S(2)}, u32[]{:S(2)}) %collective-permute-start.4) | collective-permute-done | bytes 147488 | tf_op jit(solution)/shard_map/ppermute | solution.py:511
  19.5 4.8 %collective-permute-start.7 = (bf16[288,128]{1,0:T(8,128)(2,1)S(1)}, bf16[288,128]{1,0:T(8,128)(2,1)S(1)}, u32[]{:S(2)}, u32[]{:S(2)}) collective-permute-start(bf16[288,128]{1,0:T(8,128)(2,1)S(1)} %add_convert_fusion.1), channel_id=1, source_target_pairs={{0,12},{1,13},{2,14},{3,15},{4,8},{5,9},{6,10},{7,11},{8,4},{9,5},... | collective-permute-start | bytes 221192 | tf_op jit(solution)/shard_map/ppermute | solution.py:537
  24.3 0.0 collective-permute-start.6
  24.3 0.6 %collective-permute-start.5 = (bf16[288,128]{1,0:T(8,128)(2,1)S(1)}, bf16[288,128]{1,0:T(8,128)(2,1)S(1)}, u32[]{:S(2)}, u32[]{:S(2)}) collective-permute-start(bf16[288,128]{1,0:T(8,128)(2,1)S(1)} %add_convert_fusion.1), channel_id=1, source_target_pairs={{0,4},{1,5},{2,6},{3,7},{4,0},{5,1},{6,2},{7,3},{8,12},{9,13},{10,... | collective-permute-start | bytes 221192 | tf_op jit(solution)/shard_map/ppermute | solution.py:537
  25.0 0.7 %collective-permute-start.3 = (bf16[144,128]{1,0:T(8,128)(2,1)S(1)}, bf16[144,128]{1,0:T(8,128)(2,1)S(1)}, u32[]{:S(2)}, u32[]{:S(2)}) collective-permute-start(bf16[144,128]{1,0:T(8,128)(2,1)S(1)} %get-tuple-element.38), channel_id=1, source_target_pairs={{2,4},{4,2},{6,8},{8,6},{10,12},{12,10},{3,5},{5,3},{7,9},{9,7},{1... | collective-permute-start | bytes 110600 | tf_op jit(solution)/shard_map/ppermute | solution.py:570
  25.6 1.1 %collective-permute-done.7 = bf16[288,128]{1,0:T(8,128)(2,1)S(1)} collective-permute-done((bf16[288,128]{1,0:T(8,128)(2,1)S(1)}, bf16[288,128]{1,0:T(8,128)(2,1)S(1)}, u32[]{:S(2)}, u32[]{:S(2)}) %collective-permute-start.7) | collective-permute-done | bytes 73760 | tf_op jit(solution)/shard_map/ppermute | solution.py:537
  26.8 2.9 %collective-permute-done.6 = bf16[288,128]{1,0:T(8,128)(2,1)S(1)} collective-permute-done((bf16[288,128]{1,0:T(8,128)(2,1)S(1)}, bf16[288,128]{1,0:T(8,128)(2,1)S(1)}, u32[]{:S(2)}, u32[]{:S(2)}) %collective-permute-start.6) | collective-permute-done | bytes 73760 | tf_op jit(solution)/shard_map/ppermute | solution.py:537
  29.7 0.0 collective-permute-done.5
  29.7 1.1 %collective-permute-start.10 = (bf16[288,128]{1,0:T(8,128)(2,1)S(1)}, bf16[288,128]{1,0:T(8,128)(2,1)S(1)}, u32[]{:S(2)}, u32[]{:S(2)}) collective-permute-start(bf16[288,128]{1,0:T(8,128)(2,1)S(1)} %add_convert_fusion.own), channel_id=1, source_target_pairs={{0,3},{1,2},{2,1},{3,0},{4,7},{5,6},{6,5},{7,4},{8,11},{9,10},{10,... | collective-permute-start | bytes 221192 | tf_op jit(solution)/shard_map/ppermute | solution.py:537
  30.8 0.7 %collective-permute-start.9 = (bf16[288,128]{1,0:T(8,128)(2,1)S(1)}, bf16[288,128]{1,0:T(8,128)(2,1)S(1)}, u32[]{:S(2)}, u32[]{:S(2)}) collective-permute-start(bf16[288,128]{1,0:T(8,128)(2,1)S(1)} %add_convert_fusion.own), channel_id=1, source_target_pairs={{0,1},{1,0},{2,3},{3,2},{4,5},{5,4},{6,7},{7,6},{8,9},{9,8},{10,11... | collective-permute-start | bytes 221192 | tf_op jit(solution)/shard_map/ppermute | solution.py:537
  31.5 1.8 %collective-permute-start.8 = (bf16[288,128]{1,0:T(8,128)(2,1)S(1)}, bf16[288,128]{1,0:T(8,128)(2,1)S(1)}, u32[]{:S(2)}, u32[]{:S(2)}) collective-permute-start(bf16[288,128]{1,0:T(8,128)(2,1)S(1)} %add_convert_fusion.own), channel_id=1, source_target_pairs={{0,2},{1,3},{2,0},{3,1},{4,6},{5,7},{6,4},{7,5},{8,10},{9,11},{10,... | collective-permute-start | bytes 221192 | tf_op jit(solution)/shard_map/ppermute | solution.py:537
  33.3 0.0 collective-permute-done.3.row
  33.3 1.1 %last.1 = (bf16[8,256,128]{2,1,0:T(8,128)(2,1)S(1)}, f32[8,128]{1,0:T(8,128)S(1)}) custom-call(bf16[2,272,128]{2,1,0:T(8,128)(2,1)S(1)} %get-tuple-element.35.end, bf16[2,3,272,128]{3,2,1,0:T(8,128)(2,1)S(1)} %get-tuple-element.36.ds1_next, bf16[5,3,272,128]{3,2,1,0:T(8,128)(2,1)S(1)} %get-tuple-element.37.ds1, ...), custom_call_target="tpu_custom_call" | custom-call | flops 427819008 | bytes 4194304 | tf_op jit(solution)/shard_map/last/pallas_call | solution.py:456
  34.4 0.7 %collective-permute-done.10.three = bf16[288,128]{1,0:T(8,128)(2,1)S(1)} collective-permute-done((bf16[288,128]{1,0:T(8,128)(2,1)S(1)}, bf16[288,128]{1,0:T(8,128)(2,1)S(1)}, u32[]{:S(2)}, u32[]{:S(2)}) %collective-permute-start.10) | collective-permute-done | bytes 73760 | tf_op jit(solution)/shard_map/ppermute | solution.py:537
  35.0 0.1 collective-permute-done.9.two
  35.1 0.7 %collective-permute-done.8.one = bf16[288,128]{1,0:T(8,128)(2,1)S(1)} collective-permute-done((bf16[288,128]{1,0:T(8,128)(2,1)S(1)}, bf16[288,128]{1,0:T(8,128)(2,1)S(1)}, u32[]{:S(2)}, u32[]{:S(2)}) %collective-permute-start.8) | collective-permute-done | bytes 73760 | tf_op jit(solution)/shard_map/ppermute | solution.py:537
  35.9 0.1 collective-permute-start.11
  36.0 0.2 copy.18
  36.2 1.1 %copy.19 = bf16[1,64,16,256]{3,2,1,0:T(8,128)(2,1)} copy(bf16[1,64,16,256]{3,1,2,0:T(8,128)(2,1)S(1)} %bitcast.17) | data formatting | bytes 1048576
  37.3 0.1 collective-permute-done.11.other
  37.3 1.0 %finish.1 = (f32[3,3,64,64]{3,2,1,0:T(8,128)}, f32[3,3,64,64]{3,2,1,0:T(8,128)}) custom-call(f32[288,128]{1,0:T(8,128)S(1)} %sum_four.1.part, f32[288,128]{1,0:T(8,128)S(1)} %collective-permute-done.11.other), custom_call_target="tpu_custom_call" | custom-call | tf_op jit(solution)/shard_map/finish/pallas_call | solution.py:496
  (8 shorter events, 0.2 us)
Async XLA Ops:
  0.6 1.2 %copy-start.3 = (bf16[1,64,16,256]{3,2,1,0:T(8,128)(2,1)S(1)}, bf16[1,64,16,256]{3,2,1,0:T(8,128)(2,1)}, u32[]{:S(2)}) copy-start(bf16[1,64,16,256]{3,2,1,0:T(8,128)(2,1)} %param.5) | copy-start | bytes 1572868
  2.1 3.2 %copy-start.2 = (bf16[1,64,16,256]{3,2,1,0:T(8,128)(2,1)S(1)}, bf16[1,64,16,256]{3,2,1,0:T(8,128)(2,1)}, u32[]{:S(2)}) copy-start(bf16[1,64,16,256]{3,2,1,0:T(8,128)(2,1)} %param.4) | copy-start | bytes 1572868
  2.4 4.9 %collective-permute-start = (bf16[16,8,128]{2,1,0:T(8,128)(2,1)S(1)}, bf16[16,8,128]{2,1,0:T(8,128)(2,1)S(1)}, u32[]{:S(2)}, u32[]{:S(2)}) collective-permute-start(bf16[16,8,128]{2,1,0:T(8,128)(2,1)S(1)} %edges.1), channel_id=1, source_target_pairs={{0,1},{1,0},{2,3},{3,2},{4,5},{5,4},{6,7},{7,6},{8,9},{9,8},{10,11... | collective-permute-start | bytes 98312 | tf_op jit(solution)/shard_map/ppermute | solution.py:35
  5.9 0.9 %copy-start = (bf16[3,3,64,64]{3,2,1,0:T(8,128)(2,1)S(1)}, bf16[3,3,64,64]{3,2,1,0:T(8,128)(2,1)}, u32[]{:S(2)}) copy-start(bf16[3,3,64,64]{3,2,1,0:T(8,128)(2,1)} %k1.1) | copy-start | bytes 221188
  6.0 1.0 %copy-start.1 = (bf16[3,3,64,64]{3,2,1,0:T(8,128)(2,1)S(1)}, bf16[3,3,64,64]{3,2,1,0:T(8,128)(2,1)}, u32[]{:S(2)}) copy-start(bf16[3,3,64,64]{3,2,1,0:T(8,128)(2,1)} %k2.1) | copy-start | bytes 221188
  7.4 8.7 %collective-permute-start.1 = (bf16[3,272,128]{2,1,0:T(8,128)(2,1)S(1)}, bf16[3,272,128]{2,1,0:T(8,128)(2,1)S(1)}, u32[]{:S(2)}, u32[]{:S(2)}) collective-permute-start(bf16[3,272,128]{2,1,0:T(8,128)(2,1)S(1)} %get-tuple-element.26), channel_id=1, source_target_pairs={{0,2},{2,0},{4,6},{6,4},{8,10},{10,8},{12,14},{14,12},{1,3},{3,1},... | collective-permute-start | bytes 626696 | tf_op jit(solution)/shard_map/ppermute | solution.py:560
  9.4 6.7 %collective-permute-start.2 = (bf16[2,272,128]{2,1,0:T(8,128)(2,1)S(1)}, bf16[2,272,128]{2,1,0:T(8,128)(2,1)S(1)}, u32[]{:S(2)}, u32[]{:S(2)}) collective-permute-start(bf16[2,272,128]{2,1,0:T(8,128)(2,1)S(1)} %get-tuple-element.27), channel_id=1, source_target_pairs={{2,4},{4,2},{6,8},{8,6},{10,12},{12,10},{3,5},{5,3},{7,9},{9,7},{1... | collective-permute-start | bytes 417800 | tf_op jit(solution)/shard_map/ppermute | solution.py:561
  18.1 1.4 %collective-permute-start.4 = (f32[288,128]{1,0:T(8,128)S(1)}, f32[288,128]{1,0:T(8,128)S(1)}, u32[]{:S(2)}, u32[]{:S(2)}) collective-permute-start(f32[288,128]{1,0:T(8,128)S(1)} %get-tuple-element.41), channel_id=1, source_target_pairs={{0,16},{16,0},{1,17},{17,1},{2,18},{18,2},{3,19},{19,3},{4,20},{20... | collective-permute-start | bytes 442376 | tf_op jit(solution)/shard_map/ppermute | solution.py:511
  19.5 7.2 %collective-permute-start.7 = (bf16[288,128]{1,0:T(8,128)(2,1)S(1)}, bf16[288,128]{1,0:T(8,128)(2,1)S(1)}, u32[]{:S(2)}, u32[]{:S(2)}) collective-permute-start(bf16[288,128]{1,0:T(8,128)(2,1)S(1)} %add_convert_fusion.1), channel_id=1, source_target_pairs={{0,12},{1,13},{2,14},{3,15},{4,8},{5,9},{6,10},{7,11},{8,4},{9,5},... | collective-permute-start | bytes 221192 | tf_op jit(solution)/shard_map/ppermute | solution.py:537
  24.3 5.4 %collective-permute-start.6 = (bf16[288,128]{1,0:T(8,128)(2,1)S(1)}, bf16[288,128]{1,0:T(8,128)(2,1)S(1)}, u32[]{:S(2)}, u32[]{:S(2)}) collective-permute-start(bf16[288,128]{1,0:T(8,128)(2,1)S(1)} %add_convert_fusion.1), channel_id=1, source_target_pairs={{0,8},{1,9},{2,10},{3,11},{4,12},{5,13},{6,14},{7,15},{8,0},{9,1},... | collective-permute-start | bytes 221192 | tf_op jit(solution)/shard_map/ppermute | solution.py:537
  24.3 5.4 %collective-permute-start.5 = (bf16[288,128]{1,0:T(8,128)(2,1)S(1)}, bf16[288,128]{1,0:T(8,128)(2,1)S(1)}, u32[]{:S(2)}, u32[]{:S(2)}) collective-permute-start(bf16[288,128]{1,0:T(8,128)(2,1)S(1)} %add_convert_fusion.1), channel_id=1, source_target_pairs={{0,4},{1,5},{2,6},{3,7},{4,0},{5,1},{6,2},{7,3},{8,12},{9,13},{10,... | collective-permute-start | bytes 221192 | tf_op jit(solution)/shard_map/ppermute | solution.py:537
  25.0 8.3 %collective-permute-start.3 = (bf16[144,128]{1,0:T(8,128)(2,1)S(1)}, bf16[144,128]{1,0:T(8,128)(2,1)S(1)}, u32[]{:S(2)}, u32[]{:S(2)}) collective-permute-start(bf16[144,128]{1,0:T(8,128)(2,1)S(1)} %get-tuple-element.38), channel_id=1, source_target_pairs={{2,4},{4,2},{6,8},{8,6},{10,12},{12,10},{3,5},{5,3},{7,9},{9,7},{1... | collective-permute-start | bytes 110600 | tf_op jit(solution)/shard_map/ppermute | solution.py:570
  29.7 5.3 %collective-permute-start.10 = (bf16[288,128]{1,0:T(8,128)(2,1)S(1)}, bf16[288,128]{1,0:T(8,128)(2,1)S(1)}, u32[]{:S(2)}, u32[]{:S(2)}) collective-permute-start(bf16[288,128]{1,0:T(8,128)(2,1)S(1)} %add_convert_fusion.own), channel_id=1, source_target_pairs={{0,3},{1,2},{2,1},{3,0},{4,7},{5,6},{6,5},{7,4},{8,11},{9,10},{10,... | collective-permute-start | bytes 221192 | tf_op jit(solution)/shard_map/ppermute | solution.py:537
  30.8 4.4 %collective-permute-start.9 = (bf16[288,128]{1,0:T(8,128)(2,1)S(1)}, bf16[288,128]{1,0:T(8,128)(2,1)S(1)}, u32[]{:S(2)}, u32[]{:S(2)}) collective-permute-start(bf16[288,128]{1,0:T(8,128)(2,1)S(1)} %add_convert_fusion.own), channel_id=1, source_target_pairs={{0,1},{1,0},{2,3},{3,2},{4,5},{5,4},{6,7},{7,6},{8,9},{9,8},{10,11... | collective-permute-start | bytes 221192 | tf_op jit(solution)/shard_map/ppermute | solution.py:537
  31.5 4.4 %collective-permute-start.8 = (bf16[288,128]{1,0:T(8,128)(2,1)S(1)}, bf16[288,128]{1,0:T(8,128)(2,1)S(1)}, u32[]{:S(2)}, u32[]{:S(2)}) collective-permute-start(bf16[288,128]{1,0:T(8,128)(2,1)S(1)} %add_convert_fusion.own), channel_id=1, source_target_pairs={{0,2},{1,3},{2,0},{3,1},{4,6},{5,7},{6,4},{7,5},{8,10},{9,11},{10,... | collective-permute-start | bytes 221192 | tf_op jit(solution)/shard_map/ppermute | solution.py:537
  35.9 1.4 %collective-permute-start.11 = (f32[288,128]{1,0:T(8,128)S(1)}, f32[288,128]{1,0:T(8,128)S(1)}, u32[]{:S(2)}, u32[]{:S(2)}) collective-permute-start(f32[288,128]{1,0:T(8,128)S(1)} %sum_four.1.part), channel_id=1, source_target_pairs={{0,16},{16,0},{1,17},{17,1},{2,18},{18,2},{3,19},{19,3},{4,20},{20... | collective-permute-start | bytes 442376 | tf_op jit(solution)/shard_map/ppermute | solution.py:545

commit v12 on v11

--- a/solution.py
+++ b/solution.py
@@ -88,6 +88,10 @@
                     ahead[layer, at : at + HALF, kx * LANES : (kx + 1) * LANES] = jnp.concatenate(
                         [turned.get((ky, kx), zero) for ky in kys], axis=1
                     )
+                    if layer == 1:
+                        ahead[2, at : at + HALF, kx * LANES : (kx + 1) * LANES] = jnp.concatenate(
+                            [flat.get((2 - ky, 2 - kx), zero) for ky in kys], axis=1
+                        )
                     to = ((p * 3 + kx) * 2 + r) * HALF
                     back[layer, to : to + HALF] = jnp.concatenate(
                         [flat.get((2 - ky, 2 - kx), zero) for ky in kys], axis=1
@@ -114,7 +118,7 @@
 
 
 def prep(feat, grad, kernel_one, kernel_two):
-    weights = [jax.ShapeDtypeStruct(shape, BF) for shape in ((2, 4 * HALF, 3 * LANES), (2, 12 * HALF, LANES))]
+    weights = [jax.ShapeDtypeStruct(shape, BF) for shape in ((3, 4 * HALF, 3 * LANES), (2, 12 * HALF, LANES))]
     sent = [jax.ShapeDtypeStruct((units, *feat.shape[1:]), BF) for units in (3, 2)]
     return pl.pallas_call(
         prep_body,
@@ -284,7 +288,7 @@
     top, bottom, rim = edge_masks()
     flags = (top, bottom)
     beyond = [half_lanes(side) for side in range(2)]
-    w1, w2, v2 = ahead.at[0], ahead.at[1], back.at[1]
+    w1, w2, v2 = ahead.at[0], ahead.at[1], ahead.at[2]
     rows = []
     odd = odd_place("row")
     known = jnp.where(odd, top, 0.0), jnp.where(odd, 0.0, bottom)
@@ -318,11 +322,14 @@
             pre = row_dot(*order(side, hs[side, k], inward), w2)
             sig = sigmoid(pre)
             delta = grad * (sig + pre * sig * (1.0 - sig))
-            store_shifts(delta, ds2.at[side], k)
+            if k == 1:
+                store_shifts(delta, ds2.at[side], k)
+            else:
+                ds2[side, 0, 1] = delta.astype(BF)
     for k in (1, 0):
         for side in sides:
-            inward = (ds2.at[side], 1) if k == 0 else (ds2_edge, side)
-            value = band_dot(*order(side, (ds2.at[side], k), inward), v2)
+            inward = ds2[side, 1, 1] if k == 0 else ds2_edge[side, 1]
+            value = row_dot(*order(side, ds2[side, k, 1], inward), v2)
             value = value * (slope[side] if k == 0 else slope_edge[side])
             value = rim_masked(value, rim)
             if k == 0:

time: 38.6 us -> 38.4 us (level)
  no operation moved by 1% of the time
where the time goes in v12:
time: 38.4 us; the launch traced here: 38.2 us
  starting transfers between devices  15.4 us (40%)
  waiting for transfers between devices  10.1 us (26%)
  Pallas kernels  7.32 us (19%)
  local copies, waits for them, and re-layouts  4.1 us (11%)
  between operations  0.85 us (2%)
  other arithmetic  0.39 us (1%)
    ppermute x6, starting transfers between devices, reduced(): got.append(lax.ppermute(low, AXES, perm))  9 us
    ppermute x6, waiting for transfers between devices, reduced(): got.append(lax.ppermute(low, AXES, perm))  5.51 us
    unnamed x12, local copies, waits for them, and re-layouts  3.29 us
    ppermute x1, waiting for transfers between devices, shards(): got_near = lax.ppermute(sent_near, 'row', neighbours('row', 0))  3.2 us
    ppermute x1, starting transfers between devices, swap(): got.append(lax.ppermute(turn(low, high, is_low(axis, parity)), axis, perm))  2.98 us
    pallas_call x1, Pallas kernels, inner(): pl.pallas_call(inner_body, out_shape=(jax.ShapeDtypeStruct((2, wide, LANE...  2.8 us
    ppermute x1, starting transfers between devices, shards(): got_near = lax.ppermute(sent_near, 'row', neighbours('row', 0))  1.99 us
    pallas_call x1, Pallas kernels, outer(): pl.pallas_call(rim_body, out_shape=(jax.ShapeDtypeStruct(shifts(2), BF),...  1.7 us
  transfers between devices with their start and end apart: 12, of which 8 were waited for; matrix products, arithmetic and copies ran while one was open for 6% of the time, Pallas kernels for 11%

profile of v12, /device:TPU:0, one launch (start us, length us, event | category | flops | bytes accessed | tf_op | source)
XLA Modules:
  0.0 38.2 jit_solution(15328134538102014722)
XLA Ops:
  0.6 0.0 copy-start.3
  0.7 1.2 %constant_dynamic-update-slice_fusion.1 = bf16[1,64,32,256]{3,2,1,0:T(8,128)(2,1)S(1)} fusion(bf16[1,64,16,256]{3,2,1,0:T(8,128)(2,1)} %param.4), kind=kLoop, calls=%fused_computation.13 | loop fusion | bytes 1048576
  1.8 0.0 copy-done.3
  1.8 0.1 constant_dynamic-update-slice_fusion
  1.9 0.2 slice_select_fusion.refs_0_
  2.1 0.0 copy-start.2
  2.1 0.2 edges.1
  2.4 3.0 %collective-permute-start = (bf16[16,8,128]{2,1,0:T(8,128)(2,1)S(1)}, bf16[16,8,128]{2,1,0:T(8,128)(2,1)S(1)}, u32[]{:S(2)}, u32[]{:S(2)}) collective-permute-start(bf16[16,8,128]{2,1,0:T(8,128)(2,1)S(1)} %edges.1), channel_id=1, source_target_pairs={{0,1},{1,0},{2,3},{3,2},{4,5},{5,4},{6,7},{7,6},{8,9},{9,8},{10,11... | collective-permute-start | bytes 98312 | tf_op jit(solution)/shard_map/ppermute | solution.py:35
  5.3 0.0 copy-done.2
  5.3 0.2 copy.10
  5.5 0.2 copy.11
  5.7 0.3 copy.16.f
  5.9 0.0 copy-start
  6.0 0.0 copy-start.1
  6.0 0.3 copy.17.g
  6.3 0.6 %copy-done = bf16[3,3,64,64]{3,2,1,0:T(8,128)(2,1)S(1)} copy-done((bf16[3,3,64,64]{3,2,1,0:T(8,128)(2,1)S(1)}, bf16[3,3,64,64]{3,2,1,0:T(8,128)(2,1)}, u32[]{:S(2)}) %copy-start) | copy-done | bytes 73752
  6.9 0.1 copy-done.1
  6.9 0.3 prep.1
  7.3 0.0 collective-permute-done
  7.3 0.1 frame.1
  7.4 2.0 %collective-permute-start.1 = (bf16[3,272,128]{2,1,0:T(8,128)(2,1)S(1)}, bf16[3,272,128]{2,1,0:T(8,128)(2,1)S(1)}, u32[]{:S(2)}, u32[]{:S(2)}) collective-permute-start(bf16[3,272,128]{2,1,0:T(8,128)(2,1)S(1)} %get-tuple-element.26), channel_id=1, source_target_pairs={{0,2},{2,0},{4,6},{6,4},{8,10},{10,8},{12,14},{14,12},{1,3},{3,1},... | collective-permute-start | bytes 626696 | tf_op jit(solution)/shard_map/ppermute | solution.py:567
  9.4 0.7 %collective-permute-start.2 = (bf16[2,272,128]{2,1,0:T(8,128)(2,1)S(1)}, bf16[2,272,128]{2,1,0:T(8,128)(2,1)S(1)}, u32[]{:S(2)}, u32[]{:S(2)}) collective-permute-start(bf16[2,272,128]{2,1,0:T(8,128)(2,1)S(1)} %get-tuple-element.27), channel_id=1, source_target_pairs={{2,4},{4,2},{6,8},{8,6},{10,12},{12,10},{3,5},{5,3},{7,9},{9,7},{1... | collective-permute-start | bytes 417800 | tf_op jit(solution)/shard_map/ppermute | solution.py:568
  10.1 2.8 %inner.1 = (bf16[2,272,128]{2,1,0:T(8,128)(2,1)S(1)}, bf16[2,3,272,128]{3,2,1,0:T(8,128)(2,1)S(1)}, f32[2,272,128]{2,1,0:T(8,128)S(1)}, bf16[5,3,272,128]{3,2,1,...) custom-call(bf16[8,256,128]{2,1,0:T(8,128)(2,1)S(1)} %copy.16.f, bf16[8,256,128]{2,1,0:T(8,128)(2,1)S(1)} %copy.17.g, ...), custom_call_target="tpu_custom_call" | custom-call | flops 1176502272 | bytes 4194304 | tf_op jit(solution)/shard_map/inner/pallas_call | solution.py:406
  12.9 3.2 %collective-permute-done.1 = bf16[3,272,128]{2,1,0:T(8,128)(2,1)S(1)} collective-permute-done((bf16[3,272,128]{2,1,0:T(8,128)(2,1)S(1)}, bf16[3,272,128]{2,1,0:T(8,128)(2,1)S(1)}, u32[]{:S(2)}, u32[]{:S(2)}) %collective-permute-start.1) | collective-permute-done | bytes 208928 | tf_op jit(solution)/shard_map/ppermute | solution.py:567
  16.1 0.0 collective-permute-done.2
  16.2 1.7 %outer.1 = (bf16[2,3,272,128]{3,2,1,0:T(8,128)(2,1)S(1)}, bf16[2,272,128]{2,1,0:T(8,128)(2,1)S(1)}, bf16[144,128]{1,0:T(8,128)(2,1)S(1)}, f32[288,128]{1,0:T(8,128)S(1)}, f32[288,128]{1,0:T(8,128)S(1)}) custom-call(bf16[8,256,128]{2,1,0:T(8,128)(2,1)S(1)} %copy.16.f, bf16[8,256,128]{2,1,0:T(8,128)(2,1)S(1)} %copy.17.g, ...), custom_call_target="tpu_custom_call" | custom-call | flops 748683264 | bytes 4194304 | tf_op jit(solution)/shard_map/outer/pallas_call | solution.py:437
  17.9 0.1 collective-permute-start.4
  18.0 1.4 %collective-permute-done.4 = f32[288,128]{1,0:T(8,128)S(1)} collective-permute-done((f32[288,128]{1,0:T(8,128)S(1)}, f32[288,128]{1,0:T(8,128)S(1)}, u32[]{:S(2)}, u32[]{:S(2)}) %collective-permute-start.4) | collective-permute-done | bytes 147488 | tf_op jit(solution)/shard_map/ppermute | solution.py:518
  19.4 4.8 %collective-permute-start.7 = (bf16[288,128]{1,0:T(8,128)(2,1)S(1)}, bf16[288,128]{1,0:T(8,128)(2,1)S(1)}, u32[]{:S(2)}, u32[]{:S(2)}) collective-permute-start(bf16[288,128]{1,0:T(8,128)(2,1)S(1)} %add_convert_fusion.1), channel_id=1, source_target_pairs={{0,12},{1,13},{2,14},{3,15},{4,8},{5,9},{6,10},{7,11},{8,4},{9,5},... | collective-permute-start | bytes 221192 | tf_op jit(solution)/shard_map/ppermute | solution.py:544
  24.2 0.0 collective-permute-start.6
  24.2 0.6 %collective-permute-start.5 = (bf16[288,128]{1,0:T(8,128)(2,1)S(1)}, bf16[288,128]{1,0:T(8,128)(2,1)S(1)}, u32[]{:S(2)}, u32[]{:S(2)}) collective-permute-start(bf16[288,128]{1,0:T(8,128)(2,1)S(1)} %add_convert_fusion.1), channel_id=1, source_target_pairs={{0,4},{1,5},{2,6},{3,7},{4,0},{5,1},{6,2},{7,3},{8,12},{9,13},{10,... | collective-permute-start | bytes 221192 | tf_op jit(solution)/shard_map/ppermute | solution.py:544
  24.8 0.7 %collective-permute-start.3 = (bf16[144,128]{1,0:T(8,128)(2,1)S(1)}, bf16[144,128]{1,0:T(8,128)(2,1)S(1)}, u32[]{:S(2)}, u32[]{:S(2)}) collective-permute-start(bf16[144,128]{1,0:T(8,128)(2,1)S(1)} %get-tuple-element.38), channel_id=1, source_target_pairs={{2,4},{4,2},{6,8},{8,6},{10,12},{12,10},{3,5},{5,3},{7,9},{9,7},{1... | collective-permute-start | bytes 110600 | tf_op jit(solution)/shard_map/ppermute | solution.py:577
  25.5 1.1 %collective-permute-done.7 = bf16[288,128]{1,0:T(8,128)(2,1)S(1)} collective-permute-done((bf16[288,128]{1,0:T(8,128)(2,1)S(1)}, bf16[288,128]{1,0:T(8,128)(2,1)S(1)}, u32[]{:S(2)}, u32[]{:S(2)}) %collective-permute-start.7) | collective-permute-done | bytes 73760 | tf_op jit(solution)/shard_map/ppermute | solution.py:544
  26.6 2.9 %collective-permute-done.6 = bf16[288,128]{1,0:T(8,128)(2,1)S(1)} collective-permute-done((bf16[288,128]{1,0:T(8,128)(2,1)S(1)}, bf16[288,128]{1,0:T(8,128)(2,1)S(1)}, u32[]{:S(2)}, u32[]{:S(2)}) %collective-permute-start.6) | collective-permute-done | bytes 73760 | tf_op jit(solution)/shard_map/ppermute | solution.py:544
  29.5 0.0 collective-permute-done.5
  29.6 1.1 %collective-permute-start.10 = (bf16[288,128]{1,0:T(8,128)(2,1)S(1)}, bf16[288,128]{1,0:T(8,128)(2,1)S(1)}, u32[]{:S(2)}, u32[]{:S(2)}) collective-permute-start(bf16[288,128]{1,0:T(8,128)(2,1)S(1)} %add_convert_fusion.own), channel_id=1, source_target_pairs={{0,3},{1,2},{2,1},{3,0},{4,7},{5,6},{6,5},{7,4},{8,11},{9,10},{10,... | collective-permute-start | bytes 221192 | tf_op jit(solution)/shard_map/ppermute | solution.py:544
  30.6 0.7 %collective-permute-start.9 = (bf16[288,128]{1,0:T(8,128)(2,1)S(1)}, bf16[288,128]{1,0:T(8,128)(2,1)S(1)}, u32[]{:S(2)}, u32[]{:S(2)}) collective-permute-start(bf16[288,128]{1,0:T(8,128)(2,1)S(1)} %add_convert_fusion.own), channel_id=1, source_target_pairs={{0,1},{1,0},{2,3},{3,2},{4,5},{5,4},{6,7},{7,6},{8,9},{9,8},{10,11... | collective-permute-start | bytes 221192 | tf_op jit(solution)/shard_map/ppermute | solution.py:544
  31.3 1.8 %collective-permute-start.8 = (bf16[288,128]{1,0:T(8,128)(2,1)S(1)}, bf16[288,128]{1,0:T(8,128)(2,1)S(1)}, u32[]{:S(2)}, u32[]{:S(2)}) collective-permute-start(bf16[288,128]{1,0:T(8,128)(2,1)S(1)} %add_convert_fusion.own), channel_id=1, source_target_pairs={{0,2},{1,3},{2,0},{3,1},{4,6},{5,7},{6,4},{7,5},{8,10},{9,11},{10,... | collective-permute-start | bytes 221192 | tf_op jit(solution)/shard_map/ppermute | solution.py:544
  33.1 0.0 collective-permute-done.3.row
  33.1 1.1 %last.1 = (bf16[8,256,128]{2,1,0:T(8,128)(2,1)S(1)}, f32[8,128]{1,0:T(8,128)S(1)}) custom-call(bf16[2,272,128]{2,1,0:T(8,128)(2,1)S(1)} %get-tuple-element.35.end, bf16[2,3,272,128]{3,2,1,0:T(8,128)(2,1)S(1)} %get-tuple-element.36.ds1_next, bf16[5,3,272,128]{3,2,1,0:T(8,128)(2,1)S(1)} %get-tuple-element.37.ds1, ...), custom_call_target="tpu_custom_call" | custom-call | flops 427819008 | bytes 4194304 | tf_op jit(solution)/shard_map/last/pallas_call | solution.py:463
  34.2 0.7 %collective-permute-done.10.three = bf16[288,128]{1,0:T(8,128)(2,1)S(1)} collective-permute-done((bf16[288,128]{1,0:T(8,128)(2,1)S(1)}, bf16[288,128]{1,0:T(8,128)(2,1)S(1)}, u32[]{:S(2)}, u32[]{:S(2)}) %collective-permute-start.10) | collective-permute-done | bytes 73760 | tf_op jit(solution)/shard_map/ppermute | solution.py:544
  34.9 0.1 collective-permute-done.9.two
  35.0 0.7 %collective-permute-done.8.one = bf16[288,128]{1,0:T(8,128)(2,1)S(1)} collective-permute-done((bf16[288,128]{1,0:T(8,128)(2,1)S(1)}, bf16[288,128]{1,0:T(8,128)(2,1)S(1)}, u32[]{:S(2)}, u32[]{:S(2)}) %collective-permute-start.8) | collective-permute-done | bytes 73760 | tf_op jit(solution)/shard_map/ppermute | solution.py:544
  35.7 0.1 collective-permute-start.11
  35.8 0.2 copy.18
  36.0 1.1 %copy.19 = bf16[1,64,16,256]{3,2,1,0:T(8,128)(2,1)} copy(bf16[1,64,16,256]{3,1,2,0:T(8,128)(2,1)S(1)} %bitcast.17) | data formatting | bytes 1048576
  37.1 0.1 collective-permute-done.11.other
  37.2 1.0 %finish.1 = (f32[3,3,64,64]{3,2,1,0:T(8,128)}, f32[3,3,64,64]{3,2,1,0:T(8,128)}) custom-call(f32[288,128]{1,0:T(8,128)S(1)} %sum_four.1.part, f32[288,128]{1,0:T(8,128)S(1)} %collective-permute-done.11.other), custom_call_target="tpu_custom_call" | custom-call | tf_op jit(solution)/shard_map/finish/pallas_call | solution.py:503
  (8 shorter events, 0.2 us)
Async XLA Ops:
  0.6 1.2 %copy-start.3 = (bf16[1,64,16,256]{3,2,1,0:T(8,128)(2,1)S(1)}, bf16[1,64,16,256]{3,2,1,0:T(8,128)(2,1)}, u32[]{:S(2)}) copy-start(bf16[1,64,16,256]{3,2,1,0:T(8,128)(2,1)} %param.5) | copy-start | bytes 1572868
  2.1 3.2 %copy-start.2 = (bf16[1,64,16,256]{3,2,1,0:T(8,128)(2,1)S(1)}, bf16[1,64,16,256]{3,2,1,0:T(8,128)(2,1)}, u32[]{:S(2)}) copy-start(bf16[1,64,16,256]{3,2,1,0:T(8,128)(2,1)} %param.4) | copy-start | bytes 1572868
  2.4 4.9 %collective-permute-start = (bf16[16,8,128]{2,1,0:T(8,128)(2,1)S(1)}, bf16[16,8,128]{2,1,0:T(8,128)(2,1)S(1)}, u32[]{:S(2)}, u32[]{:S(2)}) collective-permute-start(bf16[16,8,128]{2,1,0:T(8,128)(2,1)S(1)} %edges.1), channel_id=1, source_target_pairs={{0,1},{1,0},{2,3},{3,2},{4,5},{5,4},{6,7},{7,6},{8,9},{9,8},{10,11... | collective-permute-start | bytes 98312 | tf_op jit(solution)/shard_map/ppermute | solution.py:35
  5.9 0.9 %copy-start = (bf16[3,3,64,64]{3,2,1,0:T(8,128)(2,1)S(1)}, bf16[3,3,64,64]{3,2,1,0:T(8,128)(2,1)}, u32[]{:S(2)}) copy-start(bf16[3,3,64,64]{3,2,1,0:T(8,128)(2,1)} %k1.1) | copy-start | bytes 221188
  6.0 1.0 %copy-start.1 = (bf16[3,3,64,64]{3,2,1,0:T(8,128)(2,1)S(1)}, bf16[3,3,64,64]{3,2,1,0:T(8,128)(2,1)}, u32[]{:S(2)}) copy-start(bf16[3,3,64,64]{3,2,1,0:T(8,128)(2,1)} %k2.1) | copy-start | bytes 221188
  7.4 8.7 %collective-permute-start.1 = (bf16[3,272,128]{2,1,0:T(8,128)(2,1)S(1)}, bf16[3,272,128]{2,1,0:T(8,128)(2,1)S(1)}, u32[]{:S(2)}, u32[]{:S(2)}) collective-permute-start(bf16[3,272,128]{2,1,0:T(8,128)(2,1)S(1)} %get-tuple-element.26), channel_id=1, source_target_pairs={{0,2},{2,0},{4,6},{6,4},{8,10},{10,8},{12,14},{14,12},{1,3},{3,1},... | collective-permute-start | bytes 626696 | tf_op jit(solution)/shard_map/ppermute | solution.py:567
  9.4 6.7 %collective-permute-start.2 = (bf16[2,272,128]{2,1,0:T(8,128)(2,1)S(1)}, bf16[2,272,128]{2,1,0:T(8,128)(2,1)S(1)}, u32[]{:S(2)}, u32[]{:S(2)}) collective-permute-start(bf16[2,272,128]{2,1,0:T(8,128)(2,1)S(1)} %get-tuple-element.27), channel_id=1, source_target_pairs={{2,4},{4,2},{6,8},{8,6},{10,12},{12,10},{3,5},{5,3},{7,9},{9,7},{1... | collective-permute-start | bytes 417800 | tf_op jit(solution)/shard_map/ppermute | solution.py:568
  17.9 1.4 %collective-permute-start.4 = (f32[288,128]{1,0:T(8,128)S(1)}, f32[288,128]{1,0:T(8,128)S(1)}, u32[]{:S(2)}, u32[]{:S(2)}) collective-permute-start(f32[288,128]{1,0:T(8,128)S(1)} %get-tuple-element.41), channel_id=1, source_target_pairs={{0,16},{16,0},{1,17},{17,1},{2,18},{18,2},{3,19},{19,3},{4,20},{20... | collective-permute-start | bytes 442376 | tf_op jit(solution)/shard_map/ppermute | solution.py:518
  19.4 7.2 %collective-permute-start.7 = (bf16[288,128]{1,0:T(8,128)(2,1)S(1)}, bf16[288,128]{1,0:T(8,128)(2,1)S(1)}, u32[]{:S(2)}, u32[]{:S(2)}) collective-permute-start(bf16[288,128]{1,0:T(8,128)(2,1)S(1)} %add_convert_fusion.1), channel_id=1, source_target_pairs={{0,12},{1,13},{2,14},{3,15},{4,8},{5,9},{6,10},{7,11},{8,4},{9,5},... | collective-permute-start | bytes 221192 | tf_op jit(solution)/shard_map/ppermute | solution.py:544
  24.2 5.4 %collective-permute-start.6 = (bf16[288,128]{1,0:T(8,128)(2,1)S(1)}, bf16[288,128]{1,0:T(8,128)(2,1)S(1)}, u32[]{:S(2)}, u32[]{:S(2)}) collective-permute-start(bf16[288,128]{1,0:T(8,128)(2,1)S(1)} %add_convert_fusion.1), channel_id=1, source_target_pairs={{0,8},{1,9},{2,10},{3,11},{4,12},{5,13},{6,14},{7,15},{8,0},{9,1},... | collective-permute-start | bytes 221192 | tf_op jit(solution)/shard_map/ppermute | solution.py:544
  24.2 5.4 %collective-permute-start.5 = (bf16[288,128]{1,0:T(8,128)(2,1)S(1)}, bf16[288,128]{1,0:T(8,128)(2,1)S(1)}, u32[]{:S(2)}, u32[]{:S(2)}) collective-permute-start(bf16[288,128]{1,0:T(8,128)(2,1)S(1)} %add_convert_fusion.1), channel_id=1, source_target_pairs={{0,4},{1,5},{2,6},{3,7},{4,0},{5,1},{6,2},{7,3},{8,12},{9,13},{10,... | collective-permute-start | bytes 221192 | tf_op jit(solution)/shard_map/ppermute | solution.py:544
  24.8 8.3 %collective-permute-start.3 = (bf16[144,128]{1,0:T(8,128)(2,1)S(1)}, bf16[144,128]{1,0:T(8,128)(2,1)S(1)}, u32[]{:S(2)}, u32[]{:S(2)}) collective-permute-start(bf16[144,128]{1,0:T(8,128)(2,1)S(1)} %get-tuple-element.38), channel_id=1, source_target_pairs={{2,4},{4,2},{6,8},{8,6},{10,12},{12,10},{3,5},{5,3},{7,9},{9,7},{1... | collective-permute-start | bytes 110600 | tf_op jit(solution)/shard_map/ppermute | solution.py:577
  29.6 5.3 %collective-permute-start.10 = (bf16[288,128]{1,0:T(8,128)(2,1)S(1)}, bf16[288,128]{1,0:T(8,128)(2,1)S(1)}, u32[]{:S(2)}, u32[]{:S(2)}) collective-permute-start(bf16[288,128]{1,0:T(8,128)(2,1)S(1)} %add_convert_fusion.own), channel_id=1, source_target_pairs={{0,3},{1,2},{2,1},{3,0},{4,7},{5,6},{6,5},{7,4},{8,11},{9,10},{10,... | collective-permute-start | bytes 221192 | tf_op jit(solution)/shard_map/ppermute | solution.py:544
  30.6 4.4 %collective-permute-start.9 = (bf16[288,128]{1,0:T(8,128)(2,1)S(1)}, bf16[288,128]{1,0:T(8,128)(2,1)S(1)}, u32[]{:S(2)}, u32[]{:S(2)}) collective-permute-start(bf16[288,128]{1,0:T(8,128)(2,1)S(1)} %add_convert_fusion.own), channel_id=1, source_target_pairs={{0,1},{1,0},{2,3},{3,2},{4,5},{5,4},{6,7},{7,6},{8,9},{9,8},{10,11... | collective-permute-start | bytes 221192 | tf_op jit(solution)/shard_map/ppermute | solution.py:544
  31.3 4.4 %collective-permute-start.8 = (bf16[288,128]{1,0:T(8,128)(2,1)S(1)}, bf16[288,128]{1,0:T(8,128)(2,1)S(1)}, u32[]{:S(2)}, u32[]{:S(2)}) collective-permute-start(bf16[288,128]{1,0:T(8,128)(2,1)S(1)} %add_convert_fusion.own), channel_id=1, source_target_pairs={{0,2},{1,3},{2,0},{3,1},{4,6},{5,7},{6,4},{7,5},{8,10},{9,11},{10,... | collective-permute-start | bytes 221192 | tf_op jit(solution)/shard_map/ppermute | solution.py:544
  35.7 1.4 %collective-permute-start.11 = (f32[288,128]{1,0:T(8,128)S(1)}, f32[288,128]{1,0:T(8,128)S(1)}, u32[]{:S(2)}, u32[]{:S(2)}) collective-permute-start(f32[288,128]{1,0:T(8,128)S(1)} %sum_four.1.part), channel_id=1, source_target_pairs={{0,16},{16,0},{1,17},{17,1},{2,18},{18,2},{3,19},{19,3},{4,20},{20... | collective-permute-start | bytes 442376 | tf_op jit(solution)/shard_map/ppermute | solution.py:552

commit v13 on v12

--- a/solution.py
+++ b/solution.py
@@ -272,7 +272,7 @@
     for tap in range(9):
         one, two = blocks[tap][:half], blocks[tap][half:]
         mine[tap * half : (tap + 1) * half] = jnp.where(second, two, one)
-        other[tap * half : (tap + 1) * half] = jnp.where(second, one, two)
+        other[tap * half : (tap + 1) * half] = jnp.where(second, one, two).astype(BF)
 
 
 def half_lanes(side):
@@ -441,7 +441,7 @@
             jax.ShapeDtypeStruct((2, wide, LANES), BF),
             row,
             jax.ShapeDtypeStruct((9 * HALF // 2, LANES), F32),
-            jax.ShapeDtypeStruct((9 * HALF // 2, LANES), F32),
+            jax.ShapeDtypeStruct((9 * HALF // 2, LANES), BF),
         ),
         scratch_shapes=[
             pltpu.VMEM((2, 3, wide, LANES), BF),
@@ -515,7 +515,7 @@
         first = lax.axis_index("dp") == 0
         both = lax.psum([jnp.where(first, mine, other), jnp.where(first, other, mine)], AXES)
         return jnp.where(first, *both), jnp.where(first, both[1], both[0])
-    part = mine + lax.ppermute(other, "dp", swap_cores)
+    part = mine + lax.ppermute(other, "dp", swap_cores).astype(F32)
     across = [(0, 1 << b) for b in range(sizes[2].bit_length() - 1)]
     down = [(1 << b, 0) for b in range(sizes[1].bit_length() - 1)]
     bits = []

time: 38.4 us -> 38.3 us (level)
  no operation moved by 1% of the time
where the time goes in v13:
time: 38.3 us; the launch traced here: 38.1 us
  starting transfers between devices  15.4 us (40%)
  waiting for transfers between devices  10 us (26%)
  Pallas kernels  7.32 us (19%)
  local copies, waits for them, and re-layouts  4.1 us (11%)
  between operations  0.86 us (2%)
    ppermute x6, starting transfers between devices, reduced(): got.append(lax.ppermute(low, AXES, perm))  9 us
    ppermute x6, waiting for transfers between devices, reduced(): got.append(lax.ppermute(low, AXES, perm))  5.5 us
    unnamed x12, local copies, waits for them, and re-layouts  3.29 us
    ppermute x1, waiting for transfers between devices, shards(): got_near = lax.ppermute(sent_near, 'row', neighbours('row', 0))  3.2 us
    ppermute x1, starting transfers between devices, swap(): got.append(lax.ppermute(turn(low, high, is_low(axis, parity)), axis, perm))  2.98 us
    pallas_call x1, Pallas kernels, inner(): pl.pallas_call(inner_body, out_shape=(jax.ShapeDtypeStruct((2, wide, LANE...  2.8 us
    ppermute x1, starting transfers between devices, shards(): got_near = lax.ppermute(sent_near, 'row', neighbours('row', 0))  1.99 us
    pallas_call x1, Pallas kernels, outer(): pl.pallas_call(rim_body, out_shape=(jax.ShapeDtypeStruct(shifts(2), BF),...  1.7 us
  transfers between devices with their start and end apart: 12, of which 8 were waited for; matrix products, arithmetic and copies ran while one was open for 6% of the time, Pallas kernels for 11%

profile of v13, /device:TPU:0, one launch (start us, length us, event | category | flops | bytes accessed | tf_op | source)
XLA Modules:
  0.0 38.1 jit_solution(7630550591981098772)
XLA Ops:
  0.6 0.0 copy-start.3
  0.7 1.2 %constant_dynamic-update-slice_fusion.1 = bf16[1,64,32,256]{3,2,1,0:T(8,128)(2,1)S(1)} fusion(bf16[1,64,16,256]{3,2,1,0:T(8,128)(2,1)} %param.4), kind=kLoop, calls=%fused_computation.13 | loop fusion | bytes 1048576
  1.8 0.0 copy-done.3
  1.8 0.1 constant_dynamic-update-slice_fusion
  1.9 0.2 slice_select_fusion.refs_0_
  2.1 0.0 copy-start.2
  2.1 0.2 edges.1
  2.4 3.0 %collective-permute-start = (bf16[16,8,128]{2,1,0:T(8,128)(2,1)S(1)}, bf16[16,8,128]{2,1,0:T(8,128)(2,1)S(1)}, u32[]{:S(2)}, u32[]{:S(2)}) collective-permute-start(bf16[16,8,128]{2,1,0:T(8,128)(2,1)S(1)} %edges.1), channel_id=1, source_target_pairs={{0,1},{1,0},{2,3},{3,2},{4,5},{5,4},{6,7},{7,6},{8,9},{9,8},{10,11... | collective-permute-start | bytes 98312 | tf_op jit(solution)/shard_map/ppermute | solution.py:35
  5.3 0.0 copy-done.2
  5.3 0.2 copy.10
  5.5 0.2 copy.11
  5.7 0.3 copy.16.f
  5.9 0.0 copy-start
  6.0 0.0 copy-start.1
  6.0 0.3 copy.17.g
  6.3 0.6 %copy-done = bf16[3,3,64,64]{3,2,1,0:T(8,128)(2,1)S(1)} copy-done((bf16[3,3,64,64]{3,2,1,0:T(8,128)(2,1)S(1)}, bf16[3,3,64,64]{3,2,1,0:T(8,128)(2,1)}, u32[]{:S(2)}) %copy-start) | copy-done | bytes 73752
  6.9 0.1 copy-done.1
  6.9 0.3 prep.1
  7.3 0.0 collective-permute-done
  7.3 0.1 frame.1
  7.4 2.0 %collective-permute-start.1 = (bf16[3,272,128]{2,1,0:T(8,128)(2,1)S(1)}, bf16[3,272,128]{2,1,0:T(8,128)(2,1)S(1)}, u32[]{:S(2)}, u32[]{:S(2)}) collective-permute-start(bf16[3,272,128]{2,1,0:T(8,128)(2,1)S(1)} %get-tuple-element.26), channel_id=1, source_target_pairs={{0,2},{2,0},{4,6},{6,4},{8,10},{10,8},{12,14},{14,12},{1,3},{3,1},... | collective-permute-start | bytes 626696 | tf_op jit(solution)/shard_map/ppermute | solution.py:567
  9.4 0.7 %collective-permute-start.2 = (bf16[2,272,128]{2,1,0:T(8,128)(2,1)S(1)}, bf16[2,272,128]{2,1,0:T(8,128)(2,1)S(1)}, u32[]{:S(2)}, u32[]{:S(2)}) collective-permute-start(bf16[2,272,128]{2,1,0:T(8,128)(2,1)S(1)} %get-tuple-element.27), channel_id=1, source_target_pairs={{2,4},{4,2},{6,8},{8,6},{10,12},{12,10},{3,5},{5,3},{7,9},{9,7},{1... | collective-permute-start | bytes 417800 | tf_op jit(solution)/shard_map/ppermute | solution.py:568
  10.1 2.8 %inner.1 = (bf16[2,272,128]{2,1,0:T(8,128)(2,1)S(1)}, bf16[2,3,272,128]{3,2,1,0:T(8,128)(2,1)S(1)}, f32[2,272,128]{2,1,0:T(8,128)S(1)}, bf16[5,3,272,128]{3,2,1,...) custom-call(bf16[8,256,128]{2,1,0:T(8,128)(2,1)S(1)} %copy.16.f, bf16[8,256,128]{2,1,0:T(8,128)(2,1)S(1)} %copy.17.g, ...), custom_call_target="tpu_custom_call" | custom-call | flops 1176502272 | bytes 4194304 | tf_op jit(solution)/shard_map/inner/pallas_call | solution.py:406
  12.9 3.2 %collective-permute-done.1 = bf16[3,272,128]{2,1,0:T(8,128)(2,1)S(1)} collective-permute-done((bf16[3,272,128]{2,1,0:T(8,128)(2,1)S(1)}, bf16[3,272,128]{2,1,0:T(8,128)(2,1)S(1)}, u32[]{:S(2)}, u32[]{:S(2)}) %collective-permute-start.1) | collective-permute-done | bytes 208928 | tf_op jit(solution)/shard_map/ppermute | solution.py:567
  16.1 0.0 collective-permute-done.2
  16.2 1.7 %outer.1 = (bf16[2,3,272,128]{3,2,1,0:T(8,128)(2,1)S(1)}, bf16[2,272,128]{2,1,0:T(8,128)(2,1)S(1)}, bf16[144,128]{1,0:T(8,128)(2,1)S(1)}, f32[288,128]{1,0:T(8,128)S(1)}, bf16[288,128]{1,0:T(8,128)(2,1)S(1)}) custom-call(bf16[8,256,128]{2,1,0:T(8,128)(2,1)S(1)} %copy.16.f, bf16[8,256,128]{2,1,0:T(8,128)(2,1)S(1)} %copy.17.g, ...), custom_call_target="tpu_custom_call" | custom-call | flops 748683264 | bytes 4194304 | tf_op jit(solution)/shard_map/outer/pallas_call | solution.py:437
  17.9 0.1 collective-permute-start.4
  18.0 1.3 %collective-permute-done.4 = bf16[288,128]{1,0:T(8,128)(2,1)S(1)} collective-permute-done((bf16[288,128]{1,0:T(8,128)(2,1)S(1)}, bf16[288,128]{1,0:T(8,128)(2,1)S(1)}, u32[]{:S(2)}, u32[]{:S(2)}) %collective-permute-start.4) | collective-permute-done | bytes 73760 | tf_op jit(solution)/shard_map/ppermute | solution.py:518
  19.3 4.8 %collective-permute-start.7 = (bf16[288,128]{1,0:T(8,128)(2,1)S(1)}, bf16[288,128]{1,0:T(8,128)(2,1)S(1)}, u32[]{:S(2)}, u32[]{:S(2)}) collective-permute-start(bf16[288,128]{1,0:T(8,128)(2,1)S(1)} %add_convert_fusion.1), channel_id=1, source_target_pairs={{0,12},{1,13},{2,14},{3,15},{4,8},{5,9},{6,10},{7,11},{8,4},{9,5},... | collective-permute-start | bytes 221192 | tf_op jit(solution)/shard_map/ppermute | solution.py:544
  24.1 0.0 collective-permute-start.6
  24.1 0.6 %collective-permute-start.5 = (bf16[288,128]{1,0:T(8,128)(2,1)S(1)}, bf16[288,128]{1,0:T(8,128)(2,1)S(1)}, u32[]{:S(2)}, u32[]{:S(2)}) collective-permute-start(bf16[288,128]{1,0:T(8,128)(2,1)S(1)} %add_convert_fusion.1), channel_id=1, source_target_pairs={{0,4},{1,5},{2,6},{3,7},{4,0},{5,1},{6,2},{7,3},{8,12},{9,13},{10,... | collective-permute-start | bytes 221192 | tf_op jit(solution)/shard_map/ppermute | solution.py:544
  24.7 0.7 %collective-permute-start.3 = (bf16[144,128]{1,0:T(8,128)(2,1)S(1)}, bf16[144,128]{1,0:T(8,128)(2,1)S(1)}, u32[]{:S(2)}, u32[]{:S(2)}) collective-permute-start(bf16[144,128]{1,0:T(8,128)(2,1)S(1)} %get-tuple-element.38), channel_id=1, source_target_pairs={{2,4},{4,2},{6,8},{8,6},{10,12},{12,10},{3,5},{5,3},{7,9},{9,7},{1... | collective-permute-start | bytes 110600 | tf_op jit(solution)/shard_map/ppermute | solution.py:577
  25.4 1.1 %collective-permute-done.7 = bf16[288,128]{1,0:T(8,128)(2,1)S(1)} collective-permute-done((bf16[288,128]{1,0:T(8,128)(2,1)S(1)}, bf16[288,128]{1,0:T(8,128)(2,1)S(1)}, u32[]{:S(2)}, u32[]{:S(2)}) %collective-permute-start.7) | collective-permute-done | bytes 73760 | tf_op jit(solution)/shard_map/ppermute | solution.py:544
  26.5 2.9 %collective-permute-done.6 = bf16[288,128]{1,0:T(8,128)(2,1)S(1)} collective-permute-done((bf16[288,128]{1,0:T(8,128)(2,1)S(1)}, bf16[288,128]{1,0:T(8,128)(2,1)S(1)}, u32[]{:S(2)}, u32[]{:S(2)}) %collective-permute-start.6) | collective-permute-done | bytes 73760 | tf_op jit(solution)/shard_map/ppermute | solution.py:544
  29.4 0.0 collective-permute-done.5
  29.5 1.1 %collective-permute-start.10 = (bf16[288,128]{1,0:T(8,128)(2,1)S(1)}, bf16[288,128]{1,0:T(8,128)(2,1)S(1)}, u32[]{:S(2)}, u32[]{:S(2)}) collective-permute-start(bf16[288,128]{1,0:T(8,128)(2,1)S(1)} %add_convert_fusion.own), channel_id=1, source_target_pairs={{0,3},{1,2},{2,1},{3,0},{4,7},{5,6},{6,5},{7,4},{8,11},{9,10},{10,... | collective-permute-start | bytes 221192 | tf_op jit(solution)/shard_map/ppermute | solution.py:544
  30.5 0.7 %collective-permute-start.9 = (bf16[288,128]{1,0:T(8,128)(2,1)S(1)}, bf16[288,128]{1,0:T(8,128)(2,1)S(1)}, u32[]{:S(2)}, u32[]{:S(2)}) collective-permute-start(bf16[288,128]{1,0:T(8,128)(2,1)S(1)} %add_convert_fusion.own), channel_id=1, source_target_pairs={{0,1},{1,0},{2,3},{3,2},{4,5},{5,4},{6,7},{7,6},{8,9},{9,8},{10,11... | collective-permute-start | bytes 221192 | tf_op jit(solution)/shard_map/ppermute | solution.py:544
  31.2 1.8 %collective-permute-start.8 = (bf16[288,128]{1,0:T(8,128)(2,1)S(1)}, bf16[288,128]{1,0:T(8,128)(2,1)S(1)}, u32[]{:S(2)}, u32[]{:S(2)}) collective-permute-start(bf16[288,128]{1,0:T(8,128)(2,1)S(1)} %add_convert_fusion.own), channel_id=1, source_target_pairs={{0,2},{1,3},{2,0},{3,1},{4,6},{5,7},{6,4},{7,5},{8,10},{9,11},{10,... | collective-permute-start | bytes 221192 | tf_op jit(solution)/shard_map/ppermute | solution.py:544
  33.0 0.0 collective-permute-done.3.row
  33.0 1.1 %last.1 = (bf16[8,256,128]{2,1,0:T(8,128)(2,1)S(1)}, f32[8,128]{1,0:T(8,128)S(1)}) custom-call(bf16[2,272,128]{2,1,0:T(8,128)(2,1)S(1)} %get-tuple-element.35.end, bf16[2,3,272,128]{3,2,1,0:T(8,128)(2,1)S(1)} %get-tuple-element.36.ds1_next, bf16[5,3,272,128]{3,2,1,0:T(8,128)(2,1)S(1)} %get-tuple-element.37.ds1, ...), custom_call_target="tpu_custom_call" | custom-call | flops 427819008 | bytes 4194304 | tf_op jit(solution)/shard_map/last/pallas_call | solution.py:463
  34.1 0.7 %collective-permute-done.10.three = bf16[288,128]{1,0:T(8,128)(2,1)S(1)} collective-permute-done((bf16[288,128]{1,0:T(8,128)(2,1)S(1)}, bf16[288,128]{1,0:T(8,128)(2,1)S(1)}, u32[]{:S(2)}, u32[]{:S(2)}) %collective-permute-start.10) | collective-permute-done | bytes 73760 | tf_op jit(solution)/shard_map/ppermute | solution.py:544
  34.8 0.1 collective-permute-done.9.two
  34.9 0.7 %collective-permute-done.8.one = bf16[288,128]{1,0:T(8,128)(2,1)S(1)} collective-permute-done((bf16[288,128]{1,0:T(8,128)(2,1)S(1)}, bf16[288,128]{1,0:T(8,128)(2,1)S(1)}, u32[]{:S(2)}, u32[]{:S(2)}) %collective-permute-start.8) | collective-permute-done | bytes 73760 | tf_op jit(solution)/shard_map/ppermute | solution.py:544
  35.6 0.1 collective-permute-start.11
  35.7 0.2 copy.18
  35.9 1.1 %copy.19 = bf16[1,64,16,256]{3,2,1,0:T(8,128)(2,1)} copy(bf16[1,64,16,256]{3,1,2,0:T(8,128)(2,1)S(1)} %bitcast.17) | data formatting | bytes 1048576
  37.0 0.1 collective-permute-done.11.other
  37.0 1.0 %finish.1 = (f32[3,3,64,64]{3,2,1,0:T(8,128)}, f32[3,3,64,64]{3,2,1,0:T(8,128)}) custom-call(f32[288,128]{1,0:T(8,128)S(1)} %sum_four.1.part, f32[288,128]{1,0:T(8,128)S(1)} %collective-permute-done.11.other), custom_call_target="tpu_custom_call" | custom-call | tf_op jit(solution)/shard_map/finish/pallas_call | solution.py:503
  (8 shorter events, 0.2 us)
Async XLA Ops:
  0.6 1.2 %copy-start.3 = (bf16[1,64,16,256]{3,2,1,0:T(8,128)(2,1)S(1)}, bf16[1,64,16,256]{3,2,1,0:T(8,128)(2,1)}, u32[]{:S(2)}) copy-start(bf16[1,64,16,256]{3,2,1,0:T(8,128)(2,1)} %param.5) | copy-start | bytes 1572868
  2.1 3.2 %copy-start.2 = (bf16[1,64,16,256]{3,2,1,0:T(8,128)(2,1)S(1)}, bf16[1,64,16,256]{3,2,1,0:T(8,128)(2,1)}, u32[]{:S(2)}) copy-start(bf16[1,64,16,256]{3,2,1,0:T(8,128)(2,1)} %param.4) | copy-start | bytes 1572868
  2.4 4.9 %collective-permute-start = (bf16[16,8,128]{2,1,0:T(8,128)(2,1)S(1)}, bf16[16,8,128]{2,1,0:T(8,128)(2,1)S(1)}, u32[]{:S(2)}, u32[]{:S(2)}) collective-permute-start(bf16[16,8,128]{2,1,0:T(8,128)(2,1)S(1)} %edges.1), channel_id=1, source_target_pairs={{0,1},{1,0},{2,3},{3,2},{4,5},{5,4},{6,7},{7,6},{8,9},{9,8},{10,11... | collective-permute-start | bytes 98312 | tf_op jit(solution)/shard_map/ppermute | solution.py:35
  5.9 0.9 %copy-start = (bf16[3,3,64,64]{3,2,1,0:T(8,128)(2,1)S(1)}, bf16[3,3,64,64]{3,2,1,0:T(8,128)(2,1)}, u32[]{:S(2)}) copy-start(bf16[3,3,64,64]{3,2,1,0:T(8,128)(2,1)} %k1.1) | copy-start | bytes 221188
  6.0 1.0 %copy-start.1 = (bf16[3,3,64,64]{3,2,1,0:T(8,128)(2,1)S(1)}, bf16[3,3,64,64]{3,2,1,0:T(8,128)(2,1)}, u32[]{:S(2)}) copy-start(bf16[3,3,64,64]{3,2,1,0:T(8,128)(2,1)} %k2.1) | copy-start | bytes 221188
  7.4 8.7 %collective-permute-start.1 = (bf16[3,272,128]{2,1,0:T(8,128)(2,1)S(1)}, bf16[3,272,128]{2,1,0:T(8,128)(2,1)S(1)}, u32[]{:S(2)}, u32[]{:S(2)}) collective-permute-start(bf16[3,272,128]{2,1,0:T(8,128)(2,1)S(1)} %get-tuple-element.26), channel_id=1, source_target_pairs={{0,2},{2,0},{4,6},{6,4},{8,10},{10,8},{12,14},{14,12},{1,3},{3,1},... | collective-permute-start | bytes 626696 | tf_op jit(solution)/shard_map/ppermute | solution.py:567
  9.4 6.7 %collective-permute-start.2 = (bf16[2,272,128]{2,1,0:T(8,128)(2,1)S(1)}, bf16[2,272,128]{2,1,0:T(8,128)(2,1)S(1)}, u32[]{:S(2)}, u32[]{:S(2)}) collective-permute-start(bf16[2,272,128]{2,1,0:T(8,128)(2,1)S(1)} %get-tuple-element.27), channel_id=1, source_target_pairs={{2,4},{4,2},{6,8},{8,6},{10,12},{12,10},{3,5},{5,3},{7,9},{9,7},{1... | collective-permute-start | bytes 417800 | tf_op jit(solution)/shard_map/ppermute | solution.py:568
  17.9 1.3 %collective-permute-start.4 = (bf16[288,128]{1,0:T(8,128)(2,1)S(1)}, bf16[288,128]{1,0:T(8,128)(2,1)S(1)}, u32[]{:S(2)}, u32[]{:S(2)}) collective-permute-start(bf16[288,128]{1,0:T(8,128)(2,1)S(1)} %get-tuple-element.41), channel_id=1, source_target_pairs={{0,16},{16,0},{1,17},{17,1},{2,18},{18,2},{3,19},{19,3},{4,20},{20... | collective-permute-start | bytes 221192 | tf_op jit(solution)/shard_map/ppermute | solution.py:518
  19.3 7.2 %collective-permute-start.7 = (bf16[288,128]{1,0:T(8,128)(2,1)S(1)}, bf16[288,128]{1,0:T(8,128)(2,1)S(1)}, u32[]{:S(2)}, u32[]{:S(2)}) collective-permute-start(bf16[288,128]{1,0:T(8,128)(2,1)S(1)} %add_convert_fusion.1), channel_id=1, source_target_pairs={{0,12},{1,13},{2,14},{3,15},{4,8},{5,9},{6,10},{7,11},{8,4},{9,5},... | collective-permute-start | bytes 221192 | tf_op jit(solution)/shard_map/ppermute | solution.py:544
  24.1 5.3 %collective-permute-start.6 = (bf16[288,128]{1,0:T(8,128)(2,1)S(1)}, bf16[288,128]{1,0:T(8,128)(2,1)S(1)}, u32[]{:S(2)}, u32[]{:S(2)}) collective-permute-start(bf16[288,128]{1,0:T(8,128)(2,1)S(1)} %add_convert_fusion.1), channel_id=1, source_target_pairs={{0,8},{1,9},{2,10},{3,11},{4,12},{5,13},{6,14},{7,15},{8,0},{9,1},... | collective-permute-start | bytes 221192 | tf_op jit(solution)/shard_map/ppermute | solution.py:544
  24.1 5.3 %collective-permute-start.5 = (bf16[288,128]{1,0:T(8,128)(2,1)S(1)}, bf16[288,128]{1,0:T(8,128)(2,1)S(1)}, u32[]{:S(2)}, u32[]{:S(2)}) collective-permute-start(bf16[288,128]{1,0:T(8,128)(2,1)S(1)} %add_convert_fusion.1), channel_id=1, source_target_pairs={{0,4},{1,5},{2,6},{3,7},{4,0},{5,1},{6,2},{7,3},{8,12},{9,13},{10,... | collective-permute-start | bytes 221192 | tf_op jit(solution)/shard_map/ppermute | solution.py:544
  24.7 8.3 %collective-permute-start.3 = (bf16[144,128]{1,0:T(8,128)(2,1)S(1)}, bf16[144,128]{1,0:T(8,128)(2,1)S(1)}, u32[]{:S(2)}, u32[]{:S(2)}) collective-permute-start(bf16[144,128]{1,0:T(8,128)(2,1)S(1)} %get-tuple-element.38), channel_id=1, source_target_pairs={{2,4},{4,2},{6,8},{8,6},{10,12},{12,10},{3,5},{5,3},{7,9},{9,7},{1... | collective-permute-start | bytes 110600 | tf_op jit(solution)/shard_map/ppermute | solution.py:577
  29.5 5.3 %collective-permute-start.10 = (bf16[288,128]{1,0:T(8,128)(2,1)S(1)}, bf16[288,128]{1,0:T(8,128)(2,1)S(1)}, u32[]{:S(2)}, u32[]{:S(2)}) collective-permute-start(bf16[288,128]{1,0:T(8,128)(2,1)S(1)} %add_convert_fusion.own), channel_id=1, source_target_pairs={{0,3},{1,2},{2,1},{3,0},{4,7},{5,6},{6,5},{7,4},{8,11},{9,10},{10,... | collective-permute-start | bytes 221192 | tf_op jit(solution)/shard_map/ppermute | solution.py:544
  30.5 4.4 %collective-permute-start.9 = (bf16[288,128]{1,0:T(8,128)(2,1)S(1)}, bf16[288,128]{1,0:T(8,128)(2,1)S(1)}, u32[]{:S(2)}, u32[]{:S(2)}) collective-permute-start(bf16[288,128]{1,0:T(8,128)(2,1)S(1)} %add_convert_fusion.own), channel_id=1, source_target_pairs={{0,1},{1,0},{2,3},{3,2},{4,5},{5,4},{6,7},{7,6},{8,9},{9,8},{10,11... | collective-permute-start | bytes 221192 | tf_op jit(solution)/shard_map/ppermute | solution.py:544
  31.2 4.4 %collective-permute-start.8 = (bf16[288,128]{1,0:T(8,128)(2,1)S(1)}, bf16[288,128]{1,0:T(8,128)(2,1)S(1)}, u32[]{:S(2)}, u32[]{:S(2)}) collective-permute-start(bf16[288,128]{1,0:T(8,128)(2,1)S(1)} %add_convert_fusion.own), channel_id=1, source_target_pairs={{0,2},{1,3},{2,0},{3,1},{4,6},{5,7},{6,4},{7,5},{8,10},{9,11},{10,... | collective-permute-start | bytes 221192 | tf_op jit(solution)/shard_map/ppermute | solution.py:544
  35.6 1.4 %collective-permute-start.11 = (f32[288,128]{1,0:T(8,128)S(1)}, f32[288,128]{1,0:T(8,128)S(1)}, u32[]{:S(2)}, u32[]{:S(2)}) collective-permute-start(f32[288,128]{1,0:T(8,128)S(1)} %sum_four.1.part), channel_id=1, source_target_pairs={{0,16},{16,0},{1,17},{17,1},{2,18},{18,2},{3,19},{19,3},{4,20},{20... | collective-permute-start | bytes 442376 | tf_op jit(solution)/shard_map/ppermute | solution.py:552
